TPU v7x, 32 devices: a whole 2x2x4 slice. The times are simulated.
32 devices in a mesh: group: 2 (over x), pool: 8 (over z, y), tp: 2 (over core).
Axes of the slice: x: 2, y: 2, z: 4, core: 2. Of those that a mesh axis runs over, the one named last changes fastest.
Arguments:
- prompt_kv: bfloat16 [256, 2, 4, 128, 128], P(('group', 'pool'), None, 'tp'), parts along dimension 0, may hold values from -6 to 6
- prompt_lengths: int32 [16, 4], P(('group', 'pool')), parts along dimension 0, may hold values from 1 to 1664, as said below
- page_slot: int32 [256], P(('group', 'pool')), parts along dimension 0, may hold values from 0 to 383, as said below
- cache_kv: bfloat16 [768, 2, 4, 128, 128], P(('group', 'pool'), None, 'tp'), parts along dimension 0, may hold values from -6 to 6
- cache_fill: int32 [768], P(('group', 'pool')), parts along dimension 0, may hold values from 0 to 128, as said below
- page_table: int32 [256, 3], P(('group', 'pool')), parts along dimension 0, may hold values from 0 to 47, as said below
- context_lengths: int32 [256], P(('group', 'pool')), parts along dimension 0, may hold values from 1 to 384
- queries: bfloat16 [2, 256, 4096], P(None, ('group', 'pool'), 'tp'), parts along dimension 1
- new_kv: bfloat16 [2, 256, 2, 4, 128], P(None, ('group', 'pool'), None, 'tp'), parts along dimension 1, may hold values from -6 to 6
- out_weight: bfloat16 [4096, 8192], P('tp', 'pool'), may hold values from -0.09375 to 0.09375
Outputs:
- projected: bfloat16 [2, 256, 8192], P(None, 'group', ('pool', 'tp')), parts along dimension 1
There are 2 independent parts, one for each index of `group`. A program takes and returns all parts, laid end to end along the dimension named above; an argument that names none is the same for every part. Nothing has to cross between parts.
Inputs may be any that keep to these rules, and one draw needn't show every extreme that they name: `prompt_lengths`: each device's prompts take exactly 16 pages in all. `page_slot`: slots are distinct; each lands in a slot whose cache_fill is 0; every device receives exactly 16 pages; a device sends 0 or exactly 2 pages to each device. `cache_fill`: exactly 16 slots of each device are 0. `page_table`: each device's table uses each of its slots once.
All inputs are finite; a program needn't handle non-finite values.
Results may differ from a plain program's by a relative error of at most 0.0067.
Values may be sent and summed in bfloat16 or wider, within the bound.
No kernel may reach another device: no remote copies, remote signals or barrier semaphores. Data moves between devices by JAX's collectives and lax.ppermute only.
A program may use at most 128 MiB of HBM per device.

v0:
```python
import jax
import jax.numpy as jnp
from jax import lax
from jax.sharding import PartitionSpec as P

rope_base = 500000.0


def rotate(x, pos):
    half = x.shape[-1] // 2
    freq = rope_base ** (-(jnp.arange(half, dtype=jnp.float32) * 2.0) / x.shape[-1])
    angle = pos[..., None].astype(jnp.float32) * freq
    first, second = (x[..., :half], x[..., half:])
    return jnp.concatenate(
        [
            first * jnp.cos(angle) - second * jnp.sin(angle),
            second * jnp.cos(angle) + first * jnp.sin(angle),
        ],
        -1,
    )


def page_layout(lengths, pages, page_len):
    counts = (lengths + page_len - 1) // page_len
    ends = jnp.cumsum(counts)
    index = jnp.arange(pages)
    owner = jnp.sum(ends[None, :] <= index[:, None], axis=1)
    onehot = owner[:, None] == jnp.arange(lengths.shape[0])[None, :]
    first = jnp.sum(jnp.where(onehot, (ends - counts)[None, :], 0), axis=1)
    length = jnp.sum(jnp.where(onehot, lengths[None, :], 0), axis=1)
    start = (index - first) * page_len
    fill = jnp.clip(length - start, 0, page_len)
    return (start, fill)


def attend(cache, fills, page_table, context_lengths, queries, new_kv, page_len):
    rows, most = page_table.shape
    steps = queries.shape[0]
    heads, head_dim = (cache.shape[2], cache.shape[4])
    context = cache[page_table]
    page_fill = fills[page_table]
    offset = jnp.arange(most)[:, None] * page_len + jnp.arange(page_len)[None, :]
    valid = (offset[None] < context_lengths[:, None, None]) & (
        jnp.arange(page_len)[None, None, :] < page_fill[:, :, None]
    )
    grouped = queries.reshape(steps, rows, heads, -1, head_dim)
    scale = head_dim ** (-0.5)
    old = (
        jnp.einsum(
            "srkgd,rjktd->srkgjt", grouped, context[:, :, 0], preferred_element_type=jnp.float32
        )
        * scale
    )
    old = jnp.where(valid[None, :, None, None], old, -jnp.inf)
    position = context_lengths[None, :] + jnp.arange(steps)[:, None]
    fresh_keys = rotate(new_kv[:, :, 0].astype(jnp.float32), position[:, :, None]).astype(
        jnp.bfloat16
    )
    fresh = (
        jnp.einsum("srkgd,urkd->srkgu", grouped, fresh_keys, preferred_element_type=jnp.float32)
        * scale
    )
    causal = jnp.arange(steps)[None, :] <= jnp.arange(steps)[:, None]
    fresh = jnp.where(causal[:, None, None, None, :], fresh, -jnp.inf)
    top = jnp.maximum(jnp.max(old, axis=(4, 5)), jnp.max(fresh, axis=4))
    old_w = jnp.exp(old - top[..., None, None])
    fresh_w = jnp.exp(fresh - top[..., None])
    total = jnp.sum(old_w, axis=(4, 5)) + jnp.sum(fresh_w, axis=4)
    mixed = jnp.einsum(
        "srkgjt,rjktd->srkgd",
        old_w.astype(jnp.bfloat16),
        context[:, :, 1],
        preferred_element_type=jnp.float32,
    )
    mixed = mixed + jnp.einsum(
        "srkgu,urkd->srkgd",
        fresh_w.astype(jnp.bfloat16),
        new_kv[:, :, 1],
        preferred_element_type=jnp.float32,
    )
    return (mixed / total[..., None]).astype(jnp.bfloat16).reshape(steps, rows, -1)


def shards(
    prompt_kv,
    prompt_lengths,
    page_slot,
    cache_kv,
    cache_fill,
    page_table,
    context_lengths,
    queries,
    new_kv,
    out_weight,
):
    npool = lax.axis_size("pool")
    pages = prompt_kv.shape[0]
    page_len = prompt_kv.shape[3]
    cache_pages = cache_kv.shape[0]
    pair_count = (pages + npool - 1) // npool
    start, fill = page_layout(prompt_lengths[0], pages, page_len)
    target = page_slot // cache_pages
    local = page_slot % cache_pages
    earlier = jnp.arange(pages)[None, :] < jnp.arange(pages)[:, None]
    same = target[None, :] == target[:, None]
    rank = jnp.sum(earlier & same, axis=1)
    where_to = target * pair_count + rank
    width = npool * pair_count

    def place(values, empty):
        buffer = jnp.full((width,) + values.shape[1:], empty, values.dtype)
        buffer = buffer.at[where_to].set(values)
        return buffer.reshape((npool, pair_count) + values.shape[1:])

    slot_buffer = place(local, cache_pages)
    fill_buffer = place(fill, 0)
    positions = start[:, None] + jnp.arange(page_len)[None, :]
    keys = rotate(prompt_kv[:, 0].astype(jnp.float32), positions[:, None, :]).astype(jnp.bfloat16)
    moved = jnp.stack([keys, prompt_kv[:, 1]], 1)
    received, slots, fills_in = (
        lax.all_to_all(place(moved, 0.0), "pool", split_axis=0, concat_axis=0, tiled=True),
        lax.all_to_all(slot_buffer, "pool", split_axis=0, concat_axis=0, tiled=True),
        lax.all_to_all(fill_buffer, "pool", split_axis=0, concat_axis=0, tiled=True),
    )
    received = received.reshape((width,) + prompt_kv.shape[1:])
    slots = slots.reshape(width)
    fills_in = fills_in.reshape(width)
    cache = cache_kv.at[slots].set(received, mode="drop")
    fills = cache_fill.at[slots].set(fills_in, mode="drop")
    attention = attend(cache, fills, page_table, context_lengths, queries, new_kv, page_len)
    terms = jnp.einsum(
        "srh,hc->src",
        lax.all_gather(attention, "pool", axis=1, tiled=True),
        out_weight,
        preferred_element_type=jnp.float32,
    )
    return lax.psum_scatter(terms, "tp", scatter_dimension=2, tiled=True).astype(jnp.bfloat16)


def solution(mesh):
    return jax.shard_map(
        shards,
        mesh=mesh,
        in_specs=(
            P(("group", "pool"), None, "tp", None, None),
            P(("group", "pool"), None),
            P(("group", "pool")),
            P(("group", "pool"), None, "tp", None, None),
            P(("group", "pool")),
            P(("group", "pool"), None),
            P(("group", "pool")),
            P(None, ("group", "pool"), "tp"),
            P(None, ("group", "pool"), None, "tp", None),
            P("tp", "pool"),
        ),
        out_specs=P(None, "group", ("pool", "tp")),
        check_vma=False,
    )
```

profile of v0, /device:TPU:0, one launch (start us, length us, event | category | flops | bytes accessed | tf_op | source)
XLA Modules:
  0.0 178.2 jit_solution(16965450455912592160)
XLA Ops:
  6.5 8.2 %copy.104 = bf16[48,2,2,128,128]{4,3,2,1,0:T(8,128)(2,1)} copy(bf16[48,2,2,128,128]{4,3,2,1,0:T(8,128)(2,1)} %param.13) | data formatting | bytes 12582912
  16.0 0.7 all_to_all.15
  16.7 7.3 %all-to-all-start = ((s32[8,1,2]{2,1,0:T(1,128)}), s32[8,1,2]{2,1,0:T(1,128)S(1)}, u32[]{:S(2)}, u32[]{:S(2)}) async-start(s32[8,1,2]{2,1,0:T(1,128)} %bitcast), calls=%async_computation | async-start | bytes 8192 | tf_op jit(solution)/shard_map/all_to_all | solution.py:122
  24.3 3.7 %multiply_cosine_fusion = (f32[16,128,64]{2,1,0:T(8,128)S(1)}, f32[16,128,64]{2,1,0:T(8,128)S(1)}) fusion(f32[64]{0:T(128)S(1)} %multiply_power_fusion, f32[16,128]{1,0:T(8,128)S(1)} %add_convert_fusion.3), kind=kLoop, calls=%fused_computation.18 | loop fusion | flops 131072 | bytes 1057024 | tf_op jit(solution)/shard_map/cos | solution.py:16
  28.0 0.9 fusion.17
  30.2 0.7 all_to_all.18
  30.9 6.0 %all-to-all-start.2 = ((s32[8,1,2]{2,1,0:T(1,128)}), s32[8,1,2]{2,1,0:T(1,128)S(1)}, u32[]{:S(2)}, u32[]{:S(2)}) async-start(s32[8,1,2]{2,1,0:T(1,128)} %bitcast.18), calls=%async_computation.2 | async-start | bytes 8192 | tf_op jit(solution)/shard_map/all_to_all | solution.py:123
  36.9 1.9 %broadcast_in_dim.49 = bf16[16,2,2,128,128]{4,3,2,1,0:T(8,128)(2,1)} broadcast(bf16[]{:T(256)} %constant.59.clone.1), dimensions={} | broadcast | bytes 2097154 | tf_op jit(solution)/shard_map/broadcast_in_dim | solution.py:111
  38.7 5.2 %scatter_fusion = bf16[16,2,2,128,128]{4,3,2,1,0:T(8,128)(2,1)} fusion(bf16[16,2,2,128,128]{4,3,2,1,0:T(8,128)(2,1)} %broadcast_in_dim.49, s32[16]{0:T(128)S(1)} %get-tuple-element.29, bf16[16,2,2,128,128]{4,3,2,1,0:T(8,128)(2,1)S(1)} %pad_maximum_fusion), kind=kCustom, calls=%fused_computation.3 | custom fusion | bytes 6291520 | tf_op jit(solution)/shard_map/scatter | solution.py:112
  43.9 6.2 %all-to-all-start.1 = ((bf16[8,2,2,2,128,128]{5,4,3,2,1,0:T(8,128)(2,1)}), bf16[8,2,2,2,128,128]{5,4,3,2,1,0:T(8,128)(2,1)S(1)}, u32[]{:S(2)}, u32[]{:S(2)}) async-start(bf16[8,2,2,2,128,128]{5,4,3,2,1,0:T(8,128)(2,1)} %bitcast.11), calls=%async_computation.1 | async-start | bytes 4194304 | tf_op jit(solution)/shard_map/all_to_all | solution.py:121
  51.1 0.7 fusion.44
  53.8 0.8 scatter_fusion.2
  54.6 0.8 gather_fusion.1
  55.6 41.6 %all-to-all-done.1 = bf16[8,2,2,2,128,128]{5,4,3,2,1,0:T(8,128)(2,1)S(1)} async-done(((bf16[8,2,2,2,128,128]{5,4,3,2,1,0:T(8,128)(2,1)}), bf16[8,2,2,2,128,128]{5,4,3,2,1,0:T(8,128)(2,1)S(1)}, u32[]{:S(2)}, u32[]{:S(2)}) %all-to-all-start.1) | async-done | bytes 2097184 | tf_op jit(solution)/shard_map/all_to_all | solution.py:121
  97.2 5.2 %scatter_fusion.1 = bf16[48,2,2,128,128]{4,3,2,1,0:T(8,128)(2,1)} fusion(bf16[48,2,2,128,128]{4,3,2,1,0:T(8,128)(2,1)} %copy.104, s32[16]{0:T(128)S(1)} %fusion.34, bf16[16,2,2,128,128]{4,3,2,1,0:T(8,128)(2,1)S(1)} %bitcast.110), kind=kCustom, calls=%fused_computation.4 | custom fusion | bytes 6291520 | tf_op jit(solution)/shard_map/scatter | solution.py:128
  102.4 7.8 %gather_fusion = bf16[48,2,2,128,128]{4,3,2,1,0:T(8,128)(2,1)} fusion(bf16[48,2,2,128,128]{4,3,2,1,0:T(8,128)(2,1)} %scatter_fusion.1, s32[1024]{0:T(1024)S(1)} %pad_clamp_fusion), kind=kCustom, calls=%fused_computation | custom fusion | bytes 12583104 | tf_op jit(solution)/shard_map/gather | solution.py:40
  110.2 4.2 %fusion.41 = (bf16[16,3,1,2,128,128]{5,4,3,2,1,0:T(8,128)(2,1)S(1)}, bf16[16,3,1,2,128,128]{5,4,3,2,1,0:T(8,128)(2,1)S(1)}) fusion(bf16[16,3,2,2,128,128]{5,4,3,2,1,0:T(8,128)(2,1)} %bitcast.109), kind=kLoop, calls=%fused_computation.94 | loop fusion | bytes 12582912 | tf_op jit(solution)/shard_map/slice | solution.py:50
  114.4 1.3 fusion.43
  116.2 0.7 fusion.9
  117.3 0.7 reshape.297
  118.1 39.3 %all-gather.2.cloned.1.call-done = bf16[2,128,2048]{2,1,0:T(8,128)(2,1)} async-done(((bf16[2,16,2048]{2,1,0:T(8,128)(2,1)}), bf16[2,128,2048]{2,1,0:T(8,128)(2,1)}) %all-gather.2.cloned.1.call-update) | async-done | bytes 1048592 | tf_op jit(solution)/shard_map/all_gather | solution.py:133
  157.4 4.8 %fusion = f32[2,128,1024]{2,1,0:T(8,128)} fusion(bf16[2,128,2048]{2,1,0:T(8,128)(2,1)} %all-gather.2.cloned.1.call-done, bf16[2048,1024]{1,0:T(8,128)(2,1)} %param.19), kind=kOutput, calls=%fused_computation.7 | convolution fusion | flops 1073741824 | bytes 6291456 | tf_op jit(solution)/shard_map/srh,hc->src/dot_general | solution.py:131
  162.2 7.5 %reduce-scatter.2.cloned.1.call-done = f32[2,128,512]{2,1,0:T(8,128)} async-done(((f32[2,128,1024]{2,1,0:T(8,128)}), f32[2,128,512]{2,1,0:T(8,128)}) %reduce-scatter.2.cloned.1.call-update) | async-done | bytes 524304 | tf_op jit(solution)/shard_map/reduce_scatter | solution.py:137
  169.6 1.8 convert_element_type.66
  (63 shorter events, 6.8 us)
Async XLA Ops:
  6.5 17.5 %copy-start.1 = (bf16[16,2,2,128,128]{4,3,2,1,0:T(8,128)(2,1)S(1)}, bf16[16,2,2,128,128]{4,3,2,1,0:T(8,128)(2,1)}, u32[]{:S(2)}) copy-start(bf16[16,2,2,128,128]{4,3,2,1,0:T(8,128)(2,1)} %param.10) | copy-start | bytes 6291460
  6.5 8.2 %copy-start.6 = (s32[1,4]{1,0:T(1,128)S(1)}, s32[1,4]{1,0:T(1,128)}, u32[]{:S(2)}) copy-start(s32[1,4]{1,0:T(1,128)} %param.11) | copy-start | bytes 52
  6.5 8.5 %copy-start.7 = (s32[16]{0:T(128)S(1)}, s32[16]{0:T(128)}, u32[]{:S(2)}) copy-start(s32[16]{0:T(128)} %param.12) | copy-start | bytes 196
  16.7 14.2 %all-to-all-start = ((s32[8,1,2]{2,1,0:T(1,128)}), s32[8,1,2]{2,1,0:T(1,128)S(1)}, u32[]{:S(2)}, u32[]{:S(2)}) async-start(s32[8,1,2]{2,1,0:T(1,128)} %bitcast), calls=%async_computation | async-start | bytes 8192 | tf_op jit(solution)/shard_map/all_to_all | solution.py:122
  30.9 13.1 %all-to-all-start.2 = ((s32[8,1,2]{2,1,0:T(1,128)}), s32[8,1,2]{2,1,0:T(1,128)S(1)}, u32[]{:S(2)}, u32[]{:S(2)}) async-start(s32[8,1,2]{2,1,0:T(1,128)} %bitcast.18), calls=%async_computation.2 | async-start | bytes 8192 | tf_op jit(solution)/shard_map/all_to_all | solution.py:123
  43.9 6.2 %copy-start.5 = (s32[16,3]{0,1:T(4,128)S(1)}, s32[16,3]{0,1:T(4,128)}, u32[]{:S(2)}) copy-start(s32[16,3]{0,1:T(4,128)} %param.15) | copy-start | bytes 580
  43.9 6.4 %copy-start.2 = (bf16[2,16,2048]{2,1,0:T(8,128)(2,1)S(1)}, bf16[2,16,2048]{2,1,0:T(8,128)(2,1)}, u32[]{:S(2)}) copy-start(bf16[2,16,2048]{2,1,0:T(8,128)(2,1)} %param.17) | copy-start | bytes 393220
  43.9 6.6 %copy-start.4 = (s32[16]{0:T(128)S(1)}, s32[16]{0:T(128)}, u32[]{:S(2)}) copy-start(s32[16]{0:T(128)} %param.16) | copy-start | bytes 196
  43.9 7.0 %copy-start.3 = (bf16[2,16,2,2,128]{4,3,2,1,0:T(2,128)(2,1)S(1)}, bf16[2,16,2,2,128]{4,3,2,1,0:T(2,128)(2,1)}, u32[]{:S(2)}) copy-start(bf16[2,16,2,2,128]{4,3,2,1,0:T(2,128)(2,1)} %param.18) | copy-start | bytes 98308
  43.9 9.9 %copy-start = (s32[48]{0:T(128)S(1)}, s32[48]{0:T(128)}, u32[]{:S(2)}) copy-start(s32[48]{0:T(128)} %param.14) | copy-start | bytes 580
  43.9 53.3 %all-to-all-start.1 = ((bf16[8,2,2,2,128,128]{5,4,3,2,1,0:T(8,128)(2,1)}), bf16[8,2,2,2,128,128]{5,4,3,2,1,0:T(8,128)(2,1)S(1)}, u32[]{:S(2)}, u32[]{:S(2)}) async-start(bf16[8,2,2,2,128,128]{5,4,3,2,1,0:T(8,128)(2,1)} %bitcast.11), calls=%async_computation.1 | async-start | bytes 4194304 | tf_op jit(solution)/shard_map/all_to_all | solution.py:121
  50.1 107.3 %all-gather.2.cloned.1.call-start = ((), (), s32[]{:S(2)}) async-start(), calls=%async_computation.4 | async-start | bytes 1179648 | tf_op jit(solution)/shard_map/all_gather | solution.py:133
  118.0 51.6 %reduce-scatter.2.cloned.1.call-start = ((), (), s32[]{:S(2)}) async-start(), calls=%async_computation.5 | async-start | bytes 1572864 | tf_op jit(solution)/shard_map/reduce_scatter | solution.py:137
Sparse Core Ops, SparseCore 0:
  118.1 39.2 all-gather.1
  162.3 7.2 reduce-scatter.1
where the time goes:
time: 179 us; the launch traced here: 178 us
  waiting for transfers between devices  88.4 us (49%)
  local copies, waits for them, and re-layouts  38.3 us (21%)
  starting transfers between devices  19.5 us (11%)
  between operations  13.7 us (8%)
  other arithmetic  10.5 us (6%)
  matrix products  7.79 us (4%)
    all_to_all x1, waiting for transfers between devices, shards(): lax.all_to_all(place(moved, 0.0), 'pool', split_axis=0, concat_axis=0, ti...  41.6 us
    all_gather x1, waiting for transfers between devices, shards(): lax.all_gather(attention, 'pool', axis=1, tiled=True)  39.3 us
    unnamed x18, local copies, waits for them, and re-layouts  8.29 us
    gather x1, local copies, waits for them, and re-layouts, attend(): context = cache[page_table]  7.75 us
    reduce_scatter x1, waiting for transfers between devices, shards(): lax.psum_scatter(terms, 'tp', scatter_dimension=2, tiled=True)  7.46 us
    all_to_all x1, starting transfers between devices, shards(): lax.all_to_all(slot_buffer, 'pool', split_axis=0, concat_axis=0, tiled=True)  7.28 us
    scatter x3, local copies, waits for them, and re-layouts, place(): buffer = buffer.at[where_to].set(values)  6.43 us
    all_to_all x1, starting transfers between devices, shards(): lax.all_to_all(place(moved, 0.0), 'pool', split_axis=0, concat_axis=0, ti...  6.16 us
  transfers between devices with their start and end apart: 5, of which 3 were waited for; matrix products, arithmetic and copies ran while one was open for 10% of the time, Pallas kernels for 0%

commit v1 on v0

v1 whole, which is shorter than its diff:
```python
import functools

import jax
import jax.numpy as jnp
import numpy as np
from jax import lax
from jax.experimental import pallas as pl
from jax.experimental.pallas import tpu as pltpu
from jax.sharding import PartitionSpec as P

ROPE_BASE = 500000.0
BF16, F32, I32 = jnp.bfloat16, jnp.float32, jnp.int32
SMEM = pl.BlockSpec(memory_space=pltpu.SMEM)
VMEM = pl.BlockSpec(memory_space=pltpu.VMEM)
ANY = pl.BlockSpec(memory_space=pl.ANY)
CONTRACT_LAST = (((1,), (1,)), ((), ()))
PARAMS = pltpu.CompilerParams(vmem_limit_bytes=32 * 2**20)


def tables(page_len, head_dim, pages):
    half = head_dim // 2
    freq = ROPE_BASE ** (-(np.arange(half) * 2.0) / head_dim)
    freq = np.concatenate([freq, freq])[None, :]
    sign = np.concatenate([-np.ones(half), np.ones(half)])[None, :]
    token = np.arange(page_len)[:, None] * freq
    first = np.arange(pages)[:, None] * page_len * freq
    out = (np.cos(token), sign * np.sin(token), np.cos(first), sign * np.sin(first), freq, sign)
    return [jnp.asarray(x, F32) for x in out]


def rope_kernel(page_len, per, len_ref, keys_ref, ct_ref, st_ref, cp_ref, sp_ref, out_ref):
    heads, head_dim = keys_ref.shape[2], keys_ref.shape[4]
    prompts = len_ref.shape[1]
    for i in range(per):
        number, _ = page_place(len_ref, prompts, page_len, pl.program_id(0) * per + i)
        c0, s0 = cp_ref[pl.ds(number, 1), :], sp_ref[pl.ds(number, 1), :]
        ct, st = ct_ref[...], st_ref[...]
        cos = c0 * ct - s0 * st
        sin = s0 * ct + c0 * st
        for k in range(heads):
            x = keys_ref[i, 0, k].astype(F32)
            out_ref[i, k] = (x * cos + pltpu.roll(x, head_dim // 2, 1) * sin).astype(BF16)


def page_place(len_ref, prompts, page_len, n):
    begin = jnp.int32(0)
    number, fill = jnp.int32(0), jnp.int32(0)
    for q in range(prompts):
        length = len_ref[0, q]
        count = (length + page_len - 1) // page_len
        here = (n >= begin) & (n < begin + count)
        number = jnp.where(here, n - begin, number)
        fill = jnp.where(here, jnp.clip(length - (n - begin) * page_len, 0, page_len), fill)
        begin = begin + count
    return number, fill


def rotated_keys(prompt_kv, prompt_lengths, tabs):
    pages, _, heads, page_len, head_dim = prompt_kv.shape
    per = 4
    ct, st, cp, sp, _, _ = tabs
    whole = lambda x: pl.BlockSpec(x.shape, lambda i: (0, 0))
    return pl.pallas_call(
        functools.partial(rope_kernel, page_len, per),
        grid=(pages // per,),
        out_shape=jax.ShapeDtypeStruct((pages, heads, page_len, head_dim), BF16),
        in_specs=[
            SMEM,
            pl.BlockSpec((per, 1, heads, page_len, head_dim), lambda i: (i, 0, 0, 0, 0)),
            whole(ct),
            whole(st),
            whole(cp),
            whole(sp),
        ],
        out_specs=pl.BlockSpec((per, heads, page_len, head_dim), lambda i: (i, 0, 0, 0)),
        compiler_params=PARAMS,
        cost_estimate=pl.CostEstimate(flops=6_000_000, bytes_accessed=2_000_000, transcendentals=0),
        name="rope_pages",
    )(prompt_lengths, prompt_kv, ct, st, cp, sp)


def spread_queries(q_ref, qf_ref, heads):
    steps, rows, width = q_ref.shape
    head_dim = qf_ref.shape[1]
    per = width // head_dim // heads
    block = heads * steps * per
    for s in range(steps):
        for h in range(heads * per):
            k, g = divmod(h, per)
            at = k * steps * per + s * per + g
            qf_ref[pl.ds(at, rows, stride=block), :] = q_ref[s, :, h * head_dim : (h + 1) * head_dim].astype(F32)


def query_kernel(npool, cache_pages, pair, heads, pages, *refs):
    me_ref, table_ref = refs[:2]
    metas = refs[2 : 2 + npool]
    q_ref = refs[2 + npool]
    outs = refs[3 + npool : 3 + 2 * npool]
    request_ref, inverse, qf = refs[3 + 2 * npool :]
    rows = q_ref.shape[1]
    most = table_ref.shape[0] // rows
    block = qf.shape[0] // rows
    for r in range(rows):
        for j in range(most):
            inverse[table_ref[r * most + j]] = r
    spread_queries(q_ref, qf, heads)
    base = me_ref[0] * cache_pages
    for t in range(npool):
        for p in range(pair):
            request_ref[t * pair + p] = -1

        def look(n, count):
            v = metas[t][0, n] - base
            hit = (v >= 0) & (v < cache_pages)

            @pl.when(hit)
            def _():
                request_ref[t * pair + count] = inverse[v]

            return count + hit.astype(I32)

        lax.fori_loop(0, pages, look, jnp.int32(0))
        for p in range(pair):
            r = jnp.maximum(request_ref[t * pair + p], 0)
            start = pl.multiple_of(r * block, block)
            outs[t][p * block : (p + 1) * block, :] = qf[pl.ds(start, block), :].astype(BF16)


def queries_out(me, table, metas, queries, pages, cache_pages, pair, heads, head_dim):
    npool = len(metas)
    steps, rows, width = queries.shape
    block = steps * width // head_dim
    payload = jax.ShapeDtypeStruct((pair * block, head_dim), BF16)
    out = pl.pallas_call(
        functools.partial(query_kernel, npool, cache_pages, pair, heads, pages),
        out_shape=[payload] * npool + [jax.ShapeDtypeStruct((npool * pair,), I32)],
        in_specs=[SMEM] * (2 + npool) + [VMEM],
        out_specs=[VMEM] * npool + [SMEM],
        scratch_shapes=[
            pltpu.SMEM((cache_pages,), I32),
            pltpu.VMEM((rows * block, head_dim), F32),
        ],
        compiler_params=PARAMS,
        cost_estimate=pl.CostEstimate(flops=1_000_000, bytes_accessed=500_000, transcendentals=0),
        name="queries_out",
    )(me, table, *metas, queries)
    return out[:npool], out[npool]


def softmax_parts(scores, mask):
    top = jnp.max(jnp.where(mask, scores, -jnp.inf), axis=1, keepdims=True)
    seen = top > -jnp.inf
    top = jnp.where(seen, top, 0.0)
    weights = jnp.where(mask, jnp.exp(scores - top), 0.0)
    return top, weights, jnp.sum(weights, axis=1, keepdims=True)


def local_kernel(
    page_len,
    heads,
    table_ref,
    context_ref,
    fill_ref,
    position_ref,
    q_ref,
    new_ref,
    freq_ref,
    sign_ref,
    cache_ref,
    o_ref,
    top_ref,
    total_ref,
    kv,
    sems,
    qf,
    kf,
    vf,
):
    steps, rows, width = q_ref.shape
    head_dim = qf.shape[1]
    most = table_ref.shape[0] // rows
    per = width // head_dim // heads
    block = heads * steps * per
    group = steps * per
    scale = head_dim ** (-0.5)

    def copy(n):
        return pltpu.make_async_copy(cache_ref.at[table_ref[n]], kv.at[n], sems.at[n])

    for n in range(rows * most):
        copy(n).start()
    spread_queries(q_ref, qf, heads)
    kf[...] = jnp.zeros_like(kf)
    vf[...] = jnp.zeros_like(vf)
    for u in range(steps):
        angle = (position_ref[...] + u).astype(F32) * freq_ref[...]
        cos, sin = jnp.cos(angle), jnp.sin(angle) * sign_ref[...]
        for k in range(heads):
            x = new_ref[u, :, k * head_dim : (k + 1) * head_dim].astype(F32)
            at = k * group + u
            kf[pl.ds(at, rows, stride=block), :] = x * cos + pltpu.roll(x, head_dim // 2, 1) * sin
            x = new_ref[u, :, (heads + k) * head_dim : (heads + k + 1) * head_dim].astype(F32)
            vf[pl.ds(at, rows, stride=block), :] = x
    column = lax.broadcasted_iota(I32, (group, page_len), 1)
    fresh_column = lax.broadcasted_iota(I32, (group, group), 1)
    fresh_step = lax.broadcasted_iota(I32, (group, group), 0) // per
    fresh_mask = (fresh_column <= fresh_step) & (fresh_column < steps)

    def request(r):
        for j in range(most):
            copy(r * most + j).wait()
        limits = [
            jnp.minimum(fill_ref[table_ref[r * most + j]], context_ref[r] - j * page_len) for j in range(most)
        ]
        mask = jnp.concatenate([column < limit for limit in limits] + [fresh_mask], axis=1)
        for k in range(heads):
            at = pl.multiple_of(r * block + k * group, group)
            q = qf[pl.ds(at, group), :].astype(BF16)
            fresh_k = kf[pl.ds(at, group), :].astype(BF16)
            fresh_v = vf[pl.ds(at, group), :].astype(BF16)
            keys = [kv[r * most + j, 0, k] for j in range(most)] + [fresh_k]
            values = [kv[r * most + j, 1, k] for j in range(most)] + [fresh_v]
            scores = [lax.dot_general(q, x, CONTRACT_LAST, preferred_element_type=F32) for x in keys]
            top, weights, total = softmax_parts(jnp.concatenate(scores, axis=1) * scale, mask)
            weights = weights.astype(BF16)
            mixed = jnp.zeros((group, head_dim), F32)
            begin = 0
            for x in values:
                part = weights[:, begin : begin + x.shape[0]]
                mixed = mixed + jnp.dot(part, x, preferred_element_type=F32)
                begin += x.shape[0]
            o_ref[pl.ds(at, group), :] = mixed
            top_ref[pl.ds(at, group), :] = jnp.broadcast_to(top, (group, head_dim))
            total_ref[pl.ds(at, group), :] = jnp.broadcast_to(total, (group, head_dim))

    together = 2

    @pl.loop(0, rows // together)
    def _(i):
        for u in range(together):
            request(i * together + u)


def local_attention(table, context, fills, queries, new_kv, cache_kv, tabs):
    steps, rows, width = queries.shape
    slots, _, heads, page_len, head_dim = cache_kv.shape
    block = steps * width // head_dim
    flat = jax.ShapeDtypeStruct((rows * block, head_dim), F32)
    freq, sign = tabs[4:]
    return pl.pallas_call(
        functools.partial(local_kernel, page_len, heads),
        out_shape=[flat] * 3,
        in_specs=[SMEM] * 3 + [VMEM] * 5 + [ANY],
        out_specs=[VMEM] * 3,
        scratch_shapes=[
            pltpu.VMEM((table.shape[0], 2, heads, page_len, head_dim), BF16),
            pltpu.SemaphoreType.DMA((table.shape[0],)),
            pltpu.VMEM((rows * block, head_dim), F32),
            pltpu.VMEM((rows * block, head_dim), F32),
            pltpu.VMEM((rows * block, head_dim), F32),
        ],
        compiler_params=PARAMS,
        cost_estimate=pl.CostEstimate(flops=110_000_000, bytes_accessed=7_000_000, transcendentals=300_000),
        name="local_attention",
    )(
        table,
        context,
        fills,
        context[:, None],
        queries,
        new_kv.reshape(steps, rows, 2 * heads * head_dim),
        freq,
        sign,
        cache_kv,
    )


def pieces(x):
    high = x.astype(BF16).astype(F32)
    middle = (x - high).astype(BF16).astype(F32)
    return [high, middle, x - high - middle]


def arrived_kernel(npool, cache_pages, pair, page_len, heads, *refs):
    me_ref, slot_ref, len_ref = refs[:3]
    metas = refs[3 : 3 + npool]
    queries = refs[3 + npool : 3 + 2 * npool]
    keys_ref, prompt_ref = refs[3 + 2 * npool : 5 + 2 * npool]
    outs = refs[5 + 2 * npool : 5 + 3 * npool]
    values, sem, page_of, slot_of, count_of = refs[5 + 3 * npool :]
    pages = slot_ref.shape[0]
    prompts = len_ref.shape[1]
    head_dim = keys_ref.shape[3]
    block = queries[0].shape[0] // pair
    group = block // heads
    scale = head_dim ** (-0.5)
    fetch = pltpu.make_async_copy(prompt_ref.at[:, 1], values, sem)
    fetch.start()
    for s in range(npool):
        count_of[s] = 0
        for p in range(pair):
            page_of[s * pair + p] = 0
            slot_of[s * pair + p] = -1

    def place(n, _):
        slot = slot_ref[n]
        target = slot // cache_pages
        s = lax.rem(target - me_ref[0] + npool, npool)
        at = s * pair + count_of[s]
        page_of[at] = n
        slot_of[at] = slot - target * cache_pages
        count_of[s] = count_of[s] + 1
        return 0

    lax.fori_loop(0, pages, place, 0)
    fetch.wait()
    column = lax.broadcasted_iota(I32, (group, page_len), 1)
    lane = lax.broadcasted_iota(I32, (group, head_dim), 1)
    for s in range(npool):
        meta = metas[(npool - s) % npool]
        for p in range(pair):
            n = page_of[s * pair + p]
            slot = slot_of[s * pair + p]
            _, fill = page_place(len_ref, prompts, page_len, n)
            left = jnp.sum(jnp.where(meta[1:2, :] == slot, meta[2:3, :], 0), axis=1, keepdims=True)
            mask = column < jnp.minimum(left, fill)
            for k in range(heads):
                at = p * block + k * group
                q = queries[s][at : at + group, :]
                scores = lax.dot_general(q, keys_ref[n, k], CONTRACT_LAST, preferred_element_type=F32)
                top, weights, total = softmax_parts(scores * scale, mask)
                mixed = jnp.dot(weights.astype(BF16), values[n, k], preferred_element_type=F32)
                stats = jnp.zeros((group, head_dim), F32)
                for i, x in enumerate(pieces(top) + pieces(total)):
                    stats = jnp.where(lane == i, x, stats)
                at = p * 2 * block + k * group
                outs[s][at : at + group, :] = mixed.astype(BF16)
                outs[s][at + block : at + block + group, :] = stats.astype(BF16)


def arrived_attention(me, page_slot, prompt_lengths, metas, queries, keys, prompt_kv, cache_pages, pair):
    npool = len(metas)
    pages, _, heads, page_len, head_dim = prompt_kv.shape
    payload = jax.ShapeDtypeStruct((2 * queries[0].shape[0], head_dim), BF16)
    return pl.pallas_call(
        functools.partial(arrived_kernel, npool, cache_pages, pair, page_len, heads),
        out_shape=[payload] * npool,
        in_specs=[SMEM] * 3 + [VMEM] * (2 * npool + 1) + [ANY],
        out_specs=[VMEM] * npool,
        scratch_shapes=[
            pltpu.VMEM((pages, heads, page_len, head_dim), BF16),
            pltpu.SemaphoreType.DMA,
            pltpu.SMEM((npool * pair,), I32),
            pltpu.SMEM((npool * pair,), I32),
            pltpu.SMEM((npool,), I32),
        ],
        compiler_params=PARAMS,
        cost_estimate=pl.CostEstimate(flops=40_000_000, bytes_accessed=4_000_000, transcendentals=70_000),
        name="arrived_attention",
    )(me, page_slot, prompt_lengths, *metas, *queries, keys, prompt_kv)


def merge_kernel(npool, pair, heads, *refs):
    request_ref = refs[0]
    parts = refs[1 : 1 + npool]
    o_ref, top_ref, total_ref, out_ref, mixed, top, total = refs[1 + npool :]
    steps, rows, width = out_ref.shape
    head_dim = o_ref.shape[1]
    per = width // head_dim // heads
    block = heads * steps * per
    mixed[...] = o_ref[...]
    top[...] = top_ref[...]
    total[...] = total_ref[...]
    for s in range(npool):
        for p in range(pair):
            r = request_ref[s * pair + p]
            at = pl.ds(pl.multiple_of(jnp.maximum(r, 0) * block, block), block)
            begin = p * 2 * block
            o = parts[s][begin : begin + block, :].astype(F32)
            stats = parts[s][begin + block : begin + 2 * block, :].astype(F32)
            m = stats[:, 0:1] + stats[:, 1:2] + stats[:, 2:3]
            l = stats[:, 3:4] + stats[:, 4:5] + stats[:, 5:6]
            seen = (l > 0.0) & (r >= 0)
            old = top[at, :]
            new = jnp.where(seen, jnp.maximum(old, m), old)
            a = jnp.exp(old - new)
            b = jnp.where(seen, jnp.exp(m - new), 0.0)
            top[at, :] = new
            total[at, :] = total[at, :] * a + l * b
            mixed[at, :] = mixed[at, :] * a + o * b
    for s in range(steps):
        for h in range(heads * per):
            k, g = divmod(h, per)
            at = pl.ds(k * steps * per + s * per + g, rows, stride=block)
            out_ref[s, :, h * head_dim : (h + 1) * head_dim] = (mixed[at, :] / total[at, :]).astype(BF16)


def merged(request, parts, local, steps, rows, width, heads, pair):
    npool = len(parts)
    flat = local[0].shape
    return pl.pallas_call(
        functools.partial(merge_kernel, npool, pair, heads),
        out_shape=jax.ShapeDtypeStruct((steps, rows, width), BF16),
        in_specs=[SMEM] + [VMEM] * (npool + 3),
        out_specs=VMEM,
        scratch_shapes=[pltpu.VMEM(flat, F32)] * 3,
        compiler_params=PARAMS,
        cost_estimate=pl.CostEstimate(flops=2_000_000, bytes_accessed=1_500_000, transcendentals=100_000),
        name="merge",
    )(request, *parts, *local)


def project_kernel(npool, scalars, *refs):
    blocks = refs[:npool]
    weight_ref, out_ref, lhs = refs[npool:]
    steps, rows, _ = blocks[0].shape

    @pl.when(pl.program_id(0) == 0)
    def _():
        for t in range(npool):
            owner = lax.rem(scalars[0] + npool - t, npool)
            at = pl.ds(pl.multiple_of(owner * rows, rows), rows)
            for s in range(steps):
                lhs[s, at, :] = blocks[t][s]

    for s in range(steps):
        out_ref[s] = jnp.dot(lhs[s], weight_ref[...], preferred_element_type=F32)


def projection(me, first_tile, blocks, weight, columns, tile):
    npool = len(blocks)
    steps, rows, width = blocks[0].shape
    whole = pl.BlockSpec((steps, rows, width), lambda i, sc: (0, 0, 0))
    return pl.pallas_call(
        functools.partial(project_kernel, npool),
        out_shape=jax.ShapeDtypeStruct((steps, npool * rows, columns), F32),
        grid_spec=pltpu.PrefetchScalarGridSpec(
            num_scalar_prefetch=1,
            grid=(columns // tile,),
            in_specs=[whole] * npool + [pl.BlockSpec((width, tile), lambda i, sc: (0, sc[1] + i))],
            out_specs=pl.BlockSpec((steps, npool * rows, tile), lambda i, sc: (0, 0, i)),
            scratch_shapes=[pltpu.VMEM((steps, npool * rows, width), BF16)],
        ),
        compiler_params=PARAMS,
        cost_estimate=pl.CostEstimate(
            flops=2 * steps * npool * rows * width * columns, bytes_accessed=4_000_000, transcendentals=0
        ),
        name="project",
    )(jnp.stack([me, first_tile]), *blocks, weight)


def shift(x, npool, by):
    return lax.ppermute(x, "pool", [(i, (i + by) % npool) for i in range(npool)])


def swap_halves(x):
    return lax.ppermute(x, "tp", [(0, 1), (1, 0)])


def shards(
    prompt_kv,
    prompt_lengths,
    page_slot,
    cache_kv,
    cache_fill,
    page_table,
    context_lengths,
    queries,
    new_kv,
    out_weight,
):
    npool = lax.axis_size("pool")
    me = lax.axis_index("pool").astype(I32)
    pages, _, heads, page_len, head_dim = prompt_kv.shape
    cache_pages = cache_kv.shape[0]
    steps, rows, width = queries.shape
    most = page_table.shape[1]
    pair = (pages + npool - 1) // npool
    tabs = tables(page_len, head_dim, pages)
    me1 = me[None]
    table = page_table.reshape(-1)

    left = jnp.clip(context_lengths[:, None] - page_len * jnp.arange(most, dtype=I32)[None, :], 0, page_len)
    lanes = 128
    row = lambda x, empty: jnp.pad(x, (0, lanes - x.shape[0]), constant_values=empty)[None]
    meta = jnp.concatenate(
        [row(page_slot, -1), row(table, -2), row(left.reshape(-1), 0), jnp.zeros((5, lanes), I32)], axis=0
    )
    metas = [meta] + [shift(meta, npool, t) for t in range(1, npool)]
    sent, request = queries_out(me1, table, metas, queries, pages, cache_pages, pair, heads, head_dim)
    got = [sent[0]] + [shift(sent[s], npool, -s) for s in range(1, npool)]
    keys = rotated_keys(prompt_kv, prompt_lengths, tabs)
    local = local_attention(table, context_lengths, cache_fill, queries, new_kv, cache_kv, tabs)
    parts = arrived_attention(me1, page_slot, prompt_lengths, metas, got, keys, prompt_kv, cache_pages, pair)
    parts = [parts[0]] + [shift(parts[t], npool, t) for t in range(1, npool)]
    attention = merged(request, parts, local, steps, rows, width, heads, pair)
    blocks = [attention] + [shift(attention, npool, t) for t in range(1, npool)]

    half = out_weight.shape[1] // 2
    tile = min(half, 256)
    mine = lax.axis_index("tp").astype(I32)
    other_terms = projection(me, (1 - mine) * (half // tile), blocks, out_weight, half, tile)
    other_terms = swap_halves(other_terms)
    terms = projection(me, mine * (half // tile), blocks, out_weight, half, tile)
    return (terms + other_terms).astype(BF16)


def solution(mesh):
    return jax.shard_map(
        shards,
        mesh=mesh,
        in_specs=(
            P(("group", "pool"), None, "tp", None, None),
            P(("group", "pool"), None),
            P(("group", "pool")),
            P(("group", "pool"), None, "tp", None, None),
            P(("group", "pool")),
            P(("group", "pool"), None),
            P(("group", "pool")),
            P(None, ("group", "pool"), "tp"),
            P(None, ("group", "pool"), None, "tp", None),
            P("tp", "pool"),
        ),
        out_specs=P(None, "group", ("pool", "tp")),
        check_vma=False,
    )
```

time: 179 us -> 117 us (0.65)
  the two profiles are of different devices: /device:TPU:0 before, /device:TPU:15 now
where the time goes in v1:
time: 117 us
  Pallas kernels  40.7 us (35%)
  starting transfers between devices  39.1 us (33%)
  waiting for transfers between devices  18.2 us (16%)
  local copies, waits for them, and re-layouts  16.6 us (14%)
  other arithmetic  1.74 us (1%)
    ppermute x28, starting transfers between devices, shift(): lax.ppermute(x, 'pool', [(i, (i + by) % npool) for i in range(npool)])  35.8 us
    pallas_call x1, Pallas kernels, local_attention(): pl.pallas_call(functools.partial(local_kernel, page_len, heads), out_shap...  21.4 us
    ppermute x28, waiting for transfers between devices, shift(): lax.ppermute(x, 'pool', [(i, (i + by) % npool) for i in range(npool)])  18.2 us
    unnamed x39, local copies, waits for them, and re-layouts  15.5 us
    pallas_call x1, Pallas kernels, arrived_attention(): pl.pallas_call(functools.partial(arrived_kernel, npool, cache_pages, pair...  8.7 us
    pallas_call x2, Pallas kernels, projection(): pl.pallas_call(functools.partial(project_kernel, npool), out_shape=jax.Sh...  3.83 us
    pallas_call x1, Pallas kernels, queries_out(): pl.pallas_call(functools.partial(query_kernel, npool, cache_pages, pair,...  3.32 us
    ppermute x1, starting transfers between devices, swap_halves(): return lax.ppermute(x, 'tp', [(0, 1), (1, 0)])  3.3 us
  transfers between devices with their start and end apart: 29, of which 4 were waited for; matrix products, arithmetic and copies ran while one was open for 0% of the time, Pallas kernels for 21%

profile of v1, /device:TPU:15, one launch (start us, length us, event | category | flops | bytes accessed | tf_op | source)
XLA Modules:
  0.0 116.6 jit_solution(15612775746745467480)
XLA Ops:
  9.7 1.4 %collective-permute-start.6 = (s32[8,128]{1,0:T(8,128)S(1)}, s32[8,128]{1,0:T(8,128)S(1)}, u32[]{:S(2)}, u32[]{:S(2)}) collective-permute-start(s32[8,128]{1,0:T(8,128)S(1)} %add_add_fusion.refs_2_.refs_3_), channel_id=1, source_target_pairs={{0,14},{2,0},{4,2},{6,4},{8,6},{10,8},{12,10},{14,12},{1,15},{3,1}... | collective-permute-start | bytes 12296 | tf_op jit(solution)/shard_map/ppermute | solution.py:453
  11.7 1.4 %collective-permute-done.6.refs_9_.refs_10_ = s32[8,128]{1,0:T(8,128)S(1)} collective-permute-done((s32[8,128]{1,0:T(8,128)S(1)}, s32[8,128]{1,0:T(8,128)S(1)}, u32[]{:S(2)}, u32[]{:S(2)}) %collective-permute-start.6) | collective-permute-done | bytes 4128 | tf_op jit(solution)/shard_map/ppermute | solution.py:453
  13.9 3.3 %queries_out.1 = (bf16[64,128]{1,0:T(8,128)(2,1)S(1)}, bf16[64,128]{1,0:T(8,128)(2,1)S(1)}, bf16[64,128]{1,0:T(8,128)(2,1)S(1)}, bf16[64,128]{1,0:T(8,128)(2,1)S...) custom-call(s32[1]{0:T(128)} %bitcast.refs_0_, ...), custom_call_target="tpu_custom_call" | custom-call | flops 1000000 | bytes 500000 | tf_op jit(solution)/shard_map/queries_out/pallas_call | solution.py:134
  18.9 3.5 %collective-permute-start.9 = (bf16[64,128]{1,0:T(8,128)(2,1)S(1)}, bf16[64,128]{1,0:T(8,128)(2,1)S(1)}, u32[]{:S(2)}, u32[]{:S(2)}) collective-permute-start(bf16[64,128]{1,0:T(8,128)(2,1)S(1)} %get-tuple-element.29), channel_id=1, source_target_pairs={{0,10},{2,12},{4,14},{6,0},{8,2},{10,4},{12,6},{14,8},{1,11},{3,13... | collective-permute-start | bytes 49160 | tf_op jit(solution)/shard_map/ppermute | solution.py:453
  22.4 2.4 %collective-permute-start.11 = (bf16[64,128]{1,0:T(8,128)(2,1)S(1)}, bf16[64,128]{1,0:T(8,128)(2,1)S(1)}, u32[]{:S(2)}, u32[]{:S(2)}) collective-permute-start(bf16[64,128]{1,0:T(8,128)(2,1)S(1)} %get-tuple-element.31), channel_id=1, source_target_pairs={{0,6},{2,8},{4,10},{6,12},{8,14},{10,0},{12,2},{14,4},{1,7},{3,9},... | collective-permute-start | bytes 49160 | tf_op jit(solution)/shard_map/ppermute | solution.py:453
  26.0 2.3 %collective-permute-start.13 = (bf16[64,128]{1,0:T(8,128)(2,1)S(1)}, bf16[64,128]{1,0:T(8,128)(2,1)S(1)}, u32[]{:S(2)}, u32[]{:S(2)}) collective-permute-start(bf16[64,128]{1,0:T(8,128)(2,1)S(1)} %get-tuple-element.33), channel_id=1, source_target_pairs={{0,2},{2,4},{4,6},{6,8},{8,10},{10,12},{12,14},{14,0},{1,3},{3,5},... | collective-permute-start | bytes 49160 | tf_op jit(solution)/shard_map/ppermute | solution.py:453
  28.3 1.6 %copy-done.2 = bf16[16,2,2,128,128]{4,3,2,1,0:T(8,128)(2,1)S(1)} copy-done((bf16[16,2,2,128,128]{4,3,2,1,0:T(8,128)(2,1)S(1)}, bf16[16,2,2,128,128]{4,3,2,1,0:T(8,128)(2,1)}, u32[]{:S(2)}) %copy-start.2) | copy-done | bytes 2097176
  33.7 1.5 %rope_pages.1.refs_19_ = bf16[16,2,128,128]{3,2,1,0:T(8,128)(2,1)S(1)} custom-call(s32[1,4]{1,0:T(1,128)S(1)} %copy-done.12, bf16[16,2,2,128,128]{4,3,2,1,0:T(8,128)(2,1)S(1)} %copy-done.2, f32[128,128]{1,0:T(8,128)S(1)} %copy-done.7, f32[128,128]{1,0:T(8,128)S(1)} %copy-done.8, f32[16,128]{1,0:T(8,128)S(1)} %copy-done.9, f32[16,128]{1,0:T(8,128)S(1)} %copy-done.10), custom_call_target="tpu_custom_call" | custom-call | flops 6000000 | bytes 2000000 | tf_op jit(solution)/shard_map/rope_pages/pallas_call | solution.py:63
  36.6 8.7 %arrived_attention.1 = (bf16[128,128]{1,0:T(8,128)(2,1)S(1)}, bf16[128,128]{1,0:T(8,128)(2,1)S(1)}, bf16[128,128]{1,0:T(8,128)(2,1)S(1)}, bf16[128,128]{1,0:T(8,...) custom-call(s32[1]{0:T(128)} %bitcast.refs_0_, ...), custom_call_target="tpu_custom_call" | custom-call | flops 40000000 | bytes 4000000 | tf_op jit(solution)/shard_map/arrived_attention/pallas_call | solution.py:345
  45.6 2.1 %collective-permute-start.16 = (bf16[128,128]{1,0:T(8,128)(2,1)S(1)}, bf16[128,128]{1,0:T(8,128)(2,1)S(1)}, u32[]{:S(2)}, u32[]{:S(2)}) collective-permute-start(bf16[128,128]{1,0:T(8,128)(2,1)S(1)} %get-tuple-element.37), channel_id=1, source_target_pairs={{0,6},{2,8},{4,10},{6,12},{8,14},{10,0},{12,2},{14,4},{1,7},{3,9},... | collective-permute-start | bytes 98312 | tf_op jit(solution)/shard_map/ppermute | solution.py:453
  51.7 2.8 %copy-done.4 = bf16[48,2,2,128,128]{4,3,2,1,0:T(8,128)(2,1)S(1)} copy-done((bf16[48,2,2,128,128]{4,3,2,1,0:T(8,128)(2,1)S(1)}, bf16[48,2,2,128,128]{4,3,2,1,0:T(8,128)(2,1)}, u32[]{:S(2)}) %copy-start.4) | copy-done | bytes 6291480
  54.5 21.4 %local_attention.1 = (f32[512,128]{1,0:T(8,128)S(1)}, f32[512,128]{1,0:T(8,128)S(1)}, f32[512,128]{1,0:T(8,128)S(1)}) custom-call(s32[48]{0:T(128)S(1)} %reshape.19.refs_1_.table_ref, s32[16]{0:T(128)S(1)} %copy-done.11, s32[48]{0:T(128)S(1)} %copy-done.14, s32[16,1]{1,0:T(8,128)S(1)} %copy.20.position_ref, bf16[2,16,2048]{2,1,0:T(8,128)(2,1)S(1)} %copy-done.6, ...), custom_call_target="tpu_custom_call" | custom-call | flops 110000000 | bytes 7000000 | tf_op jit(solution)/shard_map/local_attention/pallas_call | solution.py:250
  75.9 2.0 %merge.1.refs_0_ = bf16[2,16,2048]{2,1,0:T(8,128)(2,1)S(1)} custom-call(s32[16]{0:T(128)S(1)} %get-tuple-element.25.refs_0_, bf16[128,128]{1,0:T(8,128)(2,1)S(1)} %get-tuple-element.34.refs_1_, bf16[128,128]{1,0:T(8,128)(2,1)S(1)} %collective-permute-done.14.refs_2_, bf16[128,128]{1,0:T(8,128)(2,1)S(1)} %collective-permute-done.15.refs_3_, ...), custom_call_target="tpu_custom_call" | custom-call | flops 2000000 | bytes 1500000 | tf_op jit(solution)/shard_map/merge/pallas_call | solution.py:401
  77.9 2.1 %collective-permute-start.21 = (bf16[2,16,2048]{2,1,0:T(8,128)(2,1)S(1)}, bf16[2,16,2048]{2,1,0:T(8,128)(2,1)S(1)}, u32[]{:S(2)}, u32[]{:S(2)}) collective-permute-start(bf16[2,16,2048]{2,1,0:T(8,128)(2,1)S(1)} %merge.1.refs_0_), channel_id=1, source_target_pairs={{0,2},{2,4},{4,6},{6,8},{8,10},{10,12},{12,14},{14,0},{1,3},{3,5},... | collective-permute-start | bytes 393224 | tf_op jit(solution)/shard_map/ppermute | solution.py:453
  80.4 3.0 %collective-permute-start.23 = (bf16[2,16,2048]{2,1,0:T(8,128)(2,1)S(1)}, bf16[2,16,2048]{2,1,0:T(8,128)(2,1)S(1)}, u32[]{:S(2)}, u32[]{:S(2)}) collective-permute-start(bf16[2,16,2048]{2,1,0:T(8,128)(2,1)S(1)} %merge.1.refs_0_), channel_id=1, source_target_pairs={{0,6},{2,8},{4,10},{6,12},{8,14},{10,0},{12,2},{14,4},{1,7},{3,9},... | collective-permute-start | bytes 393224 | tf_op jit(solution)/shard_map/ppermute | solution.py:453
  83.4 2.1 %collective-permute-start.25 = (bf16[2,16,2048]{2,1,0:T(8,128)(2,1)S(1)}, bf16[2,16,2048]{2,1,0:T(8,128)(2,1)S(1)}, u32[]{:S(2)}, u32[]{:S(2)}) collective-permute-start(bf16[2,16,2048]{2,1,0:T(8,128)(2,1)S(1)} %merge.1.refs_0_), channel_id=1, source_target_pairs={{0,10},{2,12},{4,14},{6,0},{8,2},{10,4},{12,6},{14,8},{1,11},{3,13... | collective-permute-start | bytes 393224 | tf_op jit(solution)/shard_map/ppermute | solution.py:453
  85.5 2.4 %collective-permute-start.26 = (bf16[2,16,2048]{2,1,0:T(8,128)(2,1)S(1)}, bf16[2,16,2048]{2,1,0:T(8,128)(2,1)S(1)}, u32[]{:S(2)}, u32[]{:S(2)}) collective-permute-start(bf16[2,16,2048]{2,1,0:T(8,128)(2,1)S(1)} %merge.1.refs_0_), channel_id=1, source_target_pairs={{0,12},{2,14},{4,0},{6,2},{8,4},{10,6},{12,8},{14,10},{1,13},{3,15... | collective-permute-start | bytes 393224 | tf_op jit(solution)/shard_map/ppermute | solution.py:453
  88.0 3.1 %collective-permute-done.24.refs_4_ = bf16[2,16,2048]{2,1,0:T(8,128)(2,1)S(1)} collective-permute-done((bf16[2,16,2048]{2,1,0:T(8,128)(2,1)S(1)}, bf16[2,16,2048]{2,1,0:T(8,128)(2,1)S(1)}, u32[]{:S(2)}, u32[]{:S(2)}) %collective-permute-start.24) | collective-permute-done | bytes 131104 | tf_op jit(solution)/shard_map/ppermute | solution.py:453
  91.1 13.1 %collective-permute-done.26.refs_6_ = bf16[2,16,2048]{2,1,0:T(8,128)(2,1)S(1)} collective-permute-done((bf16[2,16,2048]{2,1,0:T(8,128)(2,1)S(1)}, bf16[2,16,2048]{2,1,0:T(8,128)(2,1)S(1)}, u32[]{:S(2)}, u32[]{:S(2)}) %collective-permute-start.26) | collective-permute-done | bytes 131104 | tf_op jit(solution)/shard_map/ppermute | solution.py:453
  104.2 2.2 %copy-done = bf16[2048,1024]{1,0:T(8,128)(2,1)S(1)} copy-done((bf16[2048,1024]{1,0:T(8,128)(2,1)S(1)}, bf16[2048,1024]{1,0:T(8,128)(2,1)}, u32[]{:S(2)}) %copy-start) | copy-done | bytes 4194328
  106.4 1.9 %project.3 = f32[2,128,512]{2,1,0:T(8,128)S(1)} custom-call(s32[2]{0:T(128)S(1)} %pad_add_fusion.1.scalars, bf16[2,16,2048]{2,1,0:T(8,128)(2,1)S(1)} %merge.1.refs_0_, bf16[2,16,2048]{2,1,0:T(8,128)(2,1)S(1)} %collective-permute-done.21.refs_1_, bf16[2,16,2048]{2,1,0:T(8,128)(2,1)S(1)} %collective-permute-done.22.refs_2_, ...), custom_call_target="tpu_custom_call" | custom-call | flops 536870912 | bytes 4000000 | tf_op jit(solution)/shard_map/project/pallas_call | solution.py:434
  108.3 3.3 %collective-permute-start.28 = (f32[2,128,512]{2,1,0:T(8,128)S(1)}, f32[2,128,512]{2,1,0:T(8,128)S(1)}, u32[]{:S(2)}, u32[]{:S(2)}) collective-permute-start(f32[2,128,512]{2,1,0:T(8,128)S(1)} %project.3), channel_id=1, source_target_pairs={{0,1},{1,0},{2,3},{3,2},{4,5},{5,4},{6,7},{7,6},{8,9},{9,8},{10,11... | collective-permute-start | bytes 1572872 | tf_op jit(solution)/shard_map/ppermute | solution.py:457
  111.7 2.2 %copy-done.1 = bf16[2048,1024]{1,0:T(8,128)(2,1)S(1)} copy-done((bf16[2048,1024]{1,0:T(8,128)(2,1)S(1)}, bf16[2048,1024]{1,0:T(8,128)(2,1)}, u32[]{:S(2)}) %copy-start.1) | copy-done | bytes 4194328
  113.9 1.9 %project.2 = f32[2,128,512]{2,1,0:T(8,128)S(1)} custom-call(s32[2]{0:T(128)S(1)} %pad_add_fusion.scalars, bf16[2,16,2048]{2,1,0:T(8,128)(2,1)S(1)} %merge.1.refs_0_, bf16[2,16,2048]{2,1,0:T(8,128)(2,1)S(1)} %collective-permute-done.21.refs_1_, bf16[2,16,2048]{2,1,0:T(8,128)(2,1)S(1)} %collective-permute-done.22.refs_2_, ...), custom_call_target="tpu_custom_call" | custom-call | flops 536870912 | bytes 4000000 | tf_op jit(solution)/shard_map/project/pallas_call | solution.py:434
  (94 shorter events, 24.8 us)
Async XLA Ops:
  2.6 5.9 %collective-permute-start = (s32[8,128]{1,0:T(8,128)S(1)}, s32[8,128]{1,0:T(8,128)S(1)}, u32[]{:S(2)}, u32[]{:S(2)}) collective-permute-start(s32[8,128]{1,0:T(8,128)S(1)} %add_add_fusion.refs_2_.refs_3_), channel_id=1, source_target_pairs={{0,2},{2,4},{4,6},{6,8},{8,10},{10,12},{12,14},{14,0},{1,3},{3,5},... | collective-permute-start | bytes 12296 | tf_op jit(solution)/shard_map/ppermute | solution.py:453
  3.8 5.9 %collective-permute-start.1 = (s32[8,128]{1,0:T(8,128)S(1)}, s32[8,128]{1,0:T(8,128)S(1)}, u32[]{:S(2)}, u32[]{:S(2)}) collective-permute-start(s32[8,128]{1,0:T(8,128)S(1)} %add_add_fusion.refs_2_.refs_3_), channel_id=1, source_target_pairs={{0,4},{2,6},{4,8},{6,10},{8,12},{10,14},{12,0},{14,2},{1,5},{3,7},... | collective-permute-start | bytes 12296 | tf_op jit(solution)/shard_map/ppermute | solution.py:453
  5.1 6.0 %collective-permute-start.2 = (s32[8,128]{1,0:T(8,128)S(1)}, s32[8,128]{1,0:T(8,128)S(1)}, u32[]{:S(2)}, u32[]{:S(2)}) collective-permute-start(s32[8,128]{1,0:T(8,128)S(1)} %add_add_fusion.refs_2_.refs_3_), channel_id=1, source_target_pairs={{0,6},{2,8},{4,10},{6,12},{8,14},{10,0},{12,2},{14,4},{1,7},{3,9},... | collective-permute-start | bytes 12296 | tf_op jit(solution)/shard_map/ppermute | solution.py:453
  17.3 7.5 %collective-permute-start.7 = (bf16[64,128]{1,0:T(8,128)(2,1)S(1)}, bf16[64,128]{1,0:T(8,128)(2,1)S(1)}, u32[]{:S(2)}, u32[]{:S(2)}) collective-permute-start(bf16[64,128]{1,0:T(8,128)(2,1)S(1)} %get-tuple-element.27), channel_id=1, source_target_pairs={{0,14},{2,0},{4,2},{6,4},{8,6},{10,8},{12,10},{14,12},{1,15},{3,1}... | collective-permute-start | bytes 49160 | tf_op jit(solution)/shard_map/ppermute | solution.py:453
  17.8 8.2 %collective-permute-start.8 = (bf16[64,128]{1,0:T(8,128)(2,1)S(1)}, bf16[64,128]{1,0:T(8,128)(2,1)S(1)}, u32[]{:S(2)}, u32[]{:S(2)}) collective-permute-start(bf16[64,128]{1,0:T(8,128)(2,1)S(1)} %get-tuple-element.28), channel_id=1, source_target_pairs={{0,12},{2,14},{4,0},{6,2},{8,4},{10,6},{12,8},{14,10},{1,13},{3,15... | collective-permute-start | bytes 49160 | tf_op jit(solution)/shard_map/ppermute | solution.py:453
  18.9 16.3 %collective-permute-start.9 = (bf16[64,128]{1,0:T(8,128)(2,1)S(1)}, bf16[64,128]{1,0:T(8,128)(2,1)S(1)}, u32[]{:S(2)}, u32[]{:S(2)}) collective-permute-start(bf16[64,128]{1,0:T(8,128)(2,1)S(1)} %get-tuple-element.29), channel_id=1, source_target_pairs={{0,10},{2,12},{4,14},{6,0},{8,2},{10,4},{12,6},{14,8},{1,11},{3,13... | collective-permute-start | bytes 49160 | tf_op jit(solution)/shard_map/ppermute | solution.py:453
  22.4 12.7 %collective-permute-start.10 = (bf16[64,128]{1,0:T(8,128)(2,1)S(1)}, bf16[64,128]{1,0:T(8,128)(2,1)S(1)}, u32[]{:S(2)}, u32[]{:S(2)}) collective-permute-start(bf16[64,128]{1,0:T(8,128)(2,1)S(1)} %get-tuple-element.30), channel_id=1, source_target_pairs={{0,8},{2,10},{4,12},{6,14},{8,0},{10,2},{12,4},{14,6},{1,9},{3,11}... | collective-permute-start | bytes 49160 | tf_op jit(solution)/shard_map/ppermute | solution.py:453
  22.4 12.8 %collective-permute-start.11 = (bf16[64,128]{1,0:T(8,128)(2,1)S(1)}, bf16[64,128]{1,0:T(8,128)(2,1)S(1)}, u32[]{:S(2)}, u32[]{:S(2)}) collective-permute-start(bf16[64,128]{1,0:T(8,128)(2,1)S(1)} %get-tuple-element.31), channel_id=1, source_target_pairs={{0,6},{2,8},{4,10},{6,12},{8,14},{10,0},{12,2},{14,4},{1,7},{3,9},... | collective-permute-start | bytes 49160 | tf_op jit(solution)/shard_map/ppermute | solution.py:453
  24.8 10.4 %collective-permute-start.12 = (bf16[64,128]{1,0:T(8,128)(2,1)S(1)}, bf16[64,128]{1,0:T(8,128)(2,1)S(1)}, u32[]{:S(2)}, u32[]{:S(2)}) collective-permute-start(bf16[64,128]{1,0:T(8,128)(2,1)S(1)} %get-tuple-element.32), channel_id=1, source_target_pairs={{0,4},{2,6},{4,8},{6,10},{8,12},{10,14},{12,0},{14,2},{1,5},{3,7},... | collective-permute-start | bytes 49160 | tf_op jit(solution)/shard_map/ppermute | solution.py:453
  26.0 9.2 %collective-permute-start.13 = (bf16[64,128]{1,0:T(8,128)(2,1)S(1)}, bf16[64,128]{1,0:T(8,128)(2,1)S(1)}, u32[]{:S(2)}, u32[]{:S(2)}) collective-permute-start(bf16[64,128]{1,0:T(8,128)(2,1)S(1)} %get-tuple-element.33), channel_id=1, source_target_pairs={{0,2},{2,4},{4,6},{6,8},{8,10},{10,12},{12,14},{14,0},{1,3},{3,5},... | collective-permute-start | bytes 49160 | tf_op jit(solution)/shard_map/ppermute | solution.py:453
  45.3 5.9 %collective-permute-start.15 = (bf16[128,128]{1,0:T(8,128)(2,1)S(1)}, bf16[128,128]{1,0:T(8,128)(2,1)S(1)}, u32[]{:S(2)}, u32[]{:S(2)}) collective-permute-start(bf16[128,128]{1,0:T(8,128)(2,1)S(1)} %get-tuple-element.36), channel_id=1, source_target_pairs={{0,4},{2,6},{4,8},{6,10},{8,12},{10,14},{12,0},{14,2},{1,5},{3,7},... | collective-permute-start | bytes 98312 | tf_op jit(solution)/shard_map/ppermute | solution.py:453
  45.6 30.2 %collective-permute-start.16 = (bf16[128,128]{1,0:T(8,128)(2,1)S(1)}, bf16[128,128]{1,0:T(8,128)(2,1)S(1)}, u32[]{:S(2)}, u32[]{:S(2)}) collective-permute-start(bf16[128,128]{1,0:T(8,128)(2,1)S(1)} %get-tuple-element.37), channel_id=1, source_target_pairs={{0,6},{2,8},{4,10},{6,12},{8,14},{10,0},{12,2},{14,4},{1,7},{3,9},... | collective-permute-start | bytes 98312 | tf_op jit(solution)/shard_map/ppermute | solution.py:453
  47.7 28.2 %collective-permute-start.17 = (bf16[128,128]{1,0:T(8,128)(2,1)S(1)}, bf16[128,128]{1,0:T(8,128)(2,1)S(1)}, u32[]{:S(2)}, u32[]{:S(2)}) collective-permute-start(bf16[128,128]{1,0:T(8,128)(2,1)S(1)} %get-tuple-element.38), channel_id=1, source_target_pairs={{0,8},{2,10},{4,12},{6,14},{8,0},{10,2},{12,4},{14,6},{1,9},{3,11}... | collective-permute-start | bytes 98312 | tf_op jit(solution)/shard_map/ppermute | solution.py:453
  48.9 26.9 %collective-permute-start.18 = (bf16[128,128]{1,0:T(8,128)(2,1)S(1)}, bf16[128,128]{1,0:T(8,128)(2,1)S(1)}, u32[]{:S(2)}, u32[]{:S(2)}) collective-permute-start(bf16[128,128]{1,0:T(8,128)(2,1)S(1)} %get-tuple-element.39), channel_id=1, source_target_pairs={{0,10},{2,12},{4,14},{6,0},{8,2},{10,4},{12,6},{14,8},{1,11},{3,13... | collective-permute-start | bytes 98312 | tf_op jit(solution)/shard_map/ppermute | solution.py:453
  50.1 25.7 %collective-permute-start.19 = (bf16[128,128]{1,0:T(8,128)(2,1)S(1)}, bf16[128,128]{1,0:T(8,128)(2,1)S(1)}, u32[]{:S(2)}, u32[]{:S(2)}) collective-permute-start(bf16[128,128]{1,0:T(8,128)(2,1)S(1)} %get-tuple-element.40), channel_id=1, source_target_pairs={{0,12},{2,14},{4,0},{6,2},{8,4},{10,6},{12,8},{14,10},{1,13},{3,15... | collective-permute-start | bytes 98312 | tf_op jit(solution)/shard_map/ppermute | solution.py:453
  51.3 24.6 %collective-permute-start.20 = (bf16[128,128]{1,0:T(8,128)(2,1)S(1)}, bf16[128,128]{1,0:T(8,128)(2,1)S(1)}, u32[]{:S(2)}, u32[]{:S(2)}) collective-permute-start(bf16[128,128]{1,0:T(8,128)(2,1)S(1)} %get-tuple-element.41), channel_id=1, source_target_pairs={{0,14},{2,0},{4,2},{6,4},{8,6},{10,8},{12,10},{14,12},{1,15},{3,1}... | collective-permute-start | bytes 98312 | tf_op jit(solution)/shard_map/ppermute | solution.py:453
  77.9 7.5 %collective-permute-start.21 = (bf16[2,16,2048]{2,1,0:T(8,128)(2,1)S(1)}, bf16[2,16,2048]{2,1,0:T(8,128)(2,1)S(1)}, u32[]{:S(2)}, u32[]{:S(2)}) collective-permute-start(bf16[2,16,2048]{2,1,0:T(8,128)(2,1)S(1)} %merge.1.refs_0_), channel_id=1, source_target_pairs={{0,2},{2,4},{4,6},{6,8},{8,10},{10,12},{12,14},{14,0},{1,3},{3,5},... | collective-permute-start | bytes 393224 | tf_op jit(solution)/shard_map/ppermute | solution.py:453
  80.0 7.8 %collective-permute-start.22 = (bf16[2,16,2048]{2,1,0:T(8,128)(2,1)S(1)}, bf16[2,16,2048]{2,1,0:T(8,128)(2,1)S(1)}, u32[]{:S(2)}, u32[]{:S(2)}) collective-permute-start(bf16[2,16,2048]{2,1,0:T(8,128)(2,1)S(1)} %merge.1.refs_0_), channel_id=1, source_target_pairs={{0,4},{2,6},{4,8},{6,10},{8,12},{10,14},{12,0},{14,2},{1,5},{3,7},... | collective-permute-start | bytes 393224 | tf_op jit(solution)/shard_map/ppermute | solution.py:453
  80.4 7.6 %collective-permute-start.23 = (bf16[2,16,2048]{2,1,0:T(8,128)(2,1)S(1)}, bf16[2,16,2048]{2,1,0:T(8,128)(2,1)S(1)}, u32[]{:S(2)}, u32[]{:S(2)}) collective-permute-start(bf16[2,16,2048]{2,1,0:T(8,128)(2,1)S(1)} %merge.1.refs_0_), channel_id=1, source_target_pairs={{0,6},{2,8},{4,10},{6,12},{8,14},{10,0},{12,2},{14,4},{1,7},{3,9},... | collective-permute-start | bytes 393224 | tf_op jit(solution)/shard_map/ppermute | solution.py:453
  83.4 7.7 %collective-permute-start.24 = (bf16[2,16,2048]{2,1,0:T(8,128)(2,1)S(1)}, bf16[2,16,2048]{2,1,0:T(8,128)(2,1)S(1)}, u32[]{:S(2)}, u32[]{:S(2)}) collective-permute-start(bf16[2,16,2048]{2,1,0:T(8,128)(2,1)S(1)} %merge.1.refs_0_), channel_id=1, source_target_pairs={{0,8},{2,10},{4,12},{6,14},{8,0},{10,2},{12,4},{14,6},{1,9},{3,11}... | collective-permute-start | bytes 393224 | tf_op jit(solution)/shard_map/ppermute | solution.py:453
  83.4 7.7 %collective-permute-start.25 = (bf16[2,16,2048]{2,1,0:T(8,128)(2,1)S(1)}, bf16[2,16,2048]{2,1,0:T(8,128)(2,1)S(1)}, u32[]{:S(2)}, u32[]{:S(2)}) collective-permute-start(bf16[2,16,2048]{2,1,0:T(8,128)(2,1)S(1)} %merge.1.refs_0_), channel_id=1, source_target_pairs={{0,10},{2,12},{4,14},{6,0},{8,2},{10,4},{12,6},{14,8},{1,11},{3,13... | collective-permute-start | bytes 393224 | tf_op jit(solution)/shard_map/ppermute | solution.py:453
  85.5 18.8 %collective-permute-start.26 = (bf16[2,16,2048]{2,1,0:T(8,128)(2,1)S(1)}, bf16[2,16,2048]{2,1,0:T(8,128)(2,1)S(1)}, u32[]{:S(2)}, u32[]{:S(2)}) collective-permute-start(bf16[2,16,2048]{2,1,0:T(8,128)(2,1)S(1)} %merge.1.refs_0_), channel_id=1, source_target_pairs={{0,12},{2,14},{4,0},{6,2},{8,4},{10,6},{12,8},{14,10},{1,13},{3,15... | collective-permute-start | bytes 393224 | tf_op jit(solution)/shard_map/ppermute | solution.py:453
  87.8 16.4 %collective-permute-start.27 = (bf16[2,16,2048]{2,1,0:T(8,128)(2,1)S(1)}, bf16[2,16,2048]{2,1,0:T(8,128)(2,1)S(1)}, u32[]{:S(2)}, u32[]{:S(2)}) collective-permute-start(bf16[2,16,2048]{2,1,0:T(8,128)(2,1)S(1)} %merge.1.refs_0_), channel_id=1, source_target_pairs={{0,14},{2,0},{4,2},{6,4},{8,6},{10,8},{12,10},{14,12},{1,15},{3,1}... | collective-permute-start | bytes 393224 | tf_op jit(solution)/shard_map/ppermute | solution.py:453
  108.3 7.5 %collective-permute-start.28 = (f32[2,128,512]{2,1,0:T(8,128)S(1)}, f32[2,128,512]{2,1,0:T(8,128)S(1)}, u32[]{:S(2)}, u32[]{:S(2)}) collective-permute-start(f32[2,128,512]{2,1,0:T(8,128)S(1)} %project.3), channel_id=1, source_target_pairs={{0,1},{1,0},{2,3},{3,2},{4,5},{5,4},{6,7},{7,6},{8,9},{9,8},{10,11... | collective-permute-start | bytes 1572872 | tf_op jit(solution)/shard_map/ppermute | solution.py:457
  (24 other events, 332.9 us)

commit v2 on v1

v2 whole, which is shorter than its diff:
```python
import functools

import jax
import jax.numpy as jnp
import numpy as np
from jax import lax
from jax.experimental import pallas as pl
from jax.experimental.pallas import tpu as pltpu
from jax.sharding import PartitionSpec as P

ROPE_BASE = 500000.0
BF16, F32, I32 = jnp.bfloat16, jnp.float32, jnp.int32
SMEM = pl.BlockSpec(memory_space=pltpu.SMEM)
VMEM = pl.BlockSpec(memory_space=pltpu.VMEM)
ANY = pl.BlockSpec(memory_space=pl.ANY)
PARAMS = pltpu.CompilerParams(vmem_limit_bytes=60 * 2**20)
LANES = 128
CODES = 64
STAT_ROWS = 16
LEFT = 256


def tables(page_len, head_dim, pages):
    half = head_dim // 2
    freq = ROPE_BASE ** (-(np.arange(half) * 2.0) / head_dim)
    freq = np.concatenate([freq, freq])[None, :]
    sign = np.concatenate([-np.ones(half), np.ones(half)])[None, :]
    token = np.arange(page_len)[:, None] * freq
    first = np.arange(pages)[:, None] * page_len * freq
    out = (np.cos(token), sign * np.sin(token), np.cos(first), sign * np.sin(first), freq, sign)
    return [jnp.asarray(x, F32) for x in out]


def rope_kernel(page_len, per, len_ref, keys_ref, ct_ref, st_ref, cp_ref, sp_ref, out_ref):
    heads, head_dim = keys_ref.shape[2], keys_ref.shape[4]
    for i in range(per):
        number, _ = page_place(len_ref, page_len, pl.program_id(0) * per + i)
        c0, s0 = cp_ref[pl.ds(number, 1), :], sp_ref[pl.ds(number, 1), :]
        ct, st = ct_ref[...], st_ref[...]
        cos = c0 * ct - s0 * st
        sin = s0 * ct + c0 * st
        for k in range(heads):
            x = keys_ref[i, 0, k].astype(F32)
            out_ref[i, k] = (x * cos + pltpu.roll(x, head_dim // 2, 1) * sin).astype(BF16)


def page_place(len_ref, page_len, n):
    begin = jnp.int32(0)
    number, fill = jnp.int32(0), jnp.int32(0)
    for q in range(len_ref.shape[1]):
        length = len_ref[0, q]
        count = (length + page_len - 1) // page_len
        here = (n >= begin) & (n < begin + count)
        number = jnp.where(here, n - begin, number)
        fill = jnp.where(here, jnp.clip(length - (n - begin) * page_len, 0, page_len), fill)
        begin = begin + count
    return number, fill


def rotated_keys(prompt_kv, prompt_lengths, tabs):
    pages, _, heads, page_len, head_dim = prompt_kv.shape
    per = 4
    ct, st, cp, sp, _, _ = tabs
    whole = lambda x: pl.BlockSpec(x.shape, lambda i: (0, 0))
    return pl.pallas_call(
        functools.partial(rope_kernel, page_len, per),
        grid=(pages // per,),
        out_shape=jax.ShapeDtypeStruct((pages, heads, page_len, head_dim), BF16),
        in_specs=[
            SMEM,
            pl.BlockSpec((per, 1, heads, page_len, head_dim), lambda i: (i, 0, 0, 0, 0)),
            whole(ct),
            whole(st),
            whole(cp),
            whole(sp),
        ],
        out_specs=pl.BlockSpec((per, heads, page_len, head_dim), lambda i: (i, 0, 0, 0)),
        compiler_params=PARAMS,
        cost_estimate=pl.CostEstimate(flops=6_000_000, bytes_accessed=2_000_000, transcendentals=0),
        name="rope_pages",
    )(prompt_lengths, prompt_kv, ct, st, cp, sp)


def spread_queries(q_ref, qf_ref, heads):
    steps, rows, width = q_ref.shape
    head_dim = qf_ref.shape[1]
    per = width // head_dim // heads
    block = heads * steps * per
    for s in range(steps):
        for h in range(heads * per):
            k, g = divmod(h, per)
            at = k * steps * per + s * per + g
            qf_ref[pl.ds(at, rows, stride=block), :] = q_ref[s, :, h * head_dim : (h + 1) * head_dim].astype(F32)


def meta_kernel(npool, pair, cache_pages, page_len, slot_ref, len_ref, table_ref, context_ref, meta_ref, own_ref, count):
    items = npool * pair
    most, rows = table_ref.shape
    for e in range(npool):
        count[e] = 0
    for i in range(items):
        meta_ref[0, i] = -1
        own_ref[i] = 0
        own_ref[items + i] = 0
    for n in range(slot_ref.shape[0]):
        slot = slot_ref[n]
        target = slot // cache_pages
        at = target * pair + count[target]
        count[target] = count[target] + 1
        meta_ref[0, at] = slot - target * cache_pages
        _, fill = page_place(len_ref, page_len, n)
        own_ref[at] = n
        own_ref[items + at] = fill
    for r in range(rows):
        context = context_ref[r]
        for j in range(most):
            left = jnp.clip(context - j * page_len, 0, page_len)
            meta_ref[0, CODES + table_ref[j, r]] = r * LEFT + left


def meta_data(page_slot, prompt_lengths, table, context, npool, pair, cache_pages, page_len):
    return pl.pallas_call(
        functools.partial(meta_kernel, npool, pair, cache_pages, page_len),
        out_shape=[
            jax.ShapeDtypeStruct((1, LANES), I32),
            jax.ShapeDtypeStruct((2 * npool * pair,), I32),
        ],
        in_specs=[SMEM] * 4,
        out_specs=[SMEM] * 2,
        scratch_shapes=[pltpu.SMEM((npool,), I32)],
        compiler_params=PARAMS,
        cost_estimate=pl.CostEstimate(flops=1000, bytes_accessed=10_000, transcendentals=0),
        name="meta_data",
    )(page_slot, prompt_lengths, table, context)


def item_request(meta_ref, me, d, i):
    slot = meta_ref[d, i]
    code = meta_ref[me, CODES + jnp.maximum(slot, 0)]
    return jnp.where(slot >= 0, code // LEFT, 0), slot >= 0


def query_kernel(pair, heads, me_ref, meta_ref, q_ref, out_ref, qf):
    npool = out_ref.shape[0]
    rows = q_ref.shape[1]
    block = qf.shape[0] // rows
    me = me_ref[0]
    spread_queries(q_ref, qf, heads)
    for d in range(npool):
        for p in range(pair):
            r, _ = item_request(meta_ref, me, d, me * pair + p)
            at = pl.ds(pl.multiple_of(r * block, block), block)
            out_ref[d, p * block : (p + 1) * block, :] = qf[at, :].astype(BF16)


def queries_out(me, meta, queries, pair, heads, head_dim):
    npool = meta.shape[0]
    steps, rows, width = queries.shape
    block = steps * width // head_dim
    return pl.pallas_call(
        functools.partial(query_kernel, pair, heads),
        out_shape=jax.ShapeDtypeStruct((npool, pair * block, head_dim), BF16),
        in_specs=[SMEM, SMEM, VMEM],
        out_specs=VMEM,
        scratch_shapes=[pltpu.VMEM((rows * block, head_dim), F32)],
        compiler_params=PARAMS,
        cost_estimate=pl.CostEstimate(flops=100_000, bytes_accessed=500_000, transcendentals=0),
        name="queries_out",
    )(me, meta, queries)


def transposed_scores(queries, keys, group):
    turned = jnp.transpose(queries.astype(F32), (1, 0)).astype(BF16)
    chain = lax.broadcasted_iota(I32, turned.shape, 1) // group
    spread = [jnp.where(chain == c, turned, jnp.zeros_like(turned)) for c in range(len(keys))]
    scores = jnp.dot(
        jnp.concatenate(keys, axis=1), jnp.concatenate(spread, axis=0), preferred_element_type=F32
    )
    return scores * (queries.shape[1] ** -0.5)


def lane_values(scalars, lanes_each, shape):
    chain = lax.broadcasted_iota(I32, shape, 1) // lanes_each
    out = jnp.zeros(shape, I32)
    for i, x in enumerate(scalars):
        out = jnp.where(chain == i, x, out)
    return out


def local_kernel(
    page_len,
    heads,
    table_ref,
    context_ref,
    fill_ref,
    q_ref,
    new_ref,
    freq_ref,
    sign_ref,
    cache_ref,
    o_ref,
    stat_ref,
    kv,
    sems,
    qf,
    kf,
    vf,
    position,
):
    steps, rows, width = q_ref.shape
    head_dim = qf.shape[1]
    most = table_ref.shape[0]
    per = width // head_dim // heads
    group = steps * per
    block = heads * group
    together = LANES // block

    def copy(r, j):
        n = r * most + j
        return pltpu.make_async_copy(cache_ref.at[table_ref[j, r]], kv.at[n], sems.at[n])

    for r in range(rows):
        for j in range(most):
            copy(r, j).start()
    spread_queries(q_ref, qf, heads)
    kf[...] = jnp.zeros_like(kf)
    vf[...] = jnp.zeros_like(vf)
    for r in range(rows):
        position[r : r + 1, :] = jnp.full((1, head_dim), context_ref[r], I32)
    for u in range(steps):
        angle = (position[...] + u).astype(F32) * freq_ref[...]
        cos, sin = jnp.cos(angle), jnp.sin(angle) * sign_ref[...]
        for k in range(heads):
            x = new_ref[u, :, k * head_dim : (k + 1) * head_dim].astype(F32)
            at = k * group + u
            kf[pl.ds(at, rows, stride=block), :] = x * cos + pltpu.roll(x, head_dim // 2, 1) * sin
            x = new_ref[u, :, (heads + k) * head_dim : (heads + k + 1) * head_dim].astype(F32)
            vf[pl.ds(at, rows, stride=block), :] = x
    token = lax.broadcasted_iota(I32, (page_len, LANES), 0)
    fresh = lax.broadcasted_iota(I32, (group, LANES), 0)
    step = lax.broadcasted_iota(I32, (group, LANES), 1) % group // per
    fresh_mask = (fresh <= step) & (fresh < steps)

    for i in range(rows // together):
        requests = range(i * together, (i + 1) * together)
        chains = [(r, k) for r in requests for k in range(heads)]
        for r in requests:
            for j in range(most):
                copy(r, j).wait()
        queries = qf[i * LANES : (i + 1) * LANES, :]
        keys, values = [], []
        for r, k in chains:
            at = r * block + k * group
            page = lambda what: [kv[r * most + j, what, k] for j in range(most)]
            keys.append(jnp.concatenate(page(0) + [kf[at : at + group, :].astype(BF16)], axis=0))
            values.append(page(1) + [vf[at : at + group, :].astype(BF16)])
        scores = transposed_scores(queries, keys, group)
        mask = []
        for j in range(most):
            seen = [jnp.minimum(fill_ref[table_ref[j, r]], context_ref[r] - j * page_len) for r in requests]
            mask.append(token < lane_values(seen, block, (1, LANES)))
        parts = [
            jnp.where(m, scores[n * page_len : n * page_len + m.shape[0]], -jnp.inf)
            for n, m in enumerate(mask + [fresh_mask])
        ]
        top = functools.reduce(jnp.maximum, [jnp.max(x, axis=0, keepdims=True) for x in parts])
        parts = [jnp.exp(x - top) for x in parts]
        total = functools.reduce(jnp.add, [jnp.sum(x, axis=0, keepdims=True) for x in parts])
        stats = jnp.concatenate(
            [parts[most], jnp.broadcast_to(top, (8, LANES)), jnp.broadcast_to(total, (8, LANES))]
            + [jnp.zeros((LANES - group - 16, LANES), F32)],
            axis=0,
        )
        stats = jnp.transpose(stats, (1, 0))
        weights = [jnp.transpose(x, (1, 0)).astype(BF16) for x in parts[:most]]
        weights.append(stats[:, :group].astype(BF16))
        weights = jnp.concatenate(weights, axis=1)
        for c in range(len(chains)):
            at = i * LANES + c * group
            o_ref[at : at + group, :] = jnp.dot(
                weights[c * group : (c + 1) * group, :],
                jnp.concatenate(values[c], axis=0),
                preferred_element_type=F32,
            )
        stat_ref[i * LANES : (i + 1) * LANES, :] = stats


def local_attention(table, context, fills, queries, new_kv, cache_kv, tabs):
    steps, rows, width = queries.shape
    slots, _, heads, page_len, head_dim = cache_kv.shape
    block = steps * width // head_dim
    flat = (rows * block, head_dim)
    freq, sign = tabs[4:]
    return pl.pallas_call(
        functools.partial(local_kernel, page_len, heads),
        out_shape=[jax.ShapeDtypeStruct(flat, F32)] * 2,
        in_specs=[SMEM] * 3 + [VMEM] * 4 + [ANY],
        out_specs=[VMEM] * 2,
        scratch_shapes=[
            pltpu.VMEM((table.size, 2, heads, page_len, head_dim), BF16),
            pltpu.SemaphoreType.DMA((table.size,)),
            pltpu.VMEM(flat, F32),
            pltpu.VMEM(flat, F32),
            pltpu.VMEM(flat, F32),
            pltpu.VMEM((rows, head_dim), I32),
        ],
        compiler_params=PARAMS,
        cost_estimate=pl.CostEstimate(flops=800_000_000, bytes_accessed=12_000_000, transcendentals=400_000),
        name="local_attention",
    )(
        table,
        context,
        fills,
        queries,
        new_kv.reshape(steps, rows, 2 * heads * head_dim),
        freq,
        sign,
        cache_kv,
    )


def pieces(x):
    high = x.astype(BF16).astype(F32)
    middle = (x - high).astype(BF16).astype(F32)
    return [high, middle, x - high - middle]


def arrived_kernel(npool, pair, me_ref, meta_ref, own_ref, q_ref, keys_ref, prompt_ref, out_ref, values, sem):
    items = npool * pair
    _, heads, page_len, head_dim = keys_ref.shape
    block = q_ref.shape[0] // items
    group = block // heads
    together = LANES // block
    fetch = pltpu.make_async_copy(prompt_ref.at[:, 1], values, sem)
    fetch.start()
    fetch.wait()
    me = me_ref[0]
    token = lax.broadcasted_iota(I32, (page_len, LANES), 0)
    for i in range(items // together):
        own = range(i * together, (i + 1) * together)
        chains = [(own_ref[x], k) for x in own for k in range(heads)]
        seen = []
        for x in own:
            code = meta_ref[x // pair, CODES + jnp.maximum(meta_ref[me, x], 0)]
            seen.append(jnp.minimum(code % LEFT, own_ref[items + x]))
        scores = transposed_scores(
            q_ref[i * LANES : (i + 1) * LANES, :], [keys_ref[n, k] for n, k in chains], group
        )
        scores = jnp.where(token < lane_values(seen, block, (1, LANES)), scores, -jnp.inf)
        top = jnp.max(scores, axis=0, keepdims=True)
        top = jnp.where(top > -jnp.inf, top, 0.0)
        weights = jnp.exp(scores - top)
        stats = pieces(top) + pieces(jnp.sum(weights, axis=0, keepdims=True))
        stats = jnp.concatenate(stats + [jnp.zeros((STAT_ROWS - len(stats), LANES), F32)], axis=0).astype(BF16)
        weights = jnp.transpose(weights, (1, 0)).astype(BF16)
        for c, (n, k) in enumerate(chains):
            x, at = own[c // heads], (c % heads) * group
            at = (x % pair) * block + at
            out_ref[x // pair, at : at + group, :] = jnp.dot(
                weights[c * group : (c + 1) * group, :], values[n, k], preferred_element_type=F32
            ).astype(BF16)
        for e in sorted({x // pair for x in own}):
            out_ref[e, pair * block : pair * block + STAT_ROWS, :] = stats


def arrived_attention(me, meta, own, queries, keys, prompt_kv):
    npool, rows, head_dim = queries.shape
    pages, _, heads, page_len, _ = prompt_kv.shape
    pair = own.shape[0] // 2 // npool
    return pl.pallas_call(
        functools.partial(arrived_kernel, npool, pair),
        out_shape=jax.ShapeDtypeStruct((npool, rows + STAT_ROWS, head_dim), BF16),
        in_specs=[SMEM] * 3 + [VMEM] * 2 + [ANY],
        out_specs=VMEM,
        scratch_shapes=[
            pltpu.VMEM((pages, heads, page_len, head_dim), BF16),
            pltpu.SemaphoreType.DMA,
        ],
        compiler_params=PARAMS,
        cost_estimate=pl.CostEstimate(flops=200_000_000, bytes_accessed=4_000_000, transcendentals=70_000),
        name="arrived_attention",
    )(me, meta, own, queries.reshape(npool * rows, head_dim), keys, prompt_kv)


def merge_kernel(pair, heads, me_ref, meta_ref, parts_ref, o_ref, stat_ref, out_ref, mixed, top, total, turned):
    npool = parts_ref.shape[0]
    steps, rows, width = out_ref.shape
    head_dim = o_ref.shape[1]
    per = width // head_dim // heads
    group = steps * per
    block = heads * group
    me = me_ref[0]
    shape = top.shape
    mixed[...] = o_ref[...]
    top[...] = jnp.broadcast_to(stat_ref[:, group : group + 1], shape)
    total[...] = jnp.broadcast_to(stat_ref[:, group + 8 : group + 9], shape)
    tops, totals = [], []
    for d in range(npool):
        x = parts_ref[d, pair * block : pair * block + STAT_ROWS, :].astype(F32)
        tops.append(x[0:1] + x[1:2] + x[2:3])
        totals.append(x[3:4] + x[4:5] + x[5:6])
    empty = [jnp.zeros((LANES // 2 - npool, LANES), F32)]
    turned[...] = jnp.transpose(jnp.concatenate(tops + empty + totals + empty, axis=0), (1, 0))
    for d in range(npool):
        for p in range(pair):
            i = me * pair + p
            r, there = item_request(meta_ref, me, d, i)
            at = pl.ds(pl.multiple_of(r * block, block), block)
            lane = pl.ds(pl.multiple_of(lax.rem(i * block, LANES), block), block)
            m = jnp.broadcast_to(turned[lane, d : d + 1], (block, head_dim))
            l = jnp.broadcast_to(turned[lane, LANES // 2 + d : LANES // 2 + d + 1], (block, head_dim))
            seen = (l > 0.0) & there
            o = parts_ref[d, p * block : (p + 1) * block, :].astype(F32)
            old = top[at, :]
            new = jnp.where(seen, jnp.maximum(old, m), old)
            a = jnp.exp(old - new)
            b = jnp.where(seen, jnp.exp(m - new), 0.0)
            top[at, :] = new
            total[at, :] = total[at, :] * a + l * b
            mixed[at, :] = mixed[at, :] * a + o * b
    for s in range(steps):
        for h in range(heads * per):
            k, g = divmod(h, per)
            at = pl.ds(k * group + s * per + g, rows, stride=block)
            out_ref[s, :, h * head_dim : (h + 1) * head_dim] = (mixed[at, :] / total[at, :]).astype(BF16)


def merged(me, meta, parts, local, shape, heads, pair):
    flat = local[0].shape
    return pl.pallas_call(
        functools.partial(merge_kernel, pair, heads),
        out_shape=jax.ShapeDtypeStruct(shape, BF16),
        in_specs=[SMEM] * 2 + [VMEM] * 3,
        out_specs=VMEM,
        scratch_shapes=[pltpu.VMEM(flat, F32)] * 3 + [pltpu.VMEM((LANES, LANES), F32)],
        compiler_params=PARAMS,
        cost_estimate=pl.CostEstimate(flops=2_000_000, bytes_accessed=1_500_000, transcendentals=100_000),
        name="merge",
    )(me, meta, parts, *local)


def project_kernel(npool, scalars, *refs):
    blocks = refs[:npool]
    weight_ref, out_ref, lhs = refs[npool:]
    steps, rows, _ = blocks[0].shape

    @pl.when(pl.program_id(0) == 0)
    def _():
        for t in range(npool):
            owner = lax.rem(scalars[0] + npool - t, npool)
            at = pl.ds(pl.multiple_of(owner * rows, rows), rows)
            for s in range(steps):
                lhs[s, at, :] = blocks[t][s]

    for s in range(steps):
        out_ref[s] = jnp.dot(lhs[s], weight_ref[...], preferred_element_type=F32)


def projection(me, first_tile, blocks, weight, columns, tile):
    npool = len(blocks)
    steps, rows, width = blocks[0].shape
    whole = pl.BlockSpec((steps, rows, width), lambda i, sc: (0, 0, 0))
    return pl.pallas_call(
        functools.partial(project_kernel, npool),
        out_shape=jax.ShapeDtypeStruct((steps, npool * rows, columns), F32),
        grid_spec=pltpu.PrefetchScalarGridSpec(
            num_scalar_prefetch=1,
            grid=(columns // tile,),
            in_specs=[whole] * npool + [pl.BlockSpec((width, tile), lambda i, sc: (0, sc[1] + i))],
            out_specs=pl.BlockSpec((steps, npool * rows, tile), lambda i, sc: (0, 0, i)),
            scratch_shapes=[pltpu.VMEM((steps, npool * rows, width), BF16)],
        ),
        compiler_params=PARAMS,
        cost_estimate=pl.CostEstimate(
            flops=2 * steps * npool * rows * width * columns, bytes_accessed=4_000_000, transcendentals=0
        ),
        name="project",
    )(jnp.stack([me, first_tile]), *blocks, weight)


def shift(x, npool, by):
    return lax.ppermute(x, "pool", [(i, (i + by) % npool) for i in range(npool)])


def swap_halves(x):
    return lax.ppermute(x, "tp", [(0, 1), (1, 0)])


def shards(
    prompt_kv,
    prompt_lengths,
    page_slot,
    cache_kv,
    cache_fill,
    page_table,
    context_lengths,
    queries,
    new_kv,
    out_weight,
):
    npool = lax.axis_size("pool")
    me = lax.axis_index("pool").astype(I32)
    pages, _, heads, page_len, head_dim = prompt_kv.shape
    cache_pages = cache_kv.shape[0]
    pair = (pages + npool - 1) // npool
    tabs = tables(page_len, head_dim, pages)
    me1 = me[None]
    table = page_table.T

    mine, own = meta_data(page_slot, prompt_lengths, table, context_lengths, npool, pair, cache_pages, page_len)
    meta = lax.all_gather(mine, "pool", axis=0, tiled=True)
    keys = rotated_keys(prompt_kv, prompt_lengths, tabs)
    local = local_attention(table, context_lengths, cache_fill, queries, new_kv, cache_kv, tabs)
    sent = queries_out(me1, meta, queries, pair, heads, head_dim)
    got = lax.all_to_all(sent, "pool", split_axis=0, concat_axis=0, tiled=True)
    parts = arrived_attention(me1, meta, own, got, keys, prompt_kv)
    parts = lax.all_to_all(parts, "pool", split_axis=0, concat_axis=0, tiled=True)
    attention = merged(me1, meta, parts, local, queries.shape, heads, pair)
    blocks = [attention] + [shift(attention, npool, t) for t in range(1, npool)]

    half = out_weight.shape[1] // 2
    tile = min(half, 256)
    mine = lax.axis_index("tp").astype(I32)
    other_terms = projection(me, (1 - mine) * (half // tile), blocks, out_weight, half, tile)
    other_terms = swap_halves(other_terms)
    terms = projection(me, mine * (half // tile), blocks, out_weight, half, tile)
    return (terms + other_terms).astype(BF16)


def solution(mesh):
    return jax.shard_map(
        shards,
        mesh=mesh,
        in_specs=(
            P(("group", "pool"), None, "tp", None, None),
            P(("group", "pool"), None),
            P(("group", "pool")),
            P(("group", "pool"), None, "tp", None, None),
            P(("group", "pool")),
            P(("group", "pool"), None),
            P(("group", "pool")),
            P(None, ("group", "pool"), "tp"),
            P(None, ("group", "pool"), None, "tp", None),
            P("tp", "pool"),
        ),
        out_specs=P(None, "group", ("pool", "tp")),
        check_vma=False,
    )
```

time: 117 us -> 95.7 us (0.82)
  the two profiles are of different devices: /device:TPU:15 before, /device:TPU:0 now
where the time goes in v2:
time: 95.7 us; the launch traced here: 95 us
  Pallas kernels  31 us (32%)
  blocking collectives  22.8 us (24%)
  waiting for transfers between devices  18.2 us (19%)
  starting transfers between devices  16.6 us (17%)
  local copies, waits for them, and re-layouts  3.24 us (3%)
  other arithmetic  3.02 us (3%)
    all_gather x1, blocking collectives, shards(): meta = lax.all_gather(mine, 'pool', axis=0, tiled=True)  22.8 us
    ppermute x7, waiting for transfers between devices, shift(): lax.ppermute(x, 'pool', [(i, (i + by) % npool) for i in range(npool)])  14.6 us
    ppermute x7, starting transfers between devices, shift(): lax.ppermute(x, 'pool', [(i, (i + by) % npool) for i in range(npool)])  9.88 us
    pallas_call x1, Pallas kernels, local_attention(): pl.pallas_call(functools.partial(local_kernel, page_len, heads), out_shap...  8.21 us
    pallas_call x2, Pallas kernels, projection(): pl.pallas_call(functools.partial(project_kernel, npool), out_shape=jax.Sh...  7.88 us
    pallas_call x1, Pallas kernels, arrived_attention(): pl.pallas_call(functools.partial(arrived_kernel, npool, pair), out_shape=...  4.85 us
    pallas_call x1, Pallas kernels, rotated_keys(): pl.pallas_call(functools.partial(rope_kernel, page_len, per), grid=(pages...  3.76 us
    all_to_all x1, waiting for transfers between devices, shards(): got = lax.all_to_all(sent, 'pool', split_axis=0, concat_axis=0, tiled=True)  3.52 us
  transfers between devices with their start and end apart: 10, of which 6 were waited for; matrix products, arithmetic and copies ran while one was open for 2% of the time, Pallas kernels for 17%

profile of v2, /device:TPU:0, one launch (start us, length us, event | category | flops | bytes accessed | tf_op | source)
XLA Modules:
  0.0 95.0 jit_solution(2029417232200332574)
XLA Ops:
  0.0 1.9 %meta_data.1 = (s32[1,128]{1,0:T(1,128)}, s32[32]{0:T(128)}) custom-call(s32[16]{0:T(128)} %slot_ref.1, s32[1,4]{1,0:T(1,128)} %len_ref.3, s32[3,16]{1,0:T(4,128)} %bitcast.11, s32[16]{0:T(128)} %context_ref.3), custom_call_target="tpu_custom_call" | custom-call | flops 1000 | bytes 10000 | tf_op jit(solution)/shard_map/meta_data/pallas_call | solution.py:122
  1.9 22.8 %all-gather = s32[8,1,128]{2,1,0:T(1,128)} all-gather(s32[1,1,128]{2,1,0:T(1,128)} %bitcast.13), channel_id=1, replica_groups=mesh['group'=2,'pool'=8,'tp'=2] {'pool'}, dimensions={0}, use_global_device_ids=true | all-gather | bytes 4608 | tf_op jit(solution)/shard_map/all_gather | solution.py:511
  24.7 1.9 %queries_out.1 = bf16[8,64,128]{2,1,0:T(8,128)(2,1)} custom-call(s32[1]{0:T(128)} %bitcast.me_ref, s32[8,128]{1,0:T(8,128)} %bitcast.8, bf16[2,16,2048]{2,1,0:T(8,128)(2,1)} %q_ref.3), custom_call_target="tpu_custom_call" | custom-call | flops 100000 | bytes 500000 | tf_op jit(solution)/shard_map/queries_out/pallas_call | solution.py:160
  26.6 3.4 %all-to-all-start = ((bf16[8,64,128]{2,1,0:T(8,128)(2,1)}), bf16[8,64,128]{2,1,0:T(8,128)(2,1)S(1)}, u32[]{:S(2)}, u32[]{:S(2)}) async-start(bf16[8,64,128]{2,1,0:T(8,128)(2,1)} %queries_out.1), calls=%async_computation | async-start | bytes 262144 | tf_op jit(solution)/shard_map/all_to_all | solution.py:515
  30.0 3.8 %rope_pages.1.keys_ref = bf16[16,2,128,128]{3,2,1,0:T(8,128)(2,1)} custom-call(s32[1,4]{1,0:T(1,128)} %len_ref.3, bf16[16,2,2,128,128]{4,3,2,1,0:T(8,128)(2,1)} %prompt_ref.1, f32[128,128]{1,0:T(8,128)} %constant.24.clone.ct_ref, f32[128,128]{1,0:T(8,128)} %constant.25.clone.st_ref, f32[16,128]{1,0:T(8,128)} %constant.26.clone.cp_ref, ...), custom_call_target="tpu_custom_call" | custom-call | flops 6000000 | bytes 2000000 | tf_op jit(solution)/shard_map/rope_pages/pallas_call | solution.py:65
  33.7 3.5 %all-to-all-done = bf16[8,64,128]{2,1,0:T(8,128)(2,1)S(1)} async-done(((bf16[8,64,128]{2,1,0:T(8,128)(2,1)}), bf16[8,64,128]{2,1,0:T(8,128)(2,1)S(1)}, u32[]{:S(2)}, u32[]{:S(2)}) %all-to-all-start) | async-done | bytes 131104 | tf_op jit(solution)/shard_map/all_to_all | solution.py:515
  37.3 0.7 copy-done.8
  37.9 4.9 %arrived_attention.1 = bf16[8,80,128]{2,1,0:T(8,128)(2,1)} custom-call(s32[1]{0:T(128)} %bitcast.me_ref, s32[8,128]{1,0:T(8,128)} %bitcast.9, s32[32]{0:T(128)} %get-tuple-element.10.own_ref, bf16[512,128]{1,0:T(8,128)(2,1)} %bitcast.7, bf16[16,2,128,128]{3,2,1,0:T(8,128)(2,1)} %rope_pages.1.keys_ref, bf16[16,2,2,128,128]{4,3,2,1,0:T(8,128)(2,1)} %prompt_ref.1), custom_call_target="tpu_custom_call" | custom-call | flops 200000000 | bytes 4000000 | tf_op jit(solution)/shard_map/arrived_attention/pallas_call | solution.py:370
  42.8 3.4 %all-to-all-start.1 = ((bf16[8,80,128]{2,1,0:T(8,128)(2,1)}), bf16[8,80,128]{2,1,0:T(8,128)(2,1)S(1)}, u32[]{:S(2)}, u32[]{:S(2)}) async-start(bf16[8,80,128]{2,1,0:T(8,128)(2,1)} %arrived_attention.1), calls=%async_computation.1 | async-start | bytes 327680 | tf_op jit(solution)/shard_map/all_to_all | solution.py:517
  46.2 0.6 reshape.7.new_ref
  46.8 8.2 %local_attention.1 = (f32[512,128]{1,0:T(8,128)}, f32[512,128]{1,0:T(8,128)}) custom-call(s32[3,16]{1,0:T(4,128)} %bitcast.12, s32[16]{0:T(128)} %context_ref.3, s32[48]{0:T(128)} %fill_ref.1, bf16[2,16,2048]{2,1,0:T(8,128)(2,1)} %q_ref.3, bf16[2,16,512]{2,1,0:T(8,128)(2,1)} %reshape.7.new_ref, f32[1,128]{1,0:T(1,128)} %constant.28.clone.freq_ref, ...), custom_call_target="tpu_custom_call" | custom-call | flops 800000000 | bytes 12000000 | tf_op jit(solution)/shard_map/local_attention/pallas_call | solution.py:294
  55.0 0.6 copy-done
  55.7 2.5 %merge.1.refs_0_ = bf16[2,16,2048]{2,1,0:T(8,128)(2,1)} custom-call(s32[1]{0:T(128)} %bitcast.me_ref, s32[8,128]{1,0:T(8,128)} %bitcast.10, bf16[8,80,128]{2,1,0:T(8,128)(2,1)} %copy-done, f32[512,128]{1,0:T(8,128)} %get-tuple-element.11.o_ref, f32[512,128]{1,0:T(8,128)} %get-tuple-element.12.stat_ref), custom_call_target="tpu_custom_call" | custom-call | flops 2000000 | bytes 1500000 | tf_op jit(solution)/shard_map/merge/pallas_call | solution.py:430
  58.2 4.7 %collective-permute-start.6 = (bf16[2,16,2048]{2,1,0:T(8,128)(2,1)}, bf16[2,16,2048]{2,1,0:T(8,128)(2,1)S(1)}, u32[]{:S(2)}, u32[]{:S(2)}) collective-permute-start(bf16[2,16,2048]{2,1,0:T(8,128)(2,1)} %merge.1.refs_0_), channel_id=1, source_target_pairs={{0,14},{2,0},{4,2},{6,4},{8,6},{10,8},{12,10},{14,12},{1,15},{3,1}... | collective-permute-start | bytes 393224 | tf_op jit(solution)/shard_map/ppermute | solution.py:482
  63.4 2.9 %collective-permute-start.3 = (bf16[2,16,2048]{2,1,0:T(8,128)(2,1)}, bf16[2,16,2048]{2,1,0:T(8,128)(2,1)S(1)}, u32[]{:S(2)}, u32[]{:S(2)}) collective-permute-start(bf16[2,16,2048]{2,1,0:T(8,128)(2,1)} %merge.1.refs_0_), channel_id=1, source_target_pairs={{0,8},{2,10},{4,12},{6,14},{8,0},{10,2},{12,4},{14,6},{1,9},{3,11}... | collective-permute-start | bytes 393224 | tf_op jit(solution)/shard_map/ppermute | solution.py:482
  66.3 0.8 collective-permute-done.6.refs_7_
  67.1 1.2 %collective-permute-start.1 = (bf16[2,16,2048]{2,1,0:T(8,128)(2,1)}, bf16[2,16,2048]{2,1,0:T(8,128)(2,1)S(1)}, u32[]{:S(2)}, u32[]{:S(2)}) collective-permute-start(bf16[2,16,2048]{2,1,0:T(8,128)(2,1)} %merge.1.refs_0_), channel_id=1, source_target_pairs={{0,4},{2,6},{4,8},{6,10},{8,12},{10,14},{12,0},{14,2},{1,5},{3,7},... | collective-permute-start | bytes 393224 | tf_op jit(solution)/shard_map/ppermute | solution.py:482
  68.3 2.9 %collective-permute-done.5.refs_6_ = bf16[2,16,2048]{2,1,0:T(8,128)(2,1)S(1)} collective-permute-done((bf16[2,16,2048]{2,1,0:T(8,128)(2,1)}, bf16[2,16,2048]{2,1,0:T(8,128)(2,1)S(1)}, u32[]{:S(2)}, u32[]{:S(2)}) %collective-permute-start.5) | collective-permute-done | bytes 131104 | tf_op jit(solution)/shard_map/ppermute | solution.py:482
  72.5 8.5 %collective-permute-done.3.refs_4_ = bf16[2,16,2048]{2,1,0:T(8,128)(2,1)S(1)} collective-permute-done((bf16[2,16,2048]{2,1,0:T(8,128)(2,1)}, bf16[2,16,2048]{2,1,0:T(8,128)(2,1)S(1)}, u32[]{:S(2)}, u32[]{:S(2)}) %collective-permute-start.3) | collective-permute-done | bytes 131104 | tf_op jit(solution)/shard_map/ppermute | solution.py:482
  81.0 2.3 %collective-permute-done.2.refs_3_ = bf16[2,16,2048]{2,1,0:T(8,128)(2,1)S(1)} collective-permute-done((bf16[2,16,2048]{2,1,0:T(8,128)(2,1)}, bf16[2,16,2048]{2,1,0:T(8,128)(2,1)S(1)}, u32[]{:S(2)}, u32[]{:S(2)}) %collective-permute-start.2) | collective-permute-done | bytes 131104 | tf_op jit(solution)/shard_map/ppermute | solution.py:482
  84.0 0.7 copy-done.7
  84.7 3.9 %project.3 = f32[2,128,512]{2,1,0:T(8,128)} custom-call(s32[2]{0:T(128)} %pad_add_fusion.1.scalars, bf16[2,16,2048]{2,1,0:T(8,128)(2,1)} %merge.1.refs_0_, bf16[2,16,2048]{2,1,0:T(8,128)(2,1)} %copy-done.7, bf16[2,16,2048]{2,1,0:T(8,128)(2,1)} %copy-done.6, bf16[2,16,2048]{2,1,0:T(8,128)(2,1)} %copy-done.5, bf16[2,16,2048]{2,1,0:T(8,128)(2,1)} %copy-done.4, ...), custom_call_target="tpu_custom_call" | custom-call | flops 536870912 | bytes 4000000 | tf_op jit(solution)/shard_map/project/pallas_call | solution.py:463
  89.2 3.9 %project.2 = f32[2,128,512]{2,1,0:T(8,128)} custom-call(s32[2]{0:T(128)} %pad_add_fusion.scalars, bf16[2,16,2048]{2,1,0:T(8,128)(2,1)} %merge.1.refs_0_, bf16[2,16,2048]{2,1,0:T(8,128)(2,1)} %copy-done.7, bf16[2,16,2048]{2,1,0:T(8,128)(2,1)} %copy-done.6, bf16[2,16,2048]{2,1,0:T(8,128)(2,1)} %copy-done.5, bf16[2,16,2048]{2,1,0:T(8,128)(2,1)} %copy-done.4, ...), custom_call_target="tpu_custom_call" | custom-call | flops 536870912 | bytes 4000000 | tf_op jit(solution)/shard_map/project/pallas_call | solution.py:463
  93.2 1.8 %add_convert_fusion = bf16[2,128,512]{2,1,0:T(8,128)(2,1)} fusion(f32[2,128,512]{2,1,0:T(8,128)} %project.2, f32[2,128,512]{2,1,0:T(8,128)S(1)} %collective-permute-done.7), kind=kLoop, calls=%fused_computation | loop fusion | flops 262144 | bytes 1310720 | tf_op jit(solution)/shard_map/convert_element_type | solution.py:527
  (29 shorter events, 3.1 us)
Async XLA Ops:
  0.0 46.2 %copy-start.9 = (bf16[2,16,2,2,128]{4,3,2,1,0:T(2,128)(2,1)S(1)}, bf16[2,16,2,2,128]{4,3,2,1,0:T(2,128)(2,1)}, u32[]{:S(2)}) copy-start(bf16[2,16,2,2,128]{4,3,2,1,0:T(2,128)(2,1)} %param.24) | copy-start | bytes 98308
  26.6 10.7 %all-to-all-start = ((bf16[8,64,128]{2,1,0:T(8,128)(2,1)}), bf16[8,64,128]{2,1,0:T(8,128)(2,1)S(1)}, u32[]{:S(2)}, u32[]{:S(2)}) async-start(bf16[8,64,128]{2,1,0:T(8,128)(2,1)} %queries_out.1), calls=%async_computation | async-start | bytes 262144 | tf_op jit(solution)/shard_map/all_to_all | solution.py:515
  37.3 0.7 copy-start.8
  42.8 12.2 %all-to-all-start.1 = ((bf16[8,80,128]{2,1,0:T(8,128)(2,1)}), bf16[8,80,128]{2,1,0:T(8,128)(2,1)S(1)}, u32[]{:S(2)}, u32[]{:S(2)}) async-start(bf16[8,80,128]{2,1,0:T(8,128)(2,1)} %arrived_attention.1), calls=%async_computation.1 | async-start | bytes 327680 | tf_op jit(solution)/shard_map/all_to_all | solution.py:517
  55.0 0.7 copy-start
  58.2 8.9 %collective-permute-start.6 = (bf16[2,16,2048]{2,1,0:T(8,128)(2,1)}, bf16[2,16,2048]{2,1,0:T(8,128)(2,1)S(1)}, u32[]{:S(2)}, u32[]{:S(2)}) collective-permute-start(bf16[2,16,2048]{2,1,0:T(8,128)(2,1)} %merge.1.refs_0_), channel_id=1, source_target_pairs={{0,14},{2,0},{4,2},{6,4},{8,6},{10,8},{12,10},{14,12},{1,15},{3,1}... | collective-permute-start | bytes 393224 | tf_op jit(solution)/shard_map/ppermute | solution.py:482
  62.8 8.4 %collective-permute-start.5 = (bf16[2,16,2048]{2,1,0:T(8,128)(2,1)}, bf16[2,16,2048]{2,1,0:T(8,128)(2,1)S(1)}, u32[]{:S(2)}, u32[]{:S(2)}) collective-permute-start(bf16[2,16,2048]{2,1,0:T(8,128)(2,1)} %merge.1.refs_0_), channel_id=1, source_target_pairs={{0,12},{2,14},{4,0},{6,2},{8,4},{10,6},{12,8},{14,10},{1,13},{3,15... | collective-permute-start | bytes 393224 | tf_op jit(solution)/shard_map/ppermute | solution.py:482
  63.4 9.1 %collective-permute-start.4 = (bf16[2,16,2048]{2,1,0:T(8,128)(2,1)}, bf16[2,16,2048]{2,1,0:T(8,128)(2,1)S(1)}, u32[]{:S(2)}, u32[]{:S(2)}) collective-permute-start(bf16[2,16,2048]{2,1,0:T(8,128)(2,1)} %merge.1.refs_0_), channel_id=1, source_target_pairs={{0,10},{2,12},{4,14},{6,0},{8,2},{10,4},{12,6},{14,8},{1,11},{3,13... | collective-permute-start | bytes 393224 | tf_op jit(solution)/shard_map/ppermute | solution.py:482
  63.4 17.6 %collective-permute-start.3 = (bf16[2,16,2048]{2,1,0:T(8,128)(2,1)}, bf16[2,16,2048]{2,1,0:T(8,128)(2,1)S(1)}, u32[]{:S(2)}, u32[]{:S(2)}) collective-permute-start(bf16[2,16,2048]{2,1,0:T(8,128)(2,1)} %merge.1.refs_0_), channel_id=1, source_target_pairs={{0,8},{2,10},{4,12},{6,14},{8,0},{10,2},{12,4},{14,6},{1,9},{3,11}... | collective-permute-start | bytes 393224 | tf_op jit(solution)/shard_map/ppermute | solution.py:482
  66.3 17.0 %collective-permute-start.2 = (bf16[2,16,2048]{2,1,0:T(8,128)(2,1)}, bf16[2,16,2048]{2,1,0:T(8,128)(2,1)S(1)}, u32[]{:S(2)}, u32[]{:S(2)}) collective-permute-start(bf16[2,16,2048]{2,1,0:T(8,128)(2,1)} %merge.1.refs_0_), channel_id=1, source_target_pairs={{0,6},{2,8},{4,10},{6,12},{8,14},{10,0},{12,2},{14,4},{1,7},{3,9},... | collective-permute-start | bytes 393224 | tf_op jit(solution)/shard_map/ppermute | solution.py:482
  67.1 16.2 %copy-start.1 = (bf16[2,16,2048]{2,1,0:T(8,128)(2,1)}, bf16[2,16,2048]{2,1,0:T(8,128)(2,1)S(1)}, u32[]{:S(2)}) copy-start(bf16[2,16,2048]{2,1,0:T(8,128)(2,1)S(1)} %collective-permute-done.6.refs_7_) | copy-start | bytes 393220
  67.1 16.2 %collective-permute-start.1 = (bf16[2,16,2048]{2,1,0:T(8,128)(2,1)}, bf16[2,16,2048]{2,1,0:T(8,128)(2,1)S(1)}, u32[]{:S(2)}, u32[]{:S(2)}) collective-permute-start(bf16[2,16,2048]{2,1,0:T(8,128)(2,1)} %merge.1.refs_0_), channel_id=1, source_target_pairs={{0,4},{2,6},{4,8},{6,10},{8,12},{10,14},{12,0},{14,2},{1,5},{3,7},... | collective-permute-start | bytes 393224 | tf_op jit(solution)/shard_map/ppermute | solution.py:482
  71.2 12.1 %copy-start.2 = (bf16[2,16,2048]{2,1,0:T(8,128)(2,1)}, bf16[2,16,2048]{2,1,0:T(8,128)(2,1)S(1)}, u32[]{:S(2)}) copy-start(bf16[2,16,2048]{2,1,0:T(8,128)(2,1)S(1)} %collective-permute-done.5.refs_6_) | copy-start | bytes 393220
  71.2 12.1 %collective-permute-start = (bf16[2,16,2048]{2,1,0:T(8,128)(2,1)}, bf16[2,16,2048]{2,1,0:T(8,128)(2,1)S(1)}, u32[]{:S(2)}, u32[]{:S(2)}) collective-permute-start(bf16[2,16,2048]{2,1,0:T(8,128)(2,1)} %merge.1.refs_0_), channel_id=1, source_target_pairs={{0,2},{2,4},{4,6},{6,8},{8,10},{10,12},{12,14},{14,0},{1,3},{3,5},... | collective-permute-start | bytes 393224 | tf_op jit(solution)/shard_map/ppermute | solution.py:482
  72.5 10.9 %copy-start.3 = (bf16[2,16,2048]{2,1,0:T(8,128)(2,1)}, bf16[2,16,2048]{2,1,0:T(8,128)(2,1)S(1)}, u32[]{:S(2)}) copy-start(bf16[2,16,2048]{2,1,0:T(8,128)(2,1)S(1)} %collective-permute-done.4.refs_5_) | copy-start | bytes 393220
  81.0 2.4 %copy-start.4 = (bf16[2,16,2048]{2,1,0:T(8,128)(2,1)}, bf16[2,16,2048]{2,1,0:T(8,128)(2,1)S(1)}, u32[]{:S(2)}) copy-start(bf16[2,16,2048]{2,1,0:T(8,128)(2,1)S(1)} %collective-permute-done.3.refs_4_) | copy-start | bytes 393220
  83.3 0.7 copy-start.5
  83.3 0.7 copy-start.6
  84.0 0.7 copy-start.7
  88.6 4.5 %collective-permute-start.7 = (f32[2,128,512]{2,1,0:T(8,128)}, f32[2,128,512]{2,1,0:T(8,128)S(1)}, u32[]{:S(2)}, u32[]{:S(2)}) collective-permute-start(f32[2,128,512]{2,1,0:T(8,128)} %project.3), channel_id=1, source_target_pairs={{0,1},{1,0},{2,3},{3,2},{4,5},{5,4},{6,7},{7,6},{8,9},{9,8},{10,11... | collective-permute-start | bytes 1572872 | tf_op jit(solution)/shard_map/ppermute | solution.py:486

commit v3 on v2

--- a/solution.py
+++ b/solution.py
@@ -13,7 +13,9 @@
 SMEM = pl.BlockSpec(memory_space=pltpu.SMEM)
 VMEM = pl.BlockSpec(memory_space=pltpu.VMEM)
 ANY = pl.BlockSpec(memory_space=pl.ANY)
-PARAMS = pltpu.CompilerParams(vmem_limit_bytes=60 * 2**20)
+SMALL = pltpu.CompilerParams(vmem_limit_bytes=24 * 2**20)
+MIDDLE = pltpu.CompilerParams(vmem_limit_bytes=57 * 2**20)
+LARGE = pltpu.CompilerParams(vmem_limit_bytes=59 * 2**20)
 LANES = 128
 CODES = 64
 STAT_ROWS = 16
@@ -31,8 +33,26 @@
     return [jnp.asarray(x, F32) for x in out]
 
 
-def rope_kernel(page_len, per, len_ref, keys_ref, ct_ref, st_ref, cp_ref, sp_ref, out_ref):
-    heads, head_dim = keys_ref.shape[2], keys_ref.shape[4]
+def rope_kernel(
+    npool, cache_pages, per, slot_ref, len_ref, keys_ref, ct_ref, st_ref, cp_ref, sp_ref, out_ref, own_ref, count
+):
+    _, _, heads, page_len, head_dim = keys_ref.shape
+
+    @pl.when(pl.program_id(0) == 0)
+    def _():
+        items = own_ref.shape[0] // 2
+        for e in range(npool):
+            count[e] = 0
+        for i in range(items):
+            own_ref[i] = 0
+            own_ref[items + i] = 0
+        for n in range(slot_ref.shape[0]):
+            target = slot_ref[n] // cache_pages
+            at = target * (items // npool) + count[target]
+            count[target] = count[target] + 1
+            own_ref[at] = n
+            own_ref[items + at] = page_place(len_ref, page_len, n)[1]
+
     for i in range(per):
         number, _ = page_place(len_ref, page_len, pl.program_id(0) * per + i)
         c0, s0 = cp_ref[pl.ds(number, 1), :], sp_ref[pl.ds(number, 1), :]
@@ -57,16 +77,20 @@
     return number, fill
 
 
-def rotated_keys(prompt_kv, prompt_lengths, tabs):
+def rotated_keys(prompt_kv, page_slot, prompt_lengths, tabs, npool, pair, cache_pages):
     pages, _, heads, page_len, head_dim = prompt_kv.shape
-    per = 4
+    per = pages // 2
     ct, st, cp, sp, _, _ = tabs
     whole = lambda x: pl.BlockSpec(x.shape, lambda i: (0, 0))
     return pl.pallas_call(
-        functools.partial(rope_kernel, page_len, per),
+        functools.partial(rope_kernel, npool, cache_pages, per),
         grid=(pages // per,),
-        out_shape=jax.ShapeDtypeStruct((pages, heads, page_len, head_dim), BF16),
+        out_shape=[
+            jax.ShapeDtypeStruct((pages, heads, page_len, head_dim), BF16),
+            jax.ShapeDtypeStruct((2 * npool * pair,), I32),
+        ],
         in_specs=[
+            SMEM,
             SMEM,
             pl.BlockSpec((per, 1, heads, page_len, head_dim), lambda i: (i, 0, 0, 0, 0)),
             whole(ct),
@@ -74,11 +98,12 @@
             whole(cp),
             whole(sp),
         ],
-        out_specs=pl.BlockSpec((per, heads, page_len, head_dim), lambda i: (i, 0, 0, 0)),
-        compiler_params=PARAMS,
+        out_specs=[pl.BlockSpec((per, heads, page_len, head_dim), lambda i: (i, 0, 0, 0)), SMEM],
+        scratch_shapes=[pltpu.SMEM((npool,), I32)],
+        compiler_params=LARGE,
         cost_estimate=pl.CostEstimate(flops=6_000_000, bytes_accessed=2_000_000, transcendentals=0),
         name="rope_pages",
-    )(prompt_lengths, prompt_kv, ct, st, cp, sp)
+    )(page_slot, prompt_lengths, prompt_kv, ct, st, cp, sp)
 
 
 def spread_queries(q_ref, qf_ref, heads):
@@ -93,45 +118,44 @@
             qf_ref[pl.ds(at, rows, stride=block), :] = q_ref[s, :, h * head_dim : (h + 1) * head_dim].astype(F32)
 
 
-def meta_kernel(npool, pair, cache_pages, page_len, slot_ref, len_ref, table_ref, context_ref, meta_ref, own_ref, count):
-    items = npool * pair
+def meta_kernel(npool, pair, cache_pages, page_len, slot_ref, table_ref, context_ref, out_ref, row, count, sems):
     most, rows = table_ref.shape
     for e in range(npool):
         count[e] = 0
-    for i in range(items):
-        meta_ref[0, i] = -1
-        own_ref[i] = 0
-        own_ref[items + i] = 0
+    for i in range(npool * pair):
+        row[0, i] = -1
     for n in range(slot_ref.shape[0]):
         slot = slot_ref[n]
         target = slot // cache_pages
-        at = target * pair + count[target]
+        row[0, target * pair + count[target]] = slot - target * cache_pages
         count[target] = count[target] + 1
-        meta_ref[0, at] = slot - target * cache_pages
-        _, fill = page_place(len_ref, page_len, n)
-        own_ref[at] = n
-        own_ref[items + at] = fill
     for r in range(rows):
         context = context_ref[r]
         for j in range(most):
             left = jnp.clip(context - j * page_len, 0, page_len)
-            meta_ref[0, CODES + table_ref[j, r]] = r * LEFT + left
-
-
-def meta_data(page_slot, prompt_lengths, table, context, npool, pair, cache_pages, page_len):
+            row[0, CODES + table_ref[j, r]] = r * LEFT + left
+    copies = [pltpu.make_async_copy(row, out_ref.at[e], sems.at[e]) for e in range(npool)]
+    for x in copies:
+        x.start()
+    for x in copies:
+        x.wait()
+
+
+def meta_data(page_slot, table, context, npool, pair, cache_pages, page_len):
     return pl.pallas_call(
         functools.partial(meta_kernel, npool, pair, cache_pages, page_len),
-        out_shape=[
-            jax.ShapeDtypeStruct((1, LANES), I32),
-            jax.ShapeDtypeStruct((2 * npool * pair,), I32),
+        out_shape=jax.ShapeDtypeStruct((npool, 1, LANES), I32),
+        in_specs=[SMEM] * 3,
+        out_specs=ANY,
+        scratch_shapes=[
+            pltpu.SMEM((1, LANES), I32),
+            pltpu.SMEM((npool,), I32),
+            pltpu.SemaphoreType.DMA((npool,)),
         ],
-        in_specs=[SMEM] * 4,
-        out_specs=[SMEM] * 2,
-        scratch_shapes=[pltpu.SMEM((npool,), I32)],
-        compiler_params=PARAMS,
+        compiler_params=SMALL,
         cost_estimate=pl.CostEstimate(flops=1000, bytes_accessed=10_000, transcendentals=0),
         name="meta_data",
-    )(page_slot, prompt_lengths, table, context)
+    )(page_slot, table, context)
 
 
 def item_request(meta_ref, me, d, i):
@@ -163,7 +187,7 @@
         in_specs=[SMEM, SMEM, VMEM],
         out_specs=VMEM,
         scratch_shapes=[pltpu.VMEM((rows * block, head_dim), F32)],
-        compiler_params=PARAMS,
+        compiler_params=SMALL,
         cost_estimate=pl.CostEstimate(flops=100_000, bytes_accessed=500_000, transcendentals=0),
         name="queries_out",
     )(me, meta, queries)
@@ -177,6 +201,14 @@
         jnp.concatenate(keys, axis=1), jnp.concatenate(spread, axis=0), preferred_element_type=F32
     )
     return scores * (queries.shape[1] ** -0.5)
+
+
+def weighted_values(weights, values):
+    heads, head_dim = len(values), values[0].shape[1]
+    group = weights.shape[0] // heads
+    out = jnp.dot(weights, jnp.concatenate(values, axis=1), preferred_element_type=F32)
+    parts = [out[k * group : (k + 1) * group, k * head_dim : (k + 1) * head_dim] for k in range(heads)]
+    return jnp.concatenate(parts, axis=0)
 
 
 def lane_values(scalars, lanes_each, shape):
@@ -275,13 +307,10 @@
         weights = [jnp.transpose(x, (1, 0)).astype(BF16) for x in parts[:most]]
         weights.append(stats[:, :group].astype(BF16))
         weights = jnp.concatenate(weights, axis=1)
-        for c in range(len(chains)):
-            at = i * LANES + c * group
-            o_ref[at : at + group, :] = jnp.dot(
-                weights[c * group : (c + 1) * group, :],
-                jnp.concatenate(values[c], axis=0),
-                preferred_element_type=F32,
-            )
+        for x in range(together):
+            both = [jnp.concatenate(values[x * heads + k], axis=0) for k in range(heads)]
+            both = weighted_values(weights[x * block : (x + 1) * block, :], both)
+            o_ref[i * LANES + x * block : i * LANES + (x + 1) * block, :] = both
         stat_ref[i * LANES : (i + 1) * LANES, :] = stats
 
 
@@ -304,7 +333,7 @@
             pltpu.VMEM(flat, F32),
             pltpu.VMEM((rows, head_dim), I32),
         ],
-        compiler_params=PARAMS,
+        compiler_params=MIDDLE,
         cost_estimate=pl.CostEstimate(flops=800_000_000, bytes_accessed=12_000_000, transcendentals=400_000),
         name="local_attention",
     )(
@@ -353,12 +382,11 @@
         stats = pieces(top) + pieces(jnp.sum(weights, axis=0, keepdims=True))
         stats = jnp.concatenate(stats + [jnp.zeros((STAT_ROWS - len(stats), LANES), F32)], axis=0).astype(BF16)
         weights = jnp.transpose(weights, (1, 0)).astype(BF16)
-        for c, (n, k) in enumerate(chains):
-            x, at = own[c // heads], (c % heads) * group
-            at = (x % pair) * block + at
-            out_ref[x // pair, at : at + group, :] = jnp.dot(
-                weights[c * group : (c + 1) * group, :], values[n, k], preferred_element_type=F32
-            ).astype(BF16)
+        for c, x in enumerate(own):
+            both = [values[own_ref[x], k] for k in range(heads)]
+            both = weighted_values(weights[c * block : (c + 1) * block, :], both)
+            at = (x % pair) * block
+            out_ref[x // pair, at : at + block, :] = both.astype(BF16)
         for e in sorted({x // pair for x in own}):
             out_ref[e, pair * block : pair * block + STAT_ROWS, :] = stats
 
@@ -376,7 +404,7 @@
             pltpu.VMEM((pages, heads, page_len, head_dim), BF16),
             pltpu.SemaphoreType.DMA,
         ],
-        compiler_params=PARAMS,
+        compiler_params=LARGE,
         cost_estimate=pl.CostEstimate(flops=200_000_000, bytes_accessed=4_000_000, transcendentals=70_000),
         name="arrived_attention",
     )(me, meta, own, queries.reshape(npool * rows, head_dim), keys, prompt_kv)
@@ -433,53 +461,82 @@
         in_specs=[SMEM] * 2 + [VMEM] * 3,
         out_specs=VMEM,
         scratch_shapes=[pltpu.VMEM(flat, F32)] * 3 + [pltpu.VMEM((LANES, LANES), F32)],
-        compiler_params=PARAMS,
+        compiler_params=SMALL,
         cost_estimate=pl.CostEstimate(flops=2_000_000, bytes_accessed=1_500_000, transcendentals=100_000),
         name="merge",
     )(me, meta, parts, *local)
 
 
-def project_kernel(npool, scalars, *refs):
+def project_kernel(npool, tile, place_ref, *refs):
     blocks = refs[:npool]
-    weight_ref, out_ref, lhs = refs[npool:]
+    weight_ref, out_ref, lhs, weight, sems, weight_sems = refs[npool:]
     steps, rows, _ = blocks[0].shape
-
-    @pl.when(pl.program_id(0) == 0)
-    def _():
-        for t in range(npool):
-            owner = lax.rem(scalars[0] + npool - t, npool)
-            at = pl.ds(pl.multiple_of(owner * rows, rows), rows)
-            for s in range(steps):
-                lhs[s, at, :] = blocks[t][s]
-
-    for s in range(steps):
-        out_ref[s] = jnp.dot(lhs[s], weight_ref[...], preferred_element_type=F32)
-
-
-def projection(me, first_tile, blocks, weight, columns, tile):
+    columns = weight.shape[1]
+    every = npool * rows
+    me, first = place_ref[0], pl.multiple_of(place_ref[1], LANES)
+    fetch = []
+    for i in range(columns // tile):
+        at = pl.ds(i * tile, tile)
+        source = weight_ref.at[:, pl.ds(first + i * tile, tile)]
+        fetch.append(pltpu.make_async_copy(source, weight.at[:, at], weight_sems.at[i]))
+        fetch[i].start()
+    copies = []
+    for x, (apart, flip) in enumerate(block_order(npool)):
+        owner = owner_of(me, npool, apart, flip)
+        for s in range(steps):
+            at = pl.ds(pl.multiple_of(s * every + owner * rows, rows), rows)
+            copies.append(pltpu.make_async_copy(blocks[x].at[s], lhs.at[at], sems.at[x * steps + s]))
+            copies[-1].start()
+    for x in copies:
+        x.wait()
+    for i in range(columns // tile):
+        fetch[i].wait()
+        at = slice(i * tile, (i + 1) * tile)
+        terms = jnp.dot(lhs[...], weight[:, at], preferred_element_type=F32)
+        for s in range(steps):
+            out_ref[s, :, at] = terms[s * every : (s + 1) * every]
+
+
+def projection(me, first, blocks, weight, columns):
     npool = len(blocks)
     steps, rows, width = blocks[0].shape
-    whole = pl.BlockSpec((steps, rows, width), lambda i, sc: (0, 0, 0))
+    tile = min(columns, 256)
+    every = steps * npool * rows
     return pl.pallas_call(
-        functools.partial(project_kernel, npool),
+        functools.partial(project_kernel, npool, tile),
         out_shape=jax.ShapeDtypeStruct((steps, npool * rows, columns), F32),
-        grid_spec=pltpu.PrefetchScalarGridSpec(
-            num_scalar_prefetch=1,
-            grid=(columns // tile,),
-            in_specs=[whole] * npool + [pl.BlockSpec((width, tile), lambda i, sc: (0, sc[1] + i))],
-            out_specs=pl.BlockSpec((steps, npool * rows, tile), lambda i, sc: (0, 0, i)),
-            scratch_shapes=[pltpu.VMEM((steps, npool * rows, width), BF16)],
-        ),
-        compiler_params=PARAMS,
+        in_specs=[SMEM] + [ANY] * (npool + 1),
+        out_specs=VMEM,
+        scratch_shapes=[
+            pltpu.VMEM((every, width), BF16),
+            pltpu.VMEM((width, columns), BF16),
+            pltpu.SemaphoreType.DMA((npool * steps,)),
+            pltpu.SemaphoreType.DMA((columns // tile,)),
+        ],
+        compiler_params=MIDDLE,
         cost_estimate=pl.CostEstimate(
-            flops=2 * steps * npool * rows * width * columns, bytes_accessed=4_000_000, transcendentals=0
+            flops=2 * every * width * columns, bytes_accessed=4_000_000, transcendentals=0
         ),
         name="project",
-    )(jnp.stack([me, first_tile]), *blocks, weight)
-
-
-def shift(x, npool, by):
-    return lax.ppermute(x, "pool", [(i, (i + by) % npool) for i in range(npool)])
+    )(jnp.stack([me, first]), *blocks, weight)
+
+
+def block_order(npool):
+    return [(apart, flip) for flip in (0, 1) for apart in range(npool // 2)]
+
+
+def owner_of(me, npool, apart, flip):
+    half = npool // 2
+    pair, side = me // 2, me % 2
+    side = 1 - side if flip else side
+    return lax.rem(pair + half - apart, half) * 2 + side
+
+
+def gathered(x, npool):
+    ahead = lambda x, by: lax.ppermute(x, "pool", [(i, (i + 2 * by) % npool) for i in range(npool)])
+    across = lambda x: lax.ppermute(x, "pool", [(i, i ^ 1) for i in range(npool)])
+    straight = [x] + [ahead(x, by) for by in range(1, npool // 2)]
+    return straight + [across(y) for y in straight]
 
 
 def swap_halves(x):
@@ -507,23 +564,20 @@
     me1 = me[None]
     table = page_table.T
 
-    mine, own = meta_data(page_slot, prompt_lengths, table, context_lengths, npool, pair, cache_pages, page_len)
-    meta = lax.all_gather(mine, "pool", axis=0, tiled=True)
-    keys = rotated_keys(prompt_kv, prompt_lengths, tabs)
+    meta = meta_data(page_slot, table, context_lengths, npool, pair, cache_pages, page_len)
+    meta = lax.all_to_all(meta, "pool", split_axis=0, concat_axis=0, tiled=True).reshape(npool, LANES)
+    keys, own = rotated_keys(prompt_kv, page_slot, prompt_lengths, tabs, npool, pair, cache_pages)
     local = local_attention(table, context_lengths, cache_fill, queries, new_kv, cache_kv, tabs)
     sent = queries_out(me1, meta, queries, pair, heads, head_dim)
     got = lax.all_to_all(sent, "pool", split_axis=0, concat_axis=0, tiled=True)
     parts = arrived_attention(me1, meta, own, got, keys, prompt_kv)
     parts = lax.all_to_all(parts, "pool", split_axis=0, concat_axis=0, tiled=True)
     attention = merged(me1, meta, parts, local, queries.shape, heads, pair)
-    blocks = [attention] + [shift(attention, npool, t) for t in range(1, npool)]
-
+    blocks = gathered(attention, npool)
     half = out_weight.shape[1] // 2
-    tile = min(half, 256)
-    mine = lax.axis_index("tp").astype(I32)
-    other_terms = projection(me, (1 - mine) * (half // tile), blocks, out_weight, half, tile)
-    other_terms = swap_halves(other_terms)
-    terms = projection(me, mine * (half // tile), blocks, out_weight, half, tile)
+    core = lax.axis_index("tp").astype(I32)
+    other_terms = swap_halves(projection(me, (1 - core) * half, blocks, out_weight, half))
+    terms = projection(me, core * half, blocks, out_weight, half)
     return (terms + other_terms).astype(BF16)
 
 

time: 95.7 us -> 84.3 us (0.88)
  blocking collectives: 22.8 us -> 0 us
  starting transfers between devices: 16.6 us -> 24.9 us
  local copies, waits for them, and re-layouts: 3.24 us -> 6.76 us
  Pallas kernels: 31 us -> 29.9 us
    all_gather x1 -> x0, blocking collectives: 22.8 us -> none  [shards(): meta = lax.all_gather(mine, 'pool', axis=0, tiled=True)]
    all_to_all x0 -> x1, starting transfers between devices: none -> 7.29 us  [shards(): lax.all_to_all(meta, 'pool', split_axis=0, concat_axis=0, tiled=True)]
    ppermute x7, waiting for transfers between devices: 14.6 us -> 8.24 us  [the longest x3 4.46 us: gathered(): lax.ppermute(x, 'pool', [(i, (i + 2 * by) % npool) for i in range(npool)])]
    all_to_all x0 -> x1, waiting for transfers between devices: none -> 6.39 us  [shards(): lax.all_to_all(meta, 'pool', split_axis=0, concat_axis=0, tiled=True)]
    unnamed x20 -> x36, local copies, waits for them, and re-layouts: 2.62 us -> 6.14 us
    pallas_call x3, Pallas kernels: 11.6 us -> 12.9 us  [the longest x2 9.83 us: projection(): pl.pallas_call(functools.partial(project_kernel, npool, tile), out_shape=...]
    pallas_call x1, Pallas kernels: 2.5 us -> 1.34 us  [merged(): pl.pallas_call(functools.partial(merge_kernel, pair, heads), out_shape=ja...]
  transfers between devices with their start and end apart: 10 -> 11, of which waited for: 6 -> 6; matrix products, arithmetic and copies ran while one was open for 2% -> 2% of each run, Pallas kernels for 17% -> 19%
where the time goes in v3:
time: 84.3 us; the launch traced here: 83.5 us
  Pallas kernels  29.9 us (35%)
  starting transfers between devices  24.9 us (30%)
  waiting for transfers between devices  18.8 us (22%)
  local copies, waits for them, and re-layouts  6.76 us (8%)
  other arithmetic  3.03 us (4%)
    pallas_call x2, Pallas kernels, projection(): pl.pallas_call(functools.partial(project_kernel, npool, tile), out_shape=...  9.83 us
    pallas_call x1, Pallas kernels, local_attention(): pl.pallas_call(functools.partial(local_kernel, page_len, heads), out_shap...  7.81 us
    all_to_all x1, starting transfers between devices, shards(): lax.all_to_all(meta, 'pool', split_axis=0, concat_axis=0, tiled=True)  7.29 us
    all_to_all x1, waiting for transfers between devices, shards(): lax.all_to_all(meta, 'pool', split_axis=0, concat_axis=0, tiled=True)  6.39 us
    unnamed x36, local copies, waits for them, and re-layouts  6.14 us
    ppermute x4, starting transfers between devices, gathered(): lax.ppermute(x, 'pool', [(i, i ^ 1) for i in range(npool)])  5.84 us
    ppermute x3, starting transfers between devices, gathered(): lax.ppermute(x, 'pool', [(i, (i + 2 * by) % npool) for i in range(npool)])  4.91 us
    pallas_call x1, Pallas kernels, arrived_attention(): pl.pallas_call(functools.partial(arrived_kernel, npool, pair), out_shape=...  4.7 us
  transfers between devices with their start and end apart: 11, of which 6 were waited for; matrix products, arithmetic and copies ran while one was open for 2% of the time, Pallas kernels for 19%

profile of v3, /device:TPU:0, one launch (start us, length us, event | category | flops | bytes accessed | tf_op | source)
XLA Modules:
  0.0 83.5 jit_solution(1970578159356769232)
XLA Ops:
  2.0 1.5 %meta_data.1 = s32[8,1,128]{2,1,0:T(1,128)} custom-call(s32[16]{0:T(128)S(1)} %copy-done.8, s32[3,16]{1,0:T(4,128)S(1)} %bitcast.10, s32[16]{0:T(128)S(1)} %copy-done.7), custom_call_target="tpu_custom_call" | custom-call | flops 1000 | bytes 10000 | tf_op jit(solution)/shard_map/meta_data/pallas_call | solution.py:145
  3.5 7.3 %all-to-all-start = ((s32[8,1,128]{2,1,0:T(1,128)}), s32[8,1,128]{2,1,0:T(1,128)S(1)}, u32[]{:S(2)}, u32[]{:S(2)}) async-start(s32[8,1,128]{2,1,0:T(1,128)} %meta_data.1), calls=%async_computation | async-start | bytes 8192 | tf_op jit(solution)/shard_map/all_to_all | solution.py:568
  10.8 6.4 %all-to-all-done = s32[8,1,128]{2,1,0:T(1,128)S(1)} async-done(((s32[8,1,128]{2,1,0:T(1,128)}), s32[8,1,128]{2,1,0:T(1,128)S(1)}, u32[]{:S(2)}, u32[]{:S(2)}) %all-to-all-start) | async-done | bytes 4128 | tf_op jit(solution)/shard_map/all_to_all | solution.py:568
  18.1 1.6 %queries_out.1 = bf16[8,64,128]{2,1,0:T(8,128)(2,1)} custom-call(s32[1]{0:T(128)} %bitcast.me_ref, s32[8,128]{1,0:T(8,128)S(1)} %bitcast.6, bf16[2,16,2048]{2,1,0:T(8,128)(2,1)S(1)} %copy-done.1), custom_call_target="tpu_custom_call" | custom-call | flops 100000 | bytes 500000 | tf_op jit(solution)/shard_map/queries_out/pallas_call | solution.py:184
  19.7 3.4 %all-to-all-start.1 = ((bf16[8,64,128]{2,1,0:T(8,128)(2,1)}), bf16[8,64,128]{2,1,0:T(8,128)(2,1)S(1)}, u32[]{:S(2)}, u32[]{:S(2)}) async-start(bf16[8,64,128]{2,1,0:T(8,128)(2,1)} %queries_out.1), calls=%async_computation.1 | async-start | bytes 262144 | tf_op jit(solution)/shard_map/all_to_all | solution.py:572
  23.1 3.1 %rope_pages.1 = (bf16[16,2,128,128]{3,2,1,0:T(8,128)(2,1)}, s32[32]{0:T(128)}) custom-call(s32[16]{0:T(128)} %slot_ref.3, s32[1,4]{1,0:T(1,128)} %len_ref.1, bf16[16,2,2,128,128]{4,3,2,1,0:T(8,128)(2,1)} %prompt_ref.1, f32[128,128]{1,0:T(8,128)} %constant.24.clone.ct_ref, f32[128,128]{1,0:T(8,128)} %constant.25.clone.st_ref, ...), custom_call_target="tpu_custom_call" | custom-call | flops 6000000 | bytes 2000000 | tf_op jit(solution)/shard_map/rope_pages/pallas_call | solution.py:85
  26.2 4.2 %all-to-all-done.1 = bf16[8,64,128]{2,1,0:T(8,128)(2,1)S(1)} async-done(((bf16[8,64,128]{2,1,0:T(8,128)(2,1)}), bf16[8,64,128]{2,1,0:T(8,128)(2,1)S(1)}, u32[]{:S(2)}, u32[]{:S(2)}) %all-to-all-start.1) | async-done | bytes 131104 | tf_op jit(solution)/shard_map/all_to_all | solution.py:572
  31.0 4.7 %arrived_attention.1 = bf16[8,80,128]{2,1,0:T(8,128)(2,1)} custom-call(s32[1]{0:T(128)} %bitcast.me_ref, s32[8,128]{1,0:T(8,128)} %bitcast.7, s32[32]{0:T(128)} %get-tuple-element.9.own_ref, bf16[512,128]{1,0:T(8,128)(2,1)} %bitcast.11, bf16[16,2,128,128]{3,2,1,0:T(8,128)(2,1)} %get-tuple-element.10.keys_ref, bf16[16,2,2,128,128]{4,3,2,1,0:T(8,128)(2,1)} %prompt_ref.1), custom_call_target="tpu_custom_call" | custom-call | flops 200000000 | bytes 4000000 | tf_op jit(solution)/shard_map/arrived_attention/pallas_call | solution.py:398
  35.7 3.4 %all-to-all-start.2 = ((bf16[8,80,128]{2,1,0:T(8,128)(2,1)}), bf16[8,80,128]{2,1,0:T(8,128)(2,1)S(1)}, u32[]{:S(2)}, u32[]{:S(2)}) async-start(bf16[8,80,128]{2,1,0:T(8,128)(2,1)} %arrived_attention.1), calls=%async_computation.2 | async-start | bytes 327680 | tf_op jit(solution)/shard_map/all_to_all | solution.py:574
  39.8 7.8 %local_attention.1 = (f32[512,128]{1,0:T(8,128)}, f32[512,128]{1,0:T(8,128)}) custom-call(s32[3,16]{1,0:T(4,128)} %bitcast.9, s32[16]{0:T(128)} %context_ref.3, s32[48]{0:T(128)} %fill_ref.1, bf16[2,16,2048]{2,1,0:T(8,128)(2,1)} %q_ref.3, bf16[2,16,512]{2,1,0:T(8,128)(2,1)} %reshape.11.new_ref, f32[1,128]{1,0:T(1,128)} %constant.28.clone.freq_ref, ...), custom_call_target="tpu_custom_call" | custom-call | flops 800000000 | bytes 12000000 | tf_op jit(solution)/shard_map/local_attention/pallas_call | solution.py:323
  47.6 0.9 %copy-done.2 = f32[512,128]{1,0:T(8,128)S(1)} copy-done((f32[512,128]{1,0:T(8,128)S(1)}, f32[512,128]{1,0:T(8,128)}, u32[]{:S(2)}) %copy-start.2) | copy-done | bytes 262168
  48.6 0.9 %copy-done.3 = f32[512,128]{1,0:T(8,128)S(1)} copy-done((f32[512,128]{1,0:T(8,128)S(1)}, f32[512,128]{1,0:T(8,128)}, u32[]{:S(2)}) %copy-start.3) | copy-done | bytes 262168
  49.5 1.3 %merge.1.refs_0_ = bf16[2,16,2048]{2,1,0:T(8,128)(2,1)S(1)} custom-call(s32[1]{0:T(128)} %bitcast.me_ref, s32[8,128]{1,0:T(8,128)S(1)} %bitcast.8, bf16[8,80,128]{2,1,0:T(8,128)(2,1)S(1)} %all-to-all-done.2.parts_ref, f32[512,128]{1,0:T(8,128)S(1)} %copy-done.2, f32[512,128]{1,0:T(8,128)S(1)} %copy-done.3), custom_call_target="tpu_custom_call" | custom-call | flops 2000000 | bytes 1500000 | tf_op jit(solution)/shard_map/merge/pallas_call | solution.py:458
  50.9 3.8 %collective-permute-start.2 = (bf16[2,16,2048]{2,1,0:T(8,128)(2,1)S(1)}, bf16[2,16,2048]{2,1,0:T(8,128)(2,1)S(1)}, u32[]{:S(2)}, u32[]{:S(2)}) collective-permute-start(bf16[2,16,2048]{2,1,0:T(8,128)(2,1)S(1)} %merge.1.refs_0_), channel_id=1, source_target_pairs={{0,12},{2,14},{4,0},{6,2},{8,4},{10,6},{12,8},{14,10},{1,13},{3,15... | collective-permute-start | bytes 393224 | tf_op jit(solution)/shard_map/ppermute | solution.py:536
  54.7 1.1 %collective-permute-start = (bf16[2,16,2048]{2,1,0:T(8,128)(2,1)S(1)}, bf16[2,16,2048]{2,1,0:T(8,128)(2,1)S(1)}, u32[]{:S(2)}, u32[]{:S(2)}) collective-permute-start(bf16[2,16,2048]{2,1,0:T(8,128)(2,1)S(1)} %merge.1.refs_0_), channel_id=1, source_target_pairs={{0,4},{2,6},{4,8},{6,10},{8,12},{10,14},{12,0},{14,2},{1,5},{3,7},... | collective-permute-start | bytes 393224 | tf_op jit(solution)/shard_map/ppermute | solution.py:536
  55.8 1.5 %collective-permute-start.3 = (bf16[2,16,2048]{2,1,0:T(8,128)(2,1)S(1)}, bf16[2,16,2048]{2,1,0:T(8,128)(2,1)S(1)}, u32[]{:S(2)}, u32[]{:S(2)}) collective-permute-start(bf16[2,16,2048]{2,1,0:T(8,128)(2,1)S(1)} %merge.1.refs_0_), channel_id=1, source_target_pairs={{0,2},{2,0},{4,6},{6,4},{8,10},{10,8},{12,14},{14,12},{1,3},{3,1},... | collective-permute-start | bytes 393224 | tf_op jit(solution)/shard_map/ppermute | solution.py:537
  57.7 2.3 %collective-permute-start.6 = (bf16[2,16,2048]{2,1,0:T(8,128)(2,1)S(1)}, bf16[2,16,2048]{2,1,0:T(8,128)(2,1)S(1)}, u32[]{:S(2)}, u32[]{:S(2)}) collective-permute-start(bf16[2,16,2048]{2,1,0:T(8,128)(2,1)S(1)} %collective-permute-done.2.refs_3_), channel_id=1, source_target_pairs={{0,2},{2,0},{4,6},{6,4},{8,10},{10,8},{12,14},{14,12},{1,3},{3,1},... | collective-permute-start | bytes 393224 | tf_op jit(solution)/shard_map/ppermute | solution.py:537
  60.1 3.9 %collective-permute-done.1.refs_2_ = bf16[2,16,2048]{2,1,0:T(8,128)(2,1)S(1)} collective-permute-done((bf16[2,16,2048]{2,1,0:T(8,128)(2,1)S(1)}, bf16[2,16,2048]{2,1,0:T(8,128)(2,1)S(1)}, u32[]{:S(2)}, u32[]{:S(2)}) %collective-permute-start.1) | collective-permute-done | bytes 131104 | tf_op jit(solution)/shard_map/ppermute | solution.py:536
  64.0 1.5 %collective-permute-start.5 = (bf16[2,16,2048]{2,1,0:T(8,128)(2,1)S(1)}, bf16[2,16,2048]{2,1,0:T(8,128)(2,1)S(1)}, u32[]{:S(2)}, u32[]{:S(2)}) collective-permute-start(bf16[2,16,2048]{2,1,0:T(8,128)(2,1)S(1)} %collective-permute-done.1.refs_2_), channel_id=1, source_target_pairs={{0,2},{2,0},{4,6},{6,4},{8,10},{10,8},{12,14},{14,12},{1,3},{3,1},... | collective-permute-start | bytes 393224 | tf_op jit(solution)/shard_map/ppermute | solution.py:537
  66.7 2.4 %collective-permute-done.5.refs_6_ = bf16[2,16,2048]{2,1,0:T(8,128)(2,1)S(1)} collective-permute-done((bf16[2,16,2048]{2,1,0:T(8,128)(2,1)S(1)}, bf16[2,16,2048]{2,1,0:T(8,128)(2,1)S(1)}, u32[]{:S(2)}, u32[]{:S(2)}) %collective-permute-start.5) | collective-permute-done | bytes 131104 | tf_op jit(solution)/shard_map/ppermute | solution.py:537
  69.1 1.4 %collective-permute-done.4.refs_5_ = bf16[2,16,2048]{2,1,0:T(8,128)(2,1)S(1)} collective-permute-done((bf16[2,16,2048]{2,1,0:T(8,128)(2,1)S(1)}, bf16[2,16,2048]{2,1,0:T(8,128)(2,1)S(1)}, u32[]{:S(2)}, u32[]{:S(2)}) %collective-permute-start.4) | collective-permute-done | bytes 131104 | tf_op jit(solution)/shard_map/ppermute | solution.py:537
  71.2 4.9 %project.3 = f32[2,128,512]{2,1,0:T(8,128)} custom-call(s32[2]{0:T(128)} %pad_add_fusion.1.place_ref, bf16[2,16,2048]{2,1,0:T(8,128)(2,1)} %copy-done, bf16[2,16,2048]{2,1,0:T(8,128)(2,1)} %copy-done.11, bf16[2,16,2048]{2,1,0:T(8,128)(2,1)} %copy-done.10, bf16[2,16,2048]{2,1,0:T(8,128)(2,1)} %copy-done.9, bf16[2,16,2048]{2,1,0:T(8,128)(2,1)} %copy-done.12, ...), custom_call_target="tpu_custom_call" | custom-call | flops 536870912 | bytes 4000000 | tf_op jit(solution)/shard_map/project/pallas_call | solution.py:505
  76.8 4.9 %project.2 = f32[2,128,512]{2,1,0:T(8,128)} custom-call(s32[2]{0:T(128)} %pad_add_fusion.place_ref, bf16[2,16,2048]{2,1,0:T(8,128)(2,1)} %copy-done, bf16[2,16,2048]{2,1,0:T(8,128)(2,1)} %copy-done.11, bf16[2,16,2048]{2,1,0:T(8,128)(2,1)} %copy-done.10, bf16[2,16,2048]{2,1,0:T(8,128)(2,1)} %copy-done.9, bf16[2,16,2048]{2,1,0:T(8,128)(2,1)} %copy-done.12, ...), custom_call_target="tpu_custom_call" | custom-call | flops 536870912 | bytes 4000000 | tf_op jit(solution)/shard_map/project/pallas_call | solution.py:505
  81.7 1.8 %add_convert_fusion = bf16[2,128,512]{2,1,0:T(8,128)(2,1)} fusion(f32[2,128,512]{2,1,0:T(8,128)} %project.2, f32[2,128,512]{2,1,0:T(8,128)S(1)} %collective-permute-done.7), kind=kLoop, calls=%fused_computation | loop fusion | flops 262144 | bytes 1310720 | tf_op jit(solution)/shard_map/convert_element_type | solution.py:581
  (46 shorter events, 7.2 us)
Async XLA Ops:
  3.5 13.7 %all-to-all-start = ((s32[8,1,128]{2,1,0:T(1,128)}), s32[8,1,128]{2,1,0:T(1,128)S(1)}, u32[]{:S(2)}, u32[]{:S(2)}) async-start(s32[8,1,128]{2,1,0:T(1,128)} %meta_data.1), calls=%async_computation | async-start | bytes 8192 | tf_op jit(solution)/shard_map/all_to_all | solution.py:568
  17.2 13.2 %copy-start.4 = (s32[8,1,128]{2,1,0:T(1,128)}, s32[8,1,128]{2,1,0:T(1,128)S(1)}, u32[]{:S(2)}) copy-start(s32[8,1,128]{2,1,0:T(1,128)S(1)} %all-to-all-done) | copy-start | bytes 12292
  17.2 0.9 %copy-start.1 = (bf16[2,16,2048]{2,1,0:T(8,128)(2,1)S(1)}, bf16[2,16,2048]{2,1,0:T(8,128)(2,1)}, u32[]{:S(2)}) copy-start(bf16[2,16,2048]{2,1,0:T(8,128)(2,1)} %q_ref.3) | copy-start | bytes 393220
  18.1 21.0 %copy-start.17 = (bf16[2,16,2,2,128]{4,3,2,1,0:T(2,128)(2,1)S(1)}, bf16[2,16,2,2,128]{4,3,2,1,0:T(2,128)(2,1)}, u32[]{:S(2)}) copy-start(bf16[2,16,2,2,128]{4,3,2,1,0:T(2,128)(2,1)} %param.24) | copy-start | bytes 98308
  19.7 10.7 %all-to-all-start.1 = ((bf16[8,64,128]{2,1,0:T(8,128)(2,1)}), bf16[8,64,128]{2,1,0:T(8,128)(2,1)S(1)}, u32[]{:S(2)}, u32[]{:S(2)}) async-start(bf16[8,64,128]{2,1,0:T(8,128)(2,1)} %queries_out.1), calls=%async_computation.1 | async-start | bytes 262144 | tf_op jit(solution)/shard_map/all_to_all | solution.py:572
  35.7 11.9 %copy-start.5 = (s32[8,1,128]{2,1,0:T(1,128)S(1)}, s32[8,1,128]{2,1,0:T(1,128)}, u32[]{:S(2)}) copy-start(s32[8,1,128]{2,1,0:T(1,128)} %copy-done.4) | copy-start | bytes 12292
  35.7 11.9 %all-to-all-start.2 = ((bf16[8,80,128]{2,1,0:T(8,128)(2,1)}), bf16[8,80,128]{2,1,0:T(8,128)(2,1)S(1)}, u32[]{:S(2)}, u32[]{:S(2)}) async-start(bf16[8,80,128]{2,1,0:T(8,128)(2,1)} %arrived_attention.1), calls=%async_computation.2 | async-start | bytes 327680 | tf_op jit(solution)/shard_map/all_to_all | solution.py:574
  47.6 1.0 %copy-start.2 = (f32[512,128]{1,0:T(8,128)S(1)}, f32[512,128]{1,0:T(8,128)}, u32[]{:S(2)}) copy-start(f32[512,128]{1,0:T(8,128)} %get-tuple-element.11.o_ref) | copy-start | bytes 786436
  48.5 0.9 %copy-start.3 = (f32[512,128]{1,0:T(8,128)S(1)}, f32[512,128]{1,0:T(8,128)}, u32[]{:S(2)}) copy-start(f32[512,128]{1,0:T(8,128)} %get-tuple-element.12.stat_ref) | copy-start | bytes 786436
  50.8 19.6 %copy-start = (bf16[2,16,2048]{2,1,0:T(8,128)(2,1)}, bf16[2,16,2048]{2,1,0:T(8,128)(2,1)S(1)}, u32[]{:S(2)}) copy-start(bf16[2,16,2048]{2,1,0:T(8,128)(2,1)S(1)} %merge.1.refs_0_) | copy-start | bytes 393220
  50.9 6.9 %collective-permute-start.2 = (bf16[2,16,2048]{2,1,0:T(8,128)(2,1)S(1)}, bf16[2,16,2048]{2,1,0:T(8,128)(2,1)S(1)}, u32[]{:S(2)}, u32[]{:S(2)}) collective-permute-start(bf16[2,16,2048]{2,1,0:T(8,128)(2,1)S(1)} %merge.1.refs_0_), channel_id=1, source_target_pairs={{0,12},{2,14},{4,0},{6,2},{8,4},{10,6},{12,8},{14,10},{1,13},{3,15... | collective-permute-start | bytes 393224 | tf_op jit(solution)/shard_map/ppermute | solution.py:536
  54.6 9.4 %collective-permute-start.1 = (bf16[2,16,2048]{2,1,0:T(8,128)(2,1)S(1)}, bf16[2,16,2048]{2,1,0:T(8,128)(2,1)S(1)}, u32[]{:S(2)}, u32[]{:S(2)}) collective-permute-start(bf16[2,16,2048]{2,1,0:T(8,128)(2,1)S(1)} %merge.1.refs_0_), channel_id=1, source_target_pairs={{0,8},{2,10},{4,12},{6,14},{8,0},{10,2},{12,4},{14,6},{1,9},{3,11}... | collective-permute-start | bytes 393224 | tf_op jit(solution)/shard_map/ppermute | solution.py:536
  54.7 10.8 %collective-permute-start = (bf16[2,16,2048]{2,1,0:T(8,128)(2,1)S(1)}, bf16[2,16,2048]{2,1,0:T(8,128)(2,1)S(1)}, u32[]{:S(2)}, u32[]{:S(2)}) collective-permute-start(bf16[2,16,2048]{2,1,0:T(8,128)(2,1)S(1)} %merge.1.refs_0_), channel_id=1, source_target_pairs={{0,4},{2,6},{4,8},{6,10},{8,12},{10,14},{12,0},{14,2},{1,5},{3,7},... | collective-permute-start | bytes 393224 | tf_op jit(solution)/shard_map/ppermute | solution.py:536
  55.8 10.9 %collective-permute-start.3 = (bf16[2,16,2048]{2,1,0:T(8,128)(2,1)S(1)}, bf16[2,16,2048]{2,1,0:T(8,128)(2,1)S(1)}, u32[]{:S(2)}, u32[]{:S(2)}) collective-permute-start(bf16[2,16,2048]{2,1,0:T(8,128)(2,1)S(1)} %merge.1.refs_0_), channel_id=1, source_target_pairs={{0,2},{2,0},{4,6},{6,4},{8,10},{10,8},{12,14},{14,12},{1,3},{3,1},... | collective-permute-start | bytes 393224 | tf_op jit(solution)/shard_map/ppermute | solution.py:537
  57.7 12.7 %copy-start.9 = (bf16[2,16,2048]{2,1,0:T(8,128)(2,1)}, bf16[2,16,2048]{2,1,0:T(8,128)(2,1)S(1)}, u32[]{:S(2)}) copy-start(bf16[2,16,2048]{2,1,0:T(8,128)(2,1)S(1)} %collective-permute-done.2.refs_3_) | copy-start | bytes 393220
  57.7 8.9 %collective-permute-start.6 = (bf16[2,16,2048]{2,1,0:T(8,128)(2,1)S(1)}, bf16[2,16,2048]{2,1,0:T(8,128)(2,1)S(1)}, u32[]{:S(2)}, u32[]{:S(2)}) collective-permute-start(bf16[2,16,2048]{2,1,0:T(8,128)(2,1)S(1)} %collective-permute-done.2.refs_3_), channel_id=1, source_target_pairs={{0,2},{2,0},{4,6},{6,4},{8,10},{10,8},{12,14},{14,12},{1,3},{3,1},... | collective-permute-start | bytes 393224 | tf_op jit(solution)/shard_map/ppermute | solution.py:537
  64.0 6.5 %copy-start.10 = (bf16[2,16,2048]{2,1,0:T(8,128)(2,1)}, bf16[2,16,2048]{2,1,0:T(8,128)(2,1)S(1)}, u32[]{:S(2)}) copy-start(bf16[2,16,2048]{2,1,0:T(8,128)(2,1)S(1)} %collective-permute-done.1.refs_2_) | copy-start | bytes 393220
  64.0 5.0 %collective-permute-start.5 = (bf16[2,16,2048]{2,1,0:T(8,128)(2,1)S(1)}, bf16[2,16,2048]{2,1,0:T(8,128)(2,1)S(1)}, u32[]{:S(2)}, u32[]{:S(2)}) collective-permute-start(bf16[2,16,2048]{2,1,0:T(8,128)(2,1)S(1)} %collective-permute-done.1.refs_2_), channel_id=1, source_target_pairs={{0,2},{2,0},{4,6},{6,4},{8,10},{10,8},{12,14},{14,12},{1,3},{3,1},... | collective-permute-start | bytes 393224 | tf_op jit(solution)/shard_map/ppermute | solution.py:537
  65.5 5.0 %copy-start.11 = (bf16[2,16,2048]{2,1,0:T(8,128)(2,1)}, bf16[2,16,2048]{2,1,0:T(8,128)(2,1)S(1)}, u32[]{:S(2)}) copy-start(bf16[2,16,2048]{2,1,0:T(8,128)(2,1)S(1)} %collective-permute-done.refs_1_) | copy-start | bytes 393220
  65.5 5.0 %collective-permute-start.4 = (bf16[2,16,2048]{2,1,0:T(8,128)(2,1)S(1)}, bf16[2,16,2048]{2,1,0:T(8,128)(2,1)S(1)}, u32[]{:S(2)}, u32[]{:S(2)}) collective-permute-start(bf16[2,16,2048]{2,1,0:T(8,128)(2,1)S(1)} %collective-permute-done.refs_1_), channel_id=1, source_target_pairs={{0,2},{2,0},{4,6},{6,4},{8,10},{10,8},{12,14},{14,12},{1,3},{3,1},... | collective-permute-start | bytes 393224 | tf_op jit(solution)/shard_map/ppermute | solution.py:537
  66.7 3.8 %copy-start.12 = (bf16[2,16,2048]{2,1,0:T(8,128)(2,1)}, bf16[2,16,2048]{2,1,0:T(8,128)(2,1)S(1)}, u32[]{:S(2)}) copy-start(bf16[2,16,2048]{2,1,0:T(8,128)(2,1)S(1)} %collective-permute-done.3.refs_4_) | copy-start | bytes 393220
  66.7 3.8 %copy-start.13 = (bf16[2,16,2048]{2,1,0:T(8,128)(2,1)}, bf16[2,16,2048]{2,1,0:T(8,128)(2,1)S(1)}, u32[]{:S(2)}) copy-start(bf16[2,16,2048]{2,1,0:T(8,128)(2,1)S(1)} %collective-permute-done.6.refs_7_) | copy-start | bytes 393220
  69.1 1.5 %copy-start.14 = (bf16[2,16,2048]{2,1,0:T(8,128)(2,1)}, bf16[2,16,2048]{2,1,0:T(8,128)(2,1)S(1)}, u32[]{:S(2)}) copy-start(bf16[2,16,2048]{2,1,0:T(8,128)(2,1)S(1)} %collective-permute-done.5.refs_6_) | copy-start | bytes 393220
  76.1 5.6 %collective-permute-start.7 = (f32[2,128,512]{2,1,0:T(8,128)}, f32[2,128,512]{2,1,0:T(8,128)S(1)}, u32[]{:S(2)}, u32[]{:S(2)}) collective-permute-start(f32[2,128,512]{2,1,0:T(8,128)} %project.3), channel_id=1, source_target_pairs={{0,1},{1,0},{2,3},{3,2},{4,5},{5,4},{6,7},{7,6},{8,9},{9,8},{10,11... | collective-permute-start | bytes 1572872 | tf_op jit(solution)/shard_map/ppermute | solution.py:543
  (5 other events, 3.3 us)

commit v4 on v3

--- a/solution.py
+++ b/solution.py
@@ -13,9 +13,7 @@
 SMEM = pl.BlockSpec(memory_space=pltpu.SMEM)
 VMEM = pl.BlockSpec(memory_space=pltpu.VMEM)
 ANY = pl.BlockSpec(memory_space=pl.ANY)
-SMALL = pltpu.CompilerParams(vmem_limit_bytes=24 * 2**20)
-MIDDLE = pltpu.CompilerParams(vmem_limit_bytes=57 * 2**20)
-LARGE = pltpu.CompilerParams(vmem_limit_bytes=59 * 2**20)
+PARAMS = pltpu.CompilerParams(vmem_limit_bytes=60 * 2**20)
 LANES = 128
 CODES = 64
 STAT_ROWS = 16
@@ -100,22 +98,16 @@
         ],
         out_specs=[pl.BlockSpec((per, heads, page_len, head_dim), lambda i: (i, 0, 0, 0)), SMEM],
         scratch_shapes=[pltpu.SMEM((npool,), I32)],
-        compiler_params=LARGE,
+        compiler_params=PARAMS,
         cost_estimate=pl.CostEstimate(flops=6_000_000, bytes_accessed=2_000_000, transcendentals=0),
         name="rope_pages",
     )(page_slot, prompt_lengths, prompt_kv, ct, st, cp, sp)
 
 
-def spread_queries(q_ref, qf_ref, heads):
-    steps, rows, width = q_ref.shape
-    head_dim = qf_ref.shape[1]
-    per = width // head_dim // heads
-    block = heads * steps * per
-    for s in range(steps):
-        for h in range(heads * per):
-            k, g = divmod(h, per)
-            at = k * steps * per + s * per + g
-            qf_ref[pl.ds(at, rows, stride=block), :] = q_ref[s, :, h * head_dim : (h + 1) * head_dim].astype(F32)
+def spread_queries(queries, heads, head_dim):
+    steps, rows, width = queries.shape
+    out = queries.reshape(steps, rows, heads, -1, head_dim).transpose(1, 2, 0, 3, 4)
+    return out.reshape(rows, -1, head_dim)
 
 
 def meta_kernel(npool, pair, cache_pages, page_len, slot_ref, table_ref, context_ref, out_ref, row, count, sems):
@@ -152,7 +144,7 @@
             pltpu.SMEM((npool,), I32),
             pltpu.SemaphoreType.DMA((npool,)),
         ],
-        compiler_params=SMALL,
+        compiler_params=PARAMS,
         cost_estimate=pl.CostEstimate(flops=1000, bytes_accessed=10_000, transcendentals=0),
         name="meta_data",
     )(page_slot, table, context)
@@ -162,35 +154,6 @@
     slot = meta_ref[d, i]
     code = meta_ref[me, CODES + jnp.maximum(slot, 0)]
     return jnp.where(slot >= 0, code // LEFT, 0), slot >= 0
-
-
-def query_kernel(pair, heads, me_ref, meta_ref, q_ref, out_ref, qf):
-    npool = out_ref.shape[0]
-    rows = q_ref.shape[1]
-    block = qf.shape[0] // rows
-    me = me_ref[0]
-    spread_queries(q_ref, qf, heads)
-    for d in range(npool):
-        for p in range(pair):
-            r, _ = item_request(meta_ref, me, d, me * pair + p)
-            at = pl.ds(pl.multiple_of(r * block, block), block)
-            out_ref[d, p * block : (p + 1) * block, :] = qf[at, :].astype(BF16)
-
-
-def queries_out(me, meta, queries, pair, heads, head_dim):
-    npool = meta.shape[0]
-    steps, rows, width = queries.shape
-    block = steps * width // head_dim
-    return pl.pallas_call(
-        functools.partial(query_kernel, pair, heads),
-        out_shape=jax.ShapeDtypeStruct((npool, pair * block, head_dim), BF16),
-        in_specs=[SMEM, SMEM, VMEM],
-        out_specs=VMEM,
-        scratch_shapes=[pltpu.VMEM((rows * block, head_dim), F32)],
-        compiler_params=SMALL,
-        cost_estimate=pl.CostEstimate(flops=100_000, bytes_accessed=500_000, transcendentals=0),
-        name="queries_out",
-    )(me, meta, queries)
 
 
 def transposed_scores(queries, keys, group):
@@ -234,17 +197,15 @@
     stat_ref,
     kv,
     sems,
-    qf,
     kf,
     vf,
     position,
 ):
-    steps, rows, width = q_ref.shape
-    head_dim = qf.shape[1]
+    rows, block, head_dim = q_ref.shape
+    steps = new_ref.shape[0]
     most = table_ref.shape[0]
-    per = width // head_dim // heads
-    group = steps * per
-    block = heads * group
+    group = block // heads
+    per = group // steps
     together = LANES // block
 
     def copy(r, j):
@@ -254,7 +215,6 @@
     for r in range(rows):
         for j in range(most):
             copy(r, j).start()
-    spread_queries(q_ref, qf, heads)
     kf[...] = jnp.zeros_like(kf)
     vf[...] = jnp.zeros_like(vf)
     for r in range(rows):
@@ -279,7 +239,7 @@
         for r in requests:
             for j in range(most):
                 copy(r, j).wait()
-        queries = qf[i * LANES : (i + 1) * LANES, :]
+        queries = q_ref[i * together : (i + 1) * together].reshape(LANES, head_dim)
         keys, values = [], []
         for r, k in chains:
             at = r * block + k * group
@@ -315,9 +275,9 @@
 
 
 def local_attention(table, context, fills, queries, new_kv, cache_kv, tabs):
-    steps, rows, width = queries.shape
+    rows, block, _ = queries.shape
+    steps = new_kv.shape[0]
     slots, _, heads, page_len, head_dim = cache_kv.shape
-    block = steps * width // head_dim
     flat = (rows * block, head_dim)
     freq, sign = tabs[4:]
     return pl.pallas_call(
@@ -330,10 +290,9 @@
             pltpu.SemaphoreType.DMA((table.size,)),
             pltpu.VMEM(flat, F32),
             pltpu.VMEM(flat, F32),
-            pltpu.VMEM(flat, F32),
             pltpu.VMEM((rows, head_dim), I32),
         ],
-        compiler_params=MIDDLE,
+        compiler_params=PARAMS,
         cost_estimate=pl.CostEstimate(flops=800_000_000, bytes_accessed=12_000_000, transcendentals=400_000),
         name="local_attention",
     )(
@@ -354,28 +313,38 @@
     return [high, middle, x - high - middle]
 
 
-def arrived_kernel(npool, pair, me_ref, meta_ref, own_ref, q_ref, keys_ref, prompt_ref, out_ref, values, sem):
+def arrived_kernel(npool, pair, me_ref, meta_ref, own_ref, *refs):
+    blocks = refs[:npool]
+    keys_ref, prompt_ref, out_ref, queries, values, sem, sems = refs[npool:]
     items = npool * pair
     _, heads, page_len, head_dim = keys_ref.shape
-    block = q_ref.shape[0] // items
+    block = queries.shape[0] // items
     group = block // heads
     together = LANES // block
-    fetch = pltpu.make_async_copy(prompt_ref.at[:, 1], values, sem)
-    fetch.start()
-    fetch.wait()
     me = me_ref[0]
+    owners = [owner_of(me, npool, apart, flip) for apart, flip in block_order(npool)]
+    fetch, number, seen = [], [], []
+    for x in range(items):
+        e = owners[x // pair]
+        at = e * pair + x % pair
+        code = meta_ref[e, CODES + jnp.maximum(meta_ref[me, at], 0)]
+        source = blocks[x // pair].at[code // LEFT]
+        fetch.append(pltpu.make_async_copy(source, queries.at[pl.ds(x * block, block)], sems.at[x]))
+        fetch[x].start()
+        number.append(own_ref[at])
+        seen.append(jnp.minimum(code % LEFT, own_ref[items + at]))
+    page_values = pltpu.make_async_copy(prompt_ref.at[:, 1], values, sem)
+    page_values.start()
+    for x in fetch:
+        x.wait()
+    page_values.wait()
     token = lax.broadcasted_iota(I32, (page_len, LANES), 0)
     for i in range(items // together):
         own = range(i * together, (i + 1) * together)
-        chains = [(own_ref[x], k) for x in own for k in range(heads)]
-        seen = []
-        for x in own:
-            code = meta_ref[x // pair, CODES + jnp.maximum(meta_ref[me, x], 0)]
-            seen.append(jnp.minimum(code % LEFT, own_ref[items + x]))
-        scores = transposed_scores(
-            q_ref[i * LANES : (i + 1) * LANES, :], [keys_ref[n, k] for n, k in chains], group
-        )
-        scores = jnp.where(token < lane_values(seen, block, (1, LANES)), scores, -jnp.inf)
+        keys = [keys_ref[number[x], k] for x in own for k in range(heads)]
+        scores = transposed_scores(queries[i * LANES : (i + 1) * LANES, :], keys, group)
+        limit = lane_values([seen[x] for x in own], block, (1, LANES))
+        scores = jnp.where(token < limit, scores, -jnp.inf)
         top = jnp.max(scores, axis=0, keepdims=True)
         top = jnp.where(top > -jnp.inf, top, 0.0)
         weights = jnp.exp(scores - top)
@@ -383,31 +352,41 @@
         stats = jnp.concatenate(stats + [jnp.zeros((STAT_ROWS - len(stats), LANES), F32)], axis=0).astype(BF16)
         weights = jnp.transpose(weights, (1, 0)).astype(BF16)
         for c, x in enumerate(own):
-            both = [values[own_ref[x], k] for k in range(heads)]
+            both = [values[number[x], k] for k in range(heads)]
             both = weighted_values(weights[c * block : (c + 1) * block, :], both)
             at = (x % pair) * block
-            out_ref[x // pair, at : at + block, :] = both.astype(BF16)
-        for e in sorted({x // pair for x in own}):
-            out_ref[e, pair * block : pair * block + STAT_ROWS, :] = stats
-
-
-def arrived_attention(me, meta, own, queries, keys, prompt_kv):
-    npool, rows, head_dim = queries.shape
-    pages, _, heads, page_len, _ = prompt_kv.shape
-    pair = own.shape[0] // 2 // npool
+            out_ref[owners[x // pair], at : at + block, :] = both.astype(BF16)
+        for place in sorted({x // pair for x in own}):
+            out_ref[owners[place], pair * block : pair * block + STAT_ROWS, :] = stats
+
+
+def arrived_attention(me, meta, own, blocks, keys, prompt_kv):
+    npool = len(blocks)
+    pages, _, heads, page_len, head_dim = prompt_kv.shape
+    block = blocks[0].shape[1]
+    items = own.shape[0] // 2
+    pair = items // npool
     return pl.pallas_call(
         functools.partial(arrived_kernel, npool, pair),
-        out_shape=jax.ShapeDtypeStruct((npool, rows + STAT_ROWS, head_dim), BF16),
-        in_specs=[SMEM] * 3 + [VMEM] * 2 + [ANY],
+        out_shape=jax.ShapeDtypeStruct((npool, pair * block + STAT_ROWS, head_dim), BF16),
+        in_specs=[SMEM] * 3 + [ANY] * npool + [VMEM, ANY],
         out_specs=VMEM,
         scratch_shapes=[
+            pltpu.VMEM((items * block, head_dim), BF16),
             pltpu.VMEM((pages, heads, page_len, head_dim), BF16),
             pltpu.SemaphoreType.DMA,
+            pltpu.SemaphoreType.DMA((items,)),
         ],
-        compiler_params=LARGE,
+        compiler_params=PARAMS,
         cost_estimate=pl.CostEstimate(flops=200_000_000, bytes_accessed=4_000_000, transcendentals=70_000),
         name="arrived_attention",
-    )(me, meta, own, queries.reshape(npool * rows, head_dim), keys, prompt_kv)
+    )(me, meta, own, *[in_hbm(x) for x in blocks], keys, prompt_kv)
+
+
+def item_request(meta_ref, me, d, i):
+    slot = meta_ref[d, i]
+    code = meta_ref[me, CODES + jnp.maximum(slot, 0)]
+    return jnp.where(slot >= 0, code // LEFT, 0), slot >= 0
 
 
 def merge_kernel(pair, heads, me_ref, meta_ref, parts_ref, o_ref, stat_ref, out_ref, mixed, top, total, turned):
@@ -434,7 +413,8 @@
             i = me * pair + p
             r, there = item_request(meta_ref, me, d, i)
             at = pl.ds(pl.multiple_of(r * block, block), block)
-            lane = pl.ds(pl.multiple_of(lax.rem(i * block, LANES), block), block)
+            place = place_of(me, npool, d) * pair + p
+            lane = pl.ds(pl.multiple_of(lax.rem(place * block, LANES), block), block)
             m = jnp.broadcast_to(turned[lane, d : d + 1], (block, head_dim))
             l = jnp.broadcast_to(turned[lane, LANES // 2 + d : LANES // 2 + d + 1], (block, head_dim))
             seen = (l > 0.0) & there
@@ -461,25 +441,26 @@
         in_specs=[SMEM] * 2 + [VMEM] * 3,
         out_specs=VMEM,
         scratch_shapes=[pltpu.VMEM(flat, F32)] * 3 + [pltpu.VMEM((LANES, LANES), F32)],
-        compiler_params=SMALL,
+        compiler_params=PARAMS,
         cost_estimate=pl.CostEstimate(flops=2_000_000, bytes_accessed=1_500_000, transcendentals=100_000),
         name="merge",
-    )(me, meta, parts, *local)
-
-
-def project_kernel(npool, tile, place_ref, *refs):
+    )(me, meta, in_hbm(parts), *local)
+
+
+def project_kernel(npool, chunk, place_ref, *refs):
     blocks = refs[:npool]
-    weight_ref, out_ref, lhs, weight, sems, weight_sems = refs[npool:]
+    weight_ref, mine_ref, other_ref, lhs, weight, total, sems, weight_sems = refs[npool:]
     steps, rows, _ = blocks[0].shape
-    columns = weight.shape[1]
+    depth, columns = weight.shape
+    half = columns // 2
     every = npool * rows
-    me, first = place_ref[0], pl.multiple_of(place_ref[1], LANES)
+    me, core = place_ref[0], place_ref[1]
     fetch = []
-    for i in range(columns // tile):
-        at = pl.ds(i * tile, tile)
-        source = weight_ref.at[:, pl.ds(first + i * tile, tile)]
-        fetch.append(pltpu.make_async_copy(source, weight.at[:, at], weight_sems.at[i]))
-        fetch[i].start()
+    for i in range(depth // chunk):
+        at = pl.ds(i * chunk, chunk)
+        fetch.append(pltpu.make_async_copy(weight_ref.at[at], weight.at[at], weight_sems.at[i]))
+        if i == 0:
+            fetch[i].start()
     copies = []
     for x, (apart, flip) in enumerate(block_order(npool)):
         owner = owner_of(me, npool, apart, flip)
@@ -487,38 +468,47 @@
             at = pl.ds(pl.multiple_of(s * every + owner * rows, rows), rows)
             copies.append(pltpu.make_async_copy(blocks[x].at[s], lhs.at[at], sems.at[x * steps + s]))
             copies[-1].start()
+    for x in fetch[1:]:
+        x.start()
     for x in copies:
         x.wait()
-    for i in range(columns // tile):
+    for i in range(depth // chunk):
         fetch[i].wait()
-        at = slice(i * tile, (i + 1) * tile)
-        terms = jnp.dot(lhs[...], weight[:, at], preferred_element_type=F32)
-        for s in range(steps):
-            out_ref[s, :, at] = terms[s * every : (s + 1) * every]
-
-
-def projection(me, first, blocks, weight, columns):
+        at = slice(i * chunk, (i + 1) * chunk)
+        terms = jnp.dot(lhs[:, at], weight[at, :], preferred_element_type=F32)
+        total[...] = terms if i == 0 else total[...] + terms
+    for s in range(steps):
+        at = slice(s * every, (s + 1) * every)
+        mine = pl.ds(pl.multiple_of(core * half, LANES), half)
+        other = pl.ds(pl.multiple_of((1 - core) * half, LANES), half)
+        mine_ref[s] = total[at, mine]
+        other_ref[s] = total[at, other]
+
+
+def projection(me, core, blocks, weight):
     npool = len(blocks)
     steps, rows, width = blocks[0].shape
-    tile = min(columns, 256)
+    columns = weight.shape[1]
     every = steps * npool * rows
+    chunk = 512
     return pl.pallas_call(
-        functools.partial(project_kernel, npool, tile),
-        out_shape=jax.ShapeDtypeStruct((steps, npool * rows, columns), F32),
+        functools.partial(project_kernel, npool, chunk),
+        out_shape=[jax.ShapeDtypeStruct((steps, npool * rows, columns // 2), F32)] * 2,
         in_specs=[SMEM] + [ANY] * (npool + 1),
-        out_specs=VMEM,
+        out_specs=[VMEM] * 2,
         scratch_shapes=[
             pltpu.VMEM((every, width), BF16),
-            pltpu.VMEM((width, columns), BF16),
+            pltpu.VMEM(weight.shape, BF16),
+            pltpu.VMEM((every, columns), F32),
             pltpu.SemaphoreType.DMA((npool * steps,)),
-            pltpu.SemaphoreType.DMA((columns // tile,)),
+            pltpu.SemaphoreType.DMA((width // chunk,)),
         ],
-        compiler_params=MIDDLE,
+        compiler_params=PARAMS,
         cost_estimate=pl.CostEstimate(
-            flops=2 * every * width * columns, bytes_accessed=4_000_000, transcendentals=0
+            flops=2 * every * width * columns, bytes_accessed=6_000_000, transcendentals=0
         ),
         name="project",
-    )(jnp.stack([me, first]), *blocks, weight)
+    )(jnp.stack([me, core]), *[in_hbm(x) for x in blocks], weight)
 
 
 def block_order(npool):
@@ -530,6 +520,17 @@
     pair, side = me // 2, me % 2
     side = 1 - side if flip else side
     return lax.rem(pair + half - apart, half) * 2 + side
+
+
+def place_of(me, npool, holder):
+    half = npool // 2
+    apart = lax.rem(holder // 2 - me // 2 + half, half)
+    flip = lax.rem(me + holder, 2)
+    return flip * half + apart
+
+
+def in_hbm(x):
+    return pltpu.with_memory_space_constraint(x, pltpu.HBM)
 
 
 def gathered(x, npool):
@@ -564,20 +565,20 @@
     me1 = me[None]
     table = page_table.T
 
+    asked = spread_queries(queries, heads, head_dim)
+    asked_all = gathered(asked, npool)
     meta = meta_data(page_slot, table, context_lengths, npool, pair, cache_pages, page_len)
     meta = lax.all_to_all(meta, "pool", split_axis=0, concat_axis=0, tiled=True).reshape(npool, LANES)
+    meta = in_hbm(meta)
     keys, own = rotated_keys(prompt_kv, page_slot, prompt_lengths, tabs, npool, pair, cache_pages)
-    local = local_attention(table, context_lengths, cache_fill, queries, new_kv, cache_kv, tabs)
-    sent = queries_out(me1, meta, queries, pair, heads, head_dim)
-    got = lax.all_to_all(sent, "pool", split_axis=0, concat_axis=0, tiled=True)
-    parts = arrived_attention(me1, meta, own, got, keys, prompt_kv)
+    local = local_attention(table, context_lengths, cache_fill, asked, new_kv, cache_kv, tabs)
+    parts = arrived_attention(me1, meta, own, asked_all, keys, prompt_kv)
     parts = lax.all_to_all(parts, "pool", split_axis=0, concat_axis=0, tiled=True)
     attention = merged(me1, meta, parts, local, queries.shape, heads, pair)
     blocks = gathered(attention, npool)
-    half = out_weight.shape[1] // 2
     core = lax.axis_index("tp").astype(I32)
-    other_terms = swap_halves(projection(me, (1 - core) * half, blocks, out_weight, half))
-    terms = projection(me, core * half, blocks, out_weight, half)
+    terms, other_terms = projection(me, core, blocks, out_weight)
+    other_terms = swap_halves(other_terms)
     return (terms + other_terms).astype(BF16)
 
 

time: 84.3 us -> 81.6 us (0.968)
  starting transfers between devices: 24.9 us -> 33.2 us
  Pallas kernels: 29.9 us -> 25.5 us
  local copies, waits for them, and re-layouts: 6.76 us -> 3.63 us
  waiting for transfers between devices: 18.8 us -> 16 us
    ppermute x3 -> x6, starting transfers between devices: 4.91 us -> 12.8 us  [gathered(): lax.ppermute(x, 'pool', [(i, (i + 2 * by) % npool) for i in range(npool)])]
    pallas_call x3 -> x1, Pallas kernels: 11.4 us -> 5.47 us  [projection(): pl.pallas_call(functools.partial(project_kernel, npool, chunk), out_shape...]
    ppermute x4 -> x8, starting transfers between devices: 5.84 us -> 10.4 us  [gathered(): lax.ppermute(x, 'pool', [(i, i ^ 1) for i in range(npool)])]
    all_to_all x1 -> x0, waiting for transfers between devices: 4.2 us -> none  [shards(): got = lax.all_to_all(sent, 'pool', split_axis=0, concat_axis=0, tiled=True)]
    all_to_all x1 -> x0, starting transfers between devices: 3.37 us -> none  [shards(): got = lax.all_to_all(sent, 'pool', split_axis=0, concat_axis=0, tiled=True)]
    unnamed x36 -> x37, local copies, waits for them, and re-layouts: 6.14 us -> 2.99 us
    all_to_all x1, waiting for transfers between devices: 6.39 us -> 3.39 us  [shards(): lax.all_to_all(meta, 'pool', split_axis=0, concat_axis=0, tiled=True)]
    ppermute x3 -> x6, waiting for transfers between devices: 4.46 us -> 6.61 us  [gathered(): lax.ppermute(x, 'pool', [(i, (i + 2 * by) % npool) for i in range(npool)])]
  transfers between devices with their start and end apart: 11 -> 17, of which waited for: 6 -> 9; matrix products, arithmetic and copies ran while one was open for 2% -> 1% of each run, Pallas kernels for 19% -> 15%
where the time goes in v4:
time: 81.6 us; the launch traced here: 81.1 us
  starting transfers between devices  33.2 us (41%)
  Pallas kernels  25.5 us (31%)
  waiting for transfers between devices  16 us (20%)
  local copies, waits for them, and re-layouts  3.63 us (4%)
  other arithmetic  2.41 us (3%)
    ppermute x6, starting transfers between devices, gathered(): lax.ppermute(x, 'pool', [(i, (i + 2 * by) % npool) for i in range(npool)])  12.8 us
    ppermute x8, starting transfers between devices, gathered(): lax.ppermute(x, 'pool', [(i, i ^ 1) for i in range(npool)])  10.4 us
    pallas_call x1, Pallas kernels, local_attention(): pl.pallas_call(functools.partial(local_kernel, page_len, heads), out_shap...  7.82 us
    ppermute x6, waiting for transfers between devices, gathered(): lax.ppermute(x, 'pool', [(i, (i + 2 * by) % npool) for i in range(npool)])  6.61 us
    all_to_all x1, starting transfers between devices, shards(): lax.all_to_all(meta, 'pool', split_axis=0, concat_axis=0, tiled=True)  6.59 us
    pallas_call x1, Pallas kernels, projection(): pl.pallas_call(functools.partial(project_kernel, npool, chunk), out_shape...  5.47 us
    pallas_call x1, Pallas kernels, arrived_attention(): pl.pallas_call(functools.partial(arrived_kernel, npool, pair), out_shape=...  5.06 us
    ppermute x8, waiting for transfers between devices, gathered(): lax.ppermute(x, 'pool', [(i, i ^ 1) for i in range(npool)])  3.93 us
  transfers between devices with their start and end apart: 17, of which 9 were waited for; matrix products, arithmetic and copies ran while one was open for 1% of the time, Pallas kernels for 15%

profile of v4, /device:TPU:0, one launch (start us, length us, event | category | flops | bytes accessed | tf_op | source)
XLA Modules:
  0.0 81.1 jit_solution(4632044582089383145)
XLA Ops:
  1.0 3.1 %collective-permute-start = (bf16[16,32,128]{2,1,0:T(8,128)(2,1)S(1)}, bf16[16,32,128]{2,1,0:T(8,128)(2,1)S(1)}, u32[]{:S(2)}, u32[]{:S(2)}) collective-permute-start(bf16[16,32,128]{2,1,0:T(8,128)(2,1)S(1)} %bitcast.11), channel_id=1, source_target_pairs={{0,4},{2,6},{4,8},{6,10},{8,12},{10,14},{12,0},{14,2},{1,5},{3,7},... | collective-permute-start | bytes 393224 | tf_op jit(solution)/shard_map/ppermute | solution.py:537
  4.1 2.6 %collective-permute-start.1 = (bf16[16,32,128]{2,1,0:T(8,128)(2,1)S(1)}, bf16[16,32,128]{2,1,0:T(8,128)(2,1)S(1)}, u32[]{:S(2)}, u32[]{:S(2)}) collective-permute-start(bf16[16,32,128]{2,1,0:T(8,128)(2,1)S(1)} %bitcast.12), channel_id=1, source_target_pairs={{0,8},{2,10},{4,12},{6,14},{8,0},{10,2},{12,4},{14,6},{1,9},{3,11}... | collective-permute-start | bytes 393224 | tf_op jit(solution)/shard_map/ppermute | solution.py:537
  8.0 1.5 %collective-permute-start.3 = (bf16[16,32,128]{2,1,0:T(8,128)(2,1)S(1)}, bf16[16,32,128]{2,1,0:T(8,128)(2,1)S(1)}, u32[]{:S(2)}, u32[]{:S(2)}) collective-permute-start(bf16[16,32,128]{2,1,0:T(8,128)(2,1)S(1)} %bitcast.14), channel_id=1, source_target_pairs={{0,2},{2,0},{4,6},{6,4},{8,10},{10,8},{12,14},{14,12},{1,3},{3,1},... | collective-permute-start | bytes 393224 | tf_op jit(solution)/shard_map/ppermute | solution.py:538
  10.5 1.8 %collective-permute-start.4 = (bf16[16,32,128]{2,1,0:T(8,128)(2,1)S(1)}, bf16[16,32,128]{2,1,0:T(8,128)(2,1)S(1)}, u32[]{:S(2)}, u32[]{:S(2)}) collective-permute-start(bf16[16,32,128]{2,1,0:T(8,128)(2,1)S(1)} %collective-permute-done.refs_1_), channel_id=1, source_target_pairs={{0,2},{2,0},{4,6},{6,4},{8,10},{10,8},{12,14},{14,12},{1,3},{3,1},... | collective-permute-start | bytes 393224 | tf_op jit(solution)/shard_map/ppermute | solution.py:538
  12.3 3.0 %collective-permute-done.1.refs_2_ = bf16[16,32,128]{2,1,0:T(8,128)(2,1)S(1)} collective-permute-done((bf16[16,32,128]{2,1,0:T(8,128)(2,1)S(1)}, bf16[16,32,128]{2,1,0:T(8,128)(2,1)S(1)}, u32[]{:S(2)}, u32[]{:S(2)}) %collective-permute-start.1) | collective-permute-done | bytes 131104 | tf_op jit(solution)/shard_map/ppermute | solution.py:537
  15.3 1.5 %collective-permute-start.5 = (bf16[16,32,128]{2,1,0:T(8,128)(2,1)S(1)}, bf16[16,32,128]{2,1,0:T(8,128)(2,1)S(1)}, u32[]{:S(2)}, u32[]{:S(2)}) collective-permute-start(bf16[16,32,128]{2,1,0:T(8,128)(2,1)S(1)} %collective-permute-done.1.refs_2_), channel_id=1, source_target_pairs={{0,2},{2,0},{4,6},{6,4},{8,10},{10,8},{12,14},{14,12},{1,3},{3,1},... | collective-permute-start | bytes 393224 | tf_op jit(solution)/shard_map/ppermute | solution.py:538
  17.3 1.6 %meta_data.1 = s32[8,1,128]{2,1,0:T(1,128)} custom-call(s32[16]{0:T(128)} %slot_ref.3, s32[3,16]{1,0:T(4,128)} %bitcast.21, s32[16]{0:T(128)} %context_ref.3), custom_call_target="tpu_custom_call" | custom-call | flops 1000 | bytes 10000 | tf_op jit(solution)/shard_map/meta_data/pallas_call | solution.py:137
  18.9 6.6 %all-to-all-start = ((s32[8,1,128]{2,1,0:T(1,128)}), s32[8,1,128]{2,1,0:T(1,128)S(1)}, u32[]{:S(2)}, u32[]{:S(2)}) async-start(s32[8,1,128]{2,1,0:T(1,128)} %meta_data.1), calls=%async_computation | async-start | bytes 8192 | tf_op jit(solution)/shard_map/all_to_all | solution.py:571
  25.5 3.1 %rope_pages.1 = (bf16[16,2,128,128]{3,2,1,0:T(8,128)(2,1)}, s32[32]{0:T(128)}) custom-call(s32[16]{0:T(128)} %slot_ref.3, s32[1,4]{1,0:T(1,128)} %len_ref.1, bf16[16,2,2,128,128]{4,3,2,1,0:T(8,128)(2,1)} %refs_9_.1, f32[128,128]{1,0:T(8,128)} %constant.20.clone.ct_ref, f32[128,128]{1,0:T(8,128)} %constant.21.clone.st_ref, f32[16,128]{1,0:T(8,128)} %constant.22.clone.cp_ref, ...), custom_call_target="tpu_custom_call" | custom-call | flops 6000000 | bytes 2000000 | tf_op jit(solution)/shard_map/rope_pages/pallas_call | solution.py:83
  28.6 3.4 %all-to-all-done = s32[8,1,128]{2,1,0:T(1,128)S(1)} async-done(((s32[8,1,128]{2,1,0:T(1,128)}), s32[8,1,128]{2,1,0:T(1,128)S(1)}, u32[]{:S(2)}, u32[]{:S(2)}) %all-to-all-start) | async-done | bytes 4128 | tf_op jit(solution)/shard_map/all_to_all | solution.py:571
  32.8 5.1 %arrived_attention.1 = bf16[8,80,128]{2,1,0:T(8,128)(2,1)} custom-call(s32[1]{0:T(128)} %bitcast.me_ref, s32[8,128]{1,0:T(8,128)} %bitcast.19, s32[32]{0:T(128)} %get-tuple-element.11.own_ref, bf16[16,32,128]{2,1,0:T(8,128)(2,1)} %bitcast.15, bf16[16,32,128]{2,1,0:T(8,128)(2,1)} %copy-done.2, bf16[16,32,128]{2,1,0:T(8,128)(2,1)} %copy-done.3, ...), custom_call_target="tpu_custom_call" | custom-call | flops 200000000 | bytes 4000000 | tf_op jit(solution)/shard_map/arrived_attention/pallas_call | solution.py:369
  37.9 3.4 %all-to-all-start.1 = ((bf16[8,80,128]{2,1,0:T(8,128)(2,1)}), bf16[8,80,128]{2,1,0:T(8,128)(2,1)S(1)}, u32[]{:S(2)}, u32[]{:S(2)}) async-start(bf16[8,80,128]{2,1,0:T(8,128)(2,1)} %arrived_attention.1), calls=%async_computation.1 | async-start | bytes 327680 | tf_op jit(solution)/shard_map/all_to_all | solution.py:576
  41.9 7.8 %local_attention.1 = (f32[512,128]{1,0:T(8,128)}, f32[512,128]{1,0:T(8,128)}) custom-call(s32[3,16]{1,0:T(4,128)} %bitcast.22, s32[16]{0:T(128)} %context_ref.3, s32[48]{0:T(128)} %fill_ref.1, bf16[16,32,128]{2,1,0:T(8,128)(2,1)} %bitcast.16, bf16[2,16,512]{2,1,0:T(8,128)(2,1)} %reshape.15.new_ref, f32[1,128]{1,0:T(1,128)} %constant.24.clone.freq_ref, ...), custom_call_target="tpu_custom_call" | custom-call | flops 800000000 | bytes 12000000 | tf_op jit(solution)/shard_map/local_attention/pallas_call | solution.py:283
  50.4 2.5 %merge.1.refs_0_ = bf16[2,16,2048]{2,1,0:T(8,128)(2,1)} custom-call(s32[1]{0:T(128)} %bitcast.me_ref, s32[8,128]{1,0:T(8,128)} %bitcast.20, bf16[8,80,128]{2,1,0:T(8,128)(2,1)} %copy-done.1, f32[512,128]{1,0:T(8,128)} %get-tuple-element.13.o_ref, f32[512,128]{1,0:T(8,128)} %get-tuple-element.14.stat_ref), custom_call_target="tpu_custom_call" | custom-call | flops 2000000 | bytes 1500000 | tf_op jit(solution)/shard_map/merge/pallas_call | solution.py:438
  52.9 1.9 %collective-permute-start.7 = (bf16[2,16,2048]{2,1,0:T(8,128)(2,1)}, bf16[2,16,2048]{2,1,0:T(8,128)(2,1)S(1)}, u32[]{:S(2)}, u32[]{:S(2)}) collective-permute-start(bf16[2,16,2048]{2,1,0:T(8,128)(2,1)} %merge.1.refs_0_), channel_id=1, source_target_pairs={{0,4},{2,6},{4,8},{6,10},{8,12},{10,14},{12,0},{14,2},{1,5},{3,7},... | collective-permute-start | bytes 393224 | tf_op jit(solution)/shard_map/ppermute | solution.py:537
  54.8 2.4 %collective-permute-start.8 = (bf16[2,16,2048]{2,1,0:T(8,128)(2,1)}, bf16[2,16,2048]{2,1,0:T(8,128)(2,1)S(1)}, u32[]{:S(2)}, u32[]{:S(2)}) collective-permute-start(bf16[2,16,2048]{2,1,0:T(8,128)(2,1)} %merge.1.refs_0_), channel_id=1, source_target_pairs={{0,8},{2,10},{4,12},{6,14},{8,0},{10,2},{12,4},{14,6},{1,9},{3,11}... | collective-permute-start | bytes 393224 | tf_op jit(solution)/shard_map/ppermute | solution.py:537
  60.3 1.6 %collective-permute-start.11 = (bf16[2,16,2048]{2,1,0:T(8,128)(2,1)S(1)}, bf16[2,16,2048]{2,1,0:T(8,128)(2,1)S(1)}, u32[]{:S(2)}, u32[]{:S(2)}) collective-permute-start(bf16[2,16,2048]{2,1,0:T(8,128)(2,1)S(1)} %collective-permute-done.7.refs_1_), channel_id=1, source_target_pairs={{0,2},{2,0},{4,6},{6,4},{8,10},{10,8},{12,14},{14,12},{1,3},{3,1},... | collective-permute-start | bytes 393224 | tf_op jit(solution)/shard_map/ppermute | solution.py:538
  61.9 2.5 %collective-permute-done.8.refs_2_ = bf16[2,16,2048]{2,1,0:T(8,128)(2,1)S(1)} collective-permute-done((bf16[2,16,2048]{2,1,0:T(8,128)(2,1)}, bf16[2,16,2048]{2,1,0:T(8,128)(2,1)S(1)}, u32[]{:S(2)}, u32[]{:S(2)}) %collective-permute-start.8) | collective-permute-done | bytes 131104 | tf_op jit(solution)/shard_map/ppermute | solution.py:537
  64.4 1.6 %collective-permute-start.12 = (bf16[2,16,2048]{2,1,0:T(8,128)(2,1)S(1)}, bf16[2,16,2048]{2,1,0:T(8,128)(2,1)S(1)}, u32[]{:S(2)}, u32[]{:S(2)}) collective-permute-start(bf16[2,16,2048]{2,1,0:T(8,128)(2,1)S(1)} %collective-permute-done.8.refs_2_), channel_id=1, source_target_pairs={{0,2},{2,0},{4,6},{6,4},{8,10},{10,8},{12,14},{14,12},{1,3},{3,1},... | collective-permute-start | bytes 393224 | tf_op jit(solution)/shard_map/ppermute | solution.py:538
  67.3 2.1 %collective-permute-done.12.refs_6_ = bf16[2,16,2048]{2,1,0:T(8,128)(2,1)S(1)} collective-permute-done((bf16[2,16,2048]{2,1,0:T(8,128)(2,1)S(1)}, bf16[2,16,2048]{2,1,0:T(8,128)(2,1)S(1)}, u32[]{:S(2)}, u32[]{:S(2)}) %collective-permute-start.12) | collective-permute-done | bytes 131104 | tf_op jit(solution)/shard_map/ppermute | solution.py:538
  69.3 1.6 %collective-permute-done.13.refs_7_ = bf16[2,16,2048]{2,1,0:T(8,128)(2,1)S(1)} collective-permute-done((bf16[2,16,2048]{2,1,0:T(8,128)(2,1)S(1)}, bf16[2,16,2048]{2,1,0:T(8,128)(2,1)S(1)}, u32[]{:S(2)}, u32[]{:S(2)}) %collective-permute-start.13) | collective-permute-done | bytes 131104 | tf_op jit(solution)/shard_map/ppermute | solution.py:538
  71.6 5.5 %project.1 = (f32[2,128,512]{2,1,0:T(8,128)}, f32[2,128,512]{2,1,0:T(8,128)}) custom-call(s32[2]{0:T(128)} %pad_add_fusion.place_ref, bf16[2,16,2048]{2,1,0:T(8,128)(2,1)} %merge.1.refs_0_, bf16[2,16,2048]{2,1,0:T(8,128)(2,1)} %copy-done.7, bf16[2,16,2048]{2,1,0:T(8,128)(2,1)} %copy-done.8, bf16[2,16,2048]{2,1,0:T(8,128)(2,1)} %copy-done.10, ...), custom_call_target="tpu_custom_call" | custom-call | flops 1073741824 | bytes 6000000 | tf_op jit(solution)/shard_map/project/pallas_call | solution.py:494
  77.2 2.1 %collective-permute-done.14 = f32[2,128,512]{2,1,0:T(8,128)S(1)} collective-permute-done((f32[2,128,512]{2,1,0:T(8,128)}, f32[2,128,512]{2,1,0:T(8,128)S(1)}, u32[]{:S(2)}, u32[]{:S(2)}) %collective-permute-start.14) | collective-permute-done | bytes 524320 | tf_op jit(solution)/shard_map/ppermute | solution.py:544
  79.3 1.8 %add_convert_fusion = bf16[2,128,512]{2,1,0:T(8,128)(2,1)} fusion(f32[2,128,512]{2,1,0:T(8,128)} %get-tuple-element.15, f32[2,128,512]{2,1,0:T(8,128)S(1)} %collective-permute-done.14), kind=kLoop, calls=%fused_computation | loop fusion | flops 262144 | bytes 1310720 | tf_op jit(solution)/shard_map/convert_element_type | solution.py:582
  (57 shorter events, 10.9 us)
Async XLA Ops:
  0.0 41.3 %copy-start.17 = (bf16[2,16,2,2,128]{4,3,2,1,0:T(2,128)(2,1)S(1)}, bf16[2,16,2,2,128]{4,3,2,1,0:T(2,128)(2,1)}, u32[]{:S(2)}) copy-start(bf16[2,16,2,2,128]{4,3,2,1,0:T(2,128)(2,1)} %param.24) | copy-start | bytes 98308
  1.0 31.1 %copy-start = (bf16[2,16,2,8,128]{4,3,0,2,1:T(8,128)(2,1)}, bf16[2,16,2,8,128]{4,3,0,2,1:T(8,128)(2,1)S(1)}, u32[]{:S(2)}) copy-start(bf16[2,16,2,8,128]{4,3,0,2,1:T(8,128)(2,1)S(1)} %copy.19) | copy-start | bytes 393220
  1.0 9.5 %collective-permute-start = (bf16[16,32,128]{2,1,0:T(8,128)(2,1)S(1)}, bf16[16,32,128]{2,1,0:T(8,128)(2,1)S(1)}, u32[]{:S(2)}, u32[]{:S(2)}) collective-permute-start(bf16[16,32,128]{2,1,0:T(8,128)(2,1)S(1)} %bitcast.11), channel_id=1, source_target_pairs={{0,4},{2,6},{4,8},{6,10},{8,12},{10,14},{12,0},{14,2},{1,5},{3,7},... | collective-permute-start | bytes 393224 | tf_op jit(solution)/shard_map/ppermute | solution.py:537
  4.1 11.2 %collective-permute-start.1 = (bf16[16,32,128]{2,1,0:T(8,128)(2,1)S(1)}, bf16[16,32,128]{2,1,0:T(8,128)(2,1)S(1)}, u32[]{:S(2)}, u32[]{:S(2)}) collective-permute-start(bf16[16,32,128]{2,1,0:T(8,128)(2,1)S(1)} %bitcast.12), channel_id=1, source_target_pairs={{0,8},{2,10},{4,12},{6,14},{8,0},{10,2},{12,4},{14,6},{1,9},{3,11}... | collective-permute-start | bytes 393224 | tf_op jit(solution)/shard_map/ppermute | solution.py:537
  6.6 10.2 %collective-permute-start.2 = (bf16[16,32,128]{2,1,0:T(8,128)(2,1)S(1)}, bf16[16,32,128]{2,1,0:T(8,128)(2,1)S(1)}, u32[]{:S(2)}, u32[]{:S(2)}) collective-permute-start(bf16[16,32,128]{2,1,0:T(8,128)(2,1)S(1)} %bitcast.13), channel_id=1, source_target_pairs={{0,12},{2,14},{4,0},{6,2},{8,4},{10,6},{12,8},{14,10},{1,13},{3,15... | collective-permute-start | bytes 393224 | tf_op jit(solution)/shard_map/ppermute | solution.py:537
  8.0 24.0 %collective-permute-start.3 = (bf16[16,32,128]{2,1,0:T(8,128)(2,1)S(1)}, bf16[16,32,128]{2,1,0:T(8,128)(2,1)S(1)}, u32[]{:S(2)}, u32[]{:S(2)}) collective-permute-start(bf16[16,32,128]{2,1,0:T(8,128)(2,1)S(1)} %bitcast.14), channel_id=1, source_target_pairs={{0,2},{2,0},{4,6},{6,4},{8,10},{10,8},{12,14},{14,12},{1,3},{3,1},... | collective-permute-start | bytes 393224 | tf_op jit(solution)/shard_map/ppermute | solution.py:538
  10.5 21.6 %copy-start.2 = (bf16[16,32,128]{2,1,0:T(8,128)(2,1)}, bf16[16,32,128]{2,1,0:T(8,128)(2,1)S(1)}, u32[]{:S(2)}) copy-start(bf16[16,32,128]{2,1,0:T(8,128)(2,1)S(1)} %collective-permute-done.refs_1_) | copy-start | bytes 393220
  10.5 21.5 %collective-permute-start.4 = (bf16[16,32,128]{2,1,0:T(8,128)(2,1)S(1)}, bf16[16,32,128]{2,1,0:T(8,128)(2,1)S(1)}, u32[]{:S(2)}, u32[]{:S(2)}) collective-permute-start(bf16[16,32,128]{2,1,0:T(8,128)(2,1)S(1)} %collective-permute-done.refs_1_), channel_id=1, source_target_pairs={{0,2},{2,0},{4,6},{6,4},{8,10},{10,8},{12,14},{14,12},{1,3},{3,1},... | collective-permute-start | bytes 393224 | tf_op jit(solution)/shard_map/ppermute | solution.py:538
  15.3 16.8 %copy-start.3 = (bf16[16,32,128]{2,1,0:T(8,128)(2,1)}, bf16[16,32,128]{2,1,0:T(8,128)(2,1)S(1)}, u32[]{:S(2)}) copy-start(bf16[16,32,128]{2,1,0:T(8,128)(2,1)S(1)} %collective-permute-done.1.refs_2_) | copy-start | bytes 393220
  15.3 16.7 %collective-permute-start.5 = (bf16[16,32,128]{2,1,0:T(8,128)(2,1)S(1)}, bf16[16,32,128]{2,1,0:T(8,128)(2,1)S(1)}, u32[]{:S(2)}, u32[]{:S(2)}) collective-permute-start(bf16[16,32,128]{2,1,0:T(8,128)(2,1)S(1)} %collective-permute-done.1.refs_2_), channel_id=1, source_target_pairs={{0,2},{2,0},{4,6},{6,4},{8,10},{10,8},{12,14},{14,12},{1,3},{3,1},... | collective-permute-start | bytes 393224 | tf_op jit(solution)/shard_map/ppermute | solution.py:538
  16.8 15.3 %copy-start.4 = (bf16[16,32,128]{2,1,0:T(8,128)(2,1)}, bf16[16,32,128]{2,1,0:T(8,128)(2,1)S(1)}, u32[]{:S(2)}) copy-start(bf16[16,32,128]{2,1,0:T(8,128)(2,1)S(1)} %collective-permute-done.2.refs_3_) | copy-start | bytes 393220
  16.8 15.2 %collective-permute-start.6 = (bf16[16,32,128]{2,1,0:T(8,128)(2,1)S(1)}, bf16[16,32,128]{2,1,0:T(8,128)(2,1)S(1)}, u32[]{:S(2)}, u32[]{:S(2)}) collective-permute-start(bf16[16,32,128]{2,1,0:T(8,128)(2,1)S(1)} %collective-permute-done.2.refs_3_), channel_id=1, source_target_pairs={{0,2},{2,0},{4,6},{6,4},{8,10},{10,8},{12,14},{14,12},{1,3},{3,1},... | collective-permute-start | bytes 393224 | tf_op jit(solution)/shard_map/ppermute | solution.py:538
  18.9 13.0 %all-to-all-start = ((s32[8,1,128]{2,1,0:T(1,128)}), s32[8,1,128]{2,1,0:T(1,128)S(1)}, u32[]{:S(2)}, u32[]{:S(2)}) async-start(s32[8,1,128]{2,1,0:T(1,128)} %meta_data.1), calls=%async_computation | async-start | bytes 8192 | tf_op jit(solution)/shard_map/all_to_all | solution.py:571
  37.9 11.9 %all-to-all-start.1 = ((bf16[8,80,128]{2,1,0:T(8,128)(2,1)}), bf16[8,80,128]{2,1,0:T(8,128)(2,1)S(1)}, u32[]{:S(2)}, u32[]{:S(2)}) async-start(bf16[8,80,128]{2,1,0:T(8,128)(2,1)} %arrived_attention.1), calls=%async_computation.1 | async-start | bytes 327680 | tf_op jit(solution)/shard_map/all_to_all | solution.py:576
  52.9 7.4 %collective-permute-start.7 = (bf16[2,16,2048]{2,1,0:T(8,128)(2,1)}, bf16[2,16,2048]{2,1,0:T(8,128)(2,1)S(1)}, u32[]{:S(2)}, u32[]{:S(2)}) collective-permute-start(bf16[2,16,2048]{2,1,0:T(8,128)(2,1)} %merge.1.refs_0_), channel_id=1, source_target_pairs={{0,4},{2,6},{4,8},{6,10},{8,12},{10,14},{12,0},{14,2},{1,5},{3,7},... | collective-permute-start | bytes 393224 | tf_op jit(solution)/shard_map/ppermute | solution.py:537
  54.8 9.5 %collective-permute-start.8 = (bf16[2,16,2048]{2,1,0:T(8,128)(2,1)}, bf16[2,16,2048]{2,1,0:T(8,128)(2,1)S(1)}, u32[]{:S(2)}, u32[]{:S(2)}) collective-permute-start(bf16[2,16,2048]{2,1,0:T(8,128)(2,1)} %merge.1.refs_0_), channel_id=1, source_target_pairs={{0,8},{2,10},{4,12},{6,14},{8,0},{10,2},{12,4},{14,6},{1,9},{3,11}... | collective-permute-start | bytes 393224 | tf_op jit(solution)/shard_map/ppermute | solution.py:537
  57.2 8.7 %collective-permute-start.9 = (bf16[2,16,2048]{2,1,0:T(8,128)(2,1)}, bf16[2,16,2048]{2,1,0:T(8,128)(2,1)S(1)}, u32[]{:S(2)}, u32[]{:S(2)}) collective-permute-start(bf16[2,16,2048]{2,1,0:T(8,128)(2,1)} %merge.1.refs_0_), channel_id=1, source_target_pairs={{0,12},{2,14},{4,0},{6,2},{8,4},{10,6},{12,8},{14,10},{1,13},{3,15... | collective-permute-start | bytes 393224 | tf_op jit(solution)/shard_map/ppermute | solution.py:537
  58.7 8.3 %collective-permute-start.10 = (bf16[2,16,2048]{2,1,0:T(8,128)(2,1)}, bf16[2,16,2048]{2,1,0:T(8,128)(2,1)S(1)}, u32[]{:S(2)}, u32[]{:S(2)}) collective-permute-start(bf16[2,16,2048]{2,1,0:T(8,128)(2,1)} %merge.1.refs_0_), channel_id=1, source_target_pairs={{0,2},{2,0},{4,6},{6,4},{8,10},{10,8},{12,14},{14,12},{1,3},{3,1},... | collective-permute-start | bytes 393224 | tf_op jit(solution)/shard_map/ppermute | solution.py:538
  60.3 10.7 %copy-start.7 = (bf16[2,16,2048]{2,1,0:T(8,128)(2,1)}, bf16[2,16,2048]{2,1,0:T(8,128)(2,1)S(1)}, u32[]{:S(2)}) copy-start(bf16[2,16,2048]{2,1,0:T(8,128)(2,1)S(1)} %collective-permute-done.7.refs_1_) | copy-start | bytes 393220
  60.3 7.0 %collective-permute-start.11 = (bf16[2,16,2048]{2,1,0:T(8,128)(2,1)S(1)}, bf16[2,16,2048]{2,1,0:T(8,128)(2,1)S(1)}, u32[]{:S(2)}, u32[]{:S(2)}) collective-permute-start(bf16[2,16,2048]{2,1,0:T(8,128)(2,1)S(1)} %collective-permute-done.7.refs_1_), channel_id=1, source_target_pairs={{0,2},{2,0},{4,6},{6,4},{8,10},{10,8},{12,14},{14,12},{1,3},{3,1},... | collective-permute-start | bytes 393224 | tf_op jit(solution)/shard_map/ppermute | solution.py:538
  64.4 6.6 %copy-start.8 = (bf16[2,16,2048]{2,1,0:T(8,128)(2,1)}, bf16[2,16,2048]{2,1,0:T(8,128)(2,1)S(1)}, u32[]{:S(2)}) copy-start(bf16[2,16,2048]{2,1,0:T(8,128)(2,1)S(1)} %collective-permute-done.8.refs_2_) | copy-start | bytes 393220
  64.4 5.0 %collective-permute-start.12 = (bf16[2,16,2048]{2,1,0:T(8,128)(2,1)S(1)}, bf16[2,16,2048]{2,1,0:T(8,128)(2,1)S(1)}, u32[]{:S(2)}, u32[]{:S(2)}) collective-permute-start(bf16[2,16,2048]{2,1,0:T(8,128)(2,1)S(1)} %collective-permute-done.8.refs_2_), channel_id=1, source_target_pairs={{0,2},{2,0},{4,6},{6,4},{8,10},{10,8},{12,14},{14,12},{1,3},{3,1},... | collective-permute-start | bytes 393224 | tf_op jit(solution)/shard_map/ppermute | solution.py:538
  66.0 5.0 %collective-permute-start.13 = (bf16[2,16,2048]{2,1,0:T(8,128)(2,1)S(1)}, bf16[2,16,2048]{2,1,0:T(8,128)(2,1)S(1)}, u32[]{:S(2)}, u32[]{:S(2)}) collective-permute-start(bf16[2,16,2048]{2,1,0:T(8,128)(2,1)S(1)} %collective-permute-done.9.refs_3_), channel_id=1, source_target_pairs={{0,2},{2,0},{4,6},{6,4},{8,10},{10,8},{12,14},{14,12},{1,3},{3,1},... | collective-permute-start | bytes 393224 | tf_op jit(solution)/shard_map/ppermute | solution.py:538
  77.1 2.2 %collective-permute-start.14 = (f32[2,128,512]{2,1,0:T(8,128)}, f32[2,128,512]{2,1,0:T(8,128)S(1)}, u32[]{:S(2)}, u32[]{:S(2)}) collective-permute-start(f32[2,128,512]{2,1,0:T(8,128)} %get-tuple-element.16), channel_id=1, source_target_pairs={{0,1},{1,0},{2,3},{3,2},{4,5},{5,4},{6,7},{7,6},{8,9},{9,8},{10,11... | collective-permute-start | bytes 1572872 | tf_op jit(solution)/shard_map/ppermute | solution.py:544
  (11 other events, 19.0 us)

commit v5 on v4

--- a/solution.py
+++ b/solution.py
@@ -13,11 +13,9 @@
 SMEM = pl.BlockSpec(memory_space=pltpu.SMEM)
 VMEM = pl.BlockSpec(memory_space=pltpu.VMEM)
 ANY = pl.BlockSpec(memory_space=pl.ANY)
-PARAMS = pltpu.CompilerParams(vmem_limit_bytes=60 * 2**20)
+PARAMS = pltpu.CompilerParams(vmem_limit_bytes=24 * 2**20)
 LANES = 128
-CODES = 64
 STAT_ROWS = 16
-LEFT = 256
 
 
 def tables(page_len, head_dim, pages):
@@ -38,18 +36,21 @@
 
     @pl.when(pl.program_id(0) == 0)
     def _():
-        items = own_ref.shape[0] // 2
+        items = own_ref.shape[0] // 3
         for e in range(npool):
             count[e] = 0
         for i in range(items):
             own_ref[i] = 0
             own_ref[items + i] = 0
+            own_ref[2 * items + i] = -1
         for n in range(slot_ref.shape[0]):
-            target = slot_ref[n] // cache_pages
+            slot = slot_ref[n]
+            target = slot // cache_pages
             at = target * (items // npool) + count[target]
             count[target] = count[target] + 1
             own_ref[at] = n
             own_ref[items + at] = page_place(len_ref, page_len, n)[1]
+            own_ref[2 * items + at] = slot - target * cache_pages
 
     for i in range(per):
         number, _ = page_place(len_ref, page_len, pl.program_id(0) * per + i)
@@ -85,7 +86,7 @@
         grid=(pages // per,),
         out_shape=[
             jax.ShapeDtypeStruct((pages, heads, page_len, head_dim), BF16),
-            jax.ShapeDtypeStruct((2 * npool * pair,), I32),
+            jax.ShapeDtypeStruct((3 * npool * pair,), I32),
         ],
         in_specs=[
             SMEM,
@@ -101,65 +102,57 @@
         compiler_params=PARAMS,
         cost_estimate=pl.CostEstimate(flops=6_000_000, bytes_accessed=2_000_000, transcendentals=0),
         name="rope_pages",
-    )(page_slot, prompt_lengths, prompt_kv, ct, st, cp, sp)
-
-
-def spread_queries(queries, heads, head_dim):
-    steps, rows, width = queries.shape
-    out = queries.reshape(steps, rows, heads, -1, head_dim).transpose(1, 2, 0, 3, 4)
-    return out.reshape(rows, -1, head_dim)
-
-
-def meta_kernel(npool, pair, cache_pages, page_len, slot_ref, table_ref, context_ref, out_ref, row, count, sems):
+    )(*[in_hbm(x) for x in (page_slot, prompt_lengths, prompt_kv, ct, st, cp, sp)])
+
+
+def asked_kernel(page_len, heads, table_ref, context_ref, q_ref, out_ref, spread):
     most, rows = table_ref.shape
-    for e in range(npool):
-        count[e] = 0
-    for i in range(npool * pair):
-        row[0, i] = -1
-    for n in range(slot_ref.shape[0]):
-        slot = slot_ref[n]
-        target = slot // cache_pages
-        row[0, target * pair + count[target]] = slot - target * cache_pages
-        count[target] = count[target] + 1
+    steps, _, width = q_ref.shape
+    block, head_dim = out_ref.shape[1:]
+    per = width // head_dim // heads
+    for s in range(steps):
+        for h in range(heads * per):
+            k, g = divmod(h, per)
+            at = pl.ds(k * steps * per + s * per + g, rows, stride=block)
+            spread[at, :] = q_ref[s, :, h * head_dim : (h + 1) * head_dim].astype(F32)
+    for r in range(rows):
+        out_ref[r] = spread[r * block : (r + 1) * block, :].astype(BF16)
+    lane = lax.broadcasted_iota(I32, (block, LANES), 1)
+    line = lax.broadcasted_iota(I32, (block, LANES), 0)
+    request = jnp.zeros((block, LANES), I32)
+    left = jnp.zeros((block, LANES), I32)
     for r in range(rows):
         context = context_ref[r]
         for j in range(most):
-            left = jnp.clip(context - j * page_len, 0, page_len)
-            row[0, CODES + table_ref[j, r]] = r * LEFT + left
-    copies = [pltpu.make_async_copy(row, out_ref.at[e], sems.at[e]) for e in range(npool)]
-    for x in copies:
-        x.start()
-    for x in copies:
-        x.wait()
-
-
-def meta_data(page_slot, table, context, npool, pair, cache_pages, page_len):
+            here = lane == table_ref[j, r]
+            request = jnp.where(here, r, request)
+            left = jnp.where(here, jnp.clip(context - j * page_len, 0, page_len), left)
+    out_ref[rows] = jnp.where(line == 0, request, left).astype(F32).astype(BF16)
+
+
+def asked_queries(table, context, queries, page_len, heads, head_dim):
+    steps, rows, width = queries.shape
+    block = steps * width // head_dim
     return pl.pallas_call(
-        functools.partial(meta_kernel, npool, pair, cache_pages, page_len),
-        out_shape=jax.ShapeDtypeStruct((npool, 1, LANES), I32),
-        in_specs=[SMEM] * 3,
-        out_specs=ANY,
-        scratch_shapes=[
-            pltpu.SMEM((1, LANES), I32),
-            pltpu.SMEM((npool,), I32),
-            pltpu.SemaphoreType.DMA((npool,)),
-        ],
+        functools.partial(asked_kernel, page_len, heads),
+        out_shape=jax.ShapeDtypeStruct((rows + 1, block, head_dim), BF16),
+        in_specs=[SMEM, SMEM, VMEM],
+        out_specs=VMEM,
+        scratch_shapes=[pltpu.VMEM((rows * block, head_dim), F32)],
         compiler_params=PARAMS,
-        cost_estimate=pl.CostEstimate(flops=1000, bytes_accessed=10_000, transcendentals=0),
-        name="meta_data",
-    )(page_slot, table, context)
-
-
-def item_request(meta_ref, me, d, i):
-    slot = meta_ref[d, i]
-    code = meta_ref[me, CODES + jnp.maximum(slot, 0)]
-    return jnp.where(slot >= 0, code // LEFT, 0), slot >= 0
+        cost_estimate=pl.CostEstimate(flops=100_000, bytes_accessed=300_000, transcendentals=0),
+        name="asked_queries",
+    )(in_hbm(table), in_hbm(context), in_hbm(queries))
+
+
+def read_scalar(x, pick):
+    return jnp.max(jnp.where(pick, x, -2.0)).astype(I32)
 
 
 def transposed_scores(queries, keys, group):
     turned = jnp.transpose(queries.astype(F32), (1, 0)).astype(BF16)
-    chain = lax.broadcasted_iota(I32, turned.shape, 1) // group
-    spread = [jnp.where(chain == c, turned, jnp.zeros_like(turned)) for c in range(len(keys))]
+    chain = lax.broadcasted_iota(I32, (1, turned.shape[1]), 1) // group
+    spread = [turned * jnp.where(chain == c, 1.0, 0.0).astype(BF16) for c in range(len(keys))]
     scores = jnp.dot(
         jnp.concatenate(keys, axis=1), jnp.concatenate(spread, axis=0), preferred_element_type=F32
     )
@@ -202,6 +195,7 @@
     position,
 ):
     rows, block, head_dim = q_ref.shape
+    rows = rows - 1
     steps = new_ref.shape[0]
     most = table_ref.shape[0]
     group = block // heads
@@ -236,9 +230,10 @@
     for i in range(rows // together):
         requests = range(i * together, (i + 1) * together)
         chains = [(r, k) for r in requests for k in range(heads)]
-        for r in requests:
-            for j in range(most):
-                copy(r, j).wait()
+        if i % 2 == 0:
+            for r in range(i * together, min(rows, (i + 2) * together)):
+                for j in range(most):
+                    copy(r, j).wait()
         queries = q_ref[i * together : (i + 1) * together].reshape(LANES, head_dim)
         keys, values = [], []
         for r, k in chains:
@@ -276,6 +271,7 @@
 
 def local_attention(table, context, fills, queries, new_kv, cache_kv, tabs):
     rows, block, _ = queries.shape
+    rows = rows - 1
     steps = new_kv.shape[0]
     slots, _, heads, page_len, head_dim = cache_kv.shape
     flat = (rows * block, head_dim)
@@ -296,14 +292,10 @@
         cost_estimate=pl.CostEstimate(flops=800_000_000, bytes_accessed=12_000_000, transcendentals=400_000),
         name="local_attention",
     )(
-        table,
-        context,
-        fills,
+        *[in_hbm(x) for x in (table, context, fills)],
         queries,
         new_kv.reshape(steps, rows, 2 * heads * head_dim),
-        freq,
-        sign,
-        cache_kv,
+        *[in_hbm(x) for x in (freq, sign, cache_kv)],
     )
 
 
@@ -313,30 +305,31 @@
     return [high, middle, x - high - middle]
 
 
-def arrived_kernel(npool, pair, me_ref, meta_ref, own_ref, *refs):
+def arrived_kernel(npool, pair, me_ref, own_ref, *refs):
     blocks = refs[:npool]
-    keys_ref, prompt_ref, out_ref, queries, values, sem, sems = refs[npool:]
+    keys_ref, prompt_ref, out_ref, queries, values, sem = refs[npool:]
     items = npool * pair
     _, heads, page_len, head_dim = keys_ref.shape
-    block = queries.shape[0] // items
+    rows, block = blocks[0].shape[0] - 1, blocks[0].shape[1]
     group = block // heads
     together = LANES // block
     me = me_ref[0]
     owners = [owner_of(me, npool, apart, flip) for apart, flip in block_order(npool)]
-    fetch, number, seen = [], [], []
-    for x in range(items):
-        e = owners[x // pair]
-        at = e * pair + x % pair
-        code = meta_ref[e, CODES + jnp.maximum(meta_ref[me, at], 0)]
-        source = blocks[x // pair].at[code // LEFT]
-        fetch.append(pltpu.make_async_copy(source, queries.at[pl.ds(x * block, block)], sems.at[x]))
-        fetch[x].start()
-        number.append(own_ref[at])
-        seen.append(jnp.minimum(code % LEFT, own_ref[items + at]))
     page_values = pltpu.make_async_copy(prompt_ref.at[:, 1], values, sem)
     page_values.start()
-    for x in fetch:
-        x.wait()
+    line = lax.broadcasted_iota(I32, (STAT_ROWS, LANES), 0)
+    lane = lax.broadcasted_iota(I32, (STAT_ROWS, LANES), 1)
+    number, seen, request = [], [], []
+    for x in range(items):
+        at = owners[x // pair] * pair + x % pair
+        slot = own_ref[2 * items + at]
+        side = blocks[x // pair][rows, :STAT_ROWS, :].astype(F32)
+        reader = read_scalar(side, (lane == slot) & (line == 0))
+        left = read_scalar(side, (lane == slot) & (line == 1))
+        queries[x * block : (x + 1) * block, :] = blocks[x // pair][jnp.maximum(reader, 0)]
+        number.append(own_ref[at])
+        seen.append(jnp.minimum(left, own_ref[items + at]))
+        request.append(jnp.where(slot >= 0, reader, -1))
     page_values.wait()
     token = lax.broadcasted_iota(I32, (page_len, LANES), 0)
     for i in range(items // together):
@@ -349,6 +342,7 @@
         top = jnp.where(top > -jnp.inf, top, 0.0)
         weights = jnp.exp(scores - top)
         stats = pieces(top) + pieces(jnp.sum(weights, axis=0, keepdims=True))
+        stats.append(lane_values([request[x] for x in own], block, (1, LANES)).astype(F32))
         stats = jnp.concatenate(stats + [jnp.zeros((STAT_ROWS - len(stats), LANES), F32)], axis=0).astype(BF16)
         weights = jnp.transpose(weights, (1, 0)).astype(BF16)
         for c, x in enumerate(own):
@@ -360,36 +354,29 @@
             out_ref[owners[place], pair * block : pair * block + STAT_ROWS, :] = stats
 
 
-def arrived_attention(me, meta, own, blocks, keys, prompt_kv):
+def arrived_attention(me, own, blocks, keys, prompt_kv):
     npool = len(blocks)
     pages, _, heads, page_len, head_dim = prompt_kv.shape
     block = blocks[0].shape[1]
-    items = own.shape[0] // 2
+    items = own.shape[0] // 3
     pair = items // npool
     return pl.pallas_call(
         functools.partial(arrived_kernel, npool, pair),
         out_shape=jax.ShapeDtypeStruct((npool, pair * block + STAT_ROWS, head_dim), BF16),
-        in_specs=[SMEM] * 3 + [ANY] * npool + [VMEM, ANY],
+        in_specs=[SMEM] * 2 + [VMEM] * (npool + 1) + [ANY],
         out_specs=VMEM,
         scratch_shapes=[
             pltpu.VMEM((items * block, head_dim), BF16),
             pltpu.VMEM((pages, heads, page_len, head_dim), BF16),
             pltpu.SemaphoreType.DMA,
-            pltpu.SemaphoreType.DMA((items,)),
         ],
         compiler_params=PARAMS,
         cost_estimate=pl.CostEstimate(flops=200_000_000, bytes_accessed=4_000_000, transcendentals=70_000),
         name="arrived_attention",
-    )(me, meta, own, *[in_hbm(x) for x in blocks], keys, prompt_kv)
-
-
-def item_request(meta_ref, me, d, i):
-    slot = meta_ref[d, i]
-    code = meta_ref[me, CODES + jnp.maximum(slot, 0)]
-    return jnp.where(slot >= 0, code // LEFT, 0), slot >= 0
-
-
-def merge_kernel(pair, heads, me_ref, meta_ref, parts_ref, o_ref, stat_ref, out_ref, mixed, top, total, turned):
+    )(me, own, *blocks, keys, in_hbm(prompt_kv))
+
+
+def merge_kernel(pair, heads, me_ref, parts_ref, o_ref, stat_ref, out_ref, mixed, top, total, turned):
     npool = parts_ref.shape[0]
     steps, rows, width = out_ref.shape
     head_dim = o_ref.shape[1]
@@ -401,20 +388,22 @@
     mixed[...] = o_ref[...]
     top[...] = jnp.broadcast_to(stat_ref[:, group : group + 1], shape)
     total[...] = jnp.broadcast_to(stat_ref[:, group + 8 : group + 9], shape)
-    tops, totals = [], []
+    tops, totals, readers = [], [], []
+    chain = lax.broadcasted_iota(I32, (1, LANES), 1) // block
     for d in range(npool):
         x = parts_ref[d, pair * block : pair * block + STAT_ROWS, :].astype(F32)
         tops.append(x[0:1] + x[1:2] + x[2:3])
         totals.append(x[3:4] + x[4:5] + x[5:6])
+        readers.append(x[6:7])
     empty = [jnp.zeros((LANES // 2 - npool, LANES), F32)]
     turned[...] = jnp.transpose(jnp.concatenate(tops + empty + totals + empty, axis=0), (1, 0))
     for d in range(npool):
         for p in range(pair):
-            i = me * pair + p
-            r, there = item_request(meta_ref, me, d, i)
-            at = pl.ds(pl.multiple_of(r * block, block), block)
-            place = place_of(me, npool, d) * pair + p
-            lane = pl.ds(pl.multiple_of(lax.rem(place * block, LANES), block), block)
+            part = lax.rem(place_of(me, npool, d) * pair + p, LANES // block)
+            r = read_scalar(readers[d], chain == part)
+            there = r >= 0
+            at = pl.ds(pl.multiple_of(jnp.maximum(r, 0) * block, block), block)
+            lane = pl.ds(pl.multiple_of(part * block, block), block)
             m = jnp.broadcast_to(turned[lane, d : d + 1], (block, head_dim))
             l = jnp.broadcast_to(turned[lane, LANES // 2 + d : LANES // 2 + d + 1], (block, head_dim))
             seen = (l > 0.0) & there
@@ -433,18 +422,18 @@
             out_ref[s, :, h * head_dim : (h + 1) * head_dim] = (mixed[at, :] / total[at, :]).astype(BF16)
 
 
-def merged(me, meta, parts, local, shape, heads, pair):
+def merged(me, parts, local, shape, heads, pair):
     flat = local[0].shape
     return pl.pallas_call(
         functools.partial(merge_kernel, pair, heads),
         out_shape=jax.ShapeDtypeStruct(shape, BF16),
-        in_specs=[SMEM] * 2 + [VMEM] * 3,
+        in_specs=[SMEM] + [VMEM] * 3,
         out_specs=VMEM,
         scratch_shapes=[pltpu.VMEM(flat, F32)] * 3 + [pltpu.VMEM((LANES, LANES), F32)],
         compiler_params=PARAMS,
         cost_estimate=pl.CostEstimate(flops=2_000_000, bytes_accessed=1_500_000, transcendentals=100_000),
         name="merge",
-    )(me, meta, in_hbm(parts), *local)
+    )(me, parts, *local)
 
 
 def project_kernel(npool, chunk, place_ref, *refs):
@@ -508,7 +497,7 @@
             flops=2 * every * width * columns, bytes_accessed=6_000_000, transcendentals=0
         ),
         name="project",
-    )(jnp.stack([me, core]), *[in_hbm(x) for x in blocks], weight)
+    )(jnp.stack([me, core]), *blocks, in_hbm(weight))
 
 
 def block_order(npool):
@@ -565,16 +554,13 @@
     me1 = me[None]
     table = page_table.T
 
-    asked = spread_queries(queries, heads, head_dim)
+    asked = asked_queries(table, context_lengths, queries, page_len, heads, head_dim)
     asked_all = gathered(asked, npool)
-    meta = meta_data(page_slot, table, context_lengths, npool, pair, cache_pages, page_len)
-    meta = lax.all_to_all(meta, "pool", split_axis=0, concat_axis=0, tiled=True).reshape(npool, LANES)
-    meta = in_hbm(meta)
     keys, own = rotated_keys(prompt_kv, page_slot, prompt_lengths, tabs, npool, pair, cache_pages)
     local = local_attention(table, context_lengths, cache_fill, asked, new_kv, cache_kv, tabs)
-    parts = arrived_attention(me1, meta, own, asked_all, keys, prompt_kv)
+    parts = arrived_attention(me1, own, asked_all, keys, prompt_kv)
     parts = lax.all_to_all(parts, "pool", split_axis=0, concat_axis=0, tiled=True)
-    attention = merged(me1, meta, parts, local, queries.shape, heads, pair)
+    attention = merged(me1, parts, local, queries.shape, heads, pair)
     blocks = gathered(attention, npool)
     core = lax.axis_index("tp").astype(I32)
     terms, other_terms = projection(me, core, blocks, out_weight)

time: 81.6 us -> 68.6 us (0.84)
  Pallas kernels: 25.5 us -> 20.6 us
  starting transfers between devices: 33.2 us -> 28.8 us
  local copies, waits for them, and re-layouts: 3.63 us -> 0.02 us
  waiting for transfers between devices: 16 us -> 18 us
  other arithmetic: 2.41 us -> 0.85 us
    all_to_all x1 -> x0, starting transfers between devices: 6.59 us -> none  [shards(): lax.all_to_all(meta, 'pool', split_axis=0, concat_axis=0, tiled=True)]
    ppermute x8, waiting for transfers between devices: 3.93 us -> 8.11 us  [gathered(): lax.ppermute(x, 'pool', [(i, i ^ 1) for i in range(npool)])]
    all_to_all x1 -> x0, waiting for transfers between devices: 3.39 us -> none  [shards(): lax.all_to_all(meta, 'pool', split_axis=0, concat_axis=0, tiled=True)]
    unnamed x37 -> x2, local copies, waits for them, and re-layouts: 2.99 us -> 0.01 us
    all_to_all x1, starting transfers between devices: 3.39 us -> 5.8 us  [shards(): lax.all_to_all(parts, 'pool', split_axis=0, concat_axis=0, tiled=True)]
    pallas_call x1, Pallas kernels: 2.5 us -> 0.99 us  [merged(): pl.pallas_call(functools.partial(merge_kernel, pair, heads), out_shape=ja...]
    convert_element_type x1, other arithmetic: 1.82 us -> 0.77 us  [shards(): return (terms + other_terms).astype(BF16)]
    pallas_call x1, Pallas kernels: 5.47 us -> 4.5 us  [projection(): pl.pallas_call(functools.partial(project_kernel, npool, chunk), out_shape...]
  transfers between devices with their start and end apart: 17 -> 16, of which waited for: 9 -> 10; matrix products, arithmetic and copies ran while one was open for 1% -> 0% of each run, Pallas kernels for 15% -> 14%
where the time goes in v5:
time: 68.6 us; the launch traced here: 68.3 us
  starting transfers between devices  28.8 us (42%)
  Pallas kernels  20.6 us (30%)
  waiting for transfers between devices  18 us (26%)
  other arithmetic  0.85 us (1%)
    ppermute x6, starting transfers between devices, gathered(): lax.ppermute(x, 'pool', [(i, (i + 2 * by) % npool) for i in range(npool)])  12.3 us
    ppermute x8, starting transfers between devices, gathered(): lax.ppermute(x, 'pool', [(i, i ^ 1) for i in range(npool)])  10.6 us
    ppermute x8, waiting for transfers between devices, gathered(): lax.ppermute(x, 'pool', [(i, i ^ 1) for i in range(npool)])  8.11 us
    ppermute x6, waiting for transfers between devices, gathered(): lax.ppermute(x, 'pool', [(i, (i + 2 * by) % npool) for i in range(npool)])  7.37 us
    pallas_call x1, Pallas kernels, local_attention(): pl.pallas_call(functools.partial(local_kernel, page_len, heads), out_shap...  6.94 us
    all_to_all x1, starting transfers between devices, shards(): lax.all_to_all(parts, 'pool', split_axis=0, concat_axis=0, tiled=True)  5.8 us
    pallas_call x1, Pallas kernels, projection(): pl.pallas_call(functools.partial(project_kernel, npool, chunk), out_shape...  4.5 us
    pallas_call x1, Pallas kernels, arrived_attention(): pl.pallas_call(functools.partial(arrived_kernel, npool, pair), out_shape=...  4.18 us
  transfers between devices with their start and end apart: 16, of which 10 were waited for; matrix products, arithmetic and copies ran while one was open for 0% of the time, Pallas kernels for 14%

profile of v5, /device:TPU:0, one launch (start us, length us, event | category | flops | bytes accessed | tf_op | source)
XLA Modules:
  0.0 68.3 jit_solution(12434674681384846183)
XLA Ops:
  1.2 3.1 %collective-permute-start = (bf16[17,32,128]{2,1,0:T(8,128)(2,1)S(1)}, bf16[17,32,128]{2,1,0:T(8,128)(2,1)S(1)}, u32[]{:S(2)}, u32[]{:S(2)}) collective-permute-start(bf16[17,32,128]{2,1,0:T(8,128)(2,1)S(1)} %asked_queries.1.refs_0_.q_ref), channel_id=1, source_target_pairs={{0,4},{2,6},{4,8},{6,10},{8,12},{10,14},{12,0},{14,2},{1,5},{3,7},... | collective-permute-start | bytes 417800 | tf_op jit(solution)/shard_map/ppermute | solution.py:526
  4.3 2.6 %collective-permute-start.1 = (bf16[17,32,128]{2,1,0:T(8,128)(2,1)S(1)}, bf16[17,32,128]{2,1,0:T(8,128)(2,1)S(1)}, u32[]{:S(2)}, u32[]{:S(2)}) collective-permute-start(bf16[17,32,128]{2,1,0:T(8,128)(2,1)S(1)} %asked_queries.1.refs_0_.q_ref), channel_id=1, source_target_pairs={{0,8},{2,10},{4,12},{6,14},{8,0},{10,2},{12,4},{14,6},{1,9},{3,11}... | collective-permute-start | bytes 417800 | tf_op jit(solution)/shard_map/ppermute | solution.py:526
  6.9 1.3 %collective-permute-start.2 = (bf16[17,32,128]{2,1,0:T(8,128)(2,1)S(1)}, bf16[17,32,128]{2,1,0:T(8,128)(2,1)S(1)}, u32[]{:S(2)}, u32[]{:S(2)}) collective-permute-start(bf16[17,32,128]{2,1,0:T(8,128)(2,1)S(1)} %asked_queries.1.refs_0_.q_ref), channel_id=1, source_target_pairs={{0,12},{2,14},{4,0},{6,2},{8,4},{10,6},{12,8},{14,10},{1,13},{3,15... | collective-permute-start | bytes 417800 | tf_op jit(solution)/shard_map/ppermute | solution.py:526
  8.2 1.5 %collective-permute-start.3 = (bf16[17,32,128]{2,1,0:T(8,128)(2,1)S(1)}, bf16[17,32,128]{2,1,0:T(8,128)(2,1)S(1)}, u32[]{:S(2)}, u32[]{:S(2)}) collective-permute-start(bf16[17,32,128]{2,1,0:T(8,128)(2,1)S(1)} %asked_queries.1.refs_0_.q_ref), channel_id=1, source_target_pairs={{0,2},{2,0},{4,6},{6,4},{8,10},{10,8},{12,14},{14,12},{1,3},{3,1},... | collective-permute-start | bytes 417800 | tf_op jit(solution)/shard_map/ppermute | solution.py:527
  10.9 1.8 %collective-permute-start.4 = (bf16[17,32,128]{2,1,0:T(8,128)(2,1)S(1)}, bf16[17,32,128]{2,1,0:T(8,128)(2,1)S(1)}, u32[]{:S(2)}, u32[]{:S(2)}) collective-permute-start(bf16[17,32,128]{2,1,0:T(8,128)(2,1)S(1)} %collective-permute-done.refs_1_), channel_id=1, source_target_pairs={{0,2},{2,0},{4,6},{6,4},{8,10},{10,8},{12,14},{14,12},{1,3},{3,1},... | collective-permute-start | bytes 417800 | tf_op jit(solution)/shard_map/ppermute | solution.py:527
  12.7 3.4 %collective-permute-done.1.refs_2_ = bf16[17,32,128]{2,1,0:T(8,128)(2,1)S(1)} collective-permute-done((bf16[17,32,128]{2,1,0:T(8,128)(2,1)S(1)}, bf16[17,32,128]{2,1,0:T(8,128)(2,1)S(1)}, u32[]{:S(2)}, u32[]{:S(2)}) %collective-permute-start.1) | collective-permute-done | bytes 139296 | tf_op jit(solution)/shard_map/ppermute | solution.py:526
  16.1 1.5 %collective-permute-start.5 = (bf16[17,32,128]{2,1,0:T(8,128)(2,1)S(1)}, bf16[17,32,128]{2,1,0:T(8,128)(2,1)S(1)}, u32[]{:S(2)}, u32[]{:S(2)}) collective-permute-start(bf16[17,32,128]{2,1,0:T(8,128)(2,1)S(1)} %collective-permute-done.1.refs_2_), channel_id=1, source_target_pairs={{0,2},{2,0},{4,6},{6,4},{8,10},{10,8},{12,14},{14,12},{1,3},{3,1},... | collective-permute-start | bytes 417800 | tf_op jit(solution)/shard_map/ppermute | solution.py:527
  18.1 2.8 %rope_pages.1 = (bf16[16,2,128,128]{3,2,1,0:T(8,128)(2,1)S(1)}, s32[48]{0:T(128)S(1)}) custom-call(s32[16]{0:T(128)} %slot_ref.1, s32[1,4]{1,0:T(1,128)} %len_ref.1, bf16[16,2,2,128,128]{4,3,2,1,0:T(8,128)(2,1)} %refs_9_.1, f32[128,128]{1,0:T(8,128)} %constant.20.clone.ct_ref, f32[128,128]{1,0:T(8,128)} %constant.21.clone.st_ref, ...), custom_call_target="tpu_custom_call" | custom-call | flops 6000000 | bytes 2000000 | tf_op jit(solution)/shard_map/rope_pages/pallas_call | solution.py:84
  20.9 1.7 %collective-permute-done.5.refs_6_ = bf16[17,32,128]{2,1,0:T(8,128)(2,1)S(1)} collective-permute-done((bf16[17,32,128]{2,1,0:T(8,128)(2,1)S(1)}, bf16[17,32,128]{2,1,0:T(8,128)(2,1)S(1)}, u32[]{:S(2)}, u32[]{:S(2)}) %collective-permute-start.5) | collective-permute-done | bytes 139296 | tf_op jit(solution)/shard_map/ppermute | solution.py:527
  22.6 1.9 %collective-permute-done.6.refs_7_ = bf16[17,32,128]{2,1,0:T(8,128)(2,1)S(1)} collective-permute-done((bf16[17,32,128]{2,1,0:T(8,128)(2,1)S(1)}, bf16[17,32,128]{2,1,0:T(8,128)(2,1)S(1)}, u32[]{:S(2)}, u32[]{:S(2)}) %collective-permute-start.6) | collective-permute-done | bytes 139296 | tf_op jit(solution)/shard_map/ppermute | solution.py:527
  24.6 4.2 %arrived_attention.1 = bf16[8,80,128]{2,1,0:T(8,128)(2,1)} custom-call(s32[1]{0:T(128)} %bitcast.me_ref, s32[48]{0:T(128)S(1)} %get-tuple-element.11.own_ref, bf16[17,32,128]{2,1,0:T(8,128)(2,1)S(1)} %asked_queries.1.refs_0_.q_ref, bf16[17,32,128]{2,1,0:T(8,128)(2,1)S(1)} %collective-permute-done.refs_1_, ...), custom_call_target="tpu_custom_call" | custom-call | flops 200000000 | bytes 4000000 | tf_op jit(solution)/shard_map/arrived_attention/pallas_call | solution.py:363
  28.7 5.8 %all-to-all-start = ((bf16[8,80,128]{2,1,0:T(8,128)(2,1)}), bf16[8,80,128]{2,1,0:T(8,128)(2,1)S(1)}, u32[]{:S(2)}, u32[]{:S(2)}) async-start(bf16[8,80,128]{2,1,0:T(8,128)(2,1)} %arrived_attention.1), calls=%async_computation | async-start | bytes 327680 | tf_op jit(solution)/shard_map/all_to_all | solution.py:562
  34.6 6.9 %local_attention.1 = (f32[512,128]{1,0:T(8,128)S(1)}, f32[512,128]{1,0:T(8,128)S(1)}) custom-call(s32[3,16]{1,0:T(4,128)} %bitcast.4, s32[16]{0:T(128)} %context_ref.3, s32[48]{0:T(128)} %fill_ref.1, bf16[17,32,128]{2,1,0:T(8,128)(2,1)S(1)} %asked_queries.1.refs_0_.q_ref, bf16[2,16,512]{2,1,0:T(8,128)(2,1)S(1)} %reshape.3.new_ref, ...), custom_call_target="tpu_custom_call" | custom-call | flops 800000000 | bytes 12000000 | tf_op jit(solution)/shard_map/local_attention/pallas_call | solution.py:279
  43.1 1.5 %collective-permute-start.7 = (bf16[2,16,2048]{2,1,0:T(8,128)(2,1)S(1)}, bf16[2,16,2048]{2,1,0:T(8,128)(2,1)S(1)}, u32[]{:S(2)}, u32[]{:S(2)}) collective-permute-start(bf16[2,16,2048]{2,1,0:T(8,128)(2,1)S(1)} %merge.1.refs_0_), channel_id=1, source_target_pairs={{0,4},{2,6},{4,8},{6,10},{8,12},{10,14},{12,0},{14,2},{1,5},{3,7},... | collective-permute-start | bytes 393224 | tf_op jit(solution)/shard_map/ppermute | solution.py:526
  44.6 2.4 %collective-permute-start.8 = (bf16[2,16,2048]{2,1,0:T(8,128)(2,1)S(1)}, bf16[2,16,2048]{2,1,0:T(8,128)(2,1)S(1)}, u32[]{:S(2)}, u32[]{:S(2)}) collective-permute-start(bf16[2,16,2048]{2,1,0:T(8,128)(2,1)S(1)} %merge.1.refs_0_), channel_id=1, source_target_pairs={{0,8},{2,10},{4,12},{6,14},{8,0},{10,2},{12,4},{14,6},{1,9},{3,11}... | collective-permute-start | bytes 393224 | tf_op jit(solution)/shard_map/ppermute | solution.py:526
  46.9 1.5 %collective-permute-start.9 = (bf16[2,16,2048]{2,1,0:T(8,128)(2,1)S(1)}, bf16[2,16,2048]{2,1,0:T(8,128)(2,1)S(1)}, u32[]{:S(2)}, u32[]{:S(2)}) collective-permute-start(bf16[2,16,2048]{2,1,0:T(8,128)(2,1)S(1)} %merge.1.refs_0_), channel_id=1, source_target_pairs={{0,12},{2,14},{4,0},{6,2},{8,4},{10,6},{12,8},{14,10},{1,13},{3,15... | collective-permute-start | bytes 393224 | tf_op jit(solution)/shard_map/ppermute | solution.py:526
  48.4 1.5 %collective-permute-start.10 = (bf16[2,16,2048]{2,1,0:T(8,128)(2,1)S(1)}, bf16[2,16,2048]{2,1,0:T(8,128)(2,1)S(1)}, u32[]{:S(2)}, u32[]{:S(2)}) collective-permute-start(bf16[2,16,2048]{2,1,0:T(8,128)(2,1)S(1)} %merge.1.refs_0_), channel_id=1, source_target_pairs={{0,2},{2,0},{4,6},{6,4},{8,10},{10,8},{12,14},{14,12},{1,3},{3,1},... | collective-permute-start | bytes 393224 | tf_op jit(solution)/shard_map/ppermute | solution.py:527
  50.5 1.8 %collective-permute-start.11 = (bf16[2,16,2048]{2,1,0:T(8,128)(2,1)S(1)}, bf16[2,16,2048]{2,1,0:T(8,128)(2,1)S(1)}, u32[]{:S(2)}, u32[]{:S(2)}) collective-permute-start(bf16[2,16,2048]{2,1,0:T(8,128)(2,1)S(1)} %collective-permute-done.7.refs_1_), channel_id=1, source_target_pairs={{0,2},{2,0},{4,6},{6,4},{8,10},{10,8},{12,14},{14,12},{1,3},{3,1},... | collective-permute-start | bytes 393224 | tf_op jit(solution)/shard_map/ppermute | solution.py:527
  52.2 2.2 %collective-permute-done.8.refs_2_ = bf16[2,16,2048]{2,1,0:T(8,128)(2,1)S(1)} collective-permute-done((bf16[2,16,2048]{2,1,0:T(8,128)(2,1)S(1)}, bf16[2,16,2048]{2,1,0:T(8,128)(2,1)S(1)}, u32[]{:S(2)}, u32[]{:S(2)}) %collective-permute-start.8) | collective-permute-done | bytes 131104 | tf_op jit(solution)/shard_map/ppermute | solution.py:526
  54.5 1.4 %collective-permute-start.12 = (bf16[2,16,2048]{2,1,0:T(8,128)(2,1)S(1)}, bf16[2,16,2048]{2,1,0:T(8,128)(2,1)S(1)}, u32[]{:S(2)}, u32[]{:S(2)}) collective-permute-start(bf16[2,16,2048]{2,1,0:T(8,128)(2,1)S(1)} %collective-permute-done.8.refs_2_), channel_id=1, source_target_pairs={{0,2},{2,0},{4,6},{6,4},{8,10},{10,8},{12,14},{14,12},{1,3},{3,1},... | collective-permute-start | bytes 393224 | tf_op jit(solution)/shard_map/ppermute | solution.py:527
  56.6 3.0 %collective-permute-done.12.refs_6_ = bf16[2,16,2048]{2,1,0:T(8,128)(2,1)S(1)} collective-permute-done((bf16[2,16,2048]{2,1,0:T(8,128)(2,1)S(1)}, bf16[2,16,2048]{2,1,0:T(8,128)(2,1)S(1)}, u32[]{:S(2)}, u32[]{:S(2)}) %collective-permute-start.12) | collective-permute-done | bytes 131104 | tf_op jit(solution)/shard_map/ppermute | solution.py:527
  59.6 1.4 %collective-permute-done.13.refs_7_ = bf16[2,16,2048]{2,1,0:T(8,128)(2,1)S(1)} collective-permute-done((bf16[2,16,2048]{2,1,0:T(8,128)(2,1)S(1)}, bf16[2,16,2048]{2,1,0:T(8,128)(2,1)S(1)}, u32[]{:S(2)}, u32[]{:S(2)}) %collective-permute-start.13) | collective-permute-done | bytes 131104 | tf_op jit(solution)/shard_map/ppermute | solution.py:527
  61.0 4.5 %project.1 = (f32[2,128,512]{2,1,0:T(8,128)S(1)}, f32[2,128,512]{2,1,0:T(8,128)S(1)}) custom-call(s32[2]{0:T(128)S(1)} %pad_add_fusion.place_ref, bf16[2,16,2048]{2,1,0:T(8,128)(2,1)S(1)} %merge.1.refs_0_, bf16[2,16,2048]{2,1,0:T(8,128)(2,1)S(1)} %collective-permute-done.7.refs_1_, bf16[2,16,2048]{2,1,0:T(8,128)(2,1)S(1)} %collective-permute-done.8.refs_2_, ...), custom_call_target="tpu_custom_call" | custom-call | flops 1073741824 | bytes 6000000 | tf_op jit(solution)/shard_map/project/pallas_call | solution.py:483
  65.6 1.9 %collective-permute-done.14 = f32[2,128,512]{2,1,0:T(8,128)S(1)} collective-permute-done((f32[2,128,512]{2,1,0:T(8,128)S(1)}, f32[2,128,512]{2,1,0:T(8,128)S(1)}, u32[]{:S(2)}, u32[]{:S(2)}) %collective-permute-start.14) | collective-permute-done | bytes 524320 | tf_op jit(solution)/shard_map/ppermute | solution.py:533
  (19 shorter events, 6.6 us)
Async XLA Ops:
  0.0 34.5 %copy-start = (bf16[2,16,2,2,128]{4,3,2,1,0:T(2,128)(2,1)S(1)}, bf16[2,16,2,2,128]{4,3,2,1,0:T(2,128)(2,1)}, u32[]{:S(2)}) copy-start(bf16[2,16,2,2,128]{4,3,2,1,0:T(2,128)(2,1)} %param.24) | copy-start | bytes 98308
  1.2 9.7 %collective-permute-start = (bf16[17,32,128]{2,1,0:T(8,128)(2,1)S(1)}, bf16[17,32,128]{2,1,0:T(8,128)(2,1)S(1)}, u32[]{:S(2)}, u32[]{:S(2)}) collective-permute-start(bf16[17,32,128]{2,1,0:T(8,128)(2,1)S(1)} %asked_queries.1.refs_0_.q_ref), channel_id=1, source_target_pairs={{0,4},{2,6},{4,8},{6,10},{8,12},{10,14},{12,0},{14,2},{1,5},{3,7},... | collective-permute-start | bytes 417800 | tf_op jit(solution)/shard_map/ppermute | solution.py:526
  4.3 11.8 %collective-permute-start.1 = (bf16[17,32,128]{2,1,0:T(8,128)(2,1)S(1)}, bf16[17,32,128]{2,1,0:T(8,128)(2,1)S(1)}, u32[]{:S(2)}, u32[]{:S(2)}) collective-permute-start(bf16[17,32,128]{2,1,0:T(8,128)(2,1)S(1)} %asked_queries.1.refs_0_.q_ref), channel_id=1, source_target_pairs={{0,8},{2,10},{4,12},{6,14},{8,0},{10,2},{12,4},{14,6},{1,9},{3,11}... | collective-permute-start | bytes 417800 | tf_op jit(solution)/shard_map/ppermute | solution.py:526
  6.9 10.7 %collective-permute-start.2 = (bf16[17,32,128]{2,1,0:T(8,128)(2,1)S(1)}, bf16[17,32,128]{2,1,0:T(8,128)(2,1)S(1)}, u32[]{:S(2)}, u32[]{:S(2)}) collective-permute-start(bf16[17,32,128]{2,1,0:T(8,128)(2,1)S(1)} %asked_queries.1.refs_0_.q_ref), channel_id=1, source_target_pairs={{0,12},{2,14},{4,0},{6,2},{8,4},{10,6},{12,8},{14,10},{1,13},{3,15... | collective-permute-start | bytes 417800 | tf_op jit(solution)/shard_map/ppermute | solution.py:526
  8.2 12.6 %collective-permute-start.3 = (bf16[17,32,128]{2,1,0:T(8,128)(2,1)S(1)}, bf16[17,32,128]{2,1,0:T(8,128)(2,1)S(1)}, u32[]{:S(2)}, u32[]{:S(2)}) collective-permute-start(bf16[17,32,128]{2,1,0:T(8,128)(2,1)S(1)} %asked_queries.1.refs_0_.q_ref), channel_id=1, source_target_pairs={{0,2},{2,0},{4,6},{6,4},{8,10},{10,8},{12,14},{14,12},{1,3},{3,1},... | collective-permute-start | bytes 417800 | tf_op jit(solution)/shard_map/ppermute | solution.py:527
  10.9 9.9 %collective-permute-start.4 = (bf16[17,32,128]{2,1,0:T(8,128)(2,1)S(1)}, bf16[17,32,128]{2,1,0:T(8,128)(2,1)S(1)}, u32[]{:S(2)}, u32[]{:S(2)}) collective-permute-start(bf16[17,32,128]{2,1,0:T(8,128)(2,1)S(1)} %collective-permute-done.refs_1_), channel_id=1, source_target_pairs={{0,2},{2,0},{4,6},{6,4},{8,10},{10,8},{12,14},{14,12},{1,3},{3,1},... | collective-permute-start | bytes 417800 | tf_op jit(solution)/shard_map/ppermute | solution.py:527
  16.1 6.5 %collective-permute-start.5 = (bf16[17,32,128]{2,1,0:T(8,128)(2,1)S(1)}, bf16[17,32,128]{2,1,0:T(8,128)(2,1)S(1)}, u32[]{:S(2)}, u32[]{:S(2)}) collective-permute-start(bf16[17,32,128]{2,1,0:T(8,128)(2,1)S(1)} %collective-permute-done.1.refs_2_), channel_id=1, source_target_pairs={{0,2},{2,0},{4,6},{6,4},{8,10},{10,8},{12,14},{14,12},{1,3},{3,1},... | collective-permute-start | bytes 417800 | tf_op jit(solution)/shard_map/ppermute | solution.py:527
  17.6 7.0 %collective-permute-start.6 = (bf16[17,32,128]{2,1,0:T(8,128)(2,1)S(1)}, bf16[17,32,128]{2,1,0:T(8,128)(2,1)S(1)}, u32[]{:S(2)}, u32[]{:S(2)}) collective-permute-start(bf16[17,32,128]{2,1,0:T(8,128)(2,1)S(1)} %collective-permute-done.2.refs_3_), channel_id=1, source_target_pairs={{0,2},{2,0},{4,6},{6,4},{8,10},{10,8},{12,14},{14,12},{1,3},{3,1},... | collective-permute-start | bytes 417800 | tf_op jit(solution)/shard_map/ppermute | solution.py:527
  28.7 13.4 %all-to-all-start = ((bf16[8,80,128]{2,1,0:T(8,128)(2,1)}), bf16[8,80,128]{2,1,0:T(8,128)(2,1)S(1)}, u32[]{:S(2)}, u32[]{:S(2)}) async-start(bf16[8,80,128]{2,1,0:T(8,128)(2,1)} %arrived_attention.1), calls=%async_computation | async-start | bytes 327680 | tf_op jit(solution)/shard_map/all_to_all | solution.py:562
  43.1 7.4 %collective-permute-start.7 = (bf16[2,16,2048]{2,1,0:T(8,128)(2,1)S(1)}, bf16[2,16,2048]{2,1,0:T(8,128)(2,1)S(1)}, u32[]{:S(2)}, u32[]{:S(2)}) collective-permute-start(bf16[2,16,2048]{2,1,0:T(8,128)(2,1)S(1)} %merge.1.refs_0_), channel_id=1, source_target_pairs={{0,4},{2,6},{4,8},{6,10},{8,12},{10,14},{12,0},{14,2},{1,5},{3,7},... | collective-permute-start | bytes 393224 | tf_op jit(solution)/shard_map/ppermute | solution.py:526
  44.6 9.9 %collective-permute-start.8 = (bf16[2,16,2048]{2,1,0:T(8,128)(2,1)S(1)}, bf16[2,16,2048]{2,1,0:T(8,128)(2,1)S(1)}, u32[]{:S(2)}, u32[]{:S(2)}) collective-permute-start(bf16[2,16,2048]{2,1,0:T(8,128)(2,1)S(1)} %merge.1.refs_0_), channel_id=1, source_target_pairs={{0,8},{2,10},{4,12},{6,14},{8,0},{10,2},{12,4},{14,6},{1,9},{3,11}... | collective-permute-start | bytes 393224 | tf_op jit(solution)/shard_map/ppermute | solution.py:526
  46.9 9.0 %collective-permute-start.9 = (bf16[2,16,2048]{2,1,0:T(8,128)(2,1)S(1)}, bf16[2,16,2048]{2,1,0:T(8,128)(2,1)S(1)}, u32[]{:S(2)}, u32[]{:S(2)}) collective-permute-start(bf16[2,16,2048]{2,1,0:T(8,128)(2,1)S(1)} %merge.1.refs_0_), channel_id=1, source_target_pairs={{0,12},{2,14},{4,0},{6,2},{8,4},{10,6},{12,8},{14,10},{1,13},{3,15... | collective-permute-start | bytes 393224 | tf_op jit(solution)/shard_map/ppermute | solution.py:526
  48.4 8.2 %collective-permute-start.10 = (bf16[2,16,2048]{2,1,0:T(8,128)(2,1)S(1)}, bf16[2,16,2048]{2,1,0:T(8,128)(2,1)S(1)}, u32[]{:S(2)}, u32[]{:S(2)}) collective-permute-start(bf16[2,16,2048]{2,1,0:T(8,128)(2,1)S(1)} %merge.1.refs_0_), channel_id=1, source_target_pairs={{0,2},{2,0},{4,6},{6,4},{8,10},{10,8},{12,14},{14,12},{1,3},{3,1},... | collective-permute-start | bytes 393224 | tf_op jit(solution)/shard_map/ppermute | solution.py:527
  50.5 6.1 %collective-permute-start.11 = (bf16[2,16,2048]{2,1,0:T(8,128)(2,1)S(1)}, bf16[2,16,2048]{2,1,0:T(8,128)(2,1)S(1)}, u32[]{:S(2)}, u32[]{:S(2)}) collective-permute-start(bf16[2,16,2048]{2,1,0:T(8,128)(2,1)S(1)} %collective-permute-done.7.refs_1_), channel_id=1, source_target_pairs={{0,2},{2,0},{4,6},{6,4},{8,10},{10,8},{12,14},{14,12},{1,3},{3,1},... | collective-permute-start | bytes 393224 | tf_op jit(solution)/shard_map/ppermute | solution.py:527
  54.5 5.1 %collective-permute-start.12 = (bf16[2,16,2048]{2,1,0:T(8,128)(2,1)S(1)}, bf16[2,16,2048]{2,1,0:T(8,128)(2,1)S(1)}, u32[]{:S(2)}, u32[]{:S(2)}) collective-permute-start(bf16[2,16,2048]{2,1,0:T(8,128)(2,1)S(1)} %collective-permute-done.8.refs_2_), channel_id=1, source_target_pairs={{0,2},{2,0},{4,6},{6,4},{8,10},{10,8},{12,14},{14,12},{1,3},{3,1},... | collective-permute-start | bytes 393224 | tf_op jit(solution)/shard_map/ppermute | solution.py:527
  55.9 5.1 %collective-permute-start.13 = (bf16[2,16,2048]{2,1,0:T(8,128)(2,1)S(1)}, bf16[2,16,2048]{2,1,0:T(8,128)(2,1)S(1)}, u32[]{:S(2)}, u32[]{:S(2)}) collective-permute-start(bf16[2,16,2048]{2,1,0:T(8,128)(2,1)S(1)} %collective-permute-done.9.refs_3_), channel_id=1, source_target_pairs={{0,2},{2,0},{4,6},{6,4},{8,10},{10,8},{12,14},{14,12},{1,3},{3,1},... | collective-permute-start | bytes 393224 | tf_op jit(solution)/shard_map/ppermute | solution.py:527
  65.5 2.0 %collective-permute-start.14 = (f32[2,128,512]{2,1,0:T(8,128)S(1)}, f32[2,128,512]{2,1,0:T(8,128)S(1)}, u32[]{:S(2)}, u32[]{:S(2)}) collective-permute-start(f32[2,128,512]{2,1,0:T(8,128)S(1)} %get-tuple-element.16), channel_id=1, source_target_pairs={{0,1},{1,0},{2,3},{3,2},{4,5},{5,4},{6,7},{7,6},{8,9},{9,8},{10,11... | collective-permute-start | bytes 1572872 | tf_op jit(solution)/shard_map/ppermute | solution.py:533

commit v6 on v5

--- a/solution.py
+++ b/solution.py
@@ -16,6 +16,7 @@
 PARAMS = pltpu.CompilerParams(vmem_limit_bytes=24 * 2**20)
 LANES = 128
 STAT_ROWS = 16
+CODE = 256
 
 
 def tables(page_len, head_dim, pages):
@@ -30,9 +31,9 @@
 
 
 def rope_kernel(
-    npool, cache_pages, per, slot_ref, len_ref, keys_ref, ct_ref, st_ref, cp_ref, sp_ref, out_ref, own_ref, count
+    npool, cache_pages, per, slot_ref, len_ref, pages_ref, ct_ref, st_ref, cp_ref, sp_ref, out_ref, own_ref, count
 ):
-    _, _, heads, page_len, head_dim = keys_ref.shape
+    _, _, heads, page_len, head_dim = pages_ref.shape
 
     @pl.when(pl.program_id(0) == 0)
     def _():
@@ -59,8 +60,9 @@
         cos = c0 * ct - s0 * st
         sin = s0 * ct + c0 * st
         for k in range(heads):
-            x = keys_ref[i, 0, k].astype(F32)
-            out_ref[i, k] = (x * cos + pltpu.roll(x, head_dim // 2, 1) * sin).astype(BF16)
+            x = pages_ref[i, 0, k].astype(F32)
+            out_ref[i, 0, k] = (x * cos + pltpu.roll(x, head_dim // 2, 1) * sin).astype(BF16)
+            out_ref[i, 1, k] = pages_ref[i, 1, k]
 
 
 def page_place(len_ref, page_len, n):
@@ -76,7 +78,7 @@
     return number, fill
 
 
-def rotated_keys(prompt_kv, page_slot, prompt_lengths, tabs, npool, pair, cache_pages):
+def rotated_pages(prompt_kv, page_slot, prompt_lengths, tabs, npool, pair, cache_pages):
     pages, _, heads, page_len, head_dim = prompt_kv.shape
     per = pages // 2
     ct, st, cp, sp, _, _ = tabs
@@ -85,19 +87,19 @@
         functools.partial(rope_kernel, npool, cache_pages, per),
         grid=(pages // per,),
         out_shape=[
-            jax.ShapeDtypeStruct((pages, heads, page_len, head_dim), BF16),
+            jax.ShapeDtypeStruct(prompt_kv.shape, BF16),
             jax.ShapeDtypeStruct((3 * npool * pair,), I32),
         ],
         in_specs=[
             SMEM,
             SMEM,
-            pl.BlockSpec((per, 1, heads, page_len, head_dim), lambda i: (i, 0, 0, 0, 0)),
+            pl.BlockSpec((per,) + prompt_kv.shape[1:], lambda i: (i, 0, 0, 0, 0)),
             whole(ct),
             whole(st),
             whole(cp),
             whole(sp),
         ],
-        out_specs=[pl.BlockSpec((per, heads, page_len, head_dim), lambda i: (i, 0, 0, 0)), SMEM],
+        out_specs=[pl.BlockSpec((per,) + prompt_kv.shape[1:], lambda i: (i, 0, 0, 0, 0)), SMEM],
         scratch_shapes=[pltpu.SMEM((npool,), I32)],
         compiler_params=PARAMS,
         cost_estimate=pl.CostEstimate(flops=6_000_000, bytes_accessed=2_000_000, transcendentals=0),
@@ -307,34 +309,31 @@
 
 def arrived_kernel(npool, pair, me_ref, own_ref, *refs):
     blocks = refs[:npool]
-    keys_ref, prompt_ref, out_ref, queries, values, sem = refs[npool:]
+    pages_ref, out_ref, queries = refs[npool:]
     items = npool * pair
-    _, heads, page_len, head_dim = keys_ref.shape
+    _, _, heads, page_len, head_dim = pages_ref.shape
     rows, block = blocks[0].shape[0] - 1, blocks[0].shape[1]
     group = block // heads
     together = LANES // block
     me = me_ref[0]
     owners = [owner_of(me, npool, apart, flip) for apart, flip in block_order(npool)]
-    page_values = pltpu.make_async_copy(prompt_ref.at[:, 1], values, sem)
-    page_values.start()
-    line = lax.broadcasted_iota(I32, (STAT_ROWS, LANES), 0)
-    lane = lax.broadcasted_iota(I32, (STAT_ROWS, LANES), 1)
+    lane = lax.broadcasted_iota(I32, (1, LANES), 1)
+    codes = [x[rows, :STAT_ROWS, :].astype(F32) for x in blocks]
+    codes = [x[0:1] * CODE + x[1:2] for x in codes]
     number, seen, request = [], [], []
     for x in range(items):
         at = owners[x // pair] * pair + x % pair
         slot = own_ref[2 * items + at]
-        side = blocks[x // pair][rows, :STAT_ROWS, :].astype(F32)
-        reader = read_scalar(side, (lane == slot) & (line == 0))
-        left = read_scalar(side, (lane == slot) & (line == 1))
-        queries[x * block : (x + 1) * block, :] = blocks[x // pair][jnp.maximum(reader, 0)]
+        code = jnp.maximum(read_scalar(codes[x // pair], lane == slot), 0)
+        reader, left = code // CODE, code % CODE
+        queries[x * block : (x + 1) * block, :] = blocks[x // pair][reader]
         number.append(own_ref[at])
         seen.append(jnp.minimum(left, own_ref[items + at]))
         request.append(jnp.where(slot >= 0, reader, -1))
-    page_values.wait()
     token = lax.broadcasted_iota(I32, (page_len, LANES), 0)
     for i in range(items // together):
         own = range(i * together, (i + 1) * together)
-        keys = [keys_ref[number[x], k] for x in own for k in range(heads)]
+        keys = [pages_ref[number[x], 0, k] for x in own for k in range(heads)]
         scores = transposed_scores(queries[i * LANES : (i + 1) * LANES, :], keys, group)
         limit = lane_values([seen[x] for x in own], block, (1, LANES))
         scores = jnp.where(token < limit, scores, -jnp.inf)
@@ -346,7 +345,7 @@
         stats = jnp.concatenate(stats + [jnp.zeros((STAT_ROWS - len(stats), LANES), F32)], axis=0).astype(BF16)
         weights = jnp.transpose(weights, (1, 0)).astype(BF16)
         for c, x in enumerate(own):
-            both = [values[number[x], k] for k in range(heads)]
+            both = [pages_ref[number[x], 1, k] for k in range(heads)]
             both = weighted_values(weights[c * block : (c + 1) * block, :], both)
             at = (x % pair) * block
             out_ref[owners[x // pair], at : at + block, :] = both.astype(BF16)
@@ -354,26 +353,22 @@
             out_ref[owners[place], pair * block : pair * block + STAT_ROWS, :] = stats
 
 
-def arrived_attention(me, own, blocks, keys, prompt_kv):
+def arrived_attention(me, own, blocks, arrived):
     npool = len(blocks)
-    pages, _, heads, page_len, head_dim = prompt_kv.shape
+    head_dim = arrived.shape[4]
     block = blocks[0].shape[1]
     items = own.shape[0] // 3
     pair = items // npool
     return pl.pallas_call(
         functools.partial(arrived_kernel, npool, pair),
         out_shape=jax.ShapeDtypeStruct((npool, pair * block + STAT_ROWS, head_dim), BF16),
-        in_specs=[SMEM] * 2 + [VMEM] * (npool + 1) + [ANY],
+        in_specs=[SMEM] * 2 + [VMEM] * (npool + 1),
         out_specs=VMEM,
-        scratch_shapes=[
-            pltpu.VMEM((items * block, head_dim), BF16),
-            pltpu.VMEM((pages, heads, page_len, head_dim), BF16),
-            pltpu.SemaphoreType.DMA,
-        ],
+        scratch_shapes=[pltpu.VMEM((items * block, head_dim), BF16)],
         compiler_params=PARAMS,
         cost_estimate=pl.CostEstimate(flops=200_000_000, bytes_accessed=4_000_000, transcendentals=70_000),
         name="arrived_attention",
-    )(me, own, *blocks, keys, in_hbm(prompt_kv))
+    )(me, own, *blocks, arrived)
 
 
 def merge_kernel(pair, heads, me_ref, parts_ref, o_ref, stat_ref, out_ref, mixed, top, total, turned):
@@ -436,20 +431,34 @@
     )(me, parts, *local)
 
 
-def project_kernel(npool, chunk, place_ref, *refs):
+def fetch_kernel(weight_ref, after_ref, out_ref, sem):
+    del after_ref
+    copy = pltpu.make_async_copy(weight_ref, out_ref, sem)
+    copy.start()
+    copy.wait()
+
+
+def fetched(weight, after):
+    return pl.pallas_call(
+        fetch_kernel,
+        out_shape=pltpu.VMEM(weight.shape, weight.dtype),
+        in_specs=[ANY, ANY],
+        out_specs=ANY,
+        scratch_shapes=[pltpu.SemaphoreType.DMA],
+        compiler_params=PARAMS,
+        cost_estimate=pl.CostEstimate(flops=0, bytes_accessed=2 * weight.size * 2, transcendentals=0),
+        name="fetch_weight",
+    )(in_hbm(weight), after)
+
+
+def project_kernel(npool, place_ref, *refs):
     blocks = refs[:npool]
-    weight_ref, mine_ref, other_ref, lhs, weight, total, sems, weight_sems = refs[npool:]
+    weight_ref, mine_ref, other_ref, lhs, sems = refs[npool:]
     steps, rows, _ = blocks[0].shape
-    depth, columns = weight.shape
-    half = columns // 2
+    half = weight_ref.shape[1] // 2
+    tile = min(half, 256)
     every = npool * rows
     me, core = place_ref[0], place_ref[1]
-    fetch = []
-    for i in range(depth // chunk):
-        at = pl.ds(i * chunk, chunk)
-        fetch.append(pltpu.make_async_copy(weight_ref.at[at], weight.at[at], weight_sems.at[i]))
-        if i == 0:
-            fetch[i].start()
     copies = []
     for x, (apart, flip) in enumerate(block_order(npool)):
         owner = owner_of(me, npool, apart, flip)
@@ -457,47 +466,33 @@
             at = pl.ds(pl.multiple_of(s * every + owner * rows, rows), rows)
             copies.append(pltpu.make_async_copy(blocks[x].at[s], lhs.at[at], sems.at[x * steps + s]))
             copies[-1].start()
-    for x in fetch[1:]:
-        x.start()
     for x in copies:
         x.wait()
-    for i in range(depth // chunk):
-        fetch[i].wait()
-        at = slice(i * chunk, (i + 1) * chunk)
-        terms = jnp.dot(lhs[:, at], weight[at, :], preferred_element_type=F32)
-        total[...] = terms if i == 0 else total[...] + terms
-    for s in range(steps):
-        at = slice(s * every, (s + 1) * every)
-        mine = pl.ds(pl.multiple_of(core * half, LANES), half)
-        other = pl.ds(pl.multiple_of((1 - core) * half, LANES), half)
-        mine_ref[s] = total[at, mine]
-        other_ref[s] = total[at, other]
-
-
-def projection(me, core, blocks, weight):
+    for out_ref, first in ((mine_ref, core * half), (other_ref, (1 - core) * half)):
+        for i in range(half // tile):
+            at = pl.ds(pl.multiple_of(first + i * tile, LANES), tile)
+            terms = jnp.dot(lhs[...], weight_ref[:, at], preferred_element_type=F32)
+            for s in range(steps):
+                out_ref[s, :, i * tile : (i + 1) * tile] = terms[s * every : (s + 1) * every]
+
+
+def projection(place, blocks, weight):
     npool = len(blocks)
     steps, rows, width = blocks[0].shape
     columns = weight.shape[1]
     every = steps * npool * rows
-    chunk = 512
-    return pl.pallas_call(
-        functools.partial(project_kernel, npool, chunk),
+    return pl.pallas_call(
+        functools.partial(project_kernel, npool),
         out_shape=[jax.ShapeDtypeStruct((steps, npool * rows, columns // 2), F32)] * 2,
-        in_specs=[SMEM] + [ANY] * (npool + 1),
+        in_specs=[SMEM] + [ANY] * npool + [VMEM],
         out_specs=[VMEM] * 2,
-        scratch_shapes=[
-            pltpu.VMEM((every, width), BF16),
-            pltpu.VMEM(weight.shape, BF16),
-            pltpu.VMEM((every, columns), F32),
-            pltpu.SemaphoreType.DMA((npool * steps,)),
-            pltpu.SemaphoreType.DMA((width // chunk,)),
-        ],
+        scratch_shapes=[pltpu.VMEM((every, width), BF16), pltpu.SemaphoreType.DMA((npool * steps,))],
         compiler_params=PARAMS,
         cost_estimate=pl.CostEstimate(
             flops=2 * every * width * columns, bytes_accessed=6_000_000, transcendentals=0
         ),
         name="project",
-    )(jnp.stack([me, core]), *blocks, in_hbm(weight))
+    )(place, *blocks, weight)
 
 
 def block_order(npool):
@@ -551,19 +546,19 @@
     cache_pages = cache_kv.shape[0]
     pair = (pages + npool - 1) // npool
     tabs = tables(page_len, head_dim, pages)
-    me1 = me[None]
+    place = jnp.stack([me, lax.axis_index("tp").astype(I32)])
     table = page_table.T
 
     asked = asked_queries(table, context_lengths, queries, page_len, heads, head_dim)
     asked_all = gathered(asked, npool)
-    keys, own = rotated_keys(prompt_kv, page_slot, prompt_lengths, tabs, npool, pair, cache_pages)
+    arrived, own = rotated_pages(prompt_kv, page_slot, prompt_lengths, tabs, npool, pair, cache_pages)
     local = local_attention(table, context_lengths, cache_fill, asked, new_kv, cache_kv, tabs)
-    parts = arrived_attention(me1, own, asked_all, keys, prompt_kv)
+    parts = arrived_attention(place, own, asked_all, arrived)
     parts = lax.all_to_all(parts, "pool", split_axis=0, concat_axis=0, tiled=True)
-    attention = merged(me1, parts, local, queries.shape, heads, pair)
+    attention = merged(place, parts, local, queries.shape, heads, pair)
     blocks = gathered(attention, npool)
-    core = lax.axis_index("tp").astype(I32)
-    terms, other_terms = projection(me, core, blocks, out_weight)
+    weight = fetched(out_weight, attention)
+    terms, other_terms = projection(place, blocks, weight)
     other_terms = swap_halves(other_terms)
     return (terms + other_terms).astype(BF16)
 

time: 68.6 us -> 68.6 us (level)
  starting transfers between devices: 28.8 us -> 24 us
  waiting for transfers between devices: 18 us -> 22.2 us
    ppermute x6, waiting for transfers between devices: 7.37 us -> 14.2 us  [gathered(): lax.ppermute(x, 'pool', [(i, (i + 2 * by) % npool) for i in range(npool)])]
    ppermute x8, waiting for transfers between devices: 8.11 us -> 5.52 us  [gathered(): lax.ppermute(x, 'pool', [(i, i ^ 1) for i in range(npool)])]
    all_to_all x1, starting transfers between devices: 5.8 us -> 3.38 us  [shards(): lax.all_to_all(parts, 'pool', split_axis=0, concat_axis=0, tiled=True)]
    ppermute x6, starting transfers between devices: 12.3 us -> 10.5 us  [gathered(): lax.ppermute(x, 'pool', [(i, (i + 2 * by) % npool) for i in range(npool)])]
    pallas_call x1, Pallas kernels: 4.18 us -> 2.88 us  [arrived_attention(): pl.pallas_call(functools.partial(arrived_kernel, npool, pair), out_shape=...]
    pallas_call x2 -> x3, Pallas kernels: 7.26 us -> 8.56 us  [the longest x1 3.41 us: projection(): pl.pallas_call(functools.partial(project_kernel, npool), out_shape=[jax.S...]
  transfers between devices with their start and end apart: 16 -> 16, of which waited for: 10 -> 10; matrix products, arithmetic and copies ran while one was open for 0% -> 0% of each run, Pallas kernels for 14% -> 18%
where the time goes in v6:
time: 68.6 us; the launch traced here: 68.3 us
  starting transfers between devices  24 us (35%)
  waiting for transfers between devices  22.2 us (32%)
  Pallas kernels  21.1 us (31%)
  other arithmetic  0.85 us (1%)
    ppermute x6, waiting for transfers between devices, gathered(): lax.ppermute(x, 'pool', [(i, (i + 2 * by) % npool) for i in range(npool)])  14.2 us
    ppermute x6, starting transfers between devices, gathered(): lax.ppermute(x, 'pool', [(i, (i + 2 * by) % npool) for i in range(npool)])  10.5 us
    ppermute x8, starting transfers between devices, gathered(): lax.ppermute(x, 'pool', [(i, i ^ 1) for i in range(npool)])  10 us
    pallas_call x1, Pallas kernels, local_attention(): pl.pallas_call(functools.partial(local_kernel, page_len, heads), out_shap...  6.94 us
    ppermute x8, waiting for transfers between devices, gathered(): lax.ppermute(x, 'pool', [(i, i ^ 1) for i in range(npool)])  5.52 us
    pallas_call x1, Pallas kernels, projection(): pl.pallas_call(functools.partial(project_kernel, npool), out_shape=[jax.S...  3.41 us
    all_to_all x1, starting transfers between devices, shards(): lax.all_to_all(parts, 'pool', split_axis=0, concat_axis=0, tiled=True)  3.38 us
    pallas_call x1, Pallas kernels, rotated_pages(): pl.pallas_call(functools.partial(rope_kernel, npool, cache_pages, per), g...  2.96 us
  transfers between devices with their start and end apart: 16, of which 10 were waited for; matrix products, arithmetic and copies ran while one was open for 0% of the time, Pallas kernels for 18%

profile of v6, /device:TPU:0, one launch (start us, length us, event | category | flops | bytes accessed | tf_op | source)
XLA Modules:
  0.0 68.3 jit_solution(13927113490031244759)
XLA Ops:
  1.2 5.1 %collective-permute-start.2 = (bf16[17,32,128]{2,1,0:T(8,128)(2,1)S(1)}, bf16[17,32,128]{2,1,0:T(8,128)(2,1)S(1)}, u32[]{:S(2)}, u32[]{:S(2)}) collective-permute-start(bf16[17,32,128]{2,1,0:T(8,128)(2,1)S(1)} %asked_queries.1.refs_0_.q_ref), channel_id=1, source_target_pairs={{0,12},{2,14},{4,0},{6,2},{8,4},{10,6},{12,8},{14,10},{1,13},{3,15... | collective-permute-start | bytes 417800 | tf_op jit(solution)/shard_map/ppermute | solution.py:521
  7.3 1.5 %collective-permute-start.3 = (bf16[17,32,128]{2,1,0:T(8,128)(2,1)S(1)}, bf16[17,32,128]{2,1,0:T(8,128)(2,1)S(1)}, u32[]{:S(2)}, u32[]{:S(2)}) collective-permute-start(bf16[17,32,128]{2,1,0:T(8,128)(2,1)S(1)} %asked_queries.1.refs_0_.q_ref), channel_id=1, source_target_pairs={{0,2},{2,0},{4,6},{6,4},{8,10},{10,8},{12,14},{14,12},{1,3},{3,1},... | collective-permute-start | bytes 417800 | tf_op jit(solution)/shard_map/ppermute | solution.py:522
  8.9 1.6 %collective-permute-done.2.refs_3_ = bf16[17,32,128]{2,1,0:T(8,128)(2,1)S(1)} collective-permute-done((bf16[17,32,128]{2,1,0:T(8,128)(2,1)S(1)}, bf16[17,32,128]{2,1,0:T(8,128)(2,1)S(1)}, u32[]{:S(2)}, u32[]{:S(2)}) %collective-permute-start.2) | collective-permute-done | bytes 139296 | tf_op jit(solution)/shard_map/ppermute | solution.py:521
  10.4 1.5 %collective-permute-start.6 = (bf16[17,32,128]{2,1,0:T(8,128)(2,1)S(1)}, bf16[17,32,128]{2,1,0:T(8,128)(2,1)S(1)}, u32[]{:S(2)}, u32[]{:S(2)}) collective-permute-start(bf16[17,32,128]{2,1,0:T(8,128)(2,1)S(1)} %collective-permute-done.2.refs_3_), channel_id=1, source_target_pairs={{0,2},{2,0},{4,6},{6,4},{8,10},{10,8},{12,14},{14,12},{1,3},{3,1},... | collective-permute-start | bytes 417800 | tf_op jit(solution)/shard_map/ppermute | solution.py:522
  11.9 6.2 %collective-permute-done.1.refs_2_ = bf16[17,32,128]{2,1,0:T(8,128)(2,1)S(1)} collective-permute-done((bf16[17,32,128]{2,1,0:T(8,128)(2,1)S(1)}, bf16[17,32,128]{2,1,0:T(8,128)(2,1)S(1)}, u32[]{:S(2)}, u32[]{:S(2)}) %collective-permute-start.1) | collective-permute-done | bytes 139296 | tf_op jit(solution)/shard_map/ppermute | solution.py:521
  18.1 1.5 %collective-permute-start.5 = (bf16[17,32,128]{2,1,0:T(8,128)(2,1)S(1)}, bf16[17,32,128]{2,1,0:T(8,128)(2,1)S(1)}, u32[]{:S(2)}, u32[]{:S(2)}) collective-permute-start(bf16[17,32,128]{2,1,0:T(8,128)(2,1)S(1)} %collective-permute-done.1.refs_2_), channel_id=1, source_target_pairs={{0,2},{2,0},{4,6},{6,4},{8,10},{10,8},{12,14},{14,12},{1,3},{3,1},... | collective-permute-start | bytes 417800 | tf_op jit(solution)/shard_map/ppermute | solution.py:522
  20.2 3.0 %rope_pages.1 = (bf16[16,2,2,128,128]{4,3,2,1,0:T(8,128)(2,1)S(1)}, s32[48]{0:T(128)S(1)}) custom-call(s32[16]{0:T(128)} %slot_ref.1, s32[1,4]{1,0:T(1,128)} %len_ref.1, bf16[16,2,2,128,128]{4,3,2,1,0:T(8,128)(2,1)} %pages_ref.1, f32[128,128]{1,0:T(8,128)} %constant.20.clone.ct_ref, f32[128,128]{1,0:T(8,128)} %constant.21.clone.st_ref, ...), custom_call_target="tpu_custom_call" | custom-call | flops 6000000 | bytes 2000000 | tf_op jit(solution)/shard_map/rope_pages/pallas_call | solution.py:86
  23.2 1.3 %collective-permute-done.5.refs_6_ = bf16[17,32,128]{2,1,0:T(8,128)(2,1)S(1)} collective-permute-done((bf16[17,32,128]{2,1,0:T(8,128)(2,1)S(1)}, bf16[17,32,128]{2,1,0:T(8,128)(2,1)S(1)}, u32[]{:S(2)}, u32[]{:S(2)}) %collective-permute-start.5) | collective-permute-done | bytes 139296 | tf_op jit(solution)/shard_map/ppermute | solution.py:522
  24.6 1.5 %collective-permute-done.4.refs_5_ = bf16[17,32,128]{2,1,0:T(8,128)(2,1)S(1)} collective-permute-done((bf16[17,32,128]{2,1,0:T(8,128)(2,1)S(1)}, bf16[17,32,128]{2,1,0:T(8,128)(2,1)S(1)}, u32[]{:S(2)}, u32[]{:S(2)}) %collective-permute-start.4) | collective-permute-done | bytes 139296 | tf_op jit(solution)/shard_map/ppermute | solution.py:522
  26.1 2.9 %arrived_attention.1 = bf16[8,80,128]{2,1,0:T(8,128)(2,1)} custom-call(s32[2]{0:T(128)S(1)} %pad_add_fusion.me_ref.place_ref, s32[48]{0:T(128)S(1)} %get-tuple-element.11.own_ref, bf16[17,32,128]{2,1,0:T(8,128)(2,1)S(1)} %asked_queries.1.refs_0_.q_ref, bf16[17,32,128]{2,1,0:T(8,128)(2,1)S(1)} %collective-permute-done.refs_1_, ...), custom_call_target="tpu_custom_call" | custom-call | flops 200000000 | bytes 4000000 | tf_op jit(solution)/shard_map/arrived_attention/pallas_call | solution.py:362
  28.9 3.4 %all-to-all-start = ((bf16[8,80,128]{2,1,0:T(8,128)(2,1)}), bf16[8,80,128]{2,1,0:T(8,128)(2,1)S(1)}, u32[]{:S(2)}, u32[]{:S(2)}) async-start(bf16[8,80,128]{2,1,0:T(8,128)(2,1)} %arrived_attention.1), calls=%async_computation | async-start | bytes 327680 | tf_op jit(solution)/shard_map/all_to_all | solution.py:557
  32.4 6.9 %local_attention.1 = (f32[512,128]{1,0:T(8,128)S(1)}, f32[512,128]{1,0:T(8,128)S(1)}) custom-call(s32[3,16]{1,0:T(4,128)} %bitcast.4, s32[16]{0:T(128)} %context_ref.3, s32[48]{0:T(128)} %fill_ref.1, bf16[17,32,128]{2,1,0:T(8,128)(2,1)S(1)} %asked_queries.1.refs_0_.q_ref, bf16[2,16,512]{2,1,0:T(8,128)(2,1)S(1)} %reshape.3.new_ref, ...), custom_call_target="tpu_custom_call" | custom-call | flops 800000000 | bytes 12000000 | tf_op jit(solution)/shard_map/local_attention/pallas_call | solution.py:281
  39.8 1.5 %merge.1.after_ref.refs_0_ = bf16[2,16,2048]{2,1,0:T(8,128)(2,1)S(1)} custom-call(s32[2]{0:T(128)S(1)} %pad_add_fusion.me_ref.place_ref, bf16[8,80,128]{2,1,0:T(8,128)(2,1)S(1)} %all-to-all-done.parts_ref, f32[512,128]{1,0:T(8,128)S(1)} %get-tuple-element.13.o_ref, f32[512,128]{1,0:T(8,128)S(1)} %get-tuple-element.14.stat_ref), custom_call_target="tpu_custom_call" | custom-call | flops 2000000 | bytes 1500000 | tf_op jit(solution)/shard_map/merge/pallas_call | solution.py:422
  41.4 3.3 %collective-permute-start.9 = (bf16[2,16,2048]{2,1,0:T(8,128)(2,1)S(1)}, bf16[2,16,2048]{2,1,0:T(8,128)(2,1)S(1)}, u32[]{:S(2)}, u32[]{:S(2)}) collective-permute-start(bf16[2,16,2048]{2,1,0:T(8,128)(2,1)S(1)} %merge.1.after_ref.refs_0_), channel_id=1, source_target_pairs={{0,12},{2,14},{4,0},{6,2},{8,4},{10,6},{12,8},{14,10},{1,13},{3,15... | collective-permute-start | bytes 393224 | tf_op jit(solution)/shard_map/ppermute | solution.py:521
  45.8 1.5 %collective-permute-start.10 = (bf16[2,16,2048]{2,1,0:T(8,128)(2,1)S(1)}, bf16[2,16,2048]{2,1,0:T(8,128)(2,1)S(1)}, u32[]{:S(2)}, u32[]{:S(2)}) collective-permute-start(bf16[2,16,2048]{2,1,0:T(8,128)(2,1)S(1)} %merge.1.after_ref.refs_0_), channel_id=1, source_target_pairs={{0,2},{2,0},{4,6},{6,4},{8,10},{10,8},{12,14},{14,12},{1,3},{3,1},... | collective-permute-start | bytes 393224 | tf_op jit(solution)/shard_map/ppermute | solution.py:522
  47.2 1.4 %collective-permute-done.9.refs_3_ = bf16[2,16,2048]{2,1,0:T(8,128)(2,1)S(1)} collective-permute-done((bf16[2,16,2048]{2,1,0:T(8,128)(2,1)S(1)}, bf16[2,16,2048]{2,1,0:T(8,128)(2,1)S(1)}, u32[]{:S(2)}, u32[]{:S(2)}) %collective-permute-start.9) | collective-permute-done | bytes 131104 | tf_op jit(solution)/shard_map/ppermute | solution.py:521
  48.6 1.5 %collective-permute-start.13 = (bf16[2,16,2048]{2,1,0:T(8,128)(2,1)S(1)}, bf16[2,16,2048]{2,1,0:T(8,128)(2,1)S(1)}, u32[]{:S(2)}, u32[]{:S(2)}) collective-permute-start(bf16[2,16,2048]{2,1,0:T(8,128)(2,1)S(1)} %collective-permute-done.9.refs_3_), channel_id=1, source_target_pairs={{0,2},{2,0},{4,6},{6,4},{8,10},{10,8},{12,14},{14,12},{1,3},{3,1},... | collective-permute-start | bytes 393224 | tf_op jit(solution)/shard_map/ppermute | solution.py:522
  50.1 5.1 %collective-permute-done.8.refs_2_ = bf16[2,16,2048]{2,1,0:T(8,128)(2,1)S(1)} collective-permute-done((bf16[2,16,2048]{2,1,0:T(8,128)(2,1)S(1)}, bf16[2,16,2048]{2,1,0:T(8,128)(2,1)S(1)}, u32[]{:S(2)}, u32[]{:S(2)}) %collective-permute-start.8) | collective-permute-done | bytes 131104 | tf_op jit(solution)/shard_map/ppermute | solution.py:521
  55.2 1.5 %collective-permute-start.12 = (bf16[2,16,2048]{2,1,0:T(8,128)(2,1)S(1)}, bf16[2,16,2048]{2,1,0:T(8,128)(2,1)S(1)}, u32[]{:S(2)}, u32[]{:S(2)}) collective-permute-start(bf16[2,16,2048]{2,1,0:T(8,128)(2,1)S(1)} %collective-permute-done.8.refs_2_), channel_id=1, source_target_pairs={{0,2},{2,0},{4,6},{6,4},{8,10},{10,8},{12,14},{14,12},{1,3},{3,1},... | collective-permute-start | bytes 393224 | tf_op jit(solution)/shard_map/ppermute | solution.py:522
  57.2 2.2 %fetch_weight.1.refs_8_ = bf16[2048,1024]{1,0:T(8,128)(2,1)S(1)} custom-call(bf16[2048,1024]{1,0:T(8,128)(2,1)} %weight_ref.1, bf16[2,16,2048]{2,1,0:T(8,128)(2,1)S(1)} %merge.1.after_ref.refs_0_), custom_call_target="tpu_custom_call" | custom-call | bytes 8388608 | tf_op jit(solution)/shard_map/fetch_weight/pallas_call | solution.py:442
  59.4 1.3 %collective-permute-done.12.refs_6_ = bf16[2,16,2048]{2,1,0:T(8,128)(2,1)S(1)} collective-permute-done((bf16[2,16,2048]{2,1,0:T(8,128)(2,1)S(1)}, bf16[2,16,2048]{2,1,0:T(8,128)(2,1)S(1)}, u32[]{:S(2)}, u32[]{:S(2)}) %collective-permute-start.12) | collective-permute-done | bytes 131104 | tf_op jit(solution)/shard_map/ppermute | solution.py:522
  60.7 1.4 %collective-permute-done.11.refs_5_ = bf16[2,16,2048]{2,1,0:T(8,128)(2,1)S(1)} collective-permute-done((bf16[2,16,2048]{2,1,0:T(8,128)(2,1)S(1)}, bf16[2,16,2048]{2,1,0:T(8,128)(2,1)S(1)}, u32[]{:S(2)}, u32[]{:S(2)}) %collective-permute-start.11) | collective-permute-done | bytes 131104 | tf_op jit(solution)/shard_map/ppermute | solution.py:522
  62.1 3.4 %project.1 = (f32[2,128,512]{2,1,0:T(8,128)S(1)}, f32[2,128,512]{2,1,0:T(8,128)S(1)}) custom-call(s32[2]{0:T(128)S(1)} %pad_add_fusion.me_ref.place_ref, bf16[2,16,2048]{2,1,0:T(8,128)(2,1)S(1)} %merge.1.after_ref.refs_0_, bf16[2,16,2048]{2,1,0:T(8,128)(2,1)S(1)} %collective-permute-done.7.refs_1_, bf16[2,16,2048]{2,1,0:T(8,128)(2,1)S(1)} %collective-permute-done.8.refs_2_, ...), custom_call_target="tpu_custom_call" | custom-call | flops 1073741824 | bytes 6000000 | tf_op jit(solution)/shard_map/project/pallas_call | solution.py:484
  65.6 1.9 %collective-permute-done.14 = f32[2,128,512]{2,1,0:T(8,128)S(1)} collective-permute-done((f32[2,128,512]{2,1,0:T(8,128)S(1)}, f32[2,128,512]{2,1,0:T(8,128)S(1)}, u32[]{:S(2)}, u32[]{:S(2)}) %collective-permute-start.14) | collective-permute-done | bytes 524320 | tf_op jit(solution)/shard_map/ppermute | solution.py:528
  (20 shorter events, 5.9 us)
Async XLA Ops:
  0.0 32.3 %copy-start = (bf16[2,16,2,2,128]{4,3,2,1,0:T(2,128)(2,1)S(1)}, bf16[2,16,2,2,128]{4,3,2,1,0:T(2,128)(2,1)}, u32[]{:S(2)}) copy-start(bf16[2,16,2,2,128]{4,3,2,1,0:T(2,128)(2,1)} %param.24) | copy-start | bytes 98308
  1.2 9.2 %collective-permute-start.2 = (bf16[17,32,128]{2,1,0:T(8,128)(2,1)S(1)}, bf16[17,32,128]{2,1,0:T(8,128)(2,1)S(1)}, u32[]{:S(2)}, u32[]{:S(2)}) collective-permute-start(bf16[17,32,128]{2,1,0:T(8,128)(2,1)S(1)} %asked_queries.1.refs_0_.q_ref), channel_id=1, source_target_pairs={{0,12},{2,14},{4,0},{6,2},{8,4},{10,6},{12,8},{14,10},{1,13},{3,15... | collective-permute-start | bytes 417800 | tf_op jit(solution)/shard_map/ppermute | solution.py:521
  6.3 11.8 %collective-permute-start.1 = (bf16[17,32,128]{2,1,0:T(8,128)(2,1)S(1)}, bf16[17,32,128]{2,1,0:T(8,128)(2,1)S(1)}, u32[]{:S(2)}, u32[]{:S(2)}) collective-permute-start(bf16[17,32,128]{2,1,0:T(8,128)(2,1)S(1)} %asked_queries.1.refs_0_.q_ref), channel_id=1, source_target_pairs={{0,8},{2,10},{4,12},{6,14},{8,0},{10,2},{12,4},{14,6},{1,9},{3,11}... | collective-permute-start | bytes 417800 | tf_op jit(solution)/shard_map/ppermute | solution.py:521
  6.3 13.3 %collective-permute-start = (bf16[17,32,128]{2,1,0:T(8,128)(2,1)S(1)}, bf16[17,32,128]{2,1,0:T(8,128)(2,1)S(1)}, u32[]{:S(2)}, u32[]{:S(2)}) collective-permute-start(bf16[17,32,128]{2,1,0:T(8,128)(2,1)S(1)} %asked_queries.1.refs_0_.q_ref), channel_id=1, source_target_pairs={{0,4},{2,6},{4,8},{6,10},{8,12},{10,14},{12,0},{14,2},{1,5},{3,7},... | collective-permute-start | bytes 417800 | tf_op jit(solution)/shard_map/ppermute | solution.py:521
  7.3 15.9 %collective-permute-start.3 = (bf16[17,32,128]{2,1,0:T(8,128)(2,1)S(1)}, bf16[17,32,128]{2,1,0:T(8,128)(2,1)S(1)}, u32[]{:S(2)}, u32[]{:S(2)}) collective-permute-start(bf16[17,32,128]{2,1,0:T(8,128)(2,1)S(1)} %asked_queries.1.refs_0_.q_ref), channel_id=1, source_target_pairs={{0,2},{2,0},{4,6},{6,4},{8,10},{10,8},{12,14},{14,12},{1,3},{3,1},... | collective-permute-start | bytes 417800 | tf_op jit(solution)/shard_map/ppermute | solution.py:522
  10.4 12.8 %collective-permute-start.6 = (bf16[17,32,128]{2,1,0:T(8,128)(2,1)S(1)}, bf16[17,32,128]{2,1,0:T(8,128)(2,1)S(1)}, u32[]{:S(2)}, u32[]{:S(2)}) collective-permute-start(bf16[17,32,128]{2,1,0:T(8,128)(2,1)S(1)} %collective-permute-done.2.refs_3_), channel_id=1, source_target_pairs={{0,2},{2,0},{4,6},{6,4},{8,10},{10,8},{12,14},{14,12},{1,3},{3,1},... | collective-permute-start | bytes 417800 | tf_op jit(solution)/shard_map/ppermute | solution.py:522
  18.1 6.4 %collective-permute-start.5 = (bf16[17,32,128]{2,1,0:T(8,128)(2,1)S(1)}, bf16[17,32,128]{2,1,0:T(8,128)(2,1)S(1)}, u32[]{:S(2)}, u32[]{:S(2)}) collective-permute-start(bf16[17,32,128]{2,1,0:T(8,128)(2,1)S(1)} %collective-permute-done.1.refs_2_), channel_id=1, source_target_pairs={{0,2},{2,0},{4,6},{6,4},{8,10},{10,8},{12,14},{14,12},{1,3},{3,1},... | collective-permute-start | bytes 417800 | tf_op jit(solution)/shard_map/ppermute | solution.py:522
  19.7 6.4 %collective-permute-start.4 = (bf16[17,32,128]{2,1,0:T(8,128)(2,1)S(1)}, bf16[17,32,128]{2,1,0:T(8,128)(2,1)S(1)}, u32[]{:S(2)}, u32[]{:S(2)}) collective-permute-start(bf16[17,32,128]{2,1,0:T(8,128)(2,1)S(1)} %collective-permute-done.refs_1_), channel_id=1, source_target_pairs={{0,2},{2,0},{4,6},{6,4},{8,10},{10,8},{12,14},{14,12},{1,3},{3,1},... | collective-permute-start | bytes 417800 | tf_op jit(solution)/shard_map/ppermute | solution.py:522
  28.9 10.9 %all-to-all-start = ((bf16[8,80,128]{2,1,0:T(8,128)(2,1)}), bf16[8,80,128]{2,1,0:T(8,128)(2,1)S(1)}, u32[]{:S(2)}, u32[]{:S(2)}) async-start(bf16[8,80,128]{2,1,0:T(8,128)(2,1)} %arrived_attention.1), calls=%async_computation | async-start | bytes 327680 | tf_op jit(solution)/shard_map/all_to_all | solution.py:557
  41.4 7.2 %collective-permute-start.9 = (bf16[2,16,2048]{2,1,0:T(8,128)(2,1)S(1)}, bf16[2,16,2048]{2,1,0:T(8,128)(2,1)S(1)}, u32[]{:S(2)}, u32[]{:S(2)}) collective-permute-start(bf16[2,16,2048]{2,1,0:T(8,128)(2,1)S(1)} %merge.1.after_ref.refs_0_), channel_id=1, source_target_pairs={{0,12},{2,14},{4,0},{6,2},{8,4},{10,6},{12,8},{14,10},{1,13},{3,15... | collective-permute-start | bytes 393224 | tf_op jit(solution)/shard_map/ppermute | solution.py:521
  44.7 10.5 %collective-permute-start.8 = (bf16[2,16,2048]{2,1,0:T(8,128)(2,1)S(1)}, bf16[2,16,2048]{2,1,0:T(8,128)(2,1)S(1)}, u32[]{:S(2)}, u32[]{:S(2)}) collective-permute-start(bf16[2,16,2048]{2,1,0:T(8,128)(2,1)S(1)} %merge.1.after_ref.refs_0_), channel_id=1, source_target_pairs={{0,8},{2,10},{4,12},{6,14},{8,0},{10,2},{12,4},{14,6},{1,9},{3,11}... | collective-permute-start | bytes 393224 | tf_op jit(solution)/shard_map/ppermute | solution.py:521
  44.7 12.0 %collective-permute-start.7 = (bf16[2,16,2048]{2,1,0:T(8,128)(2,1)S(1)}, bf16[2,16,2048]{2,1,0:T(8,128)(2,1)S(1)}, u32[]{:S(2)}, u32[]{:S(2)}) collective-permute-start(bf16[2,16,2048]{2,1,0:T(8,128)(2,1)S(1)} %merge.1.after_ref.refs_0_), channel_id=1, source_target_pairs={{0,4},{2,6},{4,8},{6,10},{8,12},{10,14},{12,0},{14,2},{1,5},{3,7},... | collective-permute-start | bytes 393224 | tf_op jit(solution)/shard_map/ppermute | solution.py:521
  45.8 13.6 %collective-permute-start.10 = (bf16[2,16,2048]{2,1,0:T(8,128)(2,1)S(1)}, bf16[2,16,2048]{2,1,0:T(8,128)(2,1)S(1)}, u32[]{:S(2)}, u32[]{:S(2)}) collective-permute-start(bf16[2,16,2048]{2,1,0:T(8,128)(2,1)S(1)} %merge.1.after_ref.refs_0_), channel_id=1, source_target_pairs={{0,2},{2,0},{4,6},{6,4},{8,10},{10,8},{12,14},{14,12},{1,3},{3,1},... | collective-permute-start | bytes 393224 | tf_op jit(solution)/shard_map/ppermute | solution.py:522
  48.6 10.8 %collective-permute-start.13 = (bf16[2,16,2048]{2,1,0:T(8,128)(2,1)S(1)}, bf16[2,16,2048]{2,1,0:T(8,128)(2,1)S(1)}, u32[]{:S(2)}, u32[]{:S(2)}) collective-permute-start(bf16[2,16,2048]{2,1,0:T(8,128)(2,1)S(1)} %collective-permute-done.9.refs_3_), channel_id=1, source_target_pairs={{0,2},{2,0},{4,6},{6,4},{8,10},{10,8},{12,14},{14,12},{1,3},{3,1},... | collective-permute-start | bytes 393224 | tf_op jit(solution)/shard_map/ppermute | solution.py:522
  55.2 5.5 %collective-permute-start.12 = (bf16[2,16,2048]{2,1,0:T(8,128)(2,1)S(1)}, bf16[2,16,2048]{2,1,0:T(8,128)(2,1)S(1)}, u32[]{:S(2)}, u32[]{:S(2)}) collective-permute-start(bf16[2,16,2048]{2,1,0:T(8,128)(2,1)S(1)} %collective-permute-done.8.refs_2_), channel_id=1, source_target_pairs={{0,2},{2,0},{4,6},{6,4},{8,10},{10,8},{12,14},{14,12},{1,3},{3,1},... | collective-permute-start | bytes 393224 | tf_op jit(solution)/shard_map/ppermute | solution.py:522
  56.6 5.5 %collective-permute-start.11 = (bf16[2,16,2048]{2,1,0:T(8,128)(2,1)S(1)}, bf16[2,16,2048]{2,1,0:T(8,128)(2,1)S(1)}, u32[]{:S(2)}, u32[]{:S(2)}) collective-permute-start(bf16[2,16,2048]{2,1,0:T(8,128)(2,1)S(1)} %collective-permute-done.7.refs_1_), channel_id=1, source_target_pairs={{0,2},{2,0},{4,6},{6,4},{8,10},{10,8},{12,14},{14,12},{1,3},{3,1},... | collective-permute-start | bytes 393224 | tf_op jit(solution)/shard_map/ppermute | solution.py:522
  65.5 2.0 %collective-permute-start.14 = (f32[2,128,512]{2,1,0:T(8,128)S(1)}, f32[2,128,512]{2,1,0:T(8,128)S(1)}, u32[]{:S(2)}, u32[]{:S(2)}) collective-permute-start(f32[2,128,512]{2,1,0:T(8,128)S(1)} %get-tuple-element.16), channel_id=1, source_target_pairs={{0,1},{1,0},{2,3},{3,2},{4,5},{5,4},{6,7},{7,6},{8,9},{9,8},{10,11... | collective-permute-start | bytes 1572872 | tf_op jit(solution)/shard_map/ppermute | solution.py:528

commit v7 on v6

--- a/solution.py
+++ b/solution.py
@@ -431,43 +431,42 @@
     )(me, parts, *local)
 
 
-def fetch_kernel(weight_ref, after_ref, out_ref, sem):
-    del after_ref
-    copy = pltpu.make_async_copy(weight_ref, out_ref, sem)
-    copy.start()
-    copy.wait()
-
-
-def fetched(weight, after):
+def fetch_kernel(weight_ref, x_ref, weight_out, x_out, sems):
+    copies = [
+        pltpu.make_async_copy(weight_ref, weight_out, sems.at[0]),
+        pltpu.make_async_copy(x_ref, x_out, sems.at[1]),
+    ]
+    for copy in copies:
+        copy.start()
+    for copy in copies:
+        copy.wait()
+
+
+def fetched(weight, x):
     return pl.pallas_call(
         fetch_kernel,
-        out_shape=pltpu.VMEM(weight.shape, weight.dtype),
+        out_shape=[pltpu.VMEM(weight.shape, weight.dtype), pltpu.VMEM(x.shape, x.dtype)],
         in_specs=[ANY, ANY],
-        out_specs=ANY,
-        scratch_shapes=[pltpu.SemaphoreType.DMA],
+        out_specs=[ANY, ANY],
+        scratch_shapes=[pltpu.SemaphoreType.DMA((2,))],
         compiler_params=PARAMS,
         cost_estimate=pl.CostEstimate(flops=0, bytes_accessed=2 * weight.size * 2, transcendentals=0),
         name="fetch_weight",
-    )(in_hbm(weight), after)
+    )(in_hbm(weight), x)
 
 
 def project_kernel(npool, place_ref, *refs):
     blocks = refs[:npool]
-    weight_ref, mine_ref, other_ref, lhs, sems = refs[npool:]
+    weight_ref, mine_ref, other_ref, lhs = refs[npool:]
     steps, rows, _ = blocks[0].shape
     half = weight_ref.shape[1] // 2
     tile = min(half, 256)
     every = npool * rows
     me, core = place_ref[0], place_ref[1]
-    copies = []
     for x, (apart, flip) in enumerate(block_order(npool)):
         owner = owner_of(me, npool, apart, flip)
         for s in range(steps):
-            at = pl.ds(pl.multiple_of(s * every + owner * rows, rows), rows)
-            copies.append(pltpu.make_async_copy(blocks[x].at[s], lhs.at[at], sems.at[x * steps + s]))
-            copies[-1].start()
-    for x in copies:
-        x.wait()
+            lhs[pl.ds(pl.multiple_of(s * every + owner * rows, rows), rows), :] = blocks[x][s]
     for out_ref, first in ((mine_ref, core * half), (other_ref, (1 - core) * half)):
         for i in range(half // tile):
             at = pl.ds(pl.multiple_of(first + i * tile, LANES), tile)
@@ -484,9 +483,9 @@
     return pl.pallas_call(
         functools.partial(project_kernel, npool),
         out_shape=[jax.ShapeDtypeStruct((steps, npool * rows, columns // 2), F32)] * 2,
-        in_specs=[SMEM] + [ANY] * npool + [VMEM],
+        in_specs=[SMEM] + [VMEM] * (npool + 1),
         out_specs=[VMEM] * 2,
-        scratch_shapes=[pltpu.VMEM((every, width), BF16), pltpu.SemaphoreType.DMA((npool * steps,))],
+        scratch_shapes=[pltpu.VMEM((every, width), BF16)],
         compiler_params=PARAMS,
         cost_estimate=pl.CostEstimate(
             flops=2 * every * width * columns, bytes_accessed=6_000_000, transcendentals=0
@@ -517,10 +516,12 @@
     return pltpu.with_memory_space_constraint(x, pltpu.HBM)
 
 
-def gathered(x, npool):
+def gathered(x, npool, later=None):
+    half = npool // 2
+    later = x if later is None else later
     ahead = lambda x, by: lax.ppermute(x, "pool", [(i, (i + 2 * by) % npool) for i in range(npool)])
     across = lambda x: lax.ppermute(x, "pool", [(i, i ^ 1) for i in range(npool)])
-    straight = [x] + [ahead(x, by) for by in range(1, npool // 2)]
+    straight = [x] + [ahead(x if by == half // 2 else later, by) for by in range(1, half)]
     return straight + [across(y) for y in straight]
 
 
@@ -556,8 +557,8 @@
     parts = arrived_attention(place, own, asked_all, arrived)
     parts = lax.all_to_all(parts, "pool", split_axis=0, concat_axis=0, tiled=True)
     attention = merged(place, parts, local, queries.shape, heads, pair)
-    blocks = gathered(attention, npool)
-    weight = fetched(out_weight, attention)
+    weight, again = fetched(out_weight, attention)
+    blocks = gathered(attention, npool, again)
     terms, other_terms = projection(place, blocks, weight)
     other_terms = swap_halves(other_terms)
     return (terms + other_terms).astype(BF16)

time: 68.6 us -> 64.5 us (0.940)
  waiting for transfers between devices: 22.2 us -> 19.6 us
  Pallas kernels: 21.1 us -> 19.6 us
    ppermute x6, waiting for transfers between devices: 14.2 us -> 10.6 us  [gathered(): lax.ppermute(x, 'pool', [(i, (i + 2 * by) % npool) for i in range(npool)])]
    pallas_call x1, Pallas kernels: 3.41 us -> 1.89 us  [projection(): pl.pallas_call(functools.partial(project_kernel, npool), out_shape=[jax.S...]
    ppermute x8, waiting for transfers between devices: 5.52 us -> 6.66 us  [gathered(): lax.ppermute(x, 'pool', [(i, i ^ 1) for i in range(npool)])]
  transfers between devices with their start and end apart: 16 -> 16, of which waited for: 10 -> 11; matrix products, arithmetic and copies ran while one was open for 0% -> 0% of each run, Pallas kernels for 18% -> 19%
where the time goes in v7:
time: 64.5 us; the launch traced here: 64.2 us
  starting transfers between devices  24 us (37%)
  Pallas kernels  19.6 us (30%)
  waiting for transfers between devices  19.6 us (30%)
  other arithmetic  0.85 us (1%)
    ppermute x6, starting transfers between devices, gathered(): lax.ppermute(x, 'pool', [(i, (i + 2 * by) % npool) for i in range(npool)])  10.6 us
    ppermute x6, waiting for transfers between devices, gathered(): lax.ppermute(x, 'pool', [(i, (i + 2 * by) % npool) for i in range(npool)])  10.6 us
    ppermute x8, starting transfers between devices, gathered(): lax.ppermute(x, 'pool', [(i, i ^ 1) for i in range(npool)])  9.96 us
    pallas_call x1, Pallas kernels, local_attention(): pl.pallas_call(functools.partial(local_kernel, page_len, heads), out_shap...  6.94 us
    ppermute x8, waiting for transfers between devices, gathered(): lax.ppermute(x, 'pool', [(i, i ^ 1) for i in range(npool)])  6.66 us
    all_to_all x1, starting transfers between devices, shards(): lax.all_to_all(parts, 'pool', split_axis=0, concat_axis=0, tiled=True)  3.38 us
    pallas_call x1, Pallas kernels, rotated_pages(): pl.pallas_call(functools.partial(rope_kernel, npool, cache_pages, per), g...  2.96 us
    pallas_call x1, Pallas kernels, arrived_attention(): pl.pallas_call(functools.partial(arrived_kernel, npool, pair), out_shape=...  2.88 us
  transfers between devices with their start and end apart: 16, of which 11 were waited for; matrix products, arithmetic and copies ran while one was open for 0% of the time, Pallas kernels for 19%

profile of v7, /device:TPU:0, one launch (start us, length us, event | category | flops | bytes accessed | tf_op | source)
XLA Modules:
  0.0 64.2 jit_solution(3727621329301084912)
XLA Ops:
  1.2 5.1 %collective-permute-start.2 = (bf16[17,32,128]{2,1,0:T(8,128)(2,1)S(1)}, bf16[17,32,128]{2,1,0:T(8,128)(2,1)S(1)}, u32[]{:S(2)}, u32[]{:S(2)}) collective-permute-start(bf16[17,32,128]{2,1,0:T(8,128)(2,1)S(1)} %asked_queries.1.refs_0_.q_ref), channel_id=1, source_target_pairs={{0,12},{2,14},{4,0},{6,2},{8,4},{10,6},{12,8},{14,10},{1,13},{3,15... | collective-permute-start | bytes 417800 | tf_op jit(solution)/shard_map/ppermute | solution.py:522
  7.3 1.5 %collective-permute-start.3 = (bf16[17,32,128]{2,1,0:T(8,128)(2,1)S(1)}, bf16[17,32,128]{2,1,0:T(8,128)(2,1)S(1)}, u32[]{:S(2)}, u32[]{:S(2)}) collective-permute-start(bf16[17,32,128]{2,1,0:T(8,128)(2,1)S(1)} %asked_queries.1.refs_0_.q_ref), channel_id=1, source_target_pairs={{0,2},{2,0},{4,6},{6,4},{8,10},{10,8},{12,14},{14,12},{1,3},{3,1},... | collective-permute-start | bytes 417800 | tf_op jit(solution)/shard_map/ppermute | solution.py:523
  8.9 1.6 %collective-permute-done.2.refs_3_ = bf16[17,32,128]{2,1,0:T(8,128)(2,1)S(1)} collective-permute-done((bf16[17,32,128]{2,1,0:T(8,128)(2,1)S(1)}, bf16[17,32,128]{2,1,0:T(8,128)(2,1)S(1)}, u32[]{:S(2)}, u32[]{:S(2)}) %collective-permute-start.2) | collective-permute-done | bytes 139296 | tf_op jit(solution)/shard_map/ppermute | solution.py:522
  10.4 1.5 %collective-permute-start.6 = (bf16[17,32,128]{2,1,0:T(8,128)(2,1)S(1)}, bf16[17,32,128]{2,1,0:T(8,128)(2,1)S(1)}, u32[]{:S(2)}, u32[]{:S(2)}) collective-permute-start(bf16[17,32,128]{2,1,0:T(8,128)(2,1)S(1)} %collective-permute-done.2.refs_3_), channel_id=1, source_target_pairs={{0,2},{2,0},{4,6},{6,4},{8,10},{10,8},{12,14},{14,12},{1,3},{3,1},... | collective-permute-start | bytes 417800 | tf_op jit(solution)/shard_map/ppermute | solution.py:523
  11.9 6.2 %collective-permute-done.1.refs_2_ = bf16[17,32,128]{2,1,0:T(8,128)(2,1)S(1)} collective-permute-done((bf16[17,32,128]{2,1,0:T(8,128)(2,1)S(1)}, bf16[17,32,128]{2,1,0:T(8,128)(2,1)S(1)}, u32[]{:S(2)}, u32[]{:S(2)}) %collective-permute-start.1) | collective-permute-done | bytes 139296 | tf_op jit(solution)/shard_map/ppermute | solution.py:522
  18.1 1.5 %collective-permute-start.5 = (bf16[17,32,128]{2,1,0:T(8,128)(2,1)S(1)}, bf16[17,32,128]{2,1,0:T(8,128)(2,1)S(1)}, u32[]{:S(2)}, u32[]{:S(2)}) collective-permute-start(bf16[17,32,128]{2,1,0:T(8,128)(2,1)S(1)} %collective-permute-done.1.refs_2_), channel_id=1, source_target_pairs={{0,2},{2,0},{4,6},{6,4},{8,10},{10,8},{12,14},{14,12},{1,3},{3,1},... | collective-permute-start | bytes 417800 | tf_op jit(solution)/shard_map/ppermute | solution.py:523
  20.2 3.0 %rope_pages.1 = (bf16[16,2,2,128,128]{4,3,2,1,0:T(8,128)(2,1)S(1)}, s32[48]{0:T(128)S(1)}) custom-call(s32[16]{0:T(128)} %slot_ref.1, s32[1,4]{1,0:T(1,128)} %len_ref.1, bf16[16,2,2,128,128]{4,3,2,1,0:T(8,128)(2,1)} %pages_ref.1, f32[128,128]{1,0:T(8,128)} %constant.20.clone.ct_ref, f32[128,128]{1,0:T(8,128)} %constant.21.clone.st_ref, ...), custom_call_target="tpu_custom_call" | custom-call | flops 6000000 | bytes 2000000 | tf_op jit(solution)/shard_map/rope_pages/pallas_call | solution.py:86
  23.2 1.3 %collective-permute-done.5.refs_6_ = bf16[17,32,128]{2,1,0:T(8,128)(2,1)S(1)} collective-permute-done((bf16[17,32,128]{2,1,0:T(8,128)(2,1)S(1)}, bf16[17,32,128]{2,1,0:T(8,128)(2,1)S(1)}, u32[]{:S(2)}, u32[]{:S(2)}) %collective-permute-start.5) | collective-permute-done | bytes 139296 | tf_op jit(solution)/shard_map/ppermute | solution.py:523
  24.6 1.5 %collective-permute-done.4.refs_5_ = bf16[17,32,128]{2,1,0:T(8,128)(2,1)S(1)} collective-permute-done((bf16[17,32,128]{2,1,0:T(8,128)(2,1)S(1)}, bf16[17,32,128]{2,1,0:T(8,128)(2,1)S(1)}, u32[]{:S(2)}, u32[]{:S(2)}) %collective-permute-start.4) | collective-permute-done | bytes 139296 | tf_op jit(solution)/shard_map/ppermute | solution.py:523
  26.1 2.9 %arrived_attention.1 = bf16[8,80,128]{2,1,0:T(8,128)(2,1)} custom-call(s32[2]{0:T(128)S(1)} %pad_add_fusion.me_ref.place_ref, s32[48]{0:T(128)S(1)} %get-tuple-element.13.own_ref, bf16[17,32,128]{2,1,0:T(8,128)(2,1)S(1)} %asked_queries.1.refs_0_.q_ref, bf16[17,32,128]{2,1,0:T(8,128)(2,1)S(1)} %collective-permute-done.refs_1_, ...), custom_call_target="tpu_custom_call" | custom-call | flops 200000000 | bytes 4000000 | tf_op jit(solution)/shard_map/arrived_attention/pallas_call | solution.py:362
  28.9 3.4 %all-to-all-start = ((bf16[8,80,128]{2,1,0:T(8,128)(2,1)}), bf16[8,80,128]{2,1,0:T(8,128)(2,1)S(1)}, u32[]{:S(2)}, u32[]{:S(2)}) async-start(bf16[8,80,128]{2,1,0:T(8,128)(2,1)} %arrived_attention.1), calls=%async_computation | async-start | bytes 327680 | tf_op jit(solution)/shard_map/all_to_all | solution.py:558
  32.4 6.9 %local_attention.1 = (f32[512,128]{1,0:T(8,128)S(1)}, f32[512,128]{1,0:T(8,128)S(1)}) custom-call(s32[3,16]{1,0:T(4,128)} %bitcast.4, s32[16]{0:T(128)} %context_ref.3, s32[48]{0:T(128)} %fill_ref.1, bf16[17,32,128]{2,1,0:T(8,128)(2,1)S(1)} %asked_queries.1.refs_0_.q_ref, bf16[2,16,512]{2,1,0:T(8,128)(2,1)S(1)} %reshape.3.new_ref, ...), custom_call_target="tpu_custom_call" | custom-call | flops 800000000 | bytes 12000000 | tf_op jit(solution)/shard_map/local_attention/pallas_call | solution.py:281
  39.8 1.5 %merge.1.x_ref.refs_0_ = bf16[2,16,2048]{2,1,0:T(8,128)(2,1)S(1)} custom-call(s32[2]{0:T(128)S(1)} %pad_add_fusion.me_ref.place_ref, bf16[8,80,128]{2,1,0:T(8,128)(2,1)S(1)} %all-to-all-done.parts_ref, f32[512,128]{1,0:T(8,128)S(1)} %get-tuple-element.15.o_ref, f32[512,128]{1,0:T(8,128)S(1)} %get-tuple-element.16.stat_ref), custom_call_target="tpu_custom_call" | custom-call | flops 2000000 | bytes 1500000 | tf_op jit(solution)/shard_map/merge/pallas_call | solution.py:422
  41.4 2.4 %collective-permute-start.8 = (bf16[2,16,2048]{2,1,0:T(8,128)(2,1)S(1)}, bf16[2,16,2048]{2,1,0:T(8,128)(2,1)S(1)}, u32[]{:S(2)}, u32[]{:S(2)}) collective-permute-start(bf16[2,16,2048]{2,1,0:T(8,128)(2,1)S(1)} %merge.1.x_ref.refs_0_), channel_id=1, source_target_pairs={{0,8},{2,10},{4,12},{6,14},{8,0},{10,2},{12,4},{14,6},{1,9},{3,11}... | collective-permute-start | bytes 393224 | tf_op jit(solution)/shard_map/ppermute | solution.py:522
  43.8 2.2 %fetch_weight.1 = (bf16[2048,1024]{1,0:T(8,128)(2,1)S(1)}, bf16[2,16,2048]{2,1,0:T(8,128)(2,1)S(1)}) custom-call(bf16[2048,1024]{1,0:T(8,128)(2,1)} %weight_ref.1, bf16[2,16,2048]{2,1,0:T(8,128)(2,1)S(1)} %merge.1.x_ref.refs_0_), custom_call_target="tpu_custom_call" | custom-call | bytes 8388608 | tf_op jit(solution)/shard_map/fetch_weight/pallas_call | solution.py:446
  46.0 1.5 %collective-permute-start.9 = (bf16[2,16,2048]{2,1,0:T(8,128)(2,1)S(1)}, bf16[2,16,2048]{2,1,0:T(8,128)(2,1)S(1)}, u32[]{:S(2)}, u32[]{:S(2)}) collective-permute-start(bf16[2,16,2048]{2,1,0:T(8,128)(2,1)S(1)} %get-tuple-element.17), channel_id=1, source_target_pairs={{0,12},{2,14},{4,0},{6,2},{8,4},{10,6},{12,8},{14,10},{1,13},{3,15... | collective-permute-start | bytes 393224 | tf_op jit(solution)/shard_map/ppermute | solution.py:522
  48.0 1.5 %collective-permute-start.10 = (bf16[2,16,2048]{2,1,0:T(8,128)(2,1)S(1)}, bf16[2,16,2048]{2,1,0:T(8,128)(2,1)S(1)}, u32[]{:S(2)}, u32[]{:S(2)}) collective-permute-start(bf16[2,16,2048]{2,1,0:T(8,128)(2,1)S(1)} %merge.1.x_ref.refs_0_), channel_id=1, source_target_pairs={{0,2},{2,0},{4,6},{6,4},{8,10},{10,8},{12,14},{14,12},{1,3},{3,1},... | collective-permute-start | bytes 393224 | tf_op jit(solution)/shard_map/ppermute | solution.py:523
  50.1 2.2 %collective-permute-done.9.refs_3_ = bf16[2,16,2048]{2,1,0:T(8,128)(2,1)S(1)} collective-permute-done((bf16[2,16,2048]{2,1,0:T(8,128)(2,1)S(1)}, bf16[2,16,2048]{2,1,0:T(8,128)(2,1)S(1)}, u32[]{:S(2)}, u32[]{:S(2)}) %collective-permute-start.9) | collective-permute-done | bytes 131104 | tf_op jit(solution)/shard_map/ppermute | solution.py:522
  52.3 1.5 %collective-permute-start.13 = (bf16[2,16,2048]{2,1,0:T(8,128)(2,1)S(1)}, bf16[2,16,2048]{2,1,0:T(8,128)(2,1)S(1)}, u32[]{:S(2)}, u32[]{:S(2)}) collective-permute-start(bf16[2,16,2048]{2,1,0:T(8,128)(2,1)S(1)} %collective-permute-done.9.refs_3_), channel_id=1, source_target_pairs={{0,2},{2,0},{4,6},{6,4},{8,10},{10,8},{12,14},{14,12},{1,3},{3,1},... | collective-permute-start | bytes 393224 | tf_op jit(solution)/shard_map/ppermute | solution.py:523
  54.3 1.4 %collective-permute-start.11 = (bf16[2,16,2048]{2,1,0:T(8,128)(2,1)S(1)}, bf16[2,16,2048]{2,1,0:T(8,128)(2,1)S(1)}, u32[]{:S(2)}, u32[]{:S(2)}) collective-permute-start(bf16[2,16,2048]{2,1,0:T(8,128)(2,1)S(1)} %collective-permute-done.7.refs_1_), channel_id=1, source_target_pairs={{0,2},{2,0},{4,6},{6,4},{8,10},{10,8},{12,14},{14,12},{1,3},{3,1},... | collective-permute-start | bytes 393224 | tf_op jit(solution)/shard_map/ppermute | solution.py:523
  56.1 2.0 %collective-permute-done.13.refs_7_ = bf16[2,16,2048]{2,1,0:T(8,128)(2,1)S(1)} collective-permute-done((bf16[2,16,2048]{2,1,0:T(8,128)(2,1)S(1)}, bf16[2,16,2048]{2,1,0:T(8,128)(2,1)S(1)}, u32[]{:S(2)}, u32[]{:S(2)}) %collective-permute-start.13) | collective-permute-done | bytes 131104 | tf_op jit(solution)/shard_map/ppermute | solution.py:523
  58.1 1.4 %collective-permute-done.11.refs_5_ = bf16[2,16,2048]{2,1,0:T(8,128)(2,1)S(1)} collective-permute-done((bf16[2,16,2048]{2,1,0:T(8,128)(2,1)S(1)}, bf16[2,16,2048]{2,1,0:T(8,128)(2,1)S(1)}, u32[]{:S(2)}, u32[]{:S(2)}) %collective-permute-start.11) | collective-permute-done | bytes 131104 | tf_op jit(solution)/shard_map/ppermute | solution.py:523
  59.5 1.9 %project.1 = (f32[2,128,512]{2,1,0:T(8,128)S(1)}, f32[2,128,512]{2,1,0:T(8,128)S(1)}) custom-call(s32[2]{0:T(128)S(1)} %pad_add_fusion.me_ref.place_ref, bf16[2,16,2048]{2,1,0:T(8,128)(2,1)S(1)} %merge.1.x_ref.refs_0_, bf16[2,16,2048]{2,1,0:T(8,128)(2,1)S(1)} %collective-permute-done.7.refs_1_, bf16[2,16,2048]{2,1,0:T(8,128)(2,1)S(1)} %collective-permute-done.8.refs_2_, ...), custom_call_target="tpu_custom_call" | custom-call | flops 1073741824 | bytes 6000000 | tf_op jit(solution)/shard_map/project/pallas_call | solution.py:483
  61.5 1.9 %collective-permute-done.14 = f32[2,128,512]{2,1,0:T(8,128)S(1)} collective-permute-done((f32[2,128,512]{2,1,0:T(8,128)S(1)}, f32[2,128,512]{2,1,0:T(8,128)S(1)}, u32[]{:S(2)}, u32[]{:S(2)}) %collective-permute-start.14) | collective-permute-done | bytes 524320 | tf_op jit(solution)/shard_map/ppermute | solution.py:529
  (20 shorter events, 6.3 us)
Async XLA Ops:
  0.0 32.3 %copy-start = (bf16[2,16,2,2,128]{4,3,2,1,0:T(2,128)(2,1)S(1)}, bf16[2,16,2,2,128]{4,3,2,1,0:T(2,128)(2,1)}, u32[]{:S(2)}) copy-start(bf16[2,16,2,2,128]{4,3,2,1,0:T(2,128)(2,1)} %param.24) | copy-start | bytes 98308
  1.2 9.2 %collective-permute-start.2 = (bf16[17,32,128]{2,1,0:T(8,128)(2,1)S(1)}, bf16[17,32,128]{2,1,0:T(8,128)(2,1)S(1)}, u32[]{:S(2)}, u32[]{:S(2)}) collective-permute-start(bf16[17,32,128]{2,1,0:T(8,128)(2,1)S(1)} %asked_queries.1.refs_0_.q_ref), channel_id=1, source_target_pairs={{0,12},{2,14},{4,0},{6,2},{8,4},{10,6},{12,8},{14,10},{1,13},{3,15... | collective-permute-start | bytes 417800 | tf_op jit(solution)/shard_map/ppermute | solution.py:522
  6.3 11.8 %collective-permute-start.1 = (bf16[17,32,128]{2,1,0:T(8,128)(2,1)S(1)}, bf16[17,32,128]{2,1,0:T(8,128)(2,1)S(1)}, u32[]{:S(2)}, u32[]{:S(2)}) collective-permute-start(bf16[17,32,128]{2,1,0:T(8,128)(2,1)S(1)} %asked_queries.1.refs_0_.q_ref), channel_id=1, source_target_pairs={{0,8},{2,10},{4,12},{6,14},{8,0},{10,2},{12,4},{14,6},{1,9},{3,11}... | collective-permute-start | bytes 417800 | tf_op jit(solution)/shard_map/ppermute | solution.py:522
  6.3 13.3 %collective-permute-start = (bf16[17,32,128]{2,1,0:T(8,128)(2,1)S(1)}, bf16[17,32,128]{2,1,0:T(8,128)(2,1)S(1)}, u32[]{:S(2)}, u32[]{:S(2)}) collective-permute-start(bf16[17,32,128]{2,1,0:T(8,128)(2,1)S(1)} %asked_queries.1.refs_0_.q_ref), channel_id=1, source_target_pairs={{0,4},{2,6},{4,8},{6,10},{8,12},{10,14},{12,0},{14,2},{1,5},{3,7},... | collective-permute-start | bytes 417800 | tf_op jit(solution)/shard_map/ppermute | solution.py:522
  7.3 15.9 %collective-permute-start.3 = (bf16[17,32,128]{2,1,0:T(8,128)(2,1)S(1)}, bf16[17,32,128]{2,1,0:T(8,128)(2,1)S(1)}, u32[]{:S(2)}, u32[]{:S(2)}) collective-permute-start(bf16[17,32,128]{2,1,0:T(8,128)(2,1)S(1)} %asked_queries.1.refs_0_.q_ref), channel_id=1, source_target_pairs={{0,2},{2,0},{4,6},{6,4},{8,10},{10,8},{12,14},{14,12},{1,3},{3,1},... | collective-permute-start | bytes 417800 | tf_op jit(solution)/shard_map/ppermute | solution.py:523
  10.4 12.8 %collective-permute-start.6 = (bf16[17,32,128]{2,1,0:T(8,128)(2,1)S(1)}, bf16[17,32,128]{2,1,0:T(8,128)(2,1)S(1)}, u32[]{:S(2)}, u32[]{:S(2)}) collective-permute-start(bf16[17,32,128]{2,1,0:T(8,128)(2,1)S(1)} %collective-permute-done.2.refs_3_), channel_id=1, source_target_pairs={{0,2},{2,0},{4,6},{6,4},{8,10},{10,8},{12,14},{14,12},{1,3},{3,1},... | collective-permute-start | bytes 417800 | tf_op jit(solution)/shard_map/ppermute | solution.py:523
  18.1 6.4 %collective-permute-start.5 = (bf16[17,32,128]{2,1,0:T(8,128)(2,1)S(1)}, bf16[17,32,128]{2,1,0:T(8,128)(2,1)S(1)}, u32[]{:S(2)}, u32[]{:S(2)}) collective-permute-start(bf16[17,32,128]{2,1,0:T(8,128)(2,1)S(1)} %collective-permute-done.1.refs_2_), channel_id=1, source_target_pairs={{0,2},{2,0},{4,6},{6,4},{8,10},{10,8},{12,14},{14,12},{1,3},{3,1},... | collective-permute-start | bytes 417800 | tf_op jit(solution)/shard_map/ppermute | solution.py:523
  19.7 6.4 %collective-permute-start.4 = (bf16[17,32,128]{2,1,0:T(8,128)(2,1)S(1)}, bf16[17,32,128]{2,1,0:T(8,128)(2,1)S(1)}, u32[]{:S(2)}, u32[]{:S(2)}) collective-permute-start(bf16[17,32,128]{2,1,0:T(8,128)(2,1)S(1)} %collective-permute-done.refs_1_), channel_id=1, source_target_pairs={{0,2},{2,0},{4,6},{6,4},{8,10},{10,8},{12,14},{14,12},{1,3},{3,1},... | collective-permute-start | bytes 417800 | tf_op jit(solution)/shard_map/ppermute | solution.py:523
  28.9 10.9 %all-to-all-start = ((bf16[8,80,128]{2,1,0:T(8,128)(2,1)}), bf16[8,80,128]{2,1,0:T(8,128)(2,1)S(1)}, u32[]{:S(2)}, u32[]{:S(2)}) async-start(bf16[8,80,128]{2,1,0:T(8,128)(2,1)} %arrived_attention.1), calls=%async_computation | async-start | bytes 327680 | tf_op jit(solution)/shard_map/all_to_all | solution.py:558
  41.4 8.1 %collective-permute-start.8 = (bf16[2,16,2048]{2,1,0:T(8,128)(2,1)S(1)}, bf16[2,16,2048]{2,1,0:T(8,128)(2,1)S(1)}, u32[]{:S(2)}, u32[]{:S(2)}) collective-permute-start(bf16[2,16,2048]{2,1,0:T(8,128)(2,1)S(1)} %merge.1.x_ref.refs_0_), channel_id=1, source_target_pairs={{0,8},{2,10},{4,12},{6,14},{8,0},{10,2},{12,4},{14,6},{1,9},{3,11}... | collective-permute-start | bytes 393224 | tf_op jit(solution)/shard_map/ppermute | solution.py:522
  46.0 6.3 %collective-permute-start.9 = (bf16[2,16,2048]{2,1,0:T(8,128)(2,1)S(1)}, bf16[2,16,2048]{2,1,0:T(8,128)(2,1)S(1)}, u32[]{:S(2)}, u32[]{:S(2)}) collective-permute-start(bf16[2,16,2048]{2,1,0:T(8,128)(2,1)S(1)} %get-tuple-element.17), channel_id=1, source_target_pairs={{0,12},{2,14},{4,0},{6,2},{8,4},{10,6},{12,8},{14,10},{1,13},{3,15... | collective-permute-start | bytes 393224 | tf_op jit(solution)/shard_map/ppermute | solution.py:522
  47.5 6.9 %collective-permute-start.7 = (bf16[2,16,2048]{2,1,0:T(8,128)(2,1)S(1)}, bf16[2,16,2048]{2,1,0:T(8,128)(2,1)S(1)}, u32[]{:S(2)}, u32[]{:S(2)}) collective-permute-start(bf16[2,16,2048]{2,1,0:T(8,128)(2,1)S(1)} %get-tuple-element.17), channel_id=1, source_target_pairs={{0,4},{2,6},{4,8},{6,10},{8,12},{10,14},{12,0},{14,2},{1,5},{3,7},... | collective-permute-start | bytes 393224 | tf_op jit(solution)/shard_map/ppermute | solution.py:522
  48.0 7.7 %collective-permute-start.10 = (bf16[2,16,2048]{2,1,0:T(8,128)(2,1)S(1)}, bf16[2,16,2048]{2,1,0:T(8,128)(2,1)S(1)}, u32[]{:S(2)}, u32[]{:S(2)}) collective-permute-start(bf16[2,16,2048]{2,1,0:T(8,128)(2,1)S(1)} %merge.1.x_ref.refs_0_), channel_id=1, source_target_pairs={{0,2},{2,0},{4,6},{6,4},{8,10},{10,8},{12,14},{14,12},{1,3},{3,1},... | collective-permute-start | bytes 393224 | tf_op jit(solution)/shard_map/ppermute | solution.py:523
  49.5 6.6 %collective-permute-start.12 = (bf16[2,16,2048]{2,1,0:T(8,128)(2,1)S(1)}, bf16[2,16,2048]{2,1,0:T(8,128)(2,1)S(1)}, u32[]{:S(2)}, u32[]{:S(2)}) collective-permute-start(bf16[2,16,2048]{2,1,0:T(8,128)(2,1)S(1)} %collective-permute-done.8.refs_2_), channel_id=1, source_target_pairs={{0,2},{2,0},{4,6},{6,4},{8,10},{10,8},{12,14},{14,12},{1,3},{3,1},... | collective-permute-start | bytes 393224 | tf_op jit(solution)/shard_map/ppermute | solution.py:523
  52.3 5.9 %collective-permute-start.13 = (bf16[2,16,2048]{2,1,0:T(8,128)(2,1)S(1)}, bf16[2,16,2048]{2,1,0:T(8,128)(2,1)S(1)}, u32[]{:S(2)}, u32[]{:S(2)}) collective-permute-start(bf16[2,16,2048]{2,1,0:T(8,128)(2,1)S(1)} %collective-permute-done.9.refs_3_), channel_id=1, source_target_pairs={{0,2},{2,0},{4,6},{6,4},{8,10},{10,8},{12,14},{14,12},{1,3},{3,1},... | collective-permute-start | bytes 393224 | tf_op jit(solution)/shard_map/ppermute | solution.py:523
  54.3 5.2 %collective-permute-start.11 = (bf16[2,16,2048]{2,1,0:T(8,128)(2,1)S(1)}, bf16[2,16,2048]{2,1,0:T(8,128)(2,1)S(1)}, u32[]{:S(2)}, u32[]{:S(2)}) collective-permute-start(bf16[2,16,2048]{2,1,0:T(8,128)(2,1)S(1)} %collective-permute-done.7.refs_1_), channel_id=1, source_target_pairs={{0,2},{2,0},{4,6},{6,4},{8,10},{10,8},{12,14},{14,12},{1,3},{3,1},... | collective-permute-start | bytes 393224 | tf_op jit(solution)/shard_map/ppermute | solution.py:523
  61.4 2.0 %collective-permute-start.14 = (f32[2,128,512]{2,1,0:T(8,128)S(1)}, f32[2,128,512]{2,1,0:T(8,128)S(1)}, u32[]{:S(2)}, u32[]{:S(2)}) collective-permute-start(f32[2,128,512]{2,1,0:T(8,128)S(1)} %get-tuple-element.20), channel_id=1, source_target_pairs={{0,1},{1,0},{2,3},{3,2},{4,5},{5,4},{6,7},{7,6},{8,9},{9,8},{10,11... | collective-permute-start | bytes 1572872 | tf_op jit(solution)/shard_map/ppermute | solution.py:529

commit v8 on v7

--- a/solution.py
+++ b/solution.py
@@ -31,12 +31,13 @@
 
 
 def rope_kernel(
-    npool, cache_pages, per, slot_ref, len_ref, pages_ref, ct_ref, st_ref, cp_ref, sp_ref, out_ref, own_ref, count
+    npool, cache_pages, per, slot_ref, len_ref, x_ref, pages_ref, ct_ref, st_ref, cp_ref, sp_ref, out_ref, own_ref, x_out, count
 ):
     _, _, heads, page_len, head_dim = pages_ref.shape
 
     @pl.when(pl.program_id(0) == 0)
     def _():
+        x_out[...] = x_ref[...]
         items = own_ref.shape[0] // 3
         for e in range(npool):
             count[e] = 0
@@ -78,33 +79,35 @@
     return number, fill
 
 
-def rotated_pages(prompt_kv, page_slot, prompt_lengths, tabs, npool, pair, cache_pages):
+def rotated_pages(prompt_kv, page_slot, prompt_lengths, x, tabs, npool, pair, cache_pages):
     pages, _, heads, page_len, head_dim = prompt_kv.shape
     per = pages // 2
     ct, st, cp, sp, _, _ = tabs
-    whole = lambda x: pl.BlockSpec(x.shape, lambda i: (0, 0))
+    whole = lambda x: pl.BlockSpec(x.shape, lambda i: (0,) * x.ndim)
     return pl.pallas_call(
         functools.partial(rope_kernel, npool, cache_pages, per),
         grid=(pages // per,),
         out_shape=[
             jax.ShapeDtypeStruct(prompt_kv.shape, BF16),
             jax.ShapeDtypeStruct((3 * npool * pair,), I32),
+            jax.ShapeDtypeStruct(x.shape, x.dtype),
         ],
         in_specs=[
             SMEM,
             SMEM,
+            whole(x),
             pl.BlockSpec((per,) + prompt_kv.shape[1:], lambda i: (i, 0, 0, 0, 0)),
             whole(ct),
             whole(st),
             whole(cp),
             whole(sp),
         ],
-        out_specs=[pl.BlockSpec((per,) + prompt_kv.shape[1:], lambda i: (i, 0, 0, 0, 0)), SMEM],
+        out_specs=[pl.BlockSpec((per,) + prompt_kv.shape[1:], lambda i: (i, 0, 0, 0, 0)), SMEM, whole(x)],
         scratch_shapes=[pltpu.SMEM((npool,), I32)],
         compiler_params=PARAMS,
         cost_estimate=pl.CostEstimate(flops=6_000_000, bytes_accessed=2_000_000, transcendentals=0),
         name="rope_pages",
-    )(*[in_hbm(x) for x in (page_slot, prompt_lengths, prompt_kv, ct, st, cp, sp)])
+    )(in_hbm(page_slot), in_hbm(prompt_lengths), x, *[in_hbm(y) for y in (prompt_kv, ct, st, cp, sp)])
 
 
 def asked_kernel(page_len, heads, table_ref, context_ref, q_ref, out_ref, spread):
@@ -316,7 +319,7 @@
     group = block // heads
     together = LANES // block
     me = me_ref[0]
-    owners = [owner_of(me, npool, apart, flip) for apart, flip in block_order(npool)]
+    owners = [owner_of(me, which) for which in block_order(npool)]
     lane = lax.broadcasted_iota(I32, (1, LANES), 1)
     codes = [x[rows, :STAT_ROWS, :].astype(F32) for x in blocks]
     codes = [x[0:1] * CODE + x[1:2] for x in codes]
@@ -455,74 +458,93 @@
     )(in_hbm(weight), x)
 
 
-def project_kernel(npool, place_ref, *refs):
+def rows_kernel(npool, place_ref, *refs):
     blocks = refs[:npool]
-    weight_ref, mine_ref, other_ref, lhs = refs[npool:]
+    weight_ref, out_ref, lhs = refs[npool:]
     steps, rows, _ = blocks[0].shape
-    half = weight_ref.shape[1] // 2
-    tile = min(half, 256)
     every = npool * rows
-    me, core = place_ref[0], place_ref[1]
-    for x, (apart, flip) in enumerate(block_order(npool)):
-        owner = owner_of(me, npool, apart, flip)
+    for x, which in enumerate(block_order(npool)):
+        owner = owner_of(place_ref[0], which)
         for s in range(steps):
             lhs[pl.ds(pl.multiple_of(s * every + owner * rows, rows), rows), :] = blocks[x][s]
-    for out_ref, first in ((mine_ref, core * half), (other_ref, (1 - core) * half)):
-        for i in range(half // tile):
-            at = pl.ds(pl.multiple_of(first + i * tile, LANES), tile)
-            terms = jnp.dot(lhs[...], weight_ref[:, at], preferred_element_type=F32)
-            for s in range(steps):
-                out_ref[s, :, i * tile : (i + 1) * tile] = terms[s * every : (s + 1) * every]
-
-
-def projection(place, blocks, weight):
+    multiply(lhs, weight_ref, out_ref, 1 - place_ref[1])
+
+
+def multiply(lhs, weight_ref, out_ref, which):
+    steps, every, half = out_ref.shape
+    tile = min(half, 256)
+    for i in range(half // tile):
+        at = pl.ds(pl.multiple_of(which * half + i * tile, LANES), tile)
+        terms = jnp.dot(lhs[...], weight_ref[:, at], preferred_element_type=F32)
+        for s in range(steps):
+            out_ref[s, :, i * tile : (i + 1) * tile] = terms[s * every : (s + 1) * every]
+
+
+def other_projection(place, blocks, weight):
     npool = len(blocks)
     steps, rows, width = blocks[0].shape
-    columns = weight.shape[1]
+    half = weight.shape[1] // 2
     every = steps * npool * rows
     return pl.pallas_call(
-        functools.partial(project_kernel, npool),
-        out_shape=[jax.ShapeDtypeStruct((steps, npool * rows, columns // 2), F32)] * 2,
+        functools.partial(rows_kernel, npool),
+        out_shape=[
+            jax.ShapeDtypeStruct((steps, npool * rows, half), F32),
+            jax.ShapeDtypeStruct((every, width), BF16),
+        ],
         in_specs=[SMEM] + [VMEM] * (npool + 1),
         out_specs=[VMEM] * 2,
-        scratch_shapes=[pltpu.VMEM((every, width), BF16)],
-        compiler_params=PARAMS,
-        cost_estimate=pl.CostEstimate(
-            flops=2 * every * width * columns, bytes_accessed=6_000_000, transcendentals=0
-        ),
-        name="project",
+        compiler_params=PARAMS,
+        cost_estimate=pl.CostEstimate(flops=2 * every * width * half, bytes_accessed=4_000_000, transcendentals=0),
+        name="project_other",
     )(place, *blocks, weight)
 
 
+def own_kernel(place_ref, lhs, weight_ref, out_ref):
+    multiply(lhs, weight_ref, out_ref, place_ref[1])
+
+
+def own_projection(place, lhs, weight, steps):
+    every, width = lhs.shape
+    half = weight.shape[1] // 2
+    return pl.pallas_call(
+        own_kernel,
+        out_shape=jax.ShapeDtypeStruct((steps, every // steps, half), F32),
+        in_specs=[SMEM] + [VMEM] * 2,
+        out_specs=VMEM,
+        compiler_params=PARAMS,
+        cost_estimate=pl.CostEstimate(flops=2 * every * width * half, bytes_accessed=4_000_000, transcendentals=0),
+        name="project_own",
+    )(place, lhs, weight)
+
+
 def block_order(npool):
-    return [(apart, flip) for flip in (0, 1) for apart in range(npool // 2)]
-
-
-def owner_of(me, npool, apart, flip):
-    half = npool // 2
-    pair, side = me // 2, me % 2
-    side = 1 - side if flip else side
-    return lax.rem(pair + half - apart, half) * 2 + side
+    return [2 * apart + flip for flip in (0, 1) for apart in range(npool // 2)]
+
+
+def owner_of(me, which):
+    return jnp.bitwise_xor(me, which)
 
 
 def place_of(me, npool, holder):
-    half = npool // 2
-    apart = lax.rem(holder // 2 - me // 2 + half, half)
-    flip = lax.rem(me + holder, 2)
-    return flip * half + apart
+    which = jnp.bitwise_xor(me, holder)
+    return (which % 2) * (npool // 2) + which // 2
 
 
 def in_hbm(x):
     return pltpu.with_memory_space_constraint(x, pltpu.HBM)
 
 
-def gathered(x, npool, later=None):
-    half = npool // 2
-    later = x if later is None else later
-    ahead = lambda x, by: lax.ppermute(x, "pool", [(i, (i + 2 * by) % npool) for i in range(npool)])
-    across = lambda x: lax.ppermute(x, "pool", [(i, i ^ 1) for i in range(npool)])
-    straight = [x] + [ahead(x if by == half // 2 else later, by) for by in range(1, half)]
-    return straight + [across(y) for y in straight]
+def gathered(x, npool, later):
+    swap = lambda x, by: lax.ppermute(x, "pool", [(i, i ^ by) for i in range(npool)])
+    straight = {0: later}
+    apart = npool // 4
+    while apart:
+        for i in list(straight):
+            own = x if i == 0 and apart == npool // 4 else straight[i]
+            straight[i + apart] = swap(own, 2 * apart)
+        apart //= 2
+    straight = [straight[i] for i in range(npool // 2)]
+    return straight + [swap(y, 1) for y in straight]
 
 
 def swap_halves(x):
@@ -551,16 +573,19 @@
     table = page_table.T
 
     asked = asked_queries(table, context_lengths, queries, page_len, heads, head_dim)
-    asked_all = gathered(asked, npool)
-    arrived, own = rotated_pages(prompt_kv, page_slot, prompt_lengths, tabs, npool, pair, cache_pages)
+    arrived, own, again = rotated_pages(
+        prompt_kv, page_slot, prompt_lengths, asked, tabs, npool, pair, cache_pages
+    )
+    asked_all = gathered(asked, npool, again)
     local = local_attention(table, context_lengths, cache_fill, asked, new_kv, cache_kv, tabs)
     parts = arrived_attention(place, own, asked_all, arrived)
     parts = lax.all_to_all(parts, "pool", split_axis=0, concat_axis=0, tiled=True)
     attention = merged(place, parts, local, queries.shape, heads, pair)
     weight, again = fetched(out_weight, attention)
     blocks = gathered(attention, npool, again)
-    terms, other_terms = projection(place, blocks, weight)
+    other_terms, lhs = other_projection(place, blocks, weight)
     other_terms = swap_halves(other_terms)
+    terms = own_projection(place, lhs, weight, queries.shape[0])
     return (terms + other_terms).astype(BF16)
 
 

time: 64.5 us -> 68.2 us (1.057)
  starting transfers between devices: 24 us -> 27.7 us
  waiting for transfers between devices: 19.6 us -> 18.6 us
  Pallas kernels: 19.6 us -> 20.3 us
    all_to_all x1, starting transfers between devices: 3.38 us -> 5.61 us  [shards(): lax.all_to_all(parts, 'pool', split_axis=0, concat_axis=0, tiled=True)]
    ppermute x14, starting transfers between devices: 20.5 us -> 22 us  [gathered(): lax.ppermute(x, 'pool', [(i, i ^ by) for i in range(npool)])]
    ppermute x1, waiting for transfers between devices: 1.9 us -> 0.61 us  [swap_halves(): return lax.ppermute(x, 'tp', [(0, 1), (1, 0)])]
    pallas_call x1 -> x2, Pallas kernels: 1.89 us -> 2.61 us  [the longest x1 1.33 us: other_projection(): pl.pallas_call(functools.partial(rows_kernel, npool), out_shape=[jax.Shap...]
  transfers between devices with their start and end apart: 16 -> 16, of which waited for: 11 -> 13; matrix products, arithmetic and copies ran while one was open for 0% -> 0% of each run, Pallas kernels for 19% -> 20%
where the time goes in v8:
time: 68.2 us; the launch traced here: 67.6 us
  starting transfers between devices  27.7 us (41%)
  Pallas kernels  20.3 us (30%)
  waiting for transfers between devices  18.6 us (27%)
  other arithmetic  0.86 us (1%)
    ppermute x14, starting transfers between devices, gathered(): lax.ppermute(x, 'pool', [(i, i ^ by) for i in range(npool)])  22 us
    ppermute x14, waiting for transfers between devices, gathered(): lax.ppermute(x, 'pool', [(i, i ^ by) for i in range(npool)])  17.4 us
    pallas_call x1, Pallas kernels, local_attention(): pl.pallas_call(functools.partial(local_kernel, page_len, heads), out_shap...  6.94 us
    all_to_all x1, starting transfers between devices, shards(): lax.all_to_all(parts, 'pool', split_axis=0, concat_axis=0, tiled=True)  5.61 us
    pallas_call x1, Pallas kernels, rotated_pages(): pl.pallas_call(functools.partial(rope_kernel, npool, cache_pages, per), g...  2.96 us
    pallas_call x1, Pallas kernels, arrived_attention(): pl.pallas_call(functools.partial(arrived_kernel, npool, pair), out_shape=...  2.87 us
    pallas_call x1, Pallas kernels, fetched(): pl.pallas_call(fetch_kernel, out_shape=[pltpu.VMEM(weight.shape, weight.d...  2.21 us
    pallas_call x1, Pallas kernels, merged(): pl.pallas_call(functools.partial(merge_kernel, pair, heads), out_shape=ja...  1.53 us
  transfers between devices with their start and end apart: 16, of which 13 were waited for; matrix products, arithmetic and copies ran while one was open for 0% of the time, Pallas kernels for 20%

profile of v8, /device:TPU:0, one launch (start us, length us, event | category | flops | bytes accessed | tf_op | source)
XLA Modules:
  0.0 67.6 jit_solution(17014753691958850794)
XLA Ops:
  1.2 4.1 %collective-permute-start.1 = (bf16[17,32,128]{2,1,0:T(8,128)(2,1)S(1)}, bf16[17,32,128]{2,1,0:T(8,128)(2,1)S(1)}, u32[]{:S(2)}, u32[]{:S(2)}) collective-permute-start(bf16[17,32,128]{2,1,0:T(8,128)(2,1)S(1)} %asked_queries.1.x_ref.q_ref), channel_id=1, source_target_pairs={{0,8},{2,10},{4,12},{6,14},{8,0},{10,2},{12,4},{14,6},{1,9},{3,11}... | collective-permute-start | bytes 417800 | tf_op jit(solution)/shard_map/ppermute | solution.py:538
  5.3 3.0 %rope_pages.1 = (bf16[16,2,2,128,128]{4,3,2,1,0:T(8,128)(2,1)S(1)}, s32[48]{0:T(128)S(1)}, bf16[17,32,128]{2,1,0:T(8,128)(2,1)S(1)}) custom-call(s32[16]{0:T(128)} %slot_ref.1, s32[1,4]{1,0:T(1,128)} %len_ref.1, bf16[17,32,128]{2,1,0:T(8,128)(2,1)S(1)} %asked_queries.1.x_ref.q_ref, bf16[16,2,2,128,128]{4,3,2,1,0:T(8,128)(2,1)} %pages_ref.1, ...), custom_call_target="tpu_custom_call" | custom-call | flops 6000000 | bytes 2000000 | tf_op jit(solution)/shard_map/rope_pages/pallas_call | solution.py:87
  8.3 1.6 %collective-permute-start = (bf16[17,32,128]{2,1,0:T(8,128)(2,1)S(1)}, bf16[17,32,128]{2,1,0:T(8,128)(2,1)S(1)}, u32[]{:S(2)}, u32[]{:S(2)}) collective-permute-start(bf16[17,32,128]{2,1,0:T(8,128)(2,1)S(1)} %get-tuple-element.15.refs_0_), channel_id=1, source_target_pairs={{0,4},{2,6},{4,0},{6,2},{8,12},{10,14},{12,8},{14,10},{1,5},{3,7},... | collective-permute-start | bytes 417800 | tf_op jit(solution)/shard_map/ppermute | solution.py:538
  9.9 2.2 %collective-permute-done.1.refs_2_ = bf16[17,32,128]{2,1,0:T(8,128)(2,1)S(1)} collective-permute-done((bf16[17,32,128]{2,1,0:T(8,128)(2,1)S(1)}, bf16[17,32,128]{2,1,0:T(8,128)(2,1)S(1)}, u32[]{:S(2)}, u32[]{:S(2)}) %collective-permute-start.1) | collective-permute-done | bytes 139296 | tf_op jit(solution)/shard_map/ppermute | solution.py:538
  12.8 1.5 %collective-permute-start.3 = (bf16[17,32,128]{2,1,0:T(8,128)(2,1)S(1)}, bf16[17,32,128]{2,1,0:T(8,128)(2,1)S(1)}, u32[]{:S(2)}, u32[]{:S(2)}) collective-permute-start(bf16[17,32,128]{2,1,0:T(8,128)(2,1)S(1)} %get-tuple-element.15.refs_0_), channel_id=1, source_target_pairs={{0,2},{2,0},{4,6},{6,4},{8,10},{10,8},{12,14},{14,12},{1,3},{3,1},... | collective-permute-start | bytes 417800 | tf_op jit(solution)/shard_map/ppermute | solution.py:538
  15.1 1.6 %collective-permute-start.4 = (bf16[17,32,128]{2,1,0:T(8,128)(2,1)S(1)}, bf16[17,32,128]{2,1,0:T(8,128)(2,1)S(1)}, u32[]{:S(2)}, u32[]{:S(2)}) collective-permute-start(bf16[17,32,128]{2,1,0:T(8,128)(2,1)S(1)} %collective-permute-done.refs_1_), channel_id=1, source_target_pairs={{0,2},{2,0},{4,6},{6,4},{8,10},{10,8},{12,14},{14,12},{1,3},{3,1},... | collective-permute-start | bytes 417800 | tf_op jit(solution)/shard_map/ppermute | solution.py:538
  18.0 1.6 %collective-permute-start.6 = (bf16[17,32,128]{2,1,0:T(8,128)(2,1)S(1)}, bf16[17,32,128]{2,1,0:T(8,128)(2,1)S(1)}, u32[]{:S(2)}, u32[]{:S(2)}) collective-permute-start(bf16[17,32,128]{2,1,0:T(8,128)(2,1)S(1)} %collective-permute-done.2.refs_3_), channel_id=1, source_target_pairs={{0,2},{2,0},{4,6},{6,4},{8,10},{10,8},{12,14},{14,12},{1,3},{3,1},... | collective-permute-start | bytes 417800 | tf_op jit(solution)/shard_map/ppermute | solution.py:538
  19.6 2.7 %collective-permute-done.5.refs_6_ = bf16[17,32,128]{2,1,0:T(8,128)(2,1)S(1)} collective-permute-done((bf16[17,32,128]{2,1,0:T(8,128)(2,1)S(1)}, bf16[17,32,128]{2,1,0:T(8,128)(2,1)S(1)}, u32[]{:S(2)}, u32[]{:S(2)}) %collective-permute-start.5) | collective-permute-done | bytes 139296 | tf_op jit(solution)/shard_map/ppermute | solution.py:538
  22.3 3.0 %collective-permute-done.4.refs_5_ = bf16[17,32,128]{2,1,0:T(8,128)(2,1)S(1)} collective-permute-done((bf16[17,32,128]{2,1,0:T(8,128)(2,1)S(1)}, bf16[17,32,128]{2,1,0:T(8,128)(2,1)S(1)}, u32[]{:S(2)}, u32[]{:S(2)}) %collective-permute-start.4) | collective-permute-done | bytes 139296 | tf_op jit(solution)/shard_map/ppermute | solution.py:538
  25.3 1.7 %collective-permute-done.6.refs_7_ = bf16[17,32,128]{2,1,0:T(8,128)(2,1)S(1)} collective-permute-done((bf16[17,32,128]{2,1,0:T(8,128)(2,1)S(1)}, bf16[17,32,128]{2,1,0:T(8,128)(2,1)S(1)}, u32[]{:S(2)}, u32[]{:S(2)}) %collective-permute-start.6) | collective-permute-done | bytes 139296 | tf_op jit(solution)/shard_map/ppermute | solution.py:538
  27.0 2.9 %arrived_attention.1 = bf16[8,80,128]{2,1,0:T(8,128)(2,1)} custom-call(s32[2]{0:T(128)S(1)} %pad_add_fusion.me_ref.place_ref, s32[48]{0:T(128)S(1)} %get-tuple-element.14.own_ref, bf16[17,32,128]{2,1,0:T(8,128)(2,1)S(1)} %get-tuple-element.15.refs_0_, bf16[17,32,128]{2,1,0:T(8,128)(2,1)S(1)} %collective-permute-done.refs_1_, ...), custom_call_target="tpu_custom_call" | custom-call | flops 200000000 | bytes 4000000 | tf_op jit(solution)/shard_map/arrived_attention/pallas_call | solution.py:365
  29.9 5.6 %all-to-all-start = ((bf16[8,80,128]{2,1,0:T(8,128)(2,1)}), bf16[8,80,128]{2,1,0:T(8,128)(2,1)S(1)}, u32[]{:S(2)}, u32[]{:S(2)}) async-start(bf16[8,80,128]{2,1,0:T(8,128)(2,1)} %arrived_attention.1), calls=%async_computation | async-start | bytes 327680 | tf_op jit(solution)/shard_map/all_to_all | solution.py:582
  35.5 6.9 %local_attention.1 = (f32[512,128]{1,0:T(8,128)S(1)}, f32[512,128]{1,0:T(8,128)S(1)}) custom-call(s32[3,16]{1,0:T(4,128)} %bitcast.4, s32[16]{0:T(128)} %context_ref.3, s32[48]{0:T(128)} %fill_ref.1, bf16[17,32,128]{2,1,0:T(8,128)(2,1)S(1)} %asked_queries.1.x_ref.q_ref, bf16[2,16,512]{2,1,0:T(8,128)(2,1)S(1)} %reshape.3.new_ref, ...), custom_call_target="tpu_custom_call" | custom-call | flops 800000000 | bytes 12000000 | tf_op jit(solution)/shard_map/local_attention/pallas_call | solution.py:284
  43.1 1.5 %merge.1.x_ref = bf16[2,16,2048]{2,1,0:T(8,128)(2,1)S(1)} custom-call(s32[2]{0:T(128)S(1)} %pad_add_fusion.me_ref.place_ref, bf16[8,80,128]{2,1,0:T(8,128)(2,1)S(1)} %all-to-all-done.parts_ref, f32[512,128]{1,0:T(8,128)S(1)} %get-tuple-element.17.o_ref, f32[512,128]{1,0:T(8,128)S(1)} %get-tuple-element.18.stat_ref), custom_call_target="tpu_custom_call" | custom-call | flops 2000000 | bytes 1500000 | tf_op jit(solution)/shard_map/merge/pallas_call | solution.py:425
  44.6 2.4 %collective-permute-start.8 = (bf16[2,16,2048]{2,1,0:T(8,128)(2,1)S(1)}, bf16[2,16,2048]{2,1,0:T(8,128)(2,1)S(1)}, u32[]{:S(2)}, u32[]{:S(2)}) collective-permute-start(bf16[2,16,2048]{2,1,0:T(8,128)(2,1)S(1)} %merge.1.x_ref), channel_id=1, source_target_pairs={{0,8},{2,10},{4,12},{6,14},{8,0},{10,2},{12,4},{14,6},{1,9},{3,11}... | collective-permute-start | bytes 393224 | tf_op jit(solution)/shard_map/ppermute | solution.py:538
  47.0 2.2 %fetch_weight.1 = (bf16[2048,1024]{1,0:T(8,128)(2,1)S(1)}, bf16[2,16,2048]{2,1,0:T(8,128)(2,1)S(1)}) custom-call(bf16[2048,1024]{1,0:T(8,128)(2,1)} %weight_ref.1, bf16[2,16,2048]{2,1,0:T(8,128)(2,1)S(1)} %merge.1.x_ref), custom_call_target="tpu_custom_call" | custom-call | bytes 8388608 | tf_op jit(solution)/shard_map/fetch_weight/pallas_call | solution.py:449
  49.2 1.5 %collective-permute-start.7 = (bf16[2,16,2048]{2,1,0:T(8,128)(2,1)S(1)}, bf16[2,16,2048]{2,1,0:T(8,128)(2,1)S(1)}, u32[]{:S(2)}, u32[]{:S(2)}) collective-permute-start(bf16[2,16,2048]{2,1,0:T(8,128)(2,1)S(1)} %get-tuple-element.19.refs_0_), channel_id=1, source_target_pairs={{0,4},{2,6},{4,0},{6,2},{8,12},{10,14},{12,8},{14,10},{1,5},{3,7},... | collective-permute-start | bytes 393224 | tf_op jit(solution)/shard_map/ppermute | solution.py:538
  51.2 1.8 %collective-permute-start.9 = (bf16[2,16,2048]{2,1,0:T(8,128)(2,1)S(1)}, bf16[2,16,2048]{2,1,0:T(8,128)(2,1)S(1)}, u32[]{:S(2)}, u32[]{:S(2)}) collective-permute-start(bf16[2,16,2048]{2,1,0:T(8,128)(2,1)S(1)} %collective-permute-done.8.refs_2_), channel_id=1, source_target_pairs={{0,4},{2,6},{4,0},{6,2},{8,12},{10,14},{12,8},{14,10},{1,5},{3,7},... | collective-permute-start | bytes 393224 | tf_op jit(solution)/shard_map/ppermute | solution.py:538
  53.0 1.7 %collective-permute-start.10 = (bf16[2,16,2048]{2,1,0:T(8,128)(2,1)S(1)}, bf16[2,16,2048]{2,1,0:T(8,128)(2,1)S(1)}, u32[]{:S(2)}, u32[]{:S(2)}) collective-permute-start(bf16[2,16,2048]{2,1,0:T(8,128)(2,1)S(1)} %get-tuple-element.19.refs_0_), channel_id=1, source_target_pairs={{0,2},{2,0},{4,6},{6,4},{8,10},{10,8},{12,14},{14,12},{1,3},{3,1},... | collective-permute-start | bytes 393224 | tf_op jit(solution)/shard_map/ppermute | solution.py:538
  55.0 1.7 %collective-permute-start.11 = (bf16[2,16,2048]{2,1,0:T(8,128)(2,1)S(1)}, bf16[2,16,2048]{2,1,0:T(8,128)(2,1)S(1)}, u32[]{:S(2)}, u32[]{:S(2)}) collective-permute-start(bf16[2,16,2048]{2,1,0:T(8,128)(2,1)S(1)} %collective-permute-done.7.refs_1_), channel_id=1, source_target_pairs={{0,2},{2,0},{4,6},{6,4},{8,10},{10,8},{12,14},{14,12},{1,3},{3,1},... | collective-permute-start | bytes 393224 | tf_op jit(solution)/shard_map/ppermute | solution.py:538
  57.7 1.6 %collective-permute-done.10.refs_4_ = bf16[2,16,2048]{2,1,0:T(8,128)(2,1)S(1)} collective-permute-done((bf16[2,16,2048]{2,1,0:T(8,128)(2,1)S(1)}, bf16[2,16,2048]{2,1,0:T(8,128)(2,1)S(1)}, u32[]{:S(2)}, u32[]{:S(2)}) %collective-permute-start.10) | collective-permute-done | bytes 131104 | tf_op jit(solution)/shard_map/ppermute | solution.py:538
  59.3 1.4 %collective-permute-done.12.refs_6_ = bf16[2,16,2048]{2,1,0:T(8,128)(2,1)S(1)} collective-permute-done((bf16[2,16,2048]{2,1,0:T(8,128)(2,1)S(1)}, bf16[2,16,2048]{2,1,0:T(8,128)(2,1)S(1)}, u32[]{:S(2)}, u32[]{:S(2)}) %collective-permute-start.12) | collective-permute-done | bytes 131104 | tf_op jit(solution)/shard_map/ppermute | solution.py:538
  60.7 1.4 %collective-permute-done.11.refs_5_ = bf16[2,16,2048]{2,1,0:T(8,128)(2,1)S(1)} collective-permute-done((bf16[2,16,2048]{2,1,0:T(8,128)(2,1)S(1)}, bf16[2,16,2048]{2,1,0:T(8,128)(2,1)S(1)}, u32[]{:S(2)}, u32[]{:S(2)}) %collective-permute-start.11) | collective-permute-done | bytes 131104 | tf_op jit(solution)/shard_map/ppermute | solution.py:538
  62.1 1.4 %collective-permute-done.13.refs_7_ = bf16[2,16,2048]{2,1,0:T(8,128)(2,1)S(1)} collective-permute-done((bf16[2,16,2048]{2,1,0:T(8,128)(2,1)S(1)}, bf16[2,16,2048]{2,1,0:T(8,128)(2,1)S(1)}, u32[]{:S(2)}, u32[]{:S(2)}) %collective-permute-start.13) | collective-permute-done | bytes 131104 | tf_op jit(solution)/shard_map/ppermute | solution.py:538
  (21 shorter events, 10.4 us)
Async XLA Ops:
  0.0 35.5 %copy-start = (bf16[2,16,2,2,128]{4,3,2,1,0:T(2,128)(2,1)S(1)}, bf16[2,16,2,2,128]{4,3,2,1,0:T(2,128)(2,1)}, u32[]{:S(2)}) copy-start(bf16[2,16,2,2,128]{4,3,2,1,0:T(2,128)(2,1)} %param.24) | copy-start | bytes 98308
  1.2 10.9 %collective-permute-start.1 = (bf16[17,32,128]{2,1,0:T(8,128)(2,1)S(1)}, bf16[17,32,128]{2,1,0:T(8,128)(2,1)S(1)}, u32[]{:S(2)}, u32[]{:S(2)}) collective-permute-start(bf16[17,32,128]{2,1,0:T(8,128)(2,1)S(1)} %asked_queries.1.x_ref.q_ref), channel_id=1, source_target_pairs={{0,8},{2,10},{4,12},{6,14},{8,0},{10,2},{12,4},{14,6},{1,9},{3,11}... | collective-permute-start | bytes 417800 | tf_op jit(solution)/shard_map/ppermute | solution.py:538
  8.3 6.8 %collective-permute-start = (bf16[17,32,128]{2,1,0:T(8,128)(2,1)S(1)}, bf16[17,32,128]{2,1,0:T(8,128)(2,1)S(1)}, u32[]{:S(2)}, u32[]{:S(2)}) collective-permute-start(bf16[17,32,128]{2,1,0:T(8,128)(2,1)S(1)} %get-tuple-element.15.refs_0_), channel_id=1, source_target_pairs={{0,4},{2,6},{4,0},{6,2},{8,12},{10,14},{12,8},{14,10},{1,5},{3,7},... | collective-permute-start | bytes 417800 | tf_op jit(solution)/shard_map/ppermute | solution.py:538
  12.1 5.9 %collective-permute-start.2 = (bf16[17,32,128]{2,1,0:T(8,128)(2,1)S(1)}, bf16[17,32,128]{2,1,0:T(8,128)(2,1)S(1)}, u32[]{:S(2)}, u32[]{:S(2)}) collective-permute-start(bf16[17,32,128]{2,1,0:T(8,128)(2,1)S(1)} %collective-permute-done.1.refs_2_), channel_id=1, source_target_pairs={{0,4},{2,6},{4,0},{6,2},{8,12},{10,14},{12,8},{14,10},{1,5},{3,7},... | collective-permute-start | bytes 417800 | tf_op jit(solution)/shard_map/ppermute | solution.py:538
  12.8 6.8 %collective-permute-start.3 = (bf16[17,32,128]{2,1,0:T(8,128)(2,1)S(1)}, bf16[17,32,128]{2,1,0:T(8,128)(2,1)S(1)}, u32[]{:S(2)}, u32[]{:S(2)}) collective-permute-start(bf16[17,32,128]{2,1,0:T(8,128)(2,1)S(1)} %get-tuple-element.15.refs_0_), channel_id=1, source_target_pairs={{0,2},{2,0},{4,6},{6,4},{8,10},{10,8},{12,14},{14,12},{1,3},{3,1},... | collective-permute-start | bytes 417800 | tf_op jit(solution)/shard_map/ppermute | solution.py:538
  14.3 8.0 %collective-permute-start.5 = (bf16[17,32,128]{2,1,0:T(8,128)(2,1)S(1)}, bf16[17,32,128]{2,1,0:T(8,128)(2,1)S(1)}, u32[]{:S(2)}, u32[]{:S(2)}) collective-permute-start(bf16[17,32,128]{2,1,0:T(8,128)(2,1)S(1)} %collective-permute-done.1.refs_2_), channel_id=1, source_target_pairs={{0,2},{2,0},{4,6},{6,4},{8,10},{10,8},{12,14},{14,12},{1,3},{3,1},... | collective-permute-start | bytes 417800 | tf_op jit(solution)/shard_map/ppermute | solution.py:538
  15.1 10.2 %collective-permute-start.4 = (bf16[17,32,128]{2,1,0:T(8,128)(2,1)S(1)}, bf16[17,32,128]{2,1,0:T(8,128)(2,1)S(1)}, u32[]{:S(2)}, u32[]{:S(2)}) collective-permute-start(bf16[17,32,128]{2,1,0:T(8,128)(2,1)S(1)} %collective-permute-done.refs_1_), channel_id=1, source_target_pairs={{0,2},{2,0},{4,6},{6,4},{8,10},{10,8},{12,14},{14,12},{1,3},{3,1},... | collective-permute-start | bytes 417800 | tf_op jit(solution)/shard_map/ppermute | solution.py:538
  18.0 9.1 %collective-permute-start.6 = (bf16[17,32,128]{2,1,0:T(8,128)(2,1)S(1)}, bf16[17,32,128]{2,1,0:T(8,128)(2,1)S(1)}, u32[]{:S(2)}, u32[]{:S(2)}) collective-permute-start(bf16[17,32,128]{2,1,0:T(8,128)(2,1)S(1)} %collective-permute-done.2.refs_3_), channel_id=1, source_target_pairs={{0,2},{2,0},{4,6},{6,4},{8,10},{10,8},{12,14},{14,12},{1,3},{3,1},... | collective-permute-start | bytes 417800 | tf_op jit(solution)/shard_map/ppermute | solution.py:538
  29.9 13.2 %all-to-all-start = ((bf16[8,80,128]{2,1,0:T(8,128)(2,1)}), bf16[8,80,128]{2,1,0:T(8,128)(2,1)S(1)}, u32[]{:S(2)}, u32[]{:S(2)}) async-start(bf16[8,80,128]{2,1,0:T(8,128)(2,1)} %arrived_attention.1), calls=%async_computation | async-start | bytes 327680 | tf_op jit(solution)/shard_map/all_to_all | solution.py:582
  44.6 6.5 %collective-permute-start.8 = (bf16[2,16,2048]{2,1,0:T(8,128)(2,1)S(1)}, bf16[2,16,2048]{2,1,0:T(8,128)(2,1)S(1)}, u32[]{:S(2)}, u32[]{:S(2)}) collective-permute-start(bf16[2,16,2048]{2,1,0:T(8,128)(2,1)S(1)} %merge.1.x_ref), channel_id=1, source_target_pairs={{0,8},{2,10},{4,12},{6,14},{8,0},{10,2},{12,4},{14,6},{1,9},{3,11}... | collective-permute-start | bytes 393224 | tf_op jit(solution)/shard_map/ppermute | solution.py:538
  49.2 5.8 %collective-permute-start.7 = (bf16[2,16,2048]{2,1,0:T(8,128)(2,1)S(1)}, bf16[2,16,2048]{2,1,0:T(8,128)(2,1)S(1)}, u32[]{:S(2)}, u32[]{:S(2)}) collective-permute-start(bf16[2,16,2048]{2,1,0:T(8,128)(2,1)S(1)} %get-tuple-element.19.refs_0_), channel_id=1, source_target_pairs={{0,4},{2,6},{4,0},{6,2},{8,12},{10,14},{12,8},{14,10},{1,5},{3,7},... | collective-permute-start | bytes 393224 | tf_op jit(solution)/shard_map/ppermute | solution.py:538
  51.2 5.6 %collective-permute-start.9 = (bf16[2,16,2048]{2,1,0:T(8,128)(2,1)S(1)}, bf16[2,16,2048]{2,1,0:T(8,128)(2,1)S(1)}, u32[]{:S(2)}, u32[]{:S(2)}) collective-permute-start(bf16[2,16,2048]{2,1,0:T(8,128)(2,1)S(1)} %collective-permute-done.8.refs_2_), channel_id=1, source_target_pairs={{0,4},{2,6},{4,0},{6,2},{8,12},{10,14},{12,8},{14,10},{1,5},{3,7},... | collective-permute-start | bytes 393224 | tf_op jit(solution)/shard_map/ppermute | solution.py:538
  53.0 6.3 %collective-permute-start.10 = (bf16[2,16,2048]{2,1,0:T(8,128)(2,1)S(1)}, bf16[2,16,2048]{2,1,0:T(8,128)(2,1)S(1)}, u32[]{:S(2)}, u32[]{:S(2)}) collective-permute-start(bf16[2,16,2048]{2,1,0:T(8,128)(2,1)S(1)} %get-tuple-element.19.refs_0_), channel_id=1, source_target_pairs={{0,2},{2,0},{4,6},{6,4},{8,10},{10,8},{12,14},{14,12},{1,3},{3,1},... | collective-permute-start | bytes 393224 | tf_op jit(solution)/shard_map/ppermute | solution.py:538
  54.7 6.0 %collective-permute-start.12 = (bf16[2,16,2048]{2,1,0:T(8,128)(2,1)S(1)}, bf16[2,16,2048]{2,1,0:T(8,128)(2,1)S(1)}, u32[]{:S(2)}, u32[]{:S(2)}) collective-permute-start(bf16[2,16,2048]{2,1,0:T(8,128)(2,1)S(1)} %collective-permute-done.8.refs_2_), channel_id=1, source_target_pairs={{0,2},{2,0},{4,6},{6,4},{8,10},{10,8},{12,14},{14,12},{1,3},{3,1},... | collective-permute-start | bytes 393224 | tf_op jit(solution)/shard_map/ppermute | solution.py:538
  55.0 7.1 %collective-permute-start.11 = (bf16[2,16,2048]{2,1,0:T(8,128)(2,1)S(1)}, bf16[2,16,2048]{2,1,0:T(8,128)(2,1)S(1)}, u32[]{:S(2)}, u32[]{:S(2)}) collective-permute-start(bf16[2,16,2048]{2,1,0:T(8,128)(2,1)S(1)} %collective-permute-done.7.refs_1_), channel_id=1, source_target_pairs={{0,2},{2,0},{4,6},{6,4},{8,10},{10,8},{12,14},{14,12},{1,3},{3,1},... | collective-permute-start | bytes 393224 | tf_op jit(solution)/shard_map/ppermute | solution.py:538
  56.7 6.8 %collective-permute-start.13 = (bf16[2,16,2048]{2,1,0:T(8,128)(2,1)S(1)}, bf16[2,16,2048]{2,1,0:T(8,128)(2,1)S(1)}, u32[]{:S(2)}, u32[]{:S(2)}) collective-permute-start(bf16[2,16,2048]{2,1,0:T(8,128)(2,1)S(1)} %collective-permute-done.9.refs_3_), channel_id=1, source_target_pairs={{0,2},{2,0},{4,6},{6,4},{8,10},{10,8},{12,14},{14,12},{1,3},{3,1},... | collective-permute-start | bytes 393224 | tf_op jit(solution)/shard_map/ppermute | solution.py:538
  64.9 2.0 %collective-permute-start.14 = (f32[2,128,512]{2,1,0:T(8,128)S(1)}, f32[2,128,512]{2,1,0:T(8,128)S(1)}, u32[]{:S(2)}, u32[]{:S(2)}) collective-permute-start(f32[2,128,512]{2,1,0:T(8,128)S(1)} %get-tuple-element.22), channel_id=1, source_target_pairs={{0,1},{1,0},{2,3},{3,2},{4,5},{5,4},{6,7},{7,6},{8,9},{9,8},{10,11... | collective-permute-start | bytes 1572872 | tf_op jit(solution)/shard_map/ppermute | solution.py:551

commit v9 on v8

--- a/solution.py
+++ b/solution.py
@@ -310,28 +310,35 @@
     return [high, middle, x - high - middle]
 
 
-def arrived_kernel(npool, pair, me_ref, own_ref, *refs):
-    blocks = refs[:npool]
-    pages_ref, out_ref, queries = refs[npool:]
-    items = npool * pair
+def arrived_kernel(npool, pair, flip, me_ref, own_ref, pages_ref, *refs):
+    half = npool // 2
+    blocks = refs[:half]
+    before_ref, out_ref, queries = (None,) * (1 - flip) + refs[half:]
+    every, items = npool * pair, half * pair
     _, _, heads, page_len, head_dim = pages_ref.shape
     rows, block = blocks[0].shape[0] - 1, blocks[0].shape[1]
     group = block // heads
     together = LANES // block
     me = me_ref[0]
-    owners = [owner_of(me, which) for which in block_order(npool)]
+    owners = [owner_of(me, npool, apart, flip) for apart in range(half)]
+    if flip:
+        for apart in range(half):
+            out_ref[owner_of(me, npool, apart, 0)] = before_ref[apart]
+        where = owners
+    else:
+        where = range(half)
     lane = lax.broadcasted_iota(I32, (1, LANES), 1)
     codes = [x[rows, :STAT_ROWS, :].astype(F32) for x in blocks]
     codes = [x[0:1] * CODE + x[1:2] for x in codes]
     number, seen, request = [], [], []
     for x in range(items):
         at = owners[x // pair] * pair + x % pair
-        slot = own_ref[2 * items + at]
+        slot = own_ref[2 * every + at]
         code = jnp.maximum(read_scalar(codes[x // pair], lane == slot), 0)
         reader, left = code // CODE, code % CODE
         queries[x * block : (x + 1) * block, :] = blocks[x // pair][reader]
         number.append(own_ref[at])
-        seen.append(jnp.minimum(left, own_ref[items + at]))
+        seen.append(jnp.minimum(left, own_ref[every + at]))
         request.append(jnp.where(slot >= 0, reader, -1))
     token = lax.broadcasted_iota(I32, (page_len, LANES), 0)
     for i in range(items // together):
@@ -351,27 +358,29 @@
             both = [pages_ref[number[x], 1, k] for k in range(heads)]
             both = weighted_values(weights[c * block : (c + 1) * block, :], both)
             at = (x % pair) * block
-            out_ref[owners[x // pair], at : at + block, :] = both.astype(BF16)
+            out_ref[where[x // pair], at : at + block, :] = both.astype(BF16)
         for place in sorted({x // pair for x in own}):
-            out_ref[owners[place], pair * block : pair * block + STAT_ROWS, :] = stats
-
-
-def arrived_attention(me, own, blocks, arrived):
-    npool = len(blocks)
+            out_ref[where[place], pair * block : pair * block + STAT_ROWS, :] = stats
+
+
+def arrived_attention(me, own, blocks, arrived, before=None):
+    flip = 0 if before is None else 1
+    half = len(blocks)
+    npool = 2 * half
     head_dim = arrived.shape[4]
     block = blocks[0].shape[1]
-    items = own.shape[0] // 3
-    pair = items // npool
-    return pl.pallas_call(
-        functools.partial(arrived_kernel, npool, pair),
-        out_shape=jax.ShapeDtypeStruct((npool, pair * block + STAT_ROWS, head_dim), BF16),
-        in_specs=[SMEM] * 2 + [VMEM] * (npool + 1),
+    pair = own.shape[0] // 3 // npool
+    earlier = [before] if flip else []
+    return pl.pallas_call(
+        functools.partial(arrived_kernel, npool, pair, flip),
+        out_shape=jax.ShapeDtypeStruct((half * (1 + flip), pair * block + STAT_ROWS, head_dim), BF16),
+        in_specs=[SMEM] * 2 + [VMEM] * (1 + half + flip),
         out_specs=VMEM,
-        scratch_shapes=[pltpu.VMEM((items * block, head_dim), BF16)],
-        compiler_params=PARAMS,
-        cost_estimate=pl.CostEstimate(flops=200_000_000, bytes_accessed=4_000_000, transcendentals=70_000),
+        scratch_shapes=[pltpu.VMEM((half * pair * block, head_dim), BF16)],
+        compiler_params=PARAMS,
+        cost_estimate=pl.CostEstimate(flops=100_000_000, bytes_accessed=2_000_000, transcendentals=35_000),
         name="arrived_attention",
-    )(me, own, *blocks, arrived)
+    )(me, own, arrived, *blocks, *earlier)
 
 
 def merge_kernel(pair, heads, me_ref, parts_ref, o_ref, stat_ref, out_ref, mixed, top, total, turned):
@@ -463,8 +472,8 @@
     weight_ref, out_ref, lhs = refs[npool:]
     steps, rows, _ = blocks[0].shape
     every = npool * rows
-    for x, which in enumerate(block_order(npool)):
-        owner = owner_of(place_ref[0], which)
+    for x, (apart, flip) in enumerate(block_order(npool)):
+        owner = owner_of(place_ref[0], npool, apart, flip)
         for s in range(steps):
             lhs[pl.ds(pl.multiple_of(s * every + owner * rows, rows), rows), :] = blocks[x][s]
     multiply(lhs, weight_ref, out_ref, 1 - place_ref[1])
@@ -518,33 +527,34 @@
 
 
 def block_order(npool):
-    return [2 * apart + flip for flip in (0, 1) for apart in range(npool // 2)]
-
-
-def owner_of(me, which):
-    return jnp.bitwise_xor(me, which)
+    return [(apart, flip) for flip in (0, 1) for apart in range(npool // 2)]
+
+
+def owner_of(me, npool, apart, flip):
+    half = npool // 2
+    pair, side = me // 2, me % 2
+    side = 1 - side if flip else side
+    return lax.rem(pair + half - apart, half) * 2 + side
 
 
 def place_of(me, npool, holder):
-    which = jnp.bitwise_xor(me, holder)
-    return (which % 2) * (npool // 2) + which // 2
+    half = npool // 2
+    apart = lax.rem(holder // 2 - me // 2 + half, half)
+    flip = lax.rem(me + holder, 2)
+    return flip * half + apart
 
 
 def in_hbm(x):
     return pltpu.with_memory_space_constraint(x, pltpu.HBM)
 
 
-def gathered(x, npool, later):
-    swap = lambda x, by: lax.ppermute(x, "pool", [(i, i ^ by) for i in range(npool)])
-    straight = {0: later}
-    apart = npool // 4
-    while apart:
-        for i in list(straight):
-            own = x if i == 0 and apart == npool // 4 else straight[i]
-            straight[i + apart] = swap(own, 2 * apart)
-        apart //= 2
-    straight = [straight[i] for i in range(npool // 2)]
-    return straight + [swap(y, 1) for y in straight]
+def gathered(x, npool, later=None):
+    half = npool // 2
+    later = x if later is None else later
+    ahead = lambda x, by: lax.ppermute(x, "pool", [(i, (i + 2 * by) % npool) for i in range(npool)])
+    across = lambda x: lax.ppermute(x, "pool", [(i, i ^ 1) for i in range(npool)])
+    straight = [x] + [ahead(x if by == half // 2 else later, by) for by in range(1, half)]
+    return straight + [across(y) for y in straight]
 
 
 def swap_halves(x):
@@ -578,7 +588,9 @@
     )
     asked_all = gathered(asked, npool, again)
     local = local_attention(table, context_lengths, cache_fill, asked, new_kv, cache_kv, tabs)
-    parts = arrived_attention(place, own, asked_all, arrived)
+    half = npool // 2
+    parts = arrived_attention(place, own, asked_all[:half], arrived)
+    parts = arrived_attention(place, own, asked_all[half:], arrived, parts)
     parts = lax.all_to_all(parts, "pool", split_axis=0, concat_axis=0, tiled=True)
     attention = merged(place, parts, local, queries.shape, heads, pair)
     weight, again = fetched(out_weight, attention)

time: 68.2 us -> 66.7 us (0.978)
  waiting for transfers between devices: 18.6 us -> 16.7 us
  Pallas kernels: 20.3 us -> 21.2 us
    ppermute x14, waiting for transfers between devices: 17.4 us -> 15.5 us  [the longest x8 8.86 us: gathered(): lax.ppermute(x, 'pool', [(i, i ^ 1) for i in range(npool)])]
    pallas_call x1 -> x2, Pallas kernels: 2.87 us -> 3.78 us  [arrived_attention(): pl.pallas_call(functools.partial(arrived_kernel, npool, pair, flip), out_...]
    ppermute x14, starting transfers between devices: 22 us -> 21.3 us  [the longest x8 10.7 us: gathered(): lax.ppermute(x, 'pool', [(i, i ^ 1) for i in range(npool)])]
  transfers between devices with their start and end apart: 16 -> 16, of which waited for: 13 -> 11; matrix products, arithmetic and copies ran while one was open for 0% -> 0% of each run, Pallas kernels for 20% -> 23%
where the time goes in v9:
time: 66.7 us; the launch traced here: 66.2 us
  starting transfers between devices  27.3 us (41%)
  Pallas kernels  21.2 us (32%)
  waiting for transfers between devices  16.7 us (25%)
  other arithmetic  0.86 us (1%)
    ppermute x8, starting transfers between devices, gathered(): lax.ppermute(x, 'pool', [(i, i ^ 1) for i in range(npool)])  10.7 us
    ppermute x6, starting transfers between devices, gathered(): lax.ppermute(x, 'pool', [(i, (i + 2 * by) % npool) for i in range(npool)])  10.7 us
    ppermute x8, waiting for transfers between devices, gathered(): lax.ppermute(x, 'pool', [(i, i ^ 1) for i in range(npool)])  8.86 us
    pallas_call x1, Pallas kernels, local_attention(): pl.pallas_call(functools.partial(local_kernel, page_len, heads), out_shap...  6.93 us
    ppermute x6, waiting for transfers between devices, gathered(): lax.ppermute(x, 'pool', [(i, (i + 2 * by) % npool) for i in range(npool)])  6.67 us
    all_to_all x1, starting transfers between devices, shards(): lax.all_to_all(parts, 'pool', split_axis=0, concat_axis=0, tiled=True)  5.89 us
    pallas_call x2, Pallas kernels, arrived_attention(): pl.pallas_call(functools.partial(arrived_kernel, npool, pair, flip), out_...  3.78 us
    pallas_call x1, Pallas kernels, rotated_pages(): pl.pallas_call(functools.partial(rope_kernel, npool, cache_pages, per), g...  2.96 us
  transfers between devices with their start and end apart: 16, of which 11 were waited for; matrix products, arithmetic and copies ran while one was open for 0% of the time, Pallas kernels for 23%

profile of v9, /device:TPU:0, one launch (start us, length us, event | category | flops | bytes accessed | tf_op | source)
XLA Modules:
  0.0 66.2 jit_solution(6734490114717190848)
XLA Ops:
  1.2 4.1 %collective-permute-start.3 = (bf16[17,32,128]{2,1,0:T(8,128)(2,1)S(1)}, bf16[17,32,128]{2,1,0:T(8,128)(2,1)S(1)}, u32[]{:S(2)}, u32[]{:S(2)}) collective-permute-start(bf16[17,32,128]{2,1,0:T(8,128)(2,1)S(1)} %asked_queries.1.x_ref.refs_0_.q_ref), channel_id=1, source_target_pairs={{0,8},{2,10},{4,12},{6,14},{8,0},{10,2},{12,4},{14,6},{1,9},{3,11}... | collective-permute-start | bytes 417800 | tf_op jit(solution)/shard_map/ppermute | solution.py:554
  5.3 3.0 %rope_pages.1 = (bf16[16,2,2,128,128]{4,3,2,1,0:T(8,128)(2,1)S(1)}, s32[48]{0:T(128)S(1)}, bf16[17,32,128]{2,1,0:T(8,128)(2,1)S(1)}) custom-call(s32[16]{0:T(128)} %slot_ref.1, s32[1,4]{1,0:T(1,128)} %len_ref.1, bf16[17,32,128]{2,1,0:T(8,128)(2,1)S(1)} %asked_queries.1.x_ref.refs_0_.q_ref, bf16[16,2,2,128,128]{4,3,2,1,0:T(8,128)(2,1)} %pages_ref.1, ...), custom_call_target="tpu_custom_call" | custom-call | flops 6000000 | bytes 2000000 | tf_op jit(solution)/shard_map/rope_pages/pallas_call | solution.py:87
  8.3 1.4 %collective-permute-start.5 = (bf16[17,32,128]{2,1,0:T(8,128)(2,1)S(1)}, bf16[17,32,128]{2,1,0:T(8,128)(2,1)S(1)}, u32[]{:S(2)}, u32[]{:S(2)}) collective-permute-start(bf16[17,32,128]{2,1,0:T(8,128)(2,1)S(1)} %get-tuple-element.16), channel_id=1, source_target_pairs={{0,12},{2,14},{4,0},{6,2},{8,4},{10,6},{12,8},{14,10},{1,13},{3,15... | collective-permute-start | bytes 417800 | tf_op jit(solution)/shard_map/ppermute | solution.py:554
  10.4 1.5 %collective-permute-start = (bf16[17,32,128]{2,1,0:T(8,128)(2,1)S(1)}, bf16[17,32,128]{2,1,0:T(8,128)(2,1)S(1)}, u32[]{:S(2)}, u32[]{:S(2)}) collective-permute-start(bf16[17,32,128]{2,1,0:T(8,128)(2,1)S(1)} %asked_queries.1.x_ref.refs_0_.q_ref), channel_id=1, source_target_pairs={{0,2},{2,0},{4,6},{6,4},{8,10},{10,8},{12,14},{14,12},{1,3},{3,1},... | collective-permute-start | bytes 417800 | tf_op jit(solution)/shard_map/ppermute | solution.py:555
  12.4 1.6 %collective-permute-start.4 = (bf16[17,32,128]{2,1,0:T(8,128)(2,1)S(1)}, bf16[17,32,128]{2,1,0:T(8,128)(2,1)S(1)}, u32[]{:S(2)}, u32[]{:S(2)}) collective-permute-start(bf16[17,32,128]{2,1,0:T(8,128)(2,1)S(1)} %collective-permute-done.3.refs_2_), channel_id=1, source_target_pairs={{0,2},{2,0},{4,6},{6,4},{8,10},{10,8},{12,14},{14,12},{1,3},{3,1},... | collective-permute-start | bytes 417800 | tf_op jit(solution)/shard_map/ppermute | solution.py:555
  14.0 3.9 %collective-permute-done.5.refs_3_ = bf16[17,32,128]{2,1,0:T(8,128)(2,1)S(1)} collective-permute-done((bf16[17,32,128]{2,1,0:T(8,128)(2,1)S(1)}, bf16[17,32,128]{2,1,0:T(8,128)(2,1)S(1)}, u32[]{:S(2)}, u32[]{:S(2)}) %collective-permute-start.5) | collective-permute-done | bytes 139296 | tf_op jit(solution)/shard_map/ppermute | solution.py:554
  18.0 1.6 %collective-permute-start.6 = (bf16[17,32,128]{2,1,0:T(8,128)(2,1)S(1)}, bf16[17,32,128]{2,1,0:T(8,128)(2,1)S(1)}, u32[]{:S(2)}, u32[]{:S(2)}) collective-permute-start(bf16[17,32,128]{2,1,0:T(8,128)(2,1)S(1)} %collective-permute-done.5.refs_3_), channel_id=1, source_target_pairs={{0,2},{2,0},{4,6},{6,4},{8,10},{10,8},{12,14},{14,12},{1,3},{3,1},... | collective-permute-start | bytes 417800 | tf_op jit(solution)/shard_map/ppermute | solution.py:555
  20.1 1.6 %arrived_attention.2.refs_4_ = bf16[4,80,128]{2,1,0:T(8,128)(2,1)S(1)} custom-call(s32[2]{0:T(128)S(1)} %pad_add_fusion.me_ref.place_ref, s32[48]{0:T(128)S(1)} %get-tuple-element.14.own_ref, bf16[16,2,2,128,128]{4,3,2,1,0:T(8,128)(2,1)S(1)} %get-tuple-element.15.pages_ref, bf16[17,32,128]{2,1,0:T(8,128)(2,1)S(1)} %asked_queries.1.x_ref.refs_0_.q_ref, ...), custom_call_target="tpu_custom_call" | custom-call | flops 100000000 | bytes 2000000 | tf_op jit(solution)/shard_map/arrived_attention/pallas_call | solution.py:374
  21.6 2.9 %collective-permute-done.6.refs_3_ = bf16[17,32,128]{2,1,0:T(8,128)(2,1)S(1)} collective-permute-done((bf16[17,32,128]{2,1,0:T(8,128)(2,1)S(1)}, bf16[17,32,128]{2,1,0:T(8,128)(2,1)S(1)}, u32[]{:S(2)}, u32[]{:S(2)}) %collective-permute-start.6) | collective-permute-done | bytes 139296 | tf_op jit(solution)/shard_map/ppermute | solution.py:555
  24.5 2.0 %collective-permute-done.2.refs_1_ = bf16[17,32,128]{2,1,0:T(8,128)(2,1)S(1)} collective-permute-done((bf16[17,32,128]{2,1,0:T(8,128)(2,1)S(1)}, bf16[17,32,128]{2,1,0:T(8,128)(2,1)S(1)}, u32[]{:S(2)}, u32[]{:S(2)}) %collective-permute-start.2) | collective-permute-done | bytes 139296 | tf_op jit(solution)/shard_map/ppermute | solution.py:555
  26.5 2.2 %arrived_attention.3 = bf16[8,80,128]{2,1,0:T(8,128)(2,1)} custom-call(s32[2]{0:T(128)S(1)} %pad_add_fusion.me_ref.place_ref, s32[48]{0:T(128)S(1)} %get-tuple-element.14.own_ref, bf16[16,2,2,128,128]{4,3,2,1,0:T(8,128)(2,1)S(1)} %get-tuple-element.15.pages_ref, bf16[17,32,128]{2,1,0:T(8,128)(2,1)S(1)} %collective-permute-done.refs_0_, ...), custom_call_target="tpu_custom_call" | custom-call | flops 100000000 | bytes 2000000 | tf_op jit(solution)/shard_map/arrived_attention/pallas_call | solution.py:374
  28.7 5.9 %all-to-all-start = ((bf16[8,80,128]{2,1,0:T(8,128)(2,1)}), bf16[8,80,128]{2,1,0:T(8,128)(2,1)S(1)}, u32[]{:S(2)}, u32[]{:S(2)}) async-start(bf16[8,80,128]{2,1,0:T(8,128)(2,1)} %arrived_attention.3), calls=%async_computation | async-start | bytes 327680 | tf_op jit(solution)/shard_map/all_to_all | solution.py:594
  34.6 6.9 %local_attention.1 = (f32[512,128]{1,0:T(8,128)S(1)}, f32[512,128]{1,0:T(8,128)S(1)}) custom-call(s32[3,16]{1,0:T(4,128)} %bitcast.4, s32[16]{0:T(128)} %context_ref.3, s32[48]{0:T(128)} %fill_ref.1, bf16[17,32,128]{2,1,0:T(8,128)(2,1)S(1)} %asked_queries.1.x_ref.refs_0_.q_ref, bf16[2,16,512]{2,1,0:T(8,128)(2,1)S(1)} %reshape.3.new_ref, ...), custom_call_target="tpu_custom_call" | custom-call | flops 800000000 | bytes 12000000 | tf_op jit(solution)/shard_map/local_attention/pallas_call | solution.py:284
  42.1 1.5 %merge.1.x_ref.refs_0_ = bf16[2,16,2048]{2,1,0:T(8,128)(2,1)S(1)} custom-call(s32[2]{0:T(128)S(1)} %pad_add_fusion.me_ref.place_ref, bf16[8,80,128]{2,1,0:T(8,128)(2,1)S(1)} %all-to-all-done.parts_ref, f32[512,128]{1,0:T(8,128)S(1)} %get-tuple-element.17.o_ref, f32[512,128]{1,0:T(8,128)S(1)} %get-tuple-element.18.stat_ref), custom_call_target="tpu_custom_call" | custom-call | flops 2000000 | bytes 1500000 | tf_op jit(solution)/shard_map/merge/pallas_call | solution.py:434
  43.7 2.4 %collective-permute-start.8 = (bf16[2,16,2048]{2,1,0:T(8,128)(2,1)S(1)}, bf16[2,16,2048]{2,1,0:T(8,128)(2,1)S(1)}, u32[]{:S(2)}, u32[]{:S(2)}) collective-permute-start(bf16[2,16,2048]{2,1,0:T(8,128)(2,1)S(1)} %merge.1.x_ref.refs_0_), channel_id=1, source_target_pairs={{0,8},{2,10},{4,12},{6,14},{8,0},{10,2},{12,4},{14,6},{1,9},{3,11}... | collective-permute-start | bytes 393224 | tf_op jit(solution)/shard_map/ppermute | solution.py:554
  46.1 2.2 %fetch_weight.1 = (bf16[2048,1024]{1,0:T(8,128)(2,1)S(1)}, bf16[2,16,2048]{2,1,0:T(8,128)(2,1)S(1)}) custom-call(bf16[2048,1024]{1,0:T(8,128)(2,1)} %weight_ref.1, bf16[2,16,2048]{2,1,0:T(8,128)(2,1)S(1)} %merge.1.x_ref.refs_0_), custom_call_target="tpu_custom_call" | custom-call | bytes 8388608 | tf_op jit(solution)/shard_map/fetch_weight/pallas_call | solution.py:458
  48.3 1.5 %collective-permute-start.9 = (bf16[2,16,2048]{2,1,0:T(8,128)(2,1)S(1)}, bf16[2,16,2048]{2,1,0:T(8,128)(2,1)S(1)}, u32[]{:S(2)}, u32[]{:S(2)}) collective-permute-start(bf16[2,16,2048]{2,1,0:T(8,128)(2,1)S(1)} %get-tuple-element.19), channel_id=1, source_target_pairs={{0,12},{2,14},{4,0},{6,2},{8,4},{10,6},{12,8},{14,10},{1,13},{3,15... | collective-permute-start | bytes 393224 | tf_op jit(solution)/shard_map/ppermute | solution.py:554
  50.4 1.5 %collective-permute-start.10 = (bf16[2,16,2048]{2,1,0:T(8,128)(2,1)S(1)}, bf16[2,16,2048]{2,1,0:T(8,128)(2,1)S(1)}, u32[]{:S(2)}, u32[]{:S(2)}) collective-permute-start(bf16[2,16,2048]{2,1,0:T(8,128)(2,1)S(1)} %merge.1.x_ref.refs_0_), channel_id=1, source_target_pairs={{0,2},{2,0},{4,6},{6,4},{8,10},{10,8},{12,14},{14,12},{1,3},{3,1},... | collective-permute-start | bytes 393224 | tf_op jit(solution)/shard_map/ppermute | solution.py:555
  52.9 1.5 %collective-permute-done.9.refs_3_ = bf16[2,16,2048]{2,1,0:T(8,128)(2,1)S(1)} collective-permute-done((bf16[2,16,2048]{2,1,0:T(8,128)(2,1)S(1)}, bf16[2,16,2048]{2,1,0:T(8,128)(2,1)S(1)}, u32[]{:S(2)}, u32[]{:S(2)}) %collective-permute-start.9) | collective-permute-done | bytes 131104 | tf_op jit(solution)/shard_map/ppermute | solution.py:554
  54.5 1.5 %collective-permute-start.13 = (bf16[2,16,2048]{2,1,0:T(8,128)(2,1)S(1)}, bf16[2,16,2048]{2,1,0:T(8,128)(2,1)S(1)}, u32[]{:S(2)}, u32[]{:S(2)}) collective-permute-start(bf16[2,16,2048]{2,1,0:T(8,128)(2,1)S(1)} %collective-permute-done.9.refs_3_), channel_id=1, source_target_pairs={{0,2},{2,0},{4,6},{6,4},{8,10},{10,8},{12,14},{14,12},{1,3},{3,1},... | collective-permute-start | bytes 393224 | tf_op jit(solution)/shard_map/ppermute | solution.py:555
  56.6 1.5 %collective-permute-start.11 = (bf16[2,16,2048]{2,1,0:T(8,128)(2,1)S(1)}, bf16[2,16,2048]{2,1,0:T(8,128)(2,1)S(1)}, u32[]{:S(2)}, u32[]{:S(2)}) collective-permute-start(bf16[2,16,2048]{2,1,0:T(8,128)(2,1)S(1)} %collective-permute-done.7.refs_1_), channel_id=1, source_target_pairs={{0,2},{2,0},{4,6},{6,4},{8,10},{10,8},{12,14},{14,12},{1,3},{3,1},... | collective-permute-start | bytes 393224 | tf_op jit(solution)/shard_map/ppermute | solution.py:555
  58.6 2.1 %collective-permute-done.13.refs_7_ = bf16[2,16,2048]{2,1,0:T(8,128)(2,1)S(1)} collective-permute-done((bf16[2,16,2048]{2,1,0:T(8,128)(2,1)S(1)}, bf16[2,16,2048]{2,1,0:T(8,128)(2,1)S(1)}, u32[]{:S(2)}, u32[]{:S(2)}) %collective-permute-start.13) | collective-permute-done | bytes 131104 | tf_op jit(solution)/shard_map/ppermute | solution.py:555
  60.7 1.4 %collective-permute-done.11.refs_5_ = bf16[2,16,2048]{2,1,0:T(8,128)(2,1)S(1)} collective-permute-done((bf16[2,16,2048]{2,1,0:T(8,128)(2,1)S(1)}, bf16[2,16,2048]{2,1,0:T(8,128)(2,1)S(1)}, u32[]{:S(2)}, u32[]{:S(2)}) %collective-permute-start.11) | collective-permute-done | bytes 131104 | tf_op jit(solution)/shard_map/ppermute | solution.py:555
  62.1 1.3 %project_other.1 = (f32[2,128,512]{2,1,0:T(8,128)S(1)}, bf16[256,2048]{1,0:T(8,128)(2,1)S(1)}) custom-call(s32[2]{0:T(128)S(1)} %pad_add_fusion.me_ref.place_ref, bf16[2,16,2048]{2,1,0:T(8,128)(2,1)S(1)} %merge.1.x_ref.refs_0_, bf16[2,16,2048]{2,1,0:T(8,128)(2,1)S(1)} %collective-permute-done.7.refs_1_, ...), custom_call_target="tpu_custom_call" | custom-call | flops 536870912 | bytes 4000000 | tf_op jit(solution)/shard_map/project_other/pallas_call | solution.py:497
  (22 shorter events, 9.2 us)
Async XLA Ops:
  1.2 33.4 %copy-start = (bf16[2,16,2,2,128]{4,3,2,1,0:T(2,128)(2,1)S(1)}, bf16[2,16,2,2,128]{4,3,2,1,0:T(2,128)(2,1)}, u32[]{:S(2)}) copy-start(bf16[2,16,2,2,128]{4,3,2,1,0:T(2,128)(2,1)} %param.24) | copy-start | bytes 98308
  1.2 11.2 %collective-permute-start.3 = (bf16[17,32,128]{2,1,0:T(8,128)(2,1)S(1)}, bf16[17,32,128]{2,1,0:T(8,128)(2,1)S(1)}, u32[]{:S(2)}, u32[]{:S(2)}) collective-permute-start(bf16[17,32,128]{2,1,0:T(8,128)(2,1)S(1)} %asked_queries.1.x_ref.refs_0_.q_ref), channel_id=1, source_target_pairs={{0,8},{2,10},{4,12},{6,14},{8,0},{10,2},{12,4},{14,6},{1,9},{3,11}... | collective-permute-start | bytes 417800 | tf_op jit(solution)/shard_map/ppermute | solution.py:554
  8.3 9.7 %collective-permute-start.5 = (bf16[17,32,128]{2,1,0:T(8,128)(2,1)S(1)}, bf16[17,32,128]{2,1,0:T(8,128)(2,1)S(1)}, u32[]{:S(2)}, u32[]{:S(2)}) collective-permute-start(bf16[17,32,128]{2,1,0:T(8,128)(2,1)S(1)} %get-tuple-element.16), channel_id=1, source_target_pairs={{0,12},{2,14},{4,0},{6,2},{8,4},{10,6},{12,8},{14,10},{1,13},{3,15... | collective-permute-start | bytes 417800 | tf_op jit(solution)/shard_map/ppermute | solution.py:554
  9.7 9.8 %collective-permute-start.1 = (bf16[17,32,128]{2,1,0:T(8,128)(2,1)S(1)}, bf16[17,32,128]{2,1,0:T(8,128)(2,1)S(1)}, u32[]{:S(2)}, u32[]{:S(2)}) collective-permute-start(bf16[17,32,128]{2,1,0:T(8,128)(2,1)S(1)} %get-tuple-element.16), channel_id=1, source_target_pairs={{0,4},{2,6},{4,8},{6,10},{8,12},{10,14},{12,0},{14,2},{1,5},{3,7},... | collective-permute-start | bytes 417800 | tf_op jit(solution)/shard_map/ppermute | solution.py:554
  10.4 11.2 %collective-permute-start = (bf16[17,32,128]{2,1,0:T(8,128)(2,1)S(1)}, bf16[17,32,128]{2,1,0:T(8,128)(2,1)S(1)}, u32[]{:S(2)}, u32[]{:S(2)}) collective-permute-start(bf16[17,32,128]{2,1,0:T(8,128)(2,1)S(1)} %asked_queries.1.x_ref.refs_0_.q_ref), channel_id=1, source_target_pairs={{0,2},{2,0},{4,6},{6,4},{8,10},{10,8},{12,14},{14,12},{1,3},{3,1},... | collective-permute-start | bytes 417800 | tf_op jit(solution)/shard_map/ppermute | solution.py:555
  12.4 9.2 %collective-permute-start.4 = (bf16[17,32,128]{2,1,0:T(8,128)(2,1)S(1)}, bf16[17,32,128]{2,1,0:T(8,128)(2,1)S(1)}, u32[]{:S(2)}, u32[]{:S(2)}) collective-permute-start(bf16[17,32,128]{2,1,0:T(8,128)(2,1)S(1)} %collective-permute-done.3.refs_2_), channel_id=1, source_target_pairs={{0,2},{2,0},{4,6},{6,4},{8,10},{10,8},{12,14},{14,12},{1,3},{3,1},... | collective-permute-start | bytes 417800 | tf_op jit(solution)/shard_map/ppermute | solution.py:555
  18.0 6.5 %collective-permute-start.6 = (bf16[17,32,128]{2,1,0:T(8,128)(2,1)S(1)}, bf16[17,32,128]{2,1,0:T(8,128)(2,1)S(1)}, u32[]{:S(2)}, u32[]{:S(2)}) collective-permute-start(bf16[17,32,128]{2,1,0:T(8,128)(2,1)S(1)} %collective-permute-done.5.refs_3_), channel_id=1, source_target_pairs={{0,2},{2,0},{4,6},{6,4},{8,10},{10,8},{12,14},{14,12},{1,3},{3,1},... | collective-permute-start | bytes 417800 | tf_op jit(solution)/shard_map/ppermute | solution.py:555
  19.5 6.9 %collective-permute-start.2 = (bf16[17,32,128]{2,1,0:T(8,128)(2,1)S(1)}, bf16[17,32,128]{2,1,0:T(8,128)(2,1)S(1)}, u32[]{:S(2)}, u32[]{:S(2)}) collective-permute-start(bf16[17,32,128]{2,1,0:T(8,128)(2,1)S(1)} %collective-permute-done.1.refs_1_), channel_id=1, source_target_pairs={{0,2},{2,0},{4,6},{6,4},{8,10},{10,8},{12,14},{14,12},{1,3},{3,1},... | collective-permute-start | bytes 417800 | tf_op jit(solution)/shard_map/ppermute | solution.py:555
  28.7 13.4 %all-to-all-start = ((bf16[8,80,128]{2,1,0:T(8,128)(2,1)}), bf16[8,80,128]{2,1,0:T(8,128)(2,1)S(1)}, u32[]{:S(2)}, u32[]{:S(2)}) async-start(bf16[8,80,128]{2,1,0:T(8,128)(2,1)} %arrived_attention.3), calls=%async_computation | async-start | bytes 327680 | tf_op jit(solution)/shard_map/all_to_all | solution.py:594
  43.7 8.2 %collective-permute-start.8 = (bf16[2,16,2048]{2,1,0:T(8,128)(2,1)S(1)}, bf16[2,16,2048]{2,1,0:T(8,128)(2,1)S(1)}, u32[]{:S(2)}, u32[]{:S(2)}) collective-permute-start(bf16[2,16,2048]{2,1,0:T(8,128)(2,1)S(1)} %merge.1.x_ref.refs_0_), channel_id=1, source_target_pairs={{0,8},{2,10},{4,12},{6,14},{8,0},{10,2},{12,4},{14,6},{1,9},{3,11}... | collective-permute-start | bytes 393224 | tf_op jit(solution)/shard_map/ppermute | solution.py:554
  48.3 6.2 %collective-permute-start.9 = (bf16[2,16,2048]{2,1,0:T(8,128)(2,1)S(1)}, bf16[2,16,2048]{2,1,0:T(8,128)(2,1)S(1)}, u32[]{:S(2)}, u32[]{:S(2)}) collective-permute-start(bf16[2,16,2048]{2,1,0:T(8,128)(2,1)S(1)} %get-tuple-element.19), channel_id=1, source_target_pairs={{0,12},{2,14},{4,0},{6,2},{8,4},{10,6},{12,8},{14,10},{1,13},{3,15... | collective-permute-start | bytes 393224 | tf_op jit(solution)/shard_map/ppermute | solution.py:554
  49.8 6.8 %collective-permute-start.7 = (bf16[2,16,2048]{2,1,0:T(8,128)(2,1)S(1)}, bf16[2,16,2048]{2,1,0:T(8,128)(2,1)S(1)}, u32[]{:S(2)}, u32[]{:S(2)}) collective-permute-start(bf16[2,16,2048]{2,1,0:T(8,128)(2,1)S(1)} %get-tuple-element.19), channel_id=1, source_target_pairs={{0,4},{2,6},{4,8},{6,10},{8,12},{10,14},{12,0},{14,2},{1,5},{3,7},... | collective-permute-start | bytes 393224 | tf_op jit(solution)/shard_map/ppermute | solution.py:554
  50.4 7.7 %collective-permute-start.10 = (bf16[2,16,2048]{2,1,0:T(8,128)(2,1)S(1)}, bf16[2,16,2048]{2,1,0:T(8,128)(2,1)S(1)}, u32[]{:S(2)}, u32[]{:S(2)}) collective-permute-start(bf16[2,16,2048]{2,1,0:T(8,128)(2,1)S(1)} %merge.1.x_ref.refs_0_), channel_id=1, source_target_pairs={{0,2},{2,0},{4,6},{6,4},{8,10},{10,8},{12,14},{14,12},{1,3},{3,1},... | collective-permute-start | bytes 393224 | tf_op jit(solution)/shard_map/ppermute | solution.py:555
  51.8 6.8 %collective-permute-start.12 = (bf16[2,16,2048]{2,1,0:T(8,128)(2,1)S(1)}, bf16[2,16,2048]{2,1,0:T(8,128)(2,1)S(1)}, u32[]{:S(2)}, u32[]{:S(2)}) collective-permute-start(bf16[2,16,2048]{2,1,0:T(8,128)(2,1)S(1)} %collective-permute-done.8.refs_2_), channel_id=1, source_target_pairs={{0,2},{2,0},{4,6},{6,4},{8,10},{10,8},{12,14},{14,12},{1,3},{3,1},... | collective-permute-start | bytes 393224 | tf_op jit(solution)/shard_map/ppermute | solution.py:555
  54.5 6.3 %collective-permute-start.13 = (bf16[2,16,2048]{2,1,0:T(8,128)(2,1)S(1)}, bf16[2,16,2048]{2,1,0:T(8,128)(2,1)S(1)}, u32[]{:S(2)}, u32[]{:S(2)}) collective-permute-start(bf16[2,16,2048]{2,1,0:T(8,128)(2,1)S(1)} %collective-permute-done.9.refs_3_), channel_id=1, source_target_pairs={{0,2},{2,0},{4,6},{6,4},{8,10},{10,8},{12,14},{14,12},{1,3},{3,1},... | collective-permute-start | bytes 393224 | tf_op jit(solution)/shard_map/ppermute | solution.py:555
  56.6 5.5 %collective-permute-start.11 = (bf16[2,16,2048]{2,1,0:T(8,128)(2,1)S(1)}, bf16[2,16,2048]{2,1,0:T(8,128)(2,1)S(1)}, u32[]{:S(2)}, u32[]{:S(2)}) collective-permute-start(bf16[2,16,2048]{2,1,0:T(8,128)(2,1)S(1)} %collective-permute-done.7.refs_1_), channel_id=1, source_target_pairs={{0,2},{2,0},{4,6},{6,4},{8,10},{10,8},{12,14},{14,12},{1,3},{3,1},... | collective-permute-start | bytes 393224 | tf_op jit(solution)/shard_map/ppermute | solution.py:555
  63.5 2.0 %collective-permute-start.14 = (f32[2,128,512]{2,1,0:T(8,128)S(1)}, f32[2,128,512]{2,1,0:T(8,128)S(1)}, u32[]{:S(2)}, u32[]{:S(2)}) collective-permute-start(f32[2,128,512]{2,1,0:T(8,128)S(1)} %get-tuple-element.22), channel_id=1, source_target_pairs={{0,1},{1,0},{2,3},{3,2},{4,5},{5,4},{6,7},{7,6},{8,9},{9,8},{10,11... | collective-permute-start | bytes 1572872 | tf_op jit(solution)/shard_map/ppermute | solution.py:561

commit v10 on v8

--- a/solution.py
+++ b/solution.py
@@ -31,13 +31,12 @@
 
 
 def rope_kernel(
-    npool, cache_pages, per, slot_ref, len_ref, x_ref, pages_ref, ct_ref, st_ref, cp_ref, sp_ref, out_ref, own_ref, x_out, count
+    npool, cache_pages, per, slot_ref, len_ref, pages_ref, ct_ref, st_ref, cp_ref, sp_ref, out_ref, own_ref, count
 ):
     _, _, heads, page_len, head_dim = pages_ref.shape
 
     @pl.when(pl.program_id(0) == 0)
     def _():
-        x_out[...] = x_ref[...]
         items = own_ref.shape[0] // 3
         for e in range(npool):
             count[e] = 0
@@ -79,35 +78,33 @@
     return number, fill
 
 
-def rotated_pages(prompt_kv, page_slot, prompt_lengths, x, tabs, npool, pair, cache_pages):
+def rotated_pages(prompt_kv, page_slot, prompt_lengths, tabs, npool, pair, cache_pages):
     pages, _, heads, page_len, head_dim = prompt_kv.shape
     per = pages // 2
     ct, st, cp, sp, _, _ = tabs
-    whole = lambda x: pl.BlockSpec(x.shape, lambda i: (0,) * x.ndim)
+    whole = lambda x: pl.BlockSpec(x.shape, lambda i: (0, 0))
     return pl.pallas_call(
         functools.partial(rope_kernel, npool, cache_pages, per),
         grid=(pages // per,),
         out_shape=[
             jax.ShapeDtypeStruct(prompt_kv.shape, BF16),
             jax.ShapeDtypeStruct((3 * npool * pair,), I32),
-            jax.ShapeDtypeStruct(x.shape, x.dtype),
         ],
         in_specs=[
             SMEM,
             SMEM,
-            whole(x),
             pl.BlockSpec((per,) + prompt_kv.shape[1:], lambda i: (i, 0, 0, 0, 0)),
             whole(ct),
             whole(st),
             whole(cp),
             whole(sp),
         ],
-        out_specs=[pl.BlockSpec((per,) + prompt_kv.shape[1:], lambda i: (i, 0, 0, 0, 0)), SMEM, whole(x)],
+        out_specs=[pl.BlockSpec((per,) + prompt_kv.shape[1:], lambda i: (i, 0, 0, 0, 0)), SMEM],
         scratch_shapes=[pltpu.SMEM((npool,), I32)],
         compiler_params=PARAMS,
         cost_estimate=pl.CostEstimate(flops=6_000_000, bytes_accessed=2_000_000, transcendentals=0),
         name="rope_pages",
-    )(in_hbm(page_slot), in_hbm(prompt_lengths), x, *[in_hbm(y) for y in (prompt_kv, ct, st, cp, sp)])
+    )(*[in_hbm(x) for x in (page_slot, prompt_lengths, prompt_kv, ct, st, cp, sp)])
 
 
 def asked_kernel(page_len, heads, table_ref, context_ref, q_ref, out_ref, spread):
@@ -319,7 +316,7 @@
     group = block // heads
     together = LANES // block
     me = me_ref[0]
-    owners = [owner_of(me, which) for which in block_order(npool)]
+    owners = [owner_of(me, npool, apart, flip) for apart, flip in block_order(npool)]
     lane = lax.broadcasted_iota(I32, (1, LANES), 1)
     codes = [x[rows, :STAT_ROWS, :].astype(F32) for x in blocks]
     codes = [x[0:1] * CODE + x[1:2] for x in codes]
@@ -463,8 +460,8 @@
     weight_ref, out_ref, lhs = refs[npool:]
     steps, rows, _ = blocks[0].shape
     every = npool * rows
-    for x, which in enumerate(block_order(npool)):
-        owner = owner_of(place_ref[0], which)
+    for x, (apart, flip) in enumerate(block_order(npool)):
+        owner = owner_of(place_ref[0], npool, apart, flip)
         for s in range(steps):
             lhs[pl.ds(pl.multiple_of(s * every + owner * rows, rows), rows), :] = blocks[x][s]
     multiply(lhs, weight_ref, out_ref, 1 - place_ref[1])
@@ -517,34 +514,42 @@
     )(place, lhs, weight)
 
 
+def distances(npool):
+    half = npool // 2
+    return sorted(range(half), key=lambda apart: -abs(apart - half // 2))
+
+
 def block_order(npool):
-    return [2 * apart + flip for flip in (0, 1) for apart in range(npool // 2)]
-
-
-def owner_of(me, which):
-    return jnp.bitwise_xor(me, which)
+    return [(apart, flip) for flip in (0, 1) for apart in distances(npool)]
+
+
+def owner_of(me, npool, apart, flip):
+    half = npool // 2
+    pair, side = me // 2, me % 2
+    side = 1 - side if flip else side
+    return lax.rem(pair + half - apart, half) * 2 + side
 
 
 def place_of(me, npool, holder):
-    which = jnp.bitwise_xor(me, holder)
-    return (which % 2) * (npool // 2) + which // 2
+    half = npool // 2
+    apart = lax.rem(holder // 2 - me // 2 + half, half)
+    flip = lax.rem(me + holder, 2)
+    return flip * half + sum(jnp.where(apart == x, i, 0) for i, x in enumerate(distances(npool)))
 
 
 def in_hbm(x):
     return pltpu.with_memory_space_constraint(x, pltpu.HBM)
 
 
-def gathered(x, npool, later):
-    swap = lambda x, by: lax.ppermute(x, "pool", [(i, i ^ by) for i in range(npool)])
-    straight = {0: later}
-    apart = npool // 4
-    while apart:
-        for i in list(straight):
-            own = x if i == 0 and apart == npool // 4 else straight[i]
-            straight[i + apart] = swap(own, 2 * apart)
-        apart //= 2
-    straight = [straight[i] for i in range(npool // 2)]
-    return straight + [swap(y, 1) for y in straight]
+def gathered(x, npool, later=None):
+    half = npool // 2
+    later = x if later is None else later
+    ahead = lambda x, by: lax.ppermute(x, "pool", [(i, (i + 2 * by) % npool) for i in range(npool)])
+    across = lambda x: lax.ppermute(x, "pool", [(i, i ^ 1) for i in range(npool)])
+    straight = {0: x}
+    for by in distances(npool)[1:]:
+        straight[by] = ahead(x if by == half // 2 else later, by)
+    return list(straight.values()) + [across(y) for y in straight.values()]
 
 
 def swap_halves(x):
@@ -573,10 +578,8 @@
     table = page_table.T
 
     asked = asked_queries(table, context_lengths, queries, page_len, heads, head_dim)
-    arrived, own, again = rotated_pages(
-        prompt_kv, page_slot, prompt_lengths, asked, tabs, npool, pair, cache_pages
-    )
-    asked_all = gathered(asked, npool, again)
+    asked_all = gathered(asked, npool)
+    arrived, own = rotated_pages(prompt_kv, page_slot, prompt_lengths, tabs, npool, pair, cache_pages)
     local = local_attention(table, context_lengths, cache_fill, asked, new_kv, cache_kv, tabs)
     parts = arrived_attention(place, own, asked_all, arrived)
     parts = lax.all_to_all(parts, "pool", split_axis=0, concat_axis=0, tiled=True)

time: 68.2 us -> 67.3 us (0.987)
  waiting for transfers between devices: 18.6 us -> 15 us
  starting transfers between devices: 27.7 us -> 30.6 us
    ppermute x14, waiting for transfers between devices: 17.4 us -> 13.8 us  [the longest x6 7.34 us: gathered(): lax.ppermute(x, 'pool', [(i, (i + 2 * by) % npool) for i in range(npool)])]
    all_to_all x1, starting transfers between devices: 5.61 us -> 9.04 us  [shards(): lax.all_to_all(parts, 'pool', split_axis=0, concat_axis=0, tiled=True)]
  transfers between devices with their start and end apart: 16 -> 16, of which waited for: 13 -> 11; matrix products, arithmetic and copies ran while one was open for 0% -> 0% of each run, Pallas kernels for 20% -> 20%
where the time goes in v10:
time: 67.3 us; the launch traced here: 66.9 us
  starting transfers between devices  30.6 us (45%)
  Pallas kernels  20.3 us (30%)
  waiting for transfers between devices  15 us (22%)
  other arithmetic  0.86 us (1%)
    ppermute x8, starting transfers between devices, gathered(): lax.ppermute(x, 'pool', [(i, i ^ 1) for i in range(npool)])  10.8 us
    ppermute x6, starting transfers between devices, gathered(): lax.ppermute(x, 'pool', [(i, (i + 2 * by) % npool) for i in range(npool)])  10.6 us
    all_to_all x1, starting transfers between devices, shards(): lax.all_to_all(parts, 'pool', split_axis=0, concat_axis=0, tiled=True)  9.04 us
    ppermute x6, waiting for transfers between devices, gathered(): lax.ppermute(x, 'pool', [(i, (i + 2 * by) % npool) for i in range(npool)])  7.34 us
    pallas_call x1, Pallas kernels, local_attention(): pl.pallas_call(functools.partial(local_kernel, page_len, heads), out_shap...  6.94 us
    ppermute x8, waiting for transfers between devices, gathered(): lax.ppermute(x, 'pool', [(i, i ^ 1) for i in range(npool)])  6.47 us
    pallas_call x1, Pallas kernels, rotated_pages(): pl.pallas_call(functools.partial(rope_kernel, npool, cache_pages, per), g...  2.96 us
    pallas_call x1, Pallas kernels, arrived_attention(): pl.pallas_call(functools.partial(arrived_kernel, npool, pair), out_shape=...  2.88 us
  transfers between devices with their start and end apart: 16, of which 11 were waited for; matrix products, arithmetic and copies ran while one was open for 0% of the time, Pallas kernels for 20%

profile of v10, /device:TPU:0, one launch (start us, length us, event | category | flops | bytes accessed | tf_op | source)
XLA Modules:
  0.0 66.9 jit_solution(155580743792646504)
XLA Ops:
  0.0 1.2 %asked_queries.1.refs_0_.q_ref = bf16[17,32,128]{2,1,0:T(8,128)(2,1)S(1)} custom-call(s32[3,16]{1,0:T(4,128)} %bitcast.3, s32[16]{0:T(128)} %context_ref.3, bf16[2,16,2048]{2,1,0:T(8,128)(2,1)} %q_ref.1), custom_call_target="tpu_custom_call" | custom-call | flops 100000 | bytes 300000 | tf_op jit(solution)/shard_map/asked_queries/pallas_call | solution.py:138
  1.2 4.1 %collective-permute-start.2 = (bf16[17,32,128]{2,1,0:T(8,128)(2,1)S(1)}, bf16[17,32,128]{2,1,0:T(8,128)(2,1)S(1)}, u32[]{:S(2)}, u32[]{:S(2)}) collective-permute-start(bf16[17,32,128]{2,1,0:T(8,128)(2,1)S(1)} %asked_queries.1.refs_0_.q_ref), channel_id=1, source_target_pairs={{0,8},{2,10},{4,12},{6,14},{8,0},{10,2},{12,4},{14,6},{1,9},{3,11}... | collective-permute-start | bytes 417800 | tf_op jit(solution)/shard_map/ppermute | solution.py:547
  5.3 1.3 %collective-permute-start.1 = (bf16[17,32,128]{2,1,0:T(8,128)(2,1)S(1)}, bf16[17,32,128]{2,1,0:T(8,128)(2,1)S(1)}, u32[]{:S(2)}, u32[]{:S(2)}) collective-permute-start(bf16[17,32,128]{2,1,0:T(8,128)(2,1)S(1)} %asked_queries.1.refs_0_.q_ref), channel_id=1, source_target_pairs={{0,12},{2,14},{4,0},{6,2},{8,4},{10,6},{12,8},{14,10},{1,13},{3,15... | collective-permute-start | bytes 417800 | tf_op jit(solution)/shard_map/ppermute | solution.py:547
  7.4 1.5 %collective-permute-start.3 = (bf16[17,32,128]{2,1,0:T(8,128)(2,1)S(1)}, bf16[17,32,128]{2,1,0:T(8,128)(2,1)S(1)}, u32[]{:S(2)}, u32[]{:S(2)}) collective-permute-start(bf16[17,32,128]{2,1,0:T(8,128)(2,1)S(1)} %asked_queries.1.refs_0_.q_ref), channel_id=1, source_target_pairs={{0,2},{2,0},{4,6},{6,4},{8,10},{10,8},{12,14},{14,12},{1,3},{3,1},... | collective-permute-start | bytes 417800 | tf_op jit(solution)/shard_map/ppermute | solution.py:548
  8.9 4.8 %collective-permute-done.2.refs_3_ = bf16[17,32,128]{2,1,0:T(8,128)(2,1)S(1)} collective-permute-done((bf16[17,32,128]{2,1,0:T(8,128)(2,1)S(1)}, bf16[17,32,128]{2,1,0:T(8,128)(2,1)S(1)}, u32[]{:S(2)}, u32[]{:S(2)}) %collective-permute-start.2) | collective-permute-done | bytes 139296 | tf_op jit(solution)/shard_map/ppermute | solution.py:547
  13.6 2.2 %collective-permute-start.6 = (bf16[17,32,128]{2,1,0:T(8,128)(2,1)S(1)}, bf16[17,32,128]{2,1,0:T(8,128)(2,1)S(1)}, u32[]{:S(2)}, u32[]{:S(2)}) collective-permute-start(bf16[17,32,128]{2,1,0:T(8,128)(2,1)S(1)} %collective-permute-done.2.refs_3_), channel_id=1, source_target_pairs={{0,2},{2,0},{4,6},{6,4},{8,10},{10,8},{12,14},{14,12},{1,3},{3,1},... | collective-permute-start | bytes 417800 | tf_op jit(solution)/shard_map/ppermute | solution.py:548
  16.2 1.6 %collective-permute-start.4 = (bf16[17,32,128]{2,1,0:T(8,128)(2,1)S(1)}, bf16[17,32,128]{2,1,0:T(8,128)(2,1)S(1)}, u32[]{:S(2)}, u32[]{:S(2)}) collective-permute-start(bf16[17,32,128]{2,1,0:T(8,128)(2,1)S(1)} %collective-permute-done.refs_1_), channel_id=1, source_target_pairs={{0,2},{2,0},{4,6},{6,4},{8,10},{10,8},{12,14},{14,12},{1,3},{3,1},... | collective-permute-start | bytes 417800 | tf_op jit(solution)/shard_map/ppermute | solution.py:548
  17.8 3.0 %rope_pages.1 = (bf16[16,2,2,128,128]{4,3,2,1,0:T(8,128)(2,1)S(1)}, s32[48]{0:T(128)S(1)}) custom-call(s32[16]{0:T(128)} %slot_ref.1, s32[1,4]{1,0:T(1,128)} %len_ref.1, bf16[16,2,2,128,128]{4,3,2,1,0:T(8,128)(2,1)} %pages_ref.1, f32[128,128]{1,0:T(8,128)} %constant.20.clone.ct_ref, f32[128,128]{1,0:T(8,128)} %constant.21.clone.st_ref, ...), custom_call_target="tpu_custom_call" | custom-call | flops 6000000 | bytes 2000000 | tf_op jit(solution)/shard_map/rope_pages/pallas_call | solution.py:86
  21.8 1.5 %collective-permute-done.4.refs_5_ = bf16[17,32,128]{2,1,0:T(8,128)(2,1)S(1)} collective-permute-done((bf16[17,32,128]{2,1,0:T(8,128)(2,1)S(1)}, bf16[17,32,128]{2,1,0:T(8,128)(2,1)S(1)}, u32[]{:S(2)}, u32[]{:S(2)}) %collective-permute-start.4) | collective-permute-done | bytes 139296 | tf_op jit(solution)/shard_map/ppermute | solution.py:548
  23.3 2.9 %arrived_attention.1 = bf16[8,80,128]{2,1,0:T(8,128)(2,1)} custom-call(s32[2]{0:T(128)S(1)} %pad_add_fusion.me_ref.place_ref, s32[48]{0:T(128)S(1)} %get-tuple-element.13.own_ref, bf16[17,32,128]{2,1,0:T(8,128)(2,1)S(1)} %asked_queries.1.refs_0_.q_ref, bf16[17,32,128]{2,1,0:T(8,128)(2,1)S(1)} %collective-permute-done.refs_1_, ...), custom_call_target="tpu_custom_call" | custom-call | flops 200000000 | bytes 4000000 | tf_op jit(solution)/shard_map/arrived_attention/pallas_call | solution.py:362
  26.2 9.0 %all-to-all-start = ((bf16[8,80,128]{2,1,0:T(8,128)(2,1)}), bf16[8,80,128]{2,1,0:T(8,128)(2,1)S(1)}, u32[]{:S(2)}, u32[]{:S(2)}) async-start(bf16[8,80,128]{2,1,0:T(8,128)(2,1)} %arrived_attention.1), calls=%async_computation | async-start | bytes 327680 | tf_op jit(solution)/shard_map/all_to_all | solution.py:585
  35.3 6.9 %local_attention.1 = (f32[512,128]{1,0:T(8,128)S(1)}, f32[512,128]{1,0:T(8,128)S(1)}) custom-call(s32[3,16]{1,0:T(4,128)} %bitcast.4, s32[16]{0:T(128)} %context_ref.3, s32[48]{0:T(128)} %fill_ref.1, bf16[17,32,128]{2,1,0:T(8,128)(2,1)S(1)} %asked_queries.1.refs_0_.q_ref, bf16[2,16,512]{2,1,0:T(8,128)(2,1)S(1)} %reshape.3.new_ref, ...), custom_call_target="tpu_custom_call" | custom-call | flops 800000000 | bytes 12000000 | tf_op jit(solution)/shard_map/local_attention/pallas_call | solution.py:281
  42.8 1.5 %merge.1.x_ref.refs_0_ = bf16[2,16,2048]{2,1,0:T(8,128)(2,1)S(1)} custom-call(s32[2]{0:T(128)S(1)} %pad_add_fusion.me_ref.place_ref, bf16[8,80,128]{2,1,0:T(8,128)(2,1)S(1)} %all-to-all-done.parts_ref, f32[512,128]{1,0:T(8,128)S(1)} %get-tuple-element.15.o_ref, f32[512,128]{1,0:T(8,128)S(1)} %get-tuple-element.16.stat_ref), custom_call_target="tpu_custom_call" | custom-call | flops 2000000 | bytes 1500000 | tf_op jit(solution)/shard_map/merge/pallas_call | solution.py:422
  44.3 2.4 %collective-permute-start.9 = (bf16[2,16,2048]{2,1,0:T(8,128)(2,1)S(1)}, bf16[2,16,2048]{2,1,0:T(8,128)(2,1)S(1)}, u32[]{:S(2)}, u32[]{:S(2)}) collective-permute-start(bf16[2,16,2048]{2,1,0:T(8,128)(2,1)S(1)} %merge.1.x_ref.refs_0_), channel_id=1, source_target_pairs={{0,8},{2,10},{4,12},{6,14},{8,0},{10,2},{12,4},{14,6},{1,9},{3,11}... | collective-permute-start | bytes 393224 | tf_op jit(solution)/shard_map/ppermute | solution.py:547
  46.7 2.2 %fetch_weight.1 = (bf16[2048,1024]{1,0:T(8,128)(2,1)S(1)}, bf16[2,16,2048]{2,1,0:T(8,128)(2,1)S(1)}) custom-call(bf16[2048,1024]{1,0:T(8,128)(2,1)} %weight_ref.1, bf16[2,16,2048]{2,1,0:T(8,128)(2,1)S(1)} %merge.1.x_ref.refs_0_), custom_call_target="tpu_custom_call" | custom-call | bytes 8388608 | tf_op jit(solution)/shard_map/fetch_weight/pallas_call | solution.py:446
  48.9 1.5 %collective-permute-start.8 = (bf16[2,16,2048]{2,1,0:T(8,128)(2,1)S(1)}, bf16[2,16,2048]{2,1,0:T(8,128)(2,1)S(1)}, u32[]{:S(2)}, u32[]{:S(2)}) collective-permute-start(bf16[2,16,2048]{2,1,0:T(8,128)(2,1)S(1)} %get-tuple-element.17), channel_id=1, source_target_pairs={{0,12},{2,14},{4,0},{6,2},{8,4},{10,6},{12,8},{14,10},{1,13},{3,15... | collective-permute-start | bytes 393224 | tf_op jit(solution)/shard_map/ppermute | solution.py:547
  51.0 1.5 %collective-permute-start.10 = (bf16[2,16,2048]{2,1,0:T(8,128)(2,1)S(1)}, bf16[2,16,2048]{2,1,0:T(8,128)(2,1)S(1)}, u32[]{:S(2)}, u32[]{:S(2)}) collective-permute-start(bf16[2,16,2048]{2,1,0:T(8,128)(2,1)S(1)} %merge.1.x_ref.refs_0_), channel_id=1, source_target_pairs={{0,2},{2,0},{4,6},{6,4},{8,10},{10,8},{12,14},{14,12},{1,3},{3,1},... | collective-permute-start | bytes 393224 | tf_op jit(solution)/shard_map/ppermute | solution.py:548
  53.6 1.5 %collective-permute-done.8.refs_2_ = bf16[2,16,2048]{2,1,0:T(8,128)(2,1)S(1)} collective-permute-done((bf16[2,16,2048]{2,1,0:T(8,128)(2,1)S(1)}, bf16[2,16,2048]{2,1,0:T(8,128)(2,1)S(1)}, u32[]{:S(2)}, u32[]{:S(2)}) %collective-permute-start.8) | collective-permute-done | bytes 131104 | tf_op jit(solution)/shard_map/ppermute | solution.py:547
  55.1 1.5 %collective-permute-start.12 = (bf16[2,16,2048]{2,1,0:T(8,128)(2,1)S(1)}, bf16[2,16,2048]{2,1,0:T(8,128)(2,1)S(1)}, u32[]{:S(2)}, u32[]{:S(2)}) collective-permute-start(bf16[2,16,2048]{2,1,0:T(8,128)(2,1)S(1)} %collective-permute-done.8.refs_2_), channel_id=1, source_target_pairs={{0,2},{2,0},{4,6},{6,4},{8,10},{10,8},{12,14},{14,12},{1,3},{3,1},... | collective-permute-start | bytes 393224 | tf_op jit(solution)/shard_map/ppermute | solution.py:548
  57.3 1.5 %collective-permute-start.11 = (bf16[2,16,2048]{2,1,0:T(8,128)(2,1)S(1)}, bf16[2,16,2048]{2,1,0:T(8,128)(2,1)S(1)}, u32[]{:S(2)}, u32[]{:S(2)}) collective-permute-start(bf16[2,16,2048]{2,1,0:T(8,128)(2,1)S(1)} %collective-permute-done.7.refs_1_), channel_id=1, source_target_pairs={{0,2},{2,0},{4,6},{6,4},{8,10},{10,8},{12,14},{14,12},{1,3},{3,1},... | collective-permute-start | bytes 393224 | tf_op jit(solution)/shard_map/ppermute | solution.py:548
  59.2 2.1 %collective-permute-done.12.refs_6_ = bf16[2,16,2048]{2,1,0:T(8,128)(2,1)S(1)} collective-permute-done((bf16[2,16,2048]{2,1,0:T(8,128)(2,1)S(1)}, bf16[2,16,2048]{2,1,0:T(8,128)(2,1)S(1)}, u32[]{:S(2)}, u32[]{:S(2)}) %collective-permute-start.12) | collective-permute-done | bytes 131104 | tf_op jit(solution)/shard_map/ppermute | solution.py:548
  61.4 1.4 %collective-permute-done.11.refs_5_ = bf16[2,16,2048]{2,1,0:T(8,128)(2,1)S(1)} collective-permute-done((bf16[2,16,2048]{2,1,0:T(8,128)(2,1)S(1)}, bf16[2,16,2048]{2,1,0:T(8,128)(2,1)S(1)}, u32[]{:S(2)}, u32[]{:S(2)}) %collective-permute-start.11) | collective-permute-done | bytes 131104 | tf_op jit(solution)/shard_map/ppermute | solution.py:548
  62.8 1.3 %project_other.1 = (f32[2,128,512]{2,1,0:T(8,128)S(1)}, bf16[256,2048]{1,0:T(8,128)(2,1)S(1)}) custom-call(s32[2]{0:T(128)S(1)} %pad_add_fusion.me_ref.place_ref, bf16[2,16,2048]{2,1,0:T(8,128)(2,1)S(1)} %merge.1.x_ref.refs_0_, bf16[2,16,2048]{2,1,0:T(8,128)(2,1)S(1)} %collective-permute-done.7.refs_1_, ...), custom_call_target="tpu_custom_call" | custom-call | flops 536870912 | bytes 4000000 | tf_op jit(solution)/shard_map/project_other/pallas_call | solution.py:485
  64.2 1.3 %project_own.1 = f32[2,128,512]{2,1,0:T(8,128)S(1)} custom-call(s32[2]{0:T(128)S(1)} %pad_add_fusion.me_ref.place_ref, bf16[256,2048]{1,0:T(8,128)(2,1)S(1)} %get-tuple-element.19.lhs, bf16[2048,1024]{1,0:T(8,128)(2,1)S(1)} %get-tuple-element.18.refs_8_.weight_ref), custom_call_target="tpu_custom_call" | custom-call | flops 536870912 | bytes 4000000 | tf_op jit(solution)/shard_map/project_own/pallas_call | solution.py:506
  (21 shorter events, 7.0 us)
Async XLA Ops:
  0.0 35.2 %copy-start = (bf16[2,16,2,2,128]{4,3,2,1,0:T(2,128)(2,1)S(1)}, bf16[2,16,2,2,128]{4,3,2,1,0:T(2,128)(2,1)}, u32[]{:S(2)}) copy-start(bf16[2,16,2,2,128]{4,3,2,1,0:T(2,128)(2,1)} %param.24) | copy-start | bytes 98308
  1.2 12.4 %collective-permute-start.2 = (bf16[17,32,128]{2,1,0:T(8,128)(2,1)S(1)}, bf16[17,32,128]{2,1,0:T(8,128)(2,1)S(1)}, u32[]{:S(2)}, u32[]{:S(2)}) collective-permute-start(bf16[17,32,128]{2,1,0:T(8,128)(2,1)S(1)} %asked_queries.1.refs_0_.q_ref), channel_id=1, source_target_pairs={{0,8},{2,10},{4,12},{6,14},{8,0},{10,2},{12,4},{14,6},{1,9},{3,11}... | collective-permute-start | bytes 417800 | tf_op jit(solution)/shard_map/ppermute | solution.py:547
  5.3 10.5 %collective-permute-start.1 = (bf16[17,32,128]{2,1,0:T(8,128)(2,1)S(1)}, bf16[17,32,128]{2,1,0:T(8,128)(2,1)S(1)}, u32[]{:S(2)}, u32[]{:S(2)}) collective-permute-start(bf16[17,32,128]{2,1,0:T(8,128)(2,1)S(1)} %asked_queries.1.refs_0_.q_ref), channel_id=1, source_target_pairs={{0,12},{2,14},{4,0},{6,2},{8,4},{10,6},{12,8},{14,10},{1,13},{3,15... | collective-permute-start | bytes 417800 | tf_op jit(solution)/shard_map/ppermute | solution.py:547
  6.7 9.5 %collective-permute-start = (bf16[17,32,128]{2,1,0:T(8,128)(2,1)S(1)}, bf16[17,32,128]{2,1,0:T(8,128)(2,1)S(1)}, u32[]{:S(2)}, u32[]{:S(2)}) collective-permute-start(bf16[17,32,128]{2,1,0:T(8,128)(2,1)S(1)} %asked_queries.1.refs_0_.q_ref), channel_id=1, source_target_pairs={{0,4},{2,6},{4,8},{6,10},{8,12},{10,14},{12,0},{14,2},{1,5},{3,7},... | collective-permute-start | bytes 417800 | tf_op jit(solution)/shard_map/ppermute | solution.py:547
  7.4 13.5 %collective-permute-start.3 = (bf16[17,32,128]{2,1,0:T(8,128)(2,1)S(1)}, bf16[17,32,128]{2,1,0:T(8,128)(2,1)S(1)}, u32[]{:S(2)}, u32[]{:S(2)}) collective-permute-start(bf16[17,32,128]{2,1,0:T(8,128)(2,1)S(1)} %asked_queries.1.refs_0_.q_ref), channel_id=1, source_target_pairs={{0,2},{2,0},{4,6},{6,4},{8,10},{10,8},{12,14},{14,12},{1,3},{3,1},... | collective-permute-start | bytes 417800 | tf_op jit(solution)/shard_map/ppermute | solution.py:548
  13.6 7.2 %collective-permute-start.6 = (bf16[17,32,128]{2,1,0:T(8,128)(2,1)S(1)}, bf16[17,32,128]{2,1,0:T(8,128)(2,1)S(1)}, u32[]{:S(2)}, u32[]{:S(2)}) collective-permute-start(bf16[17,32,128]{2,1,0:T(8,128)(2,1)S(1)} %collective-permute-done.2.refs_3_), channel_id=1, source_target_pairs={{0,2},{2,0},{4,6},{6,4},{8,10},{10,8},{12,14},{14,12},{1,3},{3,1},... | collective-permute-start | bytes 417800 | tf_op jit(solution)/shard_map/ppermute | solution.py:548
  15.8 6.0 %collective-permute-start.5 = (bf16[17,32,128]{2,1,0:T(8,128)(2,1)S(1)}, bf16[17,32,128]{2,1,0:T(8,128)(2,1)S(1)}, u32[]{:S(2)}, u32[]{:S(2)}) collective-permute-start(bf16[17,32,128]{2,1,0:T(8,128)(2,1)S(1)} %collective-permute-done.1.refs_2_), channel_id=1, source_target_pairs={{0,2},{2,0},{4,6},{6,4},{8,10},{10,8},{12,14},{14,12},{1,3},{3,1},... | collective-permute-start | bytes 417800 | tf_op jit(solution)/shard_map/ppermute | solution.py:548
  16.2 7.1 %collective-permute-start.4 = (bf16[17,32,128]{2,1,0:T(8,128)(2,1)S(1)}, bf16[17,32,128]{2,1,0:T(8,128)(2,1)S(1)}, u32[]{:S(2)}, u32[]{:S(2)}) collective-permute-start(bf16[17,32,128]{2,1,0:T(8,128)(2,1)S(1)} %collective-permute-done.refs_1_), channel_id=1, source_target_pairs={{0,2},{2,0},{4,6},{6,4},{8,10},{10,8},{12,14},{14,12},{1,3},{3,1},... | collective-permute-start | bytes 417800 | tf_op jit(solution)/shard_map/ppermute | solution.py:548
  26.2 16.6 %all-to-all-start = ((bf16[8,80,128]{2,1,0:T(8,128)(2,1)}), bf16[8,80,128]{2,1,0:T(8,128)(2,1)S(1)}, u32[]{:S(2)}, u32[]{:S(2)}) async-start(bf16[8,80,128]{2,1,0:T(8,128)(2,1)} %arrived_attention.1), calls=%async_computation | async-start | bytes 327680 | tf_op jit(solution)/shard_map/all_to_all | solution.py:585
  44.3 8.2 %collective-permute-start.9 = (bf16[2,16,2048]{2,1,0:T(8,128)(2,1)S(1)}, bf16[2,16,2048]{2,1,0:T(8,128)(2,1)S(1)}, u32[]{:S(2)}, u32[]{:S(2)}) collective-permute-start(bf16[2,16,2048]{2,1,0:T(8,128)(2,1)S(1)} %merge.1.x_ref.refs_0_), channel_id=1, source_target_pairs={{0,8},{2,10},{4,12},{6,14},{8,0},{10,2},{12,4},{14,6},{1,9},{3,11}... | collective-permute-start | bytes 393224 | tf_op jit(solution)/shard_map/ppermute | solution.py:547
  48.9 6.2 %collective-permute-start.8 = (bf16[2,16,2048]{2,1,0:T(8,128)(2,1)S(1)}, bf16[2,16,2048]{2,1,0:T(8,128)(2,1)S(1)}, u32[]{:S(2)}, u32[]{:S(2)}) collective-permute-start(bf16[2,16,2048]{2,1,0:T(8,128)(2,1)S(1)} %get-tuple-element.17), channel_id=1, source_target_pairs={{0,12},{2,14},{4,0},{6,2},{8,4},{10,6},{12,8},{14,10},{1,13},{3,15... | collective-permute-start | bytes 393224 | tf_op jit(solution)/shard_map/ppermute | solution.py:547
  50.5 6.8 %collective-permute-start.7 = (bf16[2,16,2048]{2,1,0:T(8,128)(2,1)S(1)}, bf16[2,16,2048]{2,1,0:T(8,128)(2,1)S(1)}, u32[]{:S(2)}, u32[]{:S(2)}) collective-permute-start(bf16[2,16,2048]{2,1,0:T(8,128)(2,1)S(1)} %get-tuple-element.17), channel_id=1, source_target_pairs={{0,4},{2,6},{4,8},{6,10},{8,12},{10,14},{12,0},{14,2},{1,5},{3,7},... | collective-permute-start | bytes 393224 | tf_op jit(solution)/shard_map/ppermute | solution.py:547
  51.0 7.7 %collective-permute-start.10 = (bf16[2,16,2048]{2,1,0:T(8,128)(2,1)S(1)}, bf16[2,16,2048]{2,1,0:T(8,128)(2,1)S(1)}, u32[]{:S(2)}, u32[]{:S(2)}) collective-permute-start(bf16[2,16,2048]{2,1,0:T(8,128)(2,1)S(1)} %merge.1.x_ref.refs_0_), channel_id=1, source_target_pairs={{0,2},{2,0},{4,6},{6,4},{8,10},{10,8},{12,14},{14,12},{1,3},{3,1},... | collective-permute-start | bytes 393224 | tf_op jit(solution)/shard_map/ppermute | solution.py:548
  52.5 6.8 %collective-permute-start.13 = (bf16[2,16,2048]{2,1,0:T(8,128)(2,1)S(1)}, bf16[2,16,2048]{2,1,0:T(8,128)(2,1)S(1)}, u32[]{:S(2)}, u32[]{:S(2)}) collective-permute-start(bf16[2,16,2048]{2,1,0:T(8,128)(2,1)S(1)} %collective-permute-done.9.refs_3_), channel_id=1, source_target_pairs={{0,2},{2,0},{4,6},{6,4},{8,10},{10,8},{12,14},{14,12},{1,3},{3,1},... | collective-permute-start | bytes 393224 | tf_op jit(solution)/shard_map/ppermute | solution.py:548
  55.1 6.3 %collective-permute-start.12 = (bf16[2,16,2048]{2,1,0:T(8,128)(2,1)S(1)}, bf16[2,16,2048]{2,1,0:T(8,128)(2,1)S(1)}, u32[]{:S(2)}, u32[]{:S(2)}) collective-permute-start(bf16[2,16,2048]{2,1,0:T(8,128)(2,1)S(1)} %collective-permute-done.8.refs_2_), channel_id=1, source_target_pairs={{0,2},{2,0},{4,6},{6,4},{8,10},{10,8},{12,14},{14,12},{1,3},{3,1},... | collective-permute-start | bytes 393224 | tf_op jit(solution)/shard_map/ppermute | solution.py:548
  57.3 5.5 %collective-permute-start.11 = (bf16[2,16,2048]{2,1,0:T(8,128)(2,1)S(1)}, bf16[2,16,2048]{2,1,0:T(8,128)(2,1)S(1)}, u32[]{:S(2)}, u32[]{:S(2)}) collective-permute-start(bf16[2,16,2048]{2,1,0:T(8,128)(2,1)S(1)} %collective-permute-done.7.refs_1_), channel_id=1, source_target_pairs={{0,2},{2,0},{4,6},{6,4},{8,10},{10,8},{12,14},{14,12},{1,3},{3,1},... | collective-permute-start | bytes 393224 | tf_op jit(solution)/shard_map/ppermute | solution.py:548
  64.1 2.0 %collective-permute-start.14 = (f32[2,128,512]{2,1,0:T(8,128)S(1)}, f32[2,128,512]{2,1,0:T(8,128)S(1)}, u32[]{:S(2)}, u32[]{:S(2)}) collective-permute-start(f32[2,128,512]{2,1,0:T(8,128)S(1)} %get-tuple-element.20), channel_id=1, source_target_pairs={{0,1},{1,0},{2,3},{3,2},{4,5},{5,4},{6,7},{7,6},{8,9},{9,8},{10,11... | collective-permute-start | bytes 1572872 | tf_op jit(solution)/shard_map/ppermute | solution.py:556

commit v11 on v10

--- a/solution.py
+++ b/solution.py
@@ -195,6 +195,7 @@
     kf,
     vf,
     position,
+    where,
 ):
     rows, block, head_dim = q_ref.shape
     rows = rows - 1
@@ -204,13 +205,21 @@
     per = group // steps
     together = LANES // block
 
+    zeros = rows * most
+
     def copy(r, j):
         n = r * most + j
         return pltpu.make_async_copy(cache_ref.at[table_ref[j, r]], kv.at[n], sems.at[n])
 
+    def seen_tokens(r, j):
+        return jnp.minimum(fill_ref[table_ref[j, r]], context_ref[r] - j * page_len)
+
     for r in range(rows):
         for j in range(most):
-            copy(r, j).start()
+            needed = seen_tokens(r, j) > 0
+            where[r * most + j] = jnp.where(needed, r * most + j, zeros)
+            pl.when(needed)(copy(r, j).start)
+    kv[zeros] = jnp.zeros(kv.shape[1:], BF16)
     kf[...] = jnp.zeros_like(kf)
     vf[...] = jnp.zeros_like(vf)
     for r in range(rows):
@@ -235,18 +244,18 @@
         if i % 2 == 0:
             for r in range(i * together, min(rows, (i + 2) * together)):
                 for j in range(most):
-                    copy(r, j).wait()
+                    pl.when(where[r * most + j] < zeros)(copy(r, j).wait)
         queries = q_ref[i * together : (i + 1) * together].reshape(LANES, head_dim)
         keys, values = [], []
         for r, k in chains:
             at = r * block + k * group
-            page = lambda what: [kv[r * most + j, what, k] for j in range(most)]
+            page = lambda what: [kv[where[r * most + j], what, k] for j in range(most)]
             keys.append(jnp.concatenate(page(0) + [kf[at : at + group, :].astype(BF16)], axis=0))
             values.append(page(1) + [vf[at : at + group, :].astype(BF16)])
         scores = transposed_scores(queries, keys, group)
         mask = []
         for j in range(most):
-            seen = [jnp.minimum(fill_ref[table_ref[j, r]], context_ref[r] - j * page_len) for r in requests]
+            seen = [seen_tokens(r, j) for r in requests]
             mask.append(token < lane_values(seen, block, (1, LANES)))
         parts = [
             jnp.where(m, scores[n * page_len : n * page_len + m.shape[0]], -jnp.inf)
@@ -284,11 +293,12 @@
         in_specs=[SMEM] * 3 + [VMEM] * 4 + [ANY],
         out_specs=[VMEM] * 2,
         scratch_shapes=[
-            pltpu.VMEM((table.size, 2, heads, page_len, head_dim), BF16),
+            pltpu.VMEM((table.size + 1, 2, heads, page_len, head_dim), BF16),
             pltpu.SemaphoreType.DMA((table.size,)),
             pltpu.VMEM(flat, F32),
             pltpu.VMEM(flat, F32),
             pltpu.VMEM((rows, head_dim), I32),
+            pltpu.SMEM((table.size,), I32),
         ],
         compiler_params=PARAMS,
         cost_estimate=pl.CostEstimate(flops=800_000_000, bytes_accessed=12_000_000, transcendentals=400_000),
@@ -514,13 +524,8 @@
     )(place, lhs, weight)
 
 
-def distances(npool):
-    half = npool // 2
-    return sorted(range(half), key=lambda apart: -abs(apart - half // 2))
-
-
 def block_order(npool):
-    return [(apart, flip) for flip in (0, 1) for apart in distances(npool)]
+    return [(apart, flip) for flip in (0, 1) for apart in range(npool // 2)]
 
 
 def owner_of(me, npool, apart, flip):
@@ -534,7 +539,7 @@
     half = npool // 2
     apart = lax.rem(holder // 2 - me // 2 + half, half)
     flip = lax.rem(me + holder, 2)
-    return flip * half + sum(jnp.where(apart == x, i, 0) for i, x in enumerate(distances(npool)))
+    return flip * half + apart
 
 
 def in_hbm(x):
@@ -546,10 +551,8 @@
     later = x if later is None else later
     ahead = lambda x, by: lax.ppermute(x, "pool", [(i, (i + 2 * by) % npool) for i in range(npool)])
     across = lambda x: lax.ppermute(x, "pool", [(i, i ^ 1) for i in range(npool)])
-    straight = {0: x}
-    for by in distances(npool)[1:]:
-        straight[by] = ahead(x if by == half // 2 else later, by)
-    return list(straight.values()) + [across(y) for y in straight.values()]
+    straight = [x] + [ahead(x if by == half // 2 else later, by) for by in range(1, half)]
+    return straight + [across(y) for y in straight]
 
 
 def swap_halves(x):

time: 67.3 us -> 64.2 us (0.954)
  starting transfers between devices: 30.6 us -> 22.8 us
  waiting for transfers between devices: 15 us -> 20.1 us
    all_to_all x1, starting transfers between devices: 9.04 us -> 3.38 us  [shards(): lax.all_to_all(parts, 'pool', split_axis=0, concat_axis=0, tiled=True)]
    ppermute x6, waiting for transfers between devices: 7.34 us -> 11.4 us  [gathered(): lax.ppermute(x, 'pool', [(i, (i + 2 * by) % npool) for i in range(npool)])]
    ppermute x8, starting transfers between devices: 10.8 us -> 9.15 us  [gathered(): lax.ppermute(x, 'pool', [(i, i ^ 1) for i in range(npool)])]
  transfers between devices with their start and end apart: 16 -> 16, of which waited for: 11 -> 12; matrix products, arithmetic and copies ran while one was open for 0% -> 0% of each run, Pallas kernels for 20% -> 20%
where the time goes in v11:
time: 64.2 us; the launch traced here: 63.7 us
  starting transfers between devices  22.8 us (36%)
  waiting for transfers between devices  20.1 us (31%)
  Pallas kernels  19.8 us (31%)
  other arithmetic  0.86 us (1%)
    ppermute x6, waiting for transfers between devices, gathered(): lax.ppermute(x, 'pool', [(i, (i + 2 * by) % npool) for i in range(npool)])  11.4 us
    ppermute x6, starting transfers between devices, gathered(): lax.ppermute(x, 'pool', [(i, (i + 2 * by) % npool) for i in range(npool)])  10.1 us
    ppermute x8, starting transfers between devices, gathered(): lax.ppermute(x, 'pool', [(i, i ^ 1) for i in range(npool)])  9.15 us
    ppermute x8, waiting for transfers between devices, gathered(): lax.ppermute(x, 'pool', [(i, i ^ 1) for i in range(npool)])  7.06 us
    pallas_call x1, Pallas kernels, local_attention(): pl.pallas_call(functools.partial(local_kernel, page_len, heads), out_shap...  6.44 us
    all_to_all x1, starting transfers between devices, shards(): lax.all_to_all(parts, 'pool', split_axis=0, concat_axis=0, tiled=True)  3.38 us
    pallas_call x1, Pallas kernels, rotated_pages(): pl.pallas_call(functools.partial(rope_kernel, npool, cache_pages, per), g...  2.96 us
    pallas_call x1, Pallas kernels, arrived_attention(): pl.pallas_call(functools.partial(arrived_kernel, npool, pair), out_shape=...  2.88 us
  transfers between devices with their start and end apart: 16, of which 12 were waited for; matrix products, arithmetic and copies ran while one was open for 0% of the time, Pallas kernels for 20%

profile of v11, /device:TPU:0, one launch (start us, length us, event | category | flops | bytes accessed | tf_op | source)
XLA Modules:
  0.0 63.7 jit_solution(2470665426304888796)
XLA Ops:
  1.2 5.1 %collective-permute-start.2 = (bf16[17,32,128]{2,1,0:T(8,128)(2,1)S(1)}, bf16[17,32,128]{2,1,0:T(8,128)(2,1)S(1)}, u32[]{:S(2)}, u32[]{:S(2)}) collective-permute-start(bf16[17,32,128]{2,1,0:T(8,128)(2,1)S(1)} %asked_queries.1.refs_0_.q_ref), channel_id=1, source_target_pairs={{0,12},{2,14},{4,0},{6,2},{8,4},{10,6},{12,8},{14,10},{1,13},{3,15... | collective-permute-start | bytes 417800 | tf_op jit(solution)/shard_map/ppermute | solution.py:552
  7.3 1.5 %collective-permute-start.3 = (bf16[17,32,128]{2,1,0:T(8,128)(2,1)S(1)}, bf16[17,32,128]{2,1,0:T(8,128)(2,1)S(1)}, u32[]{:S(2)}, u32[]{:S(2)}) collective-permute-start(bf16[17,32,128]{2,1,0:T(8,128)(2,1)S(1)} %asked_queries.1.refs_0_.q_ref), channel_id=1, source_target_pairs={{0,2},{2,0},{4,6},{6,4},{8,10},{10,8},{12,14},{14,12},{1,3},{3,1},... | collective-permute-start | bytes 417800 | tf_op jit(solution)/shard_map/ppermute | solution.py:553
  8.9 1.6 %collective-permute-done.2.refs_3_ = bf16[17,32,128]{2,1,0:T(8,128)(2,1)S(1)} collective-permute-done((bf16[17,32,128]{2,1,0:T(8,128)(2,1)S(1)}, bf16[17,32,128]{2,1,0:T(8,128)(2,1)S(1)}, u32[]{:S(2)}, u32[]{:S(2)}) %collective-permute-start.2) | collective-permute-done | bytes 139296 | tf_op jit(solution)/shard_map/ppermute | solution.py:552
  10.4 1.5 %collective-permute-start.6 = (bf16[17,32,128]{2,1,0:T(8,128)(2,1)S(1)}, bf16[17,32,128]{2,1,0:T(8,128)(2,1)S(1)}, u32[]{:S(2)}, u32[]{:S(2)}) collective-permute-start(bf16[17,32,128]{2,1,0:T(8,128)(2,1)S(1)} %collective-permute-done.2.refs_3_), channel_id=1, source_target_pairs={{0,2},{2,0},{4,6},{6,4},{8,10},{10,8},{12,14},{14,12},{1,3},{3,1},... | collective-permute-start | bytes 417800 | tf_op jit(solution)/shard_map/ppermute | solution.py:553
  11.9 6.2 %collective-permute-done.1.refs_2_ = bf16[17,32,128]{2,1,0:T(8,128)(2,1)S(1)} collective-permute-done((bf16[17,32,128]{2,1,0:T(8,128)(2,1)S(1)}, bf16[17,32,128]{2,1,0:T(8,128)(2,1)S(1)}, u32[]{:S(2)}, u32[]{:S(2)}) %collective-permute-start.1) | collective-permute-done | bytes 139296 | tf_op jit(solution)/shard_map/ppermute | solution.py:552
  18.1 1.5 %collective-permute-start.5 = (bf16[17,32,128]{2,1,0:T(8,128)(2,1)S(1)}, bf16[17,32,128]{2,1,0:T(8,128)(2,1)S(1)}, u32[]{:S(2)}, u32[]{:S(2)}) collective-permute-start(bf16[17,32,128]{2,1,0:T(8,128)(2,1)S(1)} %collective-permute-done.1.refs_2_), channel_id=1, source_target_pairs={{0,2},{2,0},{4,6},{6,4},{8,10},{10,8},{12,14},{14,12},{1,3},{3,1},... | collective-permute-start | bytes 417800 | tf_op jit(solution)/shard_map/ppermute | solution.py:553
  20.2 3.0 %rope_pages.1 = (bf16[16,2,2,128,128]{4,3,2,1,0:T(8,128)(2,1)S(1)}, s32[48]{0:T(128)S(1)}) custom-call(s32[16]{0:T(128)} %slot_ref.1, s32[1,4]{1,0:T(1,128)} %len_ref.1, bf16[16,2,2,128,128]{4,3,2,1,0:T(8,128)(2,1)} %pages_ref.1, f32[128,128]{1,0:T(8,128)} %constant.20.clone.ct_ref, f32[128,128]{1,0:T(8,128)} %constant.21.clone.st_ref, ...), custom_call_target="tpu_custom_call" | custom-call | flops 6000000 | bytes 2000000 | tf_op jit(solution)/shard_map/rope_pages/pallas_call | solution.py:86
  23.2 1.3 %collective-permute-done.5.refs_6_ = bf16[17,32,128]{2,1,0:T(8,128)(2,1)S(1)} collective-permute-done((bf16[17,32,128]{2,1,0:T(8,128)(2,1)S(1)}, bf16[17,32,128]{2,1,0:T(8,128)(2,1)S(1)}, u32[]{:S(2)}, u32[]{:S(2)}) %collective-permute-start.5) | collective-permute-done | bytes 139296 | tf_op jit(solution)/shard_map/ppermute | solution.py:553
  24.6 1.5 %collective-permute-done.4.refs_5_ = bf16[17,32,128]{2,1,0:T(8,128)(2,1)S(1)} collective-permute-done((bf16[17,32,128]{2,1,0:T(8,128)(2,1)S(1)}, bf16[17,32,128]{2,1,0:T(8,128)(2,1)S(1)}, u32[]{:S(2)}, u32[]{:S(2)}) %collective-permute-start.4) | collective-permute-done | bytes 139296 | tf_op jit(solution)/shard_map/ppermute | solution.py:553
  26.1 2.9 %arrived_attention.1 = bf16[8,80,128]{2,1,0:T(8,128)(2,1)} custom-call(s32[2]{0:T(128)S(1)} %pad_add_fusion.me_ref.place_ref, s32[48]{0:T(128)S(1)} %get-tuple-element.13.own_ref, bf16[17,32,128]{2,1,0:T(8,128)(2,1)S(1)} %asked_queries.1.refs_0_.q_ref, bf16[17,32,128]{2,1,0:T(8,128)(2,1)S(1)} %collective-permute-done.refs_1_, ...), custom_call_target="tpu_custom_call" | custom-call | flops 200000000 | bytes 4000000 | tf_op jit(solution)/shard_map/arrived_attention/pallas_call | solution.py:372
  28.9 3.4 %all-to-all-start = ((bf16[8,80,128]{2,1,0:T(8,128)(2,1)}), bf16[8,80,128]{2,1,0:T(8,128)(2,1)S(1)}, u32[]{:S(2)}, u32[]{:S(2)}) async-start(bf16[8,80,128]{2,1,0:T(8,128)(2,1)} %arrived_attention.1), calls=%async_computation | async-start | bytes 327680 | tf_op jit(solution)/shard_map/all_to_all | solution.py:588
  32.4 6.4 %local_attention.1 = (f32[512,128]{1,0:T(8,128)S(1)}, f32[512,128]{1,0:T(8,128)S(1)}) custom-call(s32[3,16]{1,0:T(4,128)} %bitcast.4, s32[16]{0:T(128)} %context_ref.3, s32[48]{0:T(128)} %fill_ref.1, bf16[17,32,128]{2,1,0:T(8,128)(2,1)S(1)} %asked_queries.1.refs_0_.q_ref, bf16[2,16,512]{2,1,0:T(8,128)(2,1)S(1)} %reshape.3.new_ref, ...), custom_call_target="tpu_custom_call" | custom-call | flops 800000000 | bytes 12000000 | tf_op jit(solution)/shard_map/local_attention/pallas_call | solution.py:290
  39.8 1.5 %merge.1.x_ref.refs_0_ = bf16[2,16,2048]{2,1,0:T(8,128)(2,1)S(1)} custom-call(s32[2]{0:T(128)S(1)} %pad_add_fusion.me_ref.place_ref, bf16[8,80,128]{2,1,0:T(8,128)(2,1)S(1)} %all-to-all-done.parts_ref, f32[512,128]{1,0:T(8,128)S(1)} %get-tuple-element.15.o_ref, f32[512,128]{1,0:T(8,128)S(1)} %get-tuple-element.16.stat_ref), custom_call_target="tpu_custom_call" | custom-call | flops 2000000 | bytes 1500000 | tf_op jit(solution)/shard_map/merge/pallas_call | solution.py:432
  41.4 2.0 %collective-permute-start.8 = (bf16[2,16,2048]{2,1,0:T(8,128)(2,1)S(1)}, bf16[2,16,2048]{2,1,0:T(8,128)(2,1)S(1)}, u32[]{:S(2)}, u32[]{:S(2)}) collective-permute-start(bf16[2,16,2048]{2,1,0:T(8,128)(2,1)S(1)} %merge.1.x_ref.refs_0_), channel_id=1, source_target_pairs={{0,8},{2,10},{4,12},{6,14},{8,0},{10,2},{12,4},{14,6},{1,9},{3,11}... | collective-permute-start | bytes 393224 | tf_op jit(solution)/shard_map/ppermute | solution.py:552
  43.3 2.2 %fetch_weight.1 = (bf16[2048,1024]{1,0:T(8,128)(2,1)S(1)}, bf16[2,16,2048]{2,1,0:T(8,128)(2,1)S(1)}) custom-call(bf16[2048,1024]{1,0:T(8,128)(2,1)} %weight_ref.1, bf16[2,16,2048]{2,1,0:T(8,128)(2,1)S(1)} %merge.1.x_ref.refs_0_), custom_call_target="tpu_custom_call" | custom-call | bytes 8388608 | tf_op jit(solution)/shard_map/fetch_weight/pallas_call | solution.py:456
  45.5 1.5 %collective-permute-start.9 = (bf16[2,16,2048]{2,1,0:T(8,128)(2,1)S(1)}, bf16[2,16,2048]{2,1,0:T(8,128)(2,1)S(1)}, u32[]{:S(2)}, u32[]{:S(2)}) collective-permute-start(bf16[2,16,2048]{2,1,0:T(8,128)(2,1)S(1)} %get-tuple-element.17), channel_id=1, source_target_pairs={{0,12},{2,14},{4,0},{6,2},{8,4},{10,6},{12,8},{14,10},{1,13},{3,15... | collective-permute-start | bytes 393224 | tf_op jit(solution)/shard_map/ppermute | solution.py:552
  47.6 1.4 %collective-permute-start.10 = (bf16[2,16,2048]{2,1,0:T(8,128)(2,1)S(1)}, bf16[2,16,2048]{2,1,0:T(8,128)(2,1)S(1)}, u32[]{:S(2)}, u32[]{:S(2)}) collective-permute-start(bf16[2,16,2048]{2,1,0:T(8,128)(2,1)S(1)} %merge.1.x_ref.refs_0_), channel_id=1, source_target_pairs={{0,2},{2,0},{4,6},{6,4},{8,10},{10,8},{12,14},{14,12},{1,3},{3,1},... | collective-permute-start | bytes 393224 | tf_op jit(solution)/shard_map/ppermute | solution.py:553
  49.0 1.4 %collective-permute-done.8.refs_2_ = bf16[2,16,2048]{2,1,0:T(8,128)(2,1)S(1)} collective-permute-done((bf16[2,16,2048]{2,1,0:T(8,128)(2,1)S(1)}, bf16[2,16,2048]{2,1,0:T(8,128)(2,1)S(1)}, u32[]{:S(2)}, u32[]{:S(2)}) %collective-permute-start.8) | collective-permute-done | bytes 131104 | tf_op jit(solution)/shard_map/ppermute | solution.py:552
  50.4 1.7 %collective-permute-done.9.refs_3_ = bf16[2,16,2048]{2,1,0:T(8,128)(2,1)S(1)} collective-permute-done((bf16[2,16,2048]{2,1,0:T(8,128)(2,1)S(1)}, bf16[2,16,2048]{2,1,0:T(8,128)(2,1)S(1)}, u32[]{:S(2)}, u32[]{:S(2)}) %collective-permute-start.9) | collective-permute-done | bytes 131104 | tf_op jit(solution)/shard_map/ppermute | solution.py:552
  53.9 1.4 %collective-permute-start.11 = (bf16[2,16,2048]{2,1,0:T(8,128)(2,1)S(1)}, bf16[2,16,2048]{2,1,0:T(8,128)(2,1)S(1)}, u32[]{:S(2)}, u32[]{:S(2)}) collective-permute-start(bf16[2,16,2048]{2,1,0:T(8,128)(2,1)S(1)} %collective-permute-done.7.refs_1_), channel_id=1, source_target_pairs={{0,2},{2,0},{4,6},{6,4},{8,10},{10,8},{12,14},{14,12},{1,3},{3,1},... | collective-permute-start | bytes 393224 | tf_op jit(solution)/shard_map/ppermute | solution.py:553
  55.4 1.4 %collective-permute-done.12.refs_6_ = bf16[2,16,2048]{2,1,0:T(8,128)(2,1)S(1)} collective-permute-done((bf16[2,16,2048]{2,1,0:T(8,128)(2,1)S(1)}, bf16[2,16,2048]{2,1,0:T(8,128)(2,1)S(1)}, u32[]{:S(2)}, u32[]{:S(2)}) %collective-permute-start.12) | collective-permute-done | bytes 131104 | tf_op jit(solution)/shard_map/ppermute | solution.py:553
  56.7 1.4 %collective-permute-done.13.refs_7_ = bf16[2,16,2048]{2,1,0:T(8,128)(2,1)S(1)} collective-permute-done((bf16[2,16,2048]{2,1,0:T(8,128)(2,1)S(1)}, bf16[2,16,2048]{2,1,0:T(8,128)(2,1)S(1)}, u32[]{:S(2)}, u32[]{:S(2)}) %collective-permute-start.13) | collective-permute-done | bytes 131104 | tf_op jit(solution)/shard_map/ppermute | solution.py:553
  58.2 1.4 %collective-permute-done.11.refs_5_ = bf16[2,16,2048]{2,1,0:T(8,128)(2,1)S(1)} collective-permute-done((bf16[2,16,2048]{2,1,0:T(8,128)(2,1)S(1)}, bf16[2,16,2048]{2,1,0:T(8,128)(2,1)S(1)}, u32[]{:S(2)}, u32[]{:S(2)}) %collective-permute-start.11) | collective-permute-done | bytes 131104 | tf_op jit(solution)/shard_map/ppermute | solution.py:553
  59.6 1.3 %project_other.1 = (f32[2,128,512]{2,1,0:T(8,128)S(1)}, bf16[256,2048]{1,0:T(8,128)(2,1)S(1)}) custom-call(s32[2]{0:T(128)S(1)} %pad_add_fusion.me_ref.place_ref, bf16[2,16,2048]{2,1,0:T(8,128)(2,1)S(1)} %merge.1.x_ref.refs_0_, bf16[2,16,2048]{2,1,0:T(8,128)(2,1)S(1)} %collective-permute-done.7.refs_1_, ...), custom_call_target="tpu_custom_call" | custom-call | flops 536870912 | bytes 4000000 | tf_op jit(solution)/shard_map/project_other/pallas_call | solution.py:495
  (21 shorter events, 9.1 us)
Async XLA Ops:
  0.0 32.3 %copy-start = (bf16[2,16,2,2,128]{4,3,2,1,0:T(2,128)(2,1)S(1)}, bf16[2,16,2,2,128]{4,3,2,1,0:T(2,128)(2,1)}, u32[]{:S(2)}) copy-start(bf16[2,16,2,2,128]{4,3,2,1,0:T(2,128)(2,1)} %param.24) | copy-start | bytes 98308
  1.2 9.2 %collective-permute-start.2 = (bf16[17,32,128]{2,1,0:T(8,128)(2,1)S(1)}, bf16[17,32,128]{2,1,0:T(8,128)(2,1)S(1)}, u32[]{:S(2)}, u32[]{:S(2)}) collective-permute-start(bf16[17,32,128]{2,1,0:T(8,128)(2,1)S(1)} %asked_queries.1.refs_0_.q_ref), channel_id=1, source_target_pairs={{0,12},{2,14},{4,0},{6,2},{8,4},{10,6},{12,8},{14,10},{1,13},{3,15... | collective-permute-start | bytes 417800 | tf_op jit(solution)/shard_map/ppermute | solution.py:552
  6.3 11.8 %collective-permute-start.1 = (bf16[17,32,128]{2,1,0:T(8,128)(2,1)S(1)}, bf16[17,32,128]{2,1,0:T(8,128)(2,1)S(1)}, u32[]{:S(2)}, u32[]{:S(2)}) collective-permute-start(bf16[17,32,128]{2,1,0:T(8,128)(2,1)S(1)} %asked_queries.1.refs_0_.q_ref), channel_id=1, source_target_pairs={{0,8},{2,10},{4,12},{6,14},{8,0},{10,2},{12,4},{14,6},{1,9},{3,11}... | collective-permute-start | bytes 417800 | tf_op jit(solution)/shard_map/ppermute | solution.py:552
  6.3 13.3 %collective-permute-start = (bf16[17,32,128]{2,1,0:T(8,128)(2,1)S(1)}, bf16[17,32,128]{2,1,0:T(8,128)(2,1)S(1)}, u32[]{:S(2)}, u32[]{:S(2)}) collective-permute-start(bf16[17,32,128]{2,1,0:T(8,128)(2,1)S(1)} %asked_queries.1.refs_0_.q_ref), channel_id=1, source_target_pairs={{0,4},{2,6},{4,8},{6,10},{8,12},{10,14},{12,0},{14,2},{1,5},{3,7},... | collective-permute-start | bytes 417800 | tf_op jit(solution)/shard_map/ppermute | solution.py:552
  7.3 15.9 %collective-permute-start.3 = (bf16[17,32,128]{2,1,0:T(8,128)(2,1)S(1)}, bf16[17,32,128]{2,1,0:T(8,128)(2,1)S(1)}, u32[]{:S(2)}, u32[]{:S(2)}) collective-permute-start(bf16[17,32,128]{2,1,0:T(8,128)(2,1)S(1)} %asked_queries.1.refs_0_.q_ref), channel_id=1, source_target_pairs={{0,2},{2,0},{4,6},{6,4},{8,10},{10,8},{12,14},{14,12},{1,3},{3,1},... | collective-permute-start | bytes 417800 | tf_op jit(solution)/shard_map/ppermute | solution.py:553
  10.4 12.8 %collective-permute-start.6 = (bf16[17,32,128]{2,1,0:T(8,128)(2,1)S(1)}, bf16[17,32,128]{2,1,0:T(8,128)(2,1)S(1)}, u32[]{:S(2)}, u32[]{:S(2)}) collective-permute-start(bf16[17,32,128]{2,1,0:T(8,128)(2,1)S(1)} %collective-permute-done.2.refs_3_), channel_id=1, source_target_pairs={{0,2},{2,0},{4,6},{6,4},{8,10},{10,8},{12,14},{14,12},{1,3},{3,1},... | collective-permute-start | bytes 417800 | tf_op jit(solution)/shard_map/ppermute | solution.py:553
  18.1 6.4 %collective-permute-start.5 = (bf16[17,32,128]{2,1,0:T(8,128)(2,1)S(1)}, bf16[17,32,128]{2,1,0:T(8,128)(2,1)S(1)}, u32[]{:S(2)}, u32[]{:S(2)}) collective-permute-start(bf16[17,32,128]{2,1,0:T(8,128)(2,1)S(1)} %collective-permute-done.1.refs_2_), channel_id=1, source_target_pairs={{0,2},{2,0},{4,6},{6,4},{8,10},{10,8},{12,14},{14,12},{1,3},{3,1},... | collective-permute-start | bytes 417800 | tf_op jit(solution)/shard_map/ppermute | solution.py:553
  19.7 6.4 %collective-permute-start.4 = (bf16[17,32,128]{2,1,0:T(8,128)(2,1)S(1)}, bf16[17,32,128]{2,1,0:T(8,128)(2,1)S(1)}, u32[]{:S(2)}, u32[]{:S(2)}) collective-permute-start(bf16[17,32,128]{2,1,0:T(8,128)(2,1)S(1)} %collective-permute-done.refs_1_), channel_id=1, source_target_pairs={{0,2},{2,0},{4,6},{6,4},{8,10},{10,8},{12,14},{14,12},{1,3},{3,1},... | collective-permute-start | bytes 417800 | tf_op jit(solution)/shard_map/ppermute | solution.py:553
  28.9 10.9 %all-to-all-start = ((bf16[8,80,128]{2,1,0:T(8,128)(2,1)}), bf16[8,80,128]{2,1,0:T(8,128)(2,1)S(1)}, u32[]{:S(2)}, u32[]{:S(2)}) async-start(bf16[8,80,128]{2,1,0:T(8,128)(2,1)} %arrived_attention.1), calls=%async_computation | async-start | bytes 327680 | tf_op jit(solution)/shard_map/all_to_all | solution.py:588
  41.4 9.0 %collective-permute-start.8 = (bf16[2,16,2048]{2,1,0:T(8,128)(2,1)S(1)}, bf16[2,16,2048]{2,1,0:T(8,128)(2,1)S(1)}, u32[]{:S(2)}, u32[]{:S(2)}) collective-permute-start(bf16[2,16,2048]{2,1,0:T(8,128)(2,1)S(1)} %merge.1.x_ref.refs_0_), channel_id=1, source_target_pairs={{0,8},{2,10},{4,12},{6,14},{8,0},{10,2},{12,4},{14,6},{1,9},{3,11}... | collective-permute-start | bytes 393224 | tf_op jit(solution)/shard_map/ppermute | solution.py:552
  45.5 6.5 %collective-permute-start.9 = (bf16[2,16,2048]{2,1,0:T(8,128)(2,1)S(1)}, bf16[2,16,2048]{2,1,0:T(8,128)(2,1)S(1)}, u32[]{:S(2)}, u32[]{:S(2)}) collective-permute-start(bf16[2,16,2048]{2,1,0:T(8,128)(2,1)S(1)} %get-tuple-element.17), channel_id=1, source_target_pairs={{0,12},{2,14},{4,0},{6,2},{8,4},{10,6},{12,8},{14,10},{1,13},{3,15... | collective-permute-start | bytes 393224 | tf_op jit(solution)/shard_map/ppermute | solution.py:552
  47.0 6.9 %collective-permute-start.7 = (bf16[2,16,2048]{2,1,0:T(8,128)(2,1)S(1)}, bf16[2,16,2048]{2,1,0:T(8,128)(2,1)S(1)}, u32[]{:S(2)}, u32[]{:S(2)}) collective-permute-start(bf16[2,16,2048]{2,1,0:T(8,128)(2,1)S(1)} %get-tuple-element.17), channel_id=1, source_target_pairs={{0,4},{2,6},{4,8},{6,10},{8,12},{10,14},{12,0},{14,2},{1,5},{3,7},... | collective-permute-start | bytes 393224 | tf_op jit(solution)/shard_map/ppermute | solution.py:552
  47.6 7.7 %collective-permute-start.10 = (bf16[2,16,2048]{2,1,0:T(8,128)(2,1)S(1)}, bf16[2,16,2048]{2,1,0:T(8,128)(2,1)S(1)}, u32[]{:S(2)}, u32[]{:S(2)}) collective-permute-start(bf16[2,16,2048]{2,1,0:T(8,128)(2,1)S(1)} %merge.1.x_ref.refs_0_), channel_id=1, source_target_pairs={{0,2},{2,0},{4,6},{6,4},{8,10},{10,8},{12,14},{14,12},{1,3},{3,1},... | collective-permute-start | bytes 393224 | tf_op jit(solution)/shard_map/ppermute | solution.py:553
  50.4 6.3 %collective-permute-start.12 = (bf16[2,16,2048]{2,1,0:T(8,128)(2,1)S(1)}, bf16[2,16,2048]{2,1,0:T(8,128)(2,1)S(1)}, u32[]{:S(2)}, u32[]{:S(2)}) collective-permute-start(bf16[2,16,2048]{2,1,0:T(8,128)(2,1)S(1)} %collective-permute-done.8.refs_2_), channel_id=1, source_target_pairs={{0,2},{2,0},{4,6},{6,4},{8,10},{10,8},{12,14},{14,12},{1,3},{3,1},... | collective-permute-start | bytes 393224 | tf_op jit(solution)/shard_map/ppermute | solution.py:553
  52.1 6.1 %collective-permute-start.13 = (bf16[2,16,2048]{2,1,0:T(8,128)(2,1)S(1)}, bf16[2,16,2048]{2,1,0:T(8,128)(2,1)S(1)}, u32[]{:S(2)}, u32[]{:S(2)}) collective-permute-start(bf16[2,16,2048]{2,1,0:T(8,128)(2,1)S(1)} %collective-permute-done.9.refs_3_), channel_id=1, source_target_pairs={{0,2},{2,0},{4,6},{6,4},{8,10},{10,8},{12,14},{14,12},{1,3},{3,1},... | collective-permute-start | bytes 393224 | tf_op jit(solution)/shard_map/ppermute | solution.py:553
  53.9 5.6 %collective-permute-start.11 = (bf16[2,16,2048]{2,1,0:T(8,128)(2,1)S(1)}, bf16[2,16,2048]{2,1,0:T(8,128)(2,1)S(1)}, u32[]{:S(2)}, u32[]{:S(2)}) collective-permute-start(bf16[2,16,2048]{2,1,0:T(8,128)(2,1)S(1)} %collective-permute-done.7.refs_1_), channel_id=1, source_target_pairs={{0,2},{2,0},{4,6},{6,4},{8,10},{10,8},{12,14},{14,12},{1,3},{3,1},... | collective-permute-start | bytes 393224 | tf_op jit(solution)/shard_map/ppermute | solution.py:553
  60.9 2.0 %collective-permute-start.14 = (f32[2,128,512]{2,1,0:T(8,128)S(1)}, f32[2,128,512]{2,1,0:T(8,128)S(1)}, u32[]{:S(2)}, u32[]{:S(2)}) collective-permute-start(f32[2,128,512]{2,1,0:T(8,128)S(1)} %get-tuple-element.20), channel_id=1, source_target_pairs={{0,1},{1,0},{2,3},{3,2},{4,5},{5,4},{6,7},{7,6},{8,9},{9,8},{10,11... | collective-permute-start | bytes 1572872 | tf_op jit(solution)/shard_map/ppermute | solution.py:559

commit v12 on v11

--- a/solution.py
+++ b/solution.py
@@ -152,7 +152,7 @@
 
 
 def transposed_scores(queries, keys, group):
-    turned = jnp.transpose(queries.astype(F32), (1, 0)).astype(BF16)
+    turned = jnp.transpose(queries, (1, 0))
     chain = lax.broadcasted_iota(I32, (1, turned.shape[1]), 1) // group
     spread = [turned * jnp.where(chain == c, 1.0, 0.0).astype(BF16) for c in range(len(keys))]
     scores = jnp.dot(
@@ -265,19 +265,17 @@
         parts = [jnp.exp(x - top) for x in parts]
         total = functools.reduce(jnp.add, [jnp.sum(x, axis=0, keepdims=True) for x in parts])
         stats = jnp.concatenate(
-            [parts[most], jnp.broadcast_to(top, (8, LANES)), jnp.broadcast_to(total, (8, LANES))]
-            + [jnp.zeros((LANES - group - 16, LANES), F32)],
-            axis=0,
+            [parts[most], jnp.broadcast_to(top, (8, LANES)), jnp.broadcast_to(total, (8, LANES))], axis=0
         )
         stats = jnp.transpose(stats, (1, 0))
-        weights = [jnp.transpose(x, (1, 0)).astype(BF16) for x in parts[:most]]
+        weights = [jnp.transpose(x.astype(BF16), (1, 0)) for x in parts[:most]]
         weights.append(stats[:, :group].astype(BF16))
         weights = jnp.concatenate(weights, axis=1)
         for x in range(together):
             both = [jnp.concatenate(values[x * heads + k], axis=0) for k in range(heads)]
             both = weighted_values(weights[x * block : (x + 1) * block, :], both)
             o_ref[i * LANES + x * block : i * LANES + (x + 1) * block, :] = both
-        stat_ref[i * LANES : (i + 1) * LANES, :] = stats
+        stat_ref[i * LANES : (i + 1) * LANES, : stats.shape[1]] = stats
 
 
 def local_attention(table, context, fills, queries, new_kv, cache_kv, tabs):
@@ -353,7 +351,7 @@
         stats = pieces(top) + pieces(jnp.sum(weights, axis=0, keepdims=True))
         stats.append(lane_values([request[x] for x in own], block, (1, LANES)).astype(F32))
         stats = jnp.concatenate(stats + [jnp.zeros((STAT_ROWS - len(stats), LANES), F32)], axis=0).astype(BF16)
-        weights = jnp.transpose(weights, (1, 0)).astype(BF16)
+        weights = jnp.transpose(weights.astype(BF16), (1, 0))
         for c, x in enumerate(own):
             both = [pages_ref[number[x], 1, k] for k in range(heads)]
             both = weighted_values(weights[c * block : (c + 1) * block, :], both)
@@ -442,10 +440,13 @@
 
 
 def fetch_kernel(weight_ref, x_ref, weight_out, x_out, sems):
-    copies = [
-        pltpu.make_async_copy(weight_ref, weight_out, sems.at[0]),
-        pltpu.make_async_copy(x_ref, x_out, sems.at[1]),
-    ]
+    chunks = sems.shape[0] - 1
+    rows = weight_ref.shape[0] // chunks
+    copies = []
+    for i in range(chunks):
+        at = pl.ds(i * rows, rows)
+        copies.append(pltpu.make_async_copy(weight_ref.at[at], weight_out.at[at], sems.at[i]))
+    copies.append(pltpu.make_async_copy(x_ref, x_out, sems.at[chunks]))
     for copy in copies:
         copy.start()
     for copy in copies:
@@ -458,7 +459,7 @@
         out_shape=[pltpu.VMEM(weight.shape, weight.dtype), pltpu.VMEM(x.shape, x.dtype)],
         in_specs=[ANY, ANY],
         out_specs=[ANY, ANY],
-        scratch_shapes=[pltpu.SemaphoreType.DMA((2,))],
+        scratch_shapes=[pltpu.SemaphoreType.DMA((9,))],
         compiler_params=PARAMS,
         cost_estimate=pl.CostEstimate(flops=0, bytes_accessed=2 * weight.size * 2, transcendentals=0),
         name="fetch_weight",

time: 64.2 us -> 64.1 us (level)
  no operation moved by 1% of the time
where the time goes in v12:
time: 64.1 us; the launch traced here: 63.5 us
  starting transfers between devices  22.9 us (36%)
  waiting for transfers between devices  19.9 us (31%)
  Pallas kernels  19.8 us (31%)
  other arithmetic  0.86 us (1%)
    ppermute x6, waiting for transfers between devices, gathered(): lax.ppermute(x, 'pool', [(i, (i + 2 * by) % npool) for i in range(npool)])  11.2 us
    ppermute x6, starting transfers between devices, gathered(): lax.ppermute(x, 'pool', [(i, (i + 2 * by) % npool) for i in range(npool)])  10.2 us
    ppermute x8, starting transfers between devices, gathered(): lax.ppermute(x, 'pool', [(i, i ^ 1) for i in range(npool)])  9.23 us
    ppermute x8, waiting for transfers between devices, gathered(): lax.ppermute(x, 'pool', [(i, i ^ 1) for i in range(npool)])  7.05 us
    pallas_call x1, Pallas kernels, local_attention(): pl.pallas_call(functools.partial(local_kernel, page_len, heads), out_shap...  6.45 us
    all_to_all x1, starting transfers between devices, shards(): lax.all_to_all(parts, 'pool', split_axis=0, concat_axis=0, tiled=True)  3.38 us
    pallas_call x1, Pallas kernels, rotated_pages(): pl.pallas_call(functools.partial(rope_kernel, npool, cache_pages, per), g...  2.96 us
    pallas_call x1, Pallas kernels, arrived_attention(): pl.pallas_call(functools.partial(arrived_kernel, npool, pair), out_shape=...  2.79 us
  transfers between devices with their start and end apart: 16, of which 12 were waited for; matrix products, arithmetic and copies ran while one was open for 0% of the time, Pallas kernels for 20%

profile of v12, /device:TPU:0, one launch (start us, length us, event | category | flops | bytes accessed | tf_op | source)
XLA Modules:
  0.0 63.5 jit_solution(17130845416877962772)
XLA Ops:
  1.2 5.1 %collective-permute-start.2 = (bf16[17,32,128]{2,1,0:T(8,128)(2,1)S(1)}, bf16[17,32,128]{2,1,0:T(8,128)(2,1)S(1)}, u32[]{:S(2)}, u32[]{:S(2)}) collective-permute-start(bf16[17,32,128]{2,1,0:T(8,128)(2,1)S(1)} %asked_queries.1.refs_0_.q_ref), channel_id=1, source_target_pairs={{0,12},{2,14},{4,0},{6,2},{8,4},{10,6},{12,8},{14,10},{1,13},{3,15... | collective-permute-start | bytes 417800 | tf_op jit(solution)/shard_map/ppermute | solution.py:553
  7.3 1.5 %collective-permute-start.3 = (bf16[17,32,128]{2,1,0:T(8,128)(2,1)S(1)}, bf16[17,32,128]{2,1,0:T(8,128)(2,1)S(1)}, u32[]{:S(2)}, u32[]{:S(2)}) collective-permute-start(bf16[17,32,128]{2,1,0:T(8,128)(2,1)S(1)} %asked_queries.1.refs_0_.q_ref), channel_id=1, source_target_pairs={{0,2},{2,0},{4,6},{6,4},{8,10},{10,8},{12,14},{14,12},{1,3},{3,1},... | collective-permute-start | bytes 417800 | tf_op jit(solution)/shard_map/ppermute | solution.py:554
  8.9 1.6 %collective-permute-done.2.refs_3_ = bf16[17,32,128]{2,1,0:T(8,128)(2,1)S(1)} collective-permute-done((bf16[17,32,128]{2,1,0:T(8,128)(2,1)S(1)}, bf16[17,32,128]{2,1,0:T(8,128)(2,1)S(1)}, u32[]{:S(2)}, u32[]{:S(2)}) %collective-permute-start.2) | collective-permute-done | bytes 139296 | tf_op jit(solution)/shard_map/ppermute | solution.py:553
  10.4 1.5 %collective-permute-start.6 = (bf16[17,32,128]{2,1,0:T(8,128)(2,1)S(1)}, bf16[17,32,128]{2,1,0:T(8,128)(2,1)S(1)}, u32[]{:S(2)}, u32[]{:S(2)}) collective-permute-start(bf16[17,32,128]{2,1,0:T(8,128)(2,1)S(1)} %collective-permute-done.2.refs_3_), channel_id=1, source_target_pairs={{0,2},{2,0},{4,6},{6,4},{8,10},{10,8},{12,14},{14,12},{1,3},{3,1},... | collective-permute-start | bytes 417800 | tf_op jit(solution)/shard_map/ppermute | solution.py:554
  11.9 6.2 %collective-permute-done.1.refs_2_ = bf16[17,32,128]{2,1,0:T(8,128)(2,1)S(1)} collective-permute-done((bf16[17,32,128]{2,1,0:T(8,128)(2,1)S(1)}, bf16[17,32,128]{2,1,0:T(8,128)(2,1)S(1)}, u32[]{:S(2)}, u32[]{:S(2)}) %collective-permute-start.1) | collective-permute-done | bytes 139296 | tf_op jit(solution)/shard_map/ppermute | solution.py:553
  18.1 1.5 %collective-permute-start.5 = (bf16[17,32,128]{2,1,0:T(8,128)(2,1)S(1)}, bf16[17,32,128]{2,1,0:T(8,128)(2,1)S(1)}, u32[]{:S(2)}, u32[]{:S(2)}) collective-permute-start(bf16[17,32,128]{2,1,0:T(8,128)(2,1)S(1)} %collective-permute-done.1.refs_2_), channel_id=1, source_target_pairs={{0,2},{2,0},{4,6},{6,4},{8,10},{10,8},{12,14},{14,12},{1,3},{3,1},... | collective-permute-start | bytes 417800 | tf_op jit(solution)/shard_map/ppermute | solution.py:554
  20.2 3.0 %rope_pages.1 = (bf16[16,2,2,128,128]{4,3,2,1,0:T(8,128)(2,1)S(1)}, s32[48]{0:T(128)S(1)}) custom-call(s32[16]{0:T(128)} %slot_ref.1, s32[1,4]{1,0:T(1,128)} %len_ref.1, bf16[16,2,2,128,128]{4,3,2,1,0:T(8,128)(2,1)} %pages_ref.1, f32[128,128]{1,0:T(8,128)} %constant.20.clone.ct_ref, f32[128,128]{1,0:T(8,128)} %constant.21.clone.st_ref, ...), custom_call_target="tpu_custom_call" | custom-call | flops 6000000 | bytes 2000000 | tf_op jit(solution)/shard_map/rope_pages/pallas_call | solution.py:86
  23.2 1.3 %collective-permute-done.5.refs_6_ = bf16[17,32,128]{2,1,0:T(8,128)(2,1)S(1)} collective-permute-done((bf16[17,32,128]{2,1,0:T(8,128)(2,1)S(1)}, bf16[17,32,128]{2,1,0:T(8,128)(2,1)S(1)}, u32[]{:S(2)}, u32[]{:S(2)}) %collective-permute-start.5) | collective-permute-done | bytes 139296 | tf_op jit(solution)/shard_map/ppermute | solution.py:554
  24.6 1.5 %collective-permute-done.4.refs_5_ = bf16[17,32,128]{2,1,0:T(8,128)(2,1)S(1)} collective-permute-done((bf16[17,32,128]{2,1,0:T(8,128)(2,1)S(1)}, bf16[17,32,128]{2,1,0:T(8,128)(2,1)S(1)}, u32[]{:S(2)}, u32[]{:S(2)}) %collective-permute-start.4) | collective-permute-done | bytes 139296 | tf_op jit(solution)/shard_map/ppermute | solution.py:554
  26.1 2.8 %arrived_attention.1 = bf16[8,80,128]{2,1,0:T(8,128)(2,1)} custom-call(s32[2]{0:T(128)S(1)} %pad_add_fusion.me_ref.place_ref, s32[48]{0:T(128)S(1)} %get-tuple-element.13.own_ref, bf16[17,32,128]{2,1,0:T(8,128)(2,1)S(1)} %asked_queries.1.refs_0_.q_ref, bf16[17,32,128]{2,1,0:T(8,128)(2,1)S(1)} %collective-permute-done.refs_1_, ...), custom_call_target="tpu_custom_call" | custom-call | flops 200000000 | bytes 4000000 | tf_op jit(solution)/shard_map/arrived_attention/pallas_call | solution.py:370
  28.9 3.4 %all-to-all-start = ((bf16[8,80,128]{2,1,0:T(8,128)(2,1)}), bf16[8,80,128]{2,1,0:T(8,128)(2,1)S(1)}, u32[]{:S(2)}, u32[]{:S(2)}) async-start(bf16[8,80,128]{2,1,0:T(8,128)(2,1)} %arrived_attention.1), calls=%async_computation | async-start | bytes 327680 | tf_op jit(solution)/shard_map/all_to_all | solution.py:589
  32.3 6.4 %local_attention.1 = (f32[512,128]{1,0:T(8,128)S(1)}, f32[512,128]{1,0:T(8,128)S(1)}) custom-call(s32[3,16]{1,0:T(4,128)} %bitcast.4, s32[16]{0:T(128)} %context_ref.3, s32[48]{0:T(128)} %fill_ref.1, bf16[17,32,128]{2,1,0:T(8,128)(2,1)S(1)} %asked_queries.1.refs_0_.q_ref, bf16[2,16,512]{2,1,0:T(8,128)(2,1)S(1)} %reshape.3.new_ref, ...), custom_call_target="tpu_custom_call" | custom-call | flops 800000000 | bytes 12000000 | tf_op jit(solution)/shard_map/local_attention/pallas_call | solution.py:288
  39.8 1.5 %merge.1.x_ref.refs_0_ = bf16[2,16,2048]{2,1,0:T(8,128)(2,1)S(1)} custom-call(s32[2]{0:T(128)S(1)} %pad_add_fusion.me_ref.place_ref, bf16[8,80,128]{2,1,0:T(8,128)(2,1)S(1)} %all-to-all-done.parts_ref, f32[512,128]{1,0:T(8,128)S(1)} %get-tuple-element.15.o_ref, f32[512,128]{1,0:T(8,128)S(1)} %get-tuple-element.16.stat_ref), custom_call_target="tpu_custom_call" | custom-call | flops 2000000 | bytes 1500000 | tf_op jit(solution)/shard_map/merge/pallas_call | solution.py:430
  41.3 2.0 %collective-permute-start.8 = (bf16[2,16,2048]{2,1,0:T(8,128)(2,1)S(1)}, bf16[2,16,2048]{2,1,0:T(8,128)(2,1)S(1)}, u32[]{:S(2)}, u32[]{:S(2)}) collective-permute-start(bf16[2,16,2048]{2,1,0:T(8,128)(2,1)S(1)} %merge.1.x_ref.refs_0_), channel_id=1, source_target_pairs={{0,8},{2,10},{4,12},{6,14},{8,0},{10,2},{12,4},{14,6},{1,9},{3,11}... | collective-permute-start | bytes 393224 | tf_op jit(solution)/shard_map/ppermute | solution.py:553
  43.3 2.2 %fetch_weight.1 = (bf16[2048,1024]{1,0:T(8,128)(2,1)S(1)}, bf16[2,16,2048]{2,1,0:T(8,128)(2,1)S(1)}) custom-call(bf16[2048,1024]{1,0:T(8,128)(2,1)} %weight_ref.1, bf16[2,16,2048]{2,1,0:T(8,128)(2,1)S(1)} %merge.1.x_ref.refs_0_), custom_call_target="tpu_custom_call" | custom-call | bytes 8388608 | tf_op jit(solution)/shard_map/fetch_weight/pallas_call | solution.py:457
  45.5 1.4 %collective-permute-start.9 = (bf16[2,16,2048]{2,1,0:T(8,128)(2,1)S(1)}, bf16[2,16,2048]{2,1,0:T(8,128)(2,1)S(1)}, u32[]{:S(2)}, u32[]{:S(2)}) collective-permute-start(bf16[2,16,2048]{2,1,0:T(8,128)(2,1)S(1)} %get-tuple-element.17), channel_id=1, source_target_pairs={{0,12},{2,14},{4,0},{6,2},{8,4},{10,6},{12,8},{14,10},{1,13},{3,15... | collective-permute-start | bytes 393224 | tf_op jit(solution)/shard_map/ppermute | solution.py:553
  47.6 1.5 %collective-permute-start.10 = (bf16[2,16,2048]{2,1,0:T(8,128)(2,1)S(1)}, bf16[2,16,2048]{2,1,0:T(8,128)(2,1)S(1)}, u32[]{:S(2)}, u32[]{:S(2)}) collective-permute-start(bf16[2,16,2048]{2,1,0:T(8,128)(2,1)S(1)} %merge.1.x_ref.refs_0_), channel_id=1, source_target_pairs={{0,2},{2,0},{4,6},{6,4},{8,10},{10,8},{12,14},{14,12},{1,3},{3,1},... | collective-permute-start | bytes 393224 | tf_op jit(solution)/shard_map/ppermute | solution.py:554
  49.0 1.4 %collective-permute-done.8.refs_2_ = bf16[2,16,2048]{2,1,0:T(8,128)(2,1)S(1)} collective-permute-done((bf16[2,16,2048]{2,1,0:T(8,128)(2,1)S(1)}, bf16[2,16,2048]{2,1,0:T(8,128)(2,1)S(1)}, u32[]{:S(2)}, u32[]{:S(2)}) %collective-permute-start.8) | collective-permute-done | bytes 131104 | tf_op jit(solution)/shard_map/ppermute | solution.py:553
  50.4 1.5 %collective-permute-done.9.refs_3_ = bf16[2,16,2048]{2,1,0:T(8,128)(2,1)S(1)} collective-permute-done((bf16[2,16,2048]{2,1,0:T(8,128)(2,1)S(1)}, bf16[2,16,2048]{2,1,0:T(8,128)(2,1)S(1)}, u32[]{:S(2)}, u32[]{:S(2)}) %collective-permute-start.9) | collective-permute-done | bytes 131104 | tf_op jit(solution)/shard_map/ppermute | solution.py:553
  53.8 1.4 %collective-permute-start.11 = (bf16[2,16,2048]{2,1,0:T(8,128)(2,1)S(1)}, bf16[2,16,2048]{2,1,0:T(8,128)(2,1)S(1)}, u32[]{:S(2)}, u32[]{:S(2)}) collective-permute-start(bf16[2,16,2048]{2,1,0:T(8,128)(2,1)S(1)} %collective-permute-done.7.refs_1_), channel_id=1, source_target_pairs={{0,2},{2,0},{4,6},{6,4},{8,10},{10,8},{12,14},{14,12},{1,3},{3,1},... | collective-permute-start | bytes 393224 | tf_op jit(solution)/shard_map/ppermute | solution.py:554
  55.2 1.4 %collective-permute-done.12.refs_6_ = bf16[2,16,2048]{2,1,0:T(8,128)(2,1)S(1)} collective-permute-done((bf16[2,16,2048]{2,1,0:T(8,128)(2,1)S(1)}, bf16[2,16,2048]{2,1,0:T(8,128)(2,1)S(1)}, u32[]{:S(2)}, u32[]{:S(2)}) %collective-permute-start.12) | collective-permute-done | bytes 131104 | tf_op jit(solution)/shard_map/ppermute | solution.py:554
  56.6 1.4 %collective-permute-done.13.refs_7_ = bf16[2,16,2048]{2,1,0:T(8,128)(2,1)S(1)} collective-permute-done((bf16[2,16,2048]{2,1,0:T(8,128)(2,1)S(1)}, bf16[2,16,2048]{2,1,0:T(8,128)(2,1)S(1)}, u32[]{:S(2)}, u32[]{:S(2)}) %collective-permute-start.13) | collective-permute-done | bytes 131104 | tf_op jit(solution)/shard_map/ppermute | solution.py:554
  58.0 1.4 %collective-permute-done.11.refs_5_ = bf16[2,16,2048]{2,1,0:T(8,128)(2,1)S(1)} collective-permute-done((bf16[2,16,2048]{2,1,0:T(8,128)(2,1)S(1)}, bf16[2,16,2048]{2,1,0:T(8,128)(2,1)S(1)}, u32[]{:S(2)}, u32[]{:S(2)}) %collective-permute-start.11) | collective-permute-done | bytes 131104 | tf_op jit(solution)/shard_map/ppermute | solution.py:554
  59.4 1.3 %project_other.1 = (f32[2,128,512]{2,1,0:T(8,128)S(1)}, bf16[256,2048]{1,0:T(8,128)(2,1)S(1)}) custom-call(s32[2]{0:T(128)S(1)} %pad_add_fusion.me_ref.place_ref, bf16[2,16,2048]{2,1,0:T(8,128)(2,1)S(1)} %merge.1.x_ref.refs_0_, bf16[2,16,2048]{2,1,0:T(8,128)(2,1)S(1)} %collective-permute-done.7.refs_1_, ...), custom_call_target="tpu_custom_call" | custom-call | flops 536870912 | bytes 4000000 | tf_op jit(solution)/shard_map/project_other/pallas_call | solution.py:496
  (21 shorter events, 9.1 us)
Async XLA Ops:
  0.0 32.3 %copy-start = (bf16[2,16,2,2,128]{4,3,2,1,0:T(2,128)(2,1)S(1)}, bf16[2,16,2,2,128]{4,3,2,1,0:T(2,128)(2,1)}, u32[]{:S(2)}) copy-start(bf16[2,16,2,2,128]{4,3,2,1,0:T(2,128)(2,1)} %param.24) | copy-start | bytes 98308
  1.2 9.2 %collective-permute-start.2 = (bf16[17,32,128]{2,1,0:T(8,128)(2,1)S(1)}, bf16[17,32,128]{2,1,0:T(8,128)(2,1)S(1)}, u32[]{:S(2)}, u32[]{:S(2)}) collective-permute-start(bf16[17,32,128]{2,1,0:T(8,128)(2,1)S(1)} %asked_queries.1.refs_0_.q_ref), channel_id=1, source_target_pairs={{0,12},{2,14},{4,0},{6,2},{8,4},{10,6},{12,8},{14,10},{1,13},{3,15... | collective-permute-start | bytes 417800 | tf_op jit(solution)/shard_map/ppermute | solution.py:553
  6.3 11.8 %collective-permute-start.1 = (bf16[17,32,128]{2,1,0:T(8,128)(2,1)S(1)}, bf16[17,32,128]{2,1,0:T(8,128)(2,1)S(1)}, u32[]{:S(2)}, u32[]{:S(2)}) collective-permute-start(bf16[17,32,128]{2,1,0:T(8,128)(2,1)S(1)} %asked_queries.1.refs_0_.q_ref), channel_id=1, source_target_pairs={{0,8},{2,10},{4,12},{6,14},{8,0},{10,2},{12,4},{14,6},{1,9},{3,11}... | collective-permute-start | bytes 417800 | tf_op jit(solution)/shard_map/ppermute | solution.py:553
  6.3 13.3 %collective-permute-start = (bf16[17,32,128]{2,1,0:T(8,128)(2,1)S(1)}, bf16[17,32,128]{2,1,0:T(8,128)(2,1)S(1)}, u32[]{:S(2)}, u32[]{:S(2)}) collective-permute-start(bf16[17,32,128]{2,1,0:T(8,128)(2,1)S(1)} %asked_queries.1.refs_0_.q_ref), channel_id=1, source_target_pairs={{0,4},{2,6},{4,8},{6,10},{8,12},{10,14},{12,0},{14,2},{1,5},{3,7},... | collective-permute-start | bytes 417800 | tf_op jit(solution)/shard_map/ppermute | solution.py:553
  7.3 15.9 %collective-permute-start.3 = (bf16[17,32,128]{2,1,0:T(8,128)(2,1)S(1)}, bf16[17,32,128]{2,1,0:T(8,128)(2,1)S(1)}, u32[]{:S(2)}, u32[]{:S(2)}) collective-permute-start(bf16[17,32,128]{2,1,0:T(8,128)(2,1)S(1)} %asked_queries.1.refs_0_.q_ref), channel_id=1, source_target_pairs={{0,2},{2,0},{4,6},{6,4},{8,10},{10,8},{12,14},{14,12},{1,3},{3,1},... | collective-permute-start | bytes 417800 | tf_op jit(solution)/shard_map/ppermute | solution.py:554
  10.4 12.8 %collective-permute-start.6 = (bf16[17,32,128]{2,1,0:T(8,128)(2,1)S(1)}, bf16[17,32,128]{2,1,0:T(8,128)(2,1)S(1)}, u32[]{:S(2)}, u32[]{:S(2)}) collective-permute-start(bf16[17,32,128]{2,1,0:T(8,128)(2,1)S(1)} %collective-permute-done.2.refs_3_), channel_id=1, source_target_pairs={{0,2},{2,0},{4,6},{6,4},{8,10},{10,8},{12,14},{14,12},{1,3},{3,1},... | collective-permute-start | bytes 417800 | tf_op jit(solution)/shard_map/ppermute | solution.py:554
  18.1 6.4 %collective-permute-start.5 = (bf16[17,32,128]{2,1,0:T(8,128)(2,1)S(1)}, bf16[17,32,128]{2,1,0:T(8,128)(2,1)S(1)}, u32[]{:S(2)}, u32[]{:S(2)}) collective-permute-start(bf16[17,32,128]{2,1,0:T(8,128)(2,1)S(1)} %collective-permute-done.1.refs_2_), channel_id=1, source_target_pairs={{0,2},{2,0},{4,6},{6,4},{8,10},{10,8},{12,14},{14,12},{1,3},{3,1},... | collective-permute-start | bytes 417800 | tf_op jit(solution)/shard_map/ppermute | solution.py:554
  19.7 6.4 %collective-permute-start.4 = (bf16[17,32,128]{2,1,0:T(8,128)(2,1)S(1)}, bf16[17,32,128]{2,1,0:T(8,128)(2,1)S(1)}, u32[]{:S(2)}, u32[]{:S(2)}) collective-permute-start(bf16[17,32,128]{2,1,0:T(8,128)(2,1)S(1)} %collective-permute-done.refs_1_), channel_id=1, source_target_pairs={{0,2},{2,0},{4,6},{6,4},{8,10},{10,8},{12,14},{14,12},{1,3},{3,1},... | collective-permute-start | bytes 417800 | tf_op jit(solution)/shard_map/ppermute | solution.py:554
  28.9 10.9 %all-to-all-start = ((bf16[8,80,128]{2,1,0:T(8,128)(2,1)}), bf16[8,80,128]{2,1,0:T(8,128)(2,1)S(1)}, u32[]{:S(2)}, u32[]{:S(2)}) async-start(bf16[8,80,128]{2,1,0:T(8,128)(2,1)} %arrived_attention.1), calls=%async_computation | async-start | bytes 327680 | tf_op jit(solution)/shard_map/all_to_all | solution.py:589
  41.3 9.1 %collective-permute-start.8 = (bf16[2,16,2048]{2,1,0:T(8,128)(2,1)S(1)}, bf16[2,16,2048]{2,1,0:T(8,128)(2,1)S(1)}, u32[]{:S(2)}, u32[]{:S(2)}) collective-permute-start(bf16[2,16,2048]{2,1,0:T(8,128)(2,1)S(1)} %merge.1.x_ref.refs_0_), channel_id=1, source_target_pairs={{0,8},{2,10},{4,12},{6,14},{8,0},{10,2},{12,4},{14,6},{1,9},{3,11}... | collective-permute-start | bytes 393224 | tf_op jit(solution)/shard_map/ppermute | solution.py:553
  45.5 6.4 %collective-permute-start.9 = (bf16[2,16,2048]{2,1,0:T(8,128)(2,1)S(1)}, bf16[2,16,2048]{2,1,0:T(8,128)(2,1)S(1)}, u32[]{:S(2)}, u32[]{:S(2)}) collective-permute-start(bf16[2,16,2048]{2,1,0:T(8,128)(2,1)S(1)} %get-tuple-element.17), channel_id=1, source_target_pairs={{0,12},{2,14},{4,0},{6,2},{8,4},{10,6},{12,8},{14,10},{1,13},{3,15... | collective-permute-start | bytes 393224 | tf_op jit(solution)/shard_map/ppermute | solution.py:553
  46.9 6.9 %collective-permute-start.7 = (bf16[2,16,2048]{2,1,0:T(8,128)(2,1)S(1)}, bf16[2,16,2048]{2,1,0:T(8,128)(2,1)S(1)}, u32[]{:S(2)}, u32[]{:S(2)}) collective-permute-start(bf16[2,16,2048]{2,1,0:T(8,128)(2,1)S(1)} %get-tuple-element.17), channel_id=1, source_target_pairs={{0,4},{2,6},{4,8},{6,10},{8,12},{10,14},{12,0},{14,2},{1,5},{3,7},... | collective-permute-start | bytes 393224 | tf_op jit(solution)/shard_map/ppermute | solution.py:553
  47.6 7.6 %collective-permute-start.10 = (bf16[2,16,2048]{2,1,0:T(8,128)(2,1)S(1)}, bf16[2,16,2048]{2,1,0:T(8,128)(2,1)S(1)}, u32[]{:S(2)}, u32[]{:S(2)}) collective-permute-start(bf16[2,16,2048]{2,1,0:T(8,128)(2,1)S(1)} %merge.1.x_ref.refs_0_), channel_id=1, source_target_pairs={{0,2},{2,0},{4,6},{6,4},{8,10},{10,8},{12,14},{14,12},{1,3},{3,1},... | collective-permute-start | bytes 393224 | tf_op jit(solution)/shard_map/ppermute | solution.py:554
  50.4 6.2 %collective-permute-start.12 = (bf16[2,16,2048]{2,1,0:T(8,128)(2,1)S(1)}, bf16[2,16,2048]{2,1,0:T(8,128)(2,1)S(1)}, u32[]{:S(2)}, u32[]{:S(2)}) collective-permute-start(bf16[2,16,2048]{2,1,0:T(8,128)(2,1)S(1)} %collective-permute-done.8.refs_2_), channel_id=1, source_target_pairs={{0,2},{2,0},{4,6},{6,4},{8,10},{10,8},{12,14},{14,12},{1,3},{3,1},... | collective-permute-start | bytes 393224 | tf_op jit(solution)/shard_map/ppermute | solution.py:554
  51.9 6.1 %collective-permute-start.13 = (bf16[2,16,2048]{2,1,0:T(8,128)(2,1)S(1)}, bf16[2,16,2048]{2,1,0:T(8,128)(2,1)S(1)}, u32[]{:S(2)}, u32[]{:S(2)}) collective-permute-start(bf16[2,16,2048]{2,1,0:T(8,128)(2,1)S(1)} %collective-permute-done.9.refs_3_), channel_id=1, source_target_pairs={{0,2},{2,0},{4,6},{6,4},{8,10},{10,8},{12,14},{14,12},{1,3},{3,1},... | collective-permute-start | bytes 393224 | tf_op jit(solution)/shard_map/ppermute | solution.py:554
  53.8 5.6 %collective-permute-start.11 = (bf16[2,16,2048]{2,1,0:T(8,128)(2,1)S(1)}, bf16[2,16,2048]{2,1,0:T(8,128)(2,1)S(1)}, u32[]{:S(2)}, u32[]{:S(2)}) collective-permute-start(bf16[2,16,2048]{2,1,0:T(8,128)(2,1)S(1)} %collective-permute-done.7.refs_1_), channel_id=1, source_target_pairs={{0,2},{2,0},{4,6},{6,4},{8,10},{10,8},{12,14},{14,12},{1,3},{3,1},... | collective-permute-start | bytes 393224 | tf_op jit(solution)/shard_map/ppermute | solution.py:554
  60.8 2.0 %collective-permute-start.14 = (f32[2,128,512]{2,1,0:T(8,128)S(1)}, f32[2,128,512]{2,1,0:T(8,128)S(1)}, u32[]{:S(2)}, u32[]{:S(2)}) collective-permute-start(f32[2,128,512]{2,1,0:T(8,128)S(1)} %get-tuple-element.20), channel_id=1, source_target_pairs={{0,1},{1,0},{2,3},{3,2},{4,5},{5,4},{6,7},{7,6},{8,9},{9,8},{10,11... | collective-permute-start | bytes 1572872 | tf_op jit(solution)/shard_map/ppermute | solution.py:560

commit v13 on v12

--- a/solution.py
+++ b/solution.py
@@ -238,27 +238,28 @@
     step = lax.broadcasted_iota(I32, (group, LANES), 1) % group // per
     fresh_mask = (fresh <= step) & (fresh < steps)
 
-    for i in range(rows // together):
-        requests = range(i * together, (i + 1) * together)
-        chains = [(r, k) for r in requests for k in range(heads)]
+    groups = [range(i * together, (i + 1) * together) for i in range(rows // together)]
+    all_scores, all_weights = [], []
+    for i, requests in enumerate(groups):
         if i % 2 == 0:
             for r in range(i * together, min(rows, (i + 2) * together)):
                 for j in range(most):
                     pl.when(where[r * most + j] < zeros)(copy(r, j).wait)
+        keys = []
+        for r in requests:
+            for k in range(heads):
+                at = r * block + k * group
+                pages = [kv[where[r * most + j], 0, k] for j in range(most)]
+                keys.append(jnp.concatenate(pages + [kf[at : at + group, :].astype(BF16)], axis=0))
         queries = q_ref[i * together : (i + 1) * together].reshape(LANES, head_dim)
-        keys, values = [], []
-        for r, k in chains:
-            at = r * block + k * group
-            page = lambda what: [kv[where[r * most + j], what, k] for j in range(most)]
-            keys.append(jnp.concatenate(page(0) + [kf[at : at + group, :].astype(BF16)], axis=0))
-            values.append(page(1) + [vf[at : at + group, :].astype(BF16)])
-        scores = transposed_scores(queries, keys, group)
+        all_scores.append(transposed_scores(queries, keys, group))
+    for i, requests in enumerate(groups):
         mask = []
         for j in range(most):
             seen = [seen_tokens(r, j) for r in requests]
             mask.append(token < lane_values(seen, block, (1, LANES)))
         parts = [
-            jnp.where(m, scores[n * page_len : n * page_len + m.shape[0]], -jnp.inf)
+            jnp.where(m, all_scores[i][n * page_len : n * page_len + m.shape[0]], -jnp.inf)
             for n, m in enumerate(mask + [fresh_mask])
         ]
         top = functools.reduce(jnp.maximum, [jnp.max(x, axis=0, keepdims=True) for x in parts])
@@ -268,14 +269,19 @@
             [parts[most], jnp.broadcast_to(top, (8, LANES)), jnp.broadcast_to(total, (8, LANES))], axis=0
         )
         stats = jnp.transpose(stats, (1, 0))
+        stat_ref[i * LANES : (i + 1) * LANES, : stats.shape[1]] = stats
         weights = [jnp.transpose(x.astype(BF16), (1, 0)) for x in parts[:most]]
         weights.append(stats[:, :group].astype(BF16))
-        weights = jnp.concatenate(weights, axis=1)
-        for x in range(together):
-            both = [jnp.concatenate(values[x * heads + k], axis=0) for k in range(heads)]
-            both = weighted_values(weights[x * block : (x + 1) * block, :], both)
-            o_ref[i * LANES + x * block : i * LANES + (x + 1) * block, :] = both
-        stat_ref[i * LANES : (i + 1) * LANES, : stats.shape[1]] = stats
+        all_weights.append(jnp.concatenate(weights, axis=1))
+    for i, requests in enumerate(groups):
+        for x, r in enumerate(requests):
+            both = []
+            for k in range(heads):
+                at = r * block + k * group
+                pages = [kv[where[r * most + j], 1, k] for j in range(most)]
+                both.append(jnp.concatenate(pages + [vf[at : at + group, :].astype(BF16)], axis=0))
+            both = weighted_values(all_weights[i][x * block : (x + 1) * block, :], both)
+            o_ref[r * block : (r + 1) * block, :] = both
 
 
 def local_attention(table, context, fills, queries, new_kv, cache_kv, tabs):
@@ -339,26 +345,29 @@
         seen.append(jnp.minimum(left, own_ref[items + at]))
         request.append(jnp.where(slot >= 0, reader, -1))
     token = lax.broadcasted_iota(I32, (page_len, LANES), 0)
-    for i in range(items // together):
-        own = range(i * together, (i + 1) * together)
+    groups = [range(i * together, (i + 1) * together) for i in range(items // together)]
+    all_scores, all_weights = [], []
+    for i, own in enumerate(groups):
         keys = [pages_ref[number[x], 0, k] for x in own for k in range(heads)]
-        scores = transposed_scores(queries[i * LANES : (i + 1) * LANES, :], keys, group)
+        all_scores.append(transposed_scores(queries[i * LANES : (i + 1) * LANES, :], keys, group))
+    for i, own in enumerate(groups):
         limit = lane_values([seen[x] for x in own], block, (1, LANES))
-        scores = jnp.where(token < limit, scores, -jnp.inf)
+        scores = jnp.where(token < limit, all_scores[i], -jnp.inf)
         top = jnp.max(scores, axis=0, keepdims=True)
         top = jnp.where(top > -jnp.inf, top, 0.0)
         weights = jnp.exp(scores - top)
         stats = pieces(top) + pieces(jnp.sum(weights, axis=0, keepdims=True))
         stats.append(lane_values([request[x] for x in own], block, (1, LANES)).astype(F32))
         stats = jnp.concatenate(stats + [jnp.zeros((STAT_ROWS - len(stats), LANES), F32)], axis=0).astype(BF16)
-        weights = jnp.transpose(weights.astype(BF16), (1, 0))
+        for place in sorted({x // pair for x in own}):
+            out_ref[owners[place], pair * block : pair * block + STAT_ROWS, :] = stats
+        all_weights.append(jnp.transpose(weights.astype(BF16), (1, 0)))
+    for i, own in enumerate(groups):
         for c, x in enumerate(own):
             both = [pages_ref[number[x], 1, k] for k in range(heads)]
-            both = weighted_values(weights[c * block : (c + 1) * block, :], both)
+            both = weighted_values(all_weights[i][c * block : (c + 1) * block, :], both)
             at = (x % pair) * block
             out_ref[owners[x // pair], at : at + block, :] = both.astype(BF16)
-        for place in sorted({x // pair for x in own}):
-            out_ref[owners[place], pair * block : pair * block + STAT_ROWS, :] = stats
 
 
 def arrived_attention(me, own, blocks, arrived):

time: 64.1 us -> 62.1 us (0.969)
  Pallas kernels: 19.8 us -> 16.9 us
  waiting for transfers between devices: 19.9 us -> 22 us
  starting transfers between devices: 22.9 us -> 21.9 us
    pallas_call x1, Pallas kernels: 6.45 us -> 4.29 us  [local_attention(): pl.pallas_call(functools.partial(local_kernel, page_len, heads), out_shap...]
    all_to_all x1, waiting for transfers between devices: 1.01 us -> 3.17 us  [shards(): lax.all_to_all(parts, 'pool', split_axis=0, concat_axis=0, tiled=True)]
    ppermute x6, starting transfers between devices: 10.2 us -> 8.6 us  [gathered(): lax.ppermute(x, 'pool', [(i, (i + 2 * by) % npool) for i in range(npool)])]
    pallas_call x1, Pallas kernels: 2.79 us -> 2.1 us  [arrived_attention(): pl.pallas_call(functools.partial(arrived_kernel, npool, pair), out_shape=...]
  transfers between devices with their start and end apart: 16 -> 16, of which waited for: 12 -> 12; matrix products, arithmetic and copies ran while one was open for 0% -> 0% of each run, Pallas kernels for 20% -> 17%
where the time goes in v13:
time: 62.1 us; the launch traced here: 61.7 us
  waiting for transfers between devices  22 us (35%)
  starting transfers between devices  21.9 us (35%)
  Pallas kernels  16.9 us (27%)
  other arithmetic  0.86 us (1%)
    ppermute x6, waiting for transfers between devices, gathered(): lax.ppermute(x, 'pool', [(i, (i + 2 * by) % npool) for i in range(npool)])  11.2 us
    ppermute x8, starting transfers between devices, gathered(): lax.ppermute(x, 'pool', [(i, i ^ 1) for i in range(npool)])  9.81 us
    ppermute x6, starting transfers between devices, gathered(): lax.ppermute(x, 'pool', [(i, (i + 2 * by) % npool) for i in range(npool)])  8.6 us
    ppermute x8, waiting for transfers between devices, gathered(): lax.ppermute(x, 'pool', [(i, i ^ 1) for i in range(npool)])  6.94 us
    pallas_call x1, Pallas kernels, local_attention(): pl.pallas_call(functools.partial(local_kernel, page_len, heads), out_shap...  4.29 us
    all_to_all x1, starting transfers between devices, shards(): lax.all_to_all(parts, 'pool', split_axis=0, concat_axis=0, tiled=True)  3.38 us
    all_to_all x1, waiting for transfers between devices, shards(): lax.all_to_all(parts, 'pool', split_axis=0, concat_axis=0, tiled=True)  3.17 us
    pallas_call x1, Pallas kernels, rotated_pages(): pl.pallas_call(functools.partial(rope_kernel, npool, cache_pages, per), g...  2.96 us
  transfers between devices with their start and end apart: 16, of which 12 were waited for; matrix products, arithmetic and copies ran while one was open for 0% of the time, Pallas kernels for 17%

profile of v13, /device:TPU:0, one launch (start us, length us, event | category | flops | bytes accessed | tf_op | source)
XLA Modules:
  0.0 61.7 jit_solution(438548827119040098)
XLA Ops:
  1.2 5.1 %collective-permute-start.2 = (bf16[17,32,128]{2,1,0:T(8,128)(2,1)S(1)}, bf16[17,32,128]{2,1,0:T(8,128)(2,1)S(1)}, u32[]{:S(2)}, u32[]{:S(2)}) collective-permute-start(bf16[17,32,128]{2,1,0:T(8,128)(2,1)S(1)} %asked_queries.1.refs_0_.q_ref), channel_id=1, source_target_pairs={{0,12},{2,14},{4,0},{6,2},{8,4},{10,6},{12,8},{14,10},{1,13},{3,15... | collective-permute-start | bytes 417800 | tf_op jit(solution)/shard_map/ppermute | solution.py:562
  7.3 1.5 %collective-permute-start.3 = (bf16[17,32,128]{2,1,0:T(8,128)(2,1)S(1)}, bf16[17,32,128]{2,1,0:T(8,128)(2,1)S(1)}, u32[]{:S(2)}, u32[]{:S(2)}) collective-permute-start(bf16[17,32,128]{2,1,0:T(8,128)(2,1)S(1)} %asked_queries.1.refs_0_.q_ref), channel_id=1, source_target_pairs={{0,2},{2,0},{4,6},{6,4},{8,10},{10,8},{12,14},{14,12},{1,3},{3,1},... | collective-permute-start | bytes 417800 | tf_op jit(solution)/shard_map/ppermute | solution.py:563
  8.9 1.6 %collective-permute-done.2.refs_3_ = bf16[17,32,128]{2,1,0:T(8,128)(2,1)S(1)} collective-permute-done((bf16[17,32,128]{2,1,0:T(8,128)(2,1)S(1)}, bf16[17,32,128]{2,1,0:T(8,128)(2,1)S(1)}, u32[]{:S(2)}, u32[]{:S(2)}) %collective-permute-start.2) | collective-permute-done | bytes 139296 | tf_op jit(solution)/shard_map/ppermute | solution.py:562
  10.4 1.5 %collective-permute-start.6 = (bf16[17,32,128]{2,1,0:T(8,128)(2,1)S(1)}, bf16[17,32,128]{2,1,0:T(8,128)(2,1)S(1)}, u32[]{:S(2)}, u32[]{:S(2)}) collective-permute-start(bf16[17,32,128]{2,1,0:T(8,128)(2,1)S(1)} %collective-permute-done.2.refs_3_), channel_id=1, source_target_pairs={{0,2},{2,0},{4,6},{6,4},{8,10},{10,8},{12,14},{14,12},{1,3},{3,1},... | collective-permute-start | bytes 417800 | tf_op jit(solution)/shard_map/ppermute | solution.py:563
  11.9 6.2 %collective-permute-done.1.refs_2_ = bf16[17,32,128]{2,1,0:T(8,128)(2,1)S(1)} collective-permute-done((bf16[17,32,128]{2,1,0:T(8,128)(2,1)S(1)}, bf16[17,32,128]{2,1,0:T(8,128)(2,1)S(1)}, u32[]{:S(2)}, u32[]{:S(2)}) %collective-permute-start.1) | collective-permute-done | bytes 139296 | tf_op jit(solution)/shard_map/ppermute | solution.py:562
  18.1 1.5 %collective-permute-start.5 = (bf16[17,32,128]{2,1,0:T(8,128)(2,1)S(1)}, bf16[17,32,128]{2,1,0:T(8,128)(2,1)S(1)}, u32[]{:S(2)}, u32[]{:S(2)}) collective-permute-start(bf16[17,32,128]{2,1,0:T(8,128)(2,1)S(1)} %collective-permute-done.1.refs_2_), channel_id=1, source_target_pairs={{0,2},{2,0},{4,6},{6,4},{8,10},{10,8},{12,14},{14,12},{1,3},{3,1},... | collective-permute-start | bytes 417800 | tf_op jit(solution)/shard_map/ppermute | solution.py:563
  20.2 3.0 %rope_pages.1 = (bf16[16,2,2,128,128]{4,3,2,1,0:T(8,128)(2,1)S(1)}, s32[48]{0:T(128)S(1)}) custom-call(s32[16]{0:T(128)} %slot_ref.1, s32[1,4]{1,0:T(1,128)} %len_ref.1, bf16[16,2,2,128,128]{4,3,2,1,0:T(8,128)(2,1)} %pages_ref.1, f32[128,128]{1,0:T(8,128)} %constant.20.clone.ct_ref, f32[128,128]{1,0:T(8,128)} %constant.21.clone.st_ref, ...), custom_call_target="tpu_custom_call" | custom-call | flops 6000000 | bytes 2000000 | tf_op jit(solution)/shard_map/rope_pages/pallas_call | solution.py:86
  23.2 1.3 %collective-permute-done.5.refs_6_ = bf16[17,32,128]{2,1,0:T(8,128)(2,1)S(1)} collective-permute-done((bf16[17,32,128]{2,1,0:T(8,128)(2,1)S(1)}, bf16[17,32,128]{2,1,0:T(8,128)(2,1)S(1)}, u32[]{:S(2)}, u32[]{:S(2)}) %collective-permute-start.5) | collective-permute-done | bytes 139296 | tf_op jit(solution)/shard_map/ppermute | solution.py:563
  24.6 1.5 %collective-permute-done.4.refs_5_ = bf16[17,32,128]{2,1,0:T(8,128)(2,1)S(1)} collective-permute-done((bf16[17,32,128]{2,1,0:T(8,128)(2,1)S(1)}, bf16[17,32,128]{2,1,0:T(8,128)(2,1)S(1)}, u32[]{:S(2)}, u32[]{:S(2)}) %collective-permute-start.4) | collective-permute-done | bytes 139296 | tf_op jit(solution)/shard_map/ppermute | solution.py:563
  26.1 2.1 %arrived_attention.1 = bf16[8,80,128]{2,1,0:T(8,128)(2,1)} custom-call(s32[2]{0:T(128)S(1)} %pad_add_fusion.me_ref.place_ref, s32[48]{0:T(128)S(1)} %get-tuple-element.13.own_ref, bf16[17,32,128]{2,1,0:T(8,128)(2,1)S(1)} %asked_queries.1.refs_0_.q_ref, bf16[17,32,128]{2,1,0:T(8,128)(2,1)S(1)} %collective-permute-done.refs_1_, ...), custom_call_target="tpu_custom_call" | custom-call | flops 200000000 | bytes 4000000 | tf_op jit(solution)/shard_map/arrived_attention/pallas_call | solution.py:379
  28.2 3.4 %all-to-all-start = ((bf16[8,80,128]{2,1,0:T(8,128)(2,1)}), bf16[8,80,128]{2,1,0:T(8,128)(2,1)S(1)}, u32[]{:S(2)}, u32[]{:S(2)}) async-start(bf16[8,80,128]{2,1,0:T(8,128)(2,1)} %arrived_attention.1), calls=%async_computation | async-start | bytes 327680 | tf_op jit(solution)/shard_map/all_to_all | solution.py:598
  31.6 4.3 %local_attention.1 = (f32[512,128]{1,0:T(8,128)S(1)}, f32[512,128]{1,0:T(8,128)S(1)}) custom-call(s32[3,16]{1,0:T(4,128)} %bitcast.4, s32[16]{0:T(128)} %context_ref.3, s32[48]{0:T(128)} %fill_ref.1, bf16[17,32,128]{2,1,0:T(8,128)(2,1)S(1)} %asked_queries.1.refs_0_.q_ref, bf16[2,16,512]{2,1,0:T(8,128)(2,1)S(1)} %reshape.3.new_ref, ...), custom_call_target="tpu_custom_call" | custom-call | flops 800000000 | bytes 12000000 | tf_op jit(solution)/shard_map/local_attention/pallas_call | solution.py:294
  35.9 3.2 %all-to-all-done.parts_ref = bf16[8,80,128]{2,1,0:T(8,128)(2,1)S(1)} async-done(((bf16[8,80,128]{2,1,0:T(8,128)(2,1)}), bf16[8,80,128]{2,1,0:T(8,128)(2,1)S(1)}, u32[]{:S(2)}, u32[]{:S(2)}) %all-to-all-start) | async-done | bytes 163872 | tf_op jit(solution)/shard_map/all_to_all | solution.py:598
  39.1 1.5 %merge.1.x_ref.refs_0_ = bf16[2,16,2048]{2,1,0:T(8,128)(2,1)S(1)} custom-call(s32[2]{0:T(128)S(1)} %pad_add_fusion.me_ref.place_ref, bf16[8,80,128]{2,1,0:T(8,128)(2,1)S(1)} %all-to-all-done.parts_ref, f32[512,128]{1,0:T(8,128)S(1)} %get-tuple-element.15.o_ref, f32[512,128]{1,0:T(8,128)S(1)} %get-tuple-element.16.stat_ref), custom_call_target="tpu_custom_call" | custom-call | flops 2000000 | bytes 1500000 | tf_op jit(solution)/shard_map/merge/pallas_call | solution.py:439
  41.0 2.2 %fetch_weight.1 = (bf16[2048,1024]{1,0:T(8,128)(2,1)S(1)}, bf16[2,16,2048]{2,1,0:T(8,128)(2,1)S(1)}) custom-call(bf16[2048,1024]{1,0:T(8,128)(2,1)} %weight_ref.1, bf16[2,16,2048]{2,1,0:T(8,128)(2,1)S(1)} %merge.1.x_ref.refs_0_), custom_call_target="tpu_custom_call" | custom-call | bytes 8388608 | tf_op jit(solution)/shard_map/fetch_weight/pallas_call | solution.py:466
  43.2 1.9 %collective-permute-start.9 = (bf16[2,16,2048]{2,1,0:T(8,128)(2,1)S(1)}, bf16[2,16,2048]{2,1,0:T(8,128)(2,1)S(1)}, u32[]{:S(2)}, u32[]{:S(2)}) collective-permute-start(bf16[2,16,2048]{2,1,0:T(8,128)(2,1)S(1)} %get-tuple-element.17), channel_id=1, source_target_pairs={{0,12},{2,14},{4,0},{6,2},{8,4},{10,6},{12,8},{14,10},{1,13},{3,15... | collective-permute-start | bytes 393224 | tf_op jit(solution)/shard_map/ppermute | solution.py:562
  45.3 1.3 %collective-permute-start.10 = (bf16[2,16,2048]{2,1,0:T(8,128)(2,1)S(1)}, bf16[2,16,2048]{2,1,0:T(8,128)(2,1)S(1)}, u32[]{:S(2)}, u32[]{:S(2)}) collective-permute-start(bf16[2,16,2048]{2,1,0:T(8,128)(2,1)S(1)} %merge.1.x_ref.refs_0_), channel_id=1, source_target_pairs={{0,2},{2,0},{4,6},{6,4},{8,10},{10,8},{12,14},{14,12},{1,3},{3,1},... | collective-permute-start | bytes 393224 | tf_op jit(solution)/shard_map/ppermute | solution.py:563
  46.7 3.2 %collective-permute-done.8.refs_2_ = bf16[2,16,2048]{2,1,0:T(8,128)(2,1)S(1)} collective-permute-done((bf16[2,16,2048]{2,1,0:T(8,128)(2,1)S(1)}, bf16[2,16,2048]{2,1,0:T(8,128)(2,1)S(1)}, u32[]{:S(2)}, u32[]{:S(2)}) %collective-permute-start.8) | collective-permute-done | bytes 131104 | tf_op jit(solution)/shard_map/ppermute | solution.py:562
  52.0 1.5 %collective-permute-start.11 = (bf16[2,16,2048]{2,1,0:T(8,128)(2,1)S(1)}, bf16[2,16,2048]{2,1,0:T(8,128)(2,1)S(1)}, u32[]{:S(2)}, u32[]{:S(2)}) collective-permute-start(bf16[2,16,2048]{2,1,0:T(8,128)(2,1)S(1)} %collective-permute-done.7.refs_1_), channel_id=1, source_target_pairs={{0,2},{2,0},{4,6},{6,4},{8,10},{10,8},{12,14},{14,12},{1,3},{3,1},... | collective-permute-start | bytes 393224 | tf_op jit(solution)/shard_map/ppermute | solution.py:563
  53.5 1.3 %collective-permute-done.12.refs_6_ = bf16[2,16,2048]{2,1,0:T(8,128)(2,1)S(1)} collective-permute-done((bf16[2,16,2048]{2,1,0:T(8,128)(2,1)S(1)}, bf16[2,16,2048]{2,1,0:T(8,128)(2,1)S(1)}, u32[]{:S(2)}, u32[]{:S(2)}) %collective-permute-start.12) | collective-permute-done | bytes 131104 | tf_op jit(solution)/shard_map/ppermute | solution.py:563
  54.8 1.4 %collective-permute-done.13.refs_7_ = bf16[2,16,2048]{2,1,0:T(8,128)(2,1)S(1)} collective-permute-done((bf16[2,16,2048]{2,1,0:T(8,128)(2,1)S(1)}, bf16[2,16,2048]{2,1,0:T(8,128)(2,1)S(1)}, u32[]{:S(2)}, u32[]{:S(2)}) %collective-permute-start.13) | collective-permute-done | bytes 131104 | tf_op jit(solution)/shard_map/ppermute | solution.py:563
  56.2 1.4 %collective-permute-done.11.refs_5_ = bf16[2,16,2048]{2,1,0:T(8,128)(2,1)S(1)} collective-permute-done((bf16[2,16,2048]{2,1,0:T(8,128)(2,1)S(1)}, bf16[2,16,2048]{2,1,0:T(8,128)(2,1)S(1)}, u32[]{:S(2)}, u32[]{:S(2)}) %collective-permute-start.11) | collective-permute-done | bytes 131104 | tf_op jit(solution)/shard_map/ppermute | solution.py:563
  57.6 1.3 %project_other.1 = (f32[2,128,512]{2,1,0:T(8,128)S(1)}, bf16[256,2048]{1,0:T(8,128)(2,1)S(1)}) custom-call(s32[2]{0:T(128)S(1)} %pad_add_fusion.me_ref.place_ref, bf16[2,16,2048]{2,1,0:T(8,128)(2,1)S(1)} %merge.1.x_ref.refs_0_, bf16[2,16,2048]{2,1,0:T(8,128)(2,1)S(1)} %collective-permute-done.7.refs_1_, ...), custom_call_target="tpu_custom_call" | custom-call | flops 536870912 | bytes 4000000 | tf_op jit(solution)/shard_map/project_other/pallas_call | solution.py:505
  59.1 1.3 %project_own.1 = f32[2,128,512]{2,1,0:T(8,128)S(1)} custom-call(s32[2]{0:T(128)S(1)} %pad_add_fusion.me_ref.place_ref, bf16[256,2048]{1,0:T(8,128)(2,1)S(1)} %get-tuple-element.19.lhs, bf16[2048,1024]{1,0:T(8,128)(2,1)S(1)} %get-tuple-element.18.refs_8_.weight_ref), custom_call_target="tpu_custom_call" | custom-call | flops 536870912 | bytes 4000000 | tf_op jit(solution)/shard_map/project_own/pallas_call | solution.py:526
  (21 shorter events, 7.1 us)
Async XLA Ops:
  0.0 31.6 %copy-start = (bf16[2,16,2,2,128]{4,3,2,1,0:T(2,128)(2,1)S(1)}, bf16[2,16,2,2,128]{4,3,2,1,0:T(2,128)(2,1)}, u32[]{:S(2)}) copy-start(bf16[2,16,2,2,128]{4,3,2,1,0:T(2,128)(2,1)} %param.24) | copy-start | bytes 98308
  1.2 9.2 %collective-permute-start.2 = (bf16[17,32,128]{2,1,0:T(8,128)(2,1)S(1)}, bf16[17,32,128]{2,1,0:T(8,128)(2,1)S(1)}, u32[]{:S(2)}, u32[]{:S(2)}) collective-permute-start(bf16[17,32,128]{2,1,0:T(8,128)(2,1)S(1)} %asked_queries.1.refs_0_.q_ref), channel_id=1, source_target_pairs={{0,12},{2,14},{4,0},{6,2},{8,4},{10,6},{12,8},{14,10},{1,13},{3,15... | collective-permute-start | bytes 417800 | tf_op jit(solution)/shard_map/ppermute | solution.py:562
  6.3 11.8 %collective-permute-start.1 = (bf16[17,32,128]{2,1,0:T(8,128)(2,1)S(1)}, bf16[17,32,128]{2,1,0:T(8,128)(2,1)S(1)}, u32[]{:S(2)}, u32[]{:S(2)}) collective-permute-start(bf16[17,32,128]{2,1,0:T(8,128)(2,1)S(1)} %asked_queries.1.refs_0_.q_ref), channel_id=1, source_target_pairs={{0,8},{2,10},{4,12},{6,14},{8,0},{10,2},{12,4},{14,6},{1,9},{3,11}... | collective-permute-start | bytes 417800 | tf_op jit(solution)/shard_map/ppermute | solution.py:562
  6.3 13.3 %collective-permute-start = (bf16[17,32,128]{2,1,0:T(8,128)(2,1)S(1)}, bf16[17,32,128]{2,1,0:T(8,128)(2,1)S(1)}, u32[]{:S(2)}, u32[]{:S(2)}) collective-permute-start(bf16[17,32,128]{2,1,0:T(8,128)(2,1)S(1)} %asked_queries.1.refs_0_.q_ref), channel_id=1, source_target_pairs={{0,4},{2,6},{4,8},{6,10},{8,12},{10,14},{12,0},{14,2},{1,5},{3,7},... | collective-permute-start | bytes 417800 | tf_op jit(solution)/shard_map/ppermute | solution.py:562
  7.3 15.9 %collective-permute-start.3 = (bf16[17,32,128]{2,1,0:T(8,128)(2,1)S(1)}, bf16[17,32,128]{2,1,0:T(8,128)(2,1)S(1)}, u32[]{:S(2)}, u32[]{:S(2)}) collective-permute-start(bf16[17,32,128]{2,1,0:T(8,128)(2,1)S(1)} %asked_queries.1.refs_0_.q_ref), channel_id=1, source_target_pairs={{0,2},{2,0},{4,6},{6,4},{8,10},{10,8},{12,14},{14,12},{1,3},{3,1},... | collective-permute-start | bytes 417800 | tf_op jit(solution)/shard_map/ppermute | solution.py:563
  10.4 12.8 %collective-permute-start.6 = (bf16[17,32,128]{2,1,0:T(8,128)(2,1)S(1)}, bf16[17,32,128]{2,1,0:T(8,128)(2,1)S(1)}, u32[]{:S(2)}, u32[]{:S(2)}) collective-permute-start(bf16[17,32,128]{2,1,0:T(8,128)(2,1)S(1)} %collective-permute-done.2.refs_3_), channel_id=1, source_target_pairs={{0,2},{2,0},{4,6},{6,4},{8,10},{10,8},{12,14},{14,12},{1,3},{3,1},... | collective-permute-start | bytes 417800 | tf_op jit(solution)/shard_map/ppermute | solution.py:563
  18.1 6.4 %collective-permute-start.5 = (bf16[17,32,128]{2,1,0:T(8,128)(2,1)S(1)}, bf16[17,32,128]{2,1,0:T(8,128)(2,1)S(1)}, u32[]{:S(2)}, u32[]{:S(2)}) collective-permute-start(bf16[17,32,128]{2,1,0:T(8,128)(2,1)S(1)} %collective-permute-done.1.refs_2_), channel_id=1, source_target_pairs={{0,2},{2,0},{4,6},{6,4},{8,10},{10,8},{12,14},{14,12},{1,3},{3,1},... | collective-permute-start | bytes 417800 | tf_op jit(solution)/shard_map/ppermute | solution.py:563
  19.7 6.4 %collective-permute-start.4 = (bf16[17,32,128]{2,1,0:T(8,128)(2,1)S(1)}, bf16[17,32,128]{2,1,0:T(8,128)(2,1)S(1)}, u32[]{:S(2)}, u32[]{:S(2)}) collective-permute-start(bf16[17,32,128]{2,1,0:T(8,128)(2,1)S(1)} %collective-permute-done.refs_1_), channel_id=1, source_target_pairs={{0,2},{2,0},{4,6},{6,4},{8,10},{10,8},{12,14},{14,12},{1,3},{3,1},... | collective-permute-start | bytes 417800 | tf_op jit(solution)/shard_map/ppermute | solution.py:563
  28.2 10.9 %all-to-all-start = ((bf16[8,80,128]{2,1,0:T(8,128)(2,1)}), bf16[8,80,128]{2,1,0:T(8,128)(2,1)S(1)}, u32[]{:S(2)}, u32[]{:S(2)}) async-start(bf16[8,80,128]{2,1,0:T(8,128)(2,1)} %arrived_attention.1), calls=%async_computation | async-start | bytes 327680 | tf_op jit(solution)/shard_map/all_to_all | solution.py:598
  40.6 9.3 %collective-permute-start.8 = (bf16[2,16,2048]{2,1,0:T(8,128)(2,1)S(1)}, bf16[2,16,2048]{2,1,0:T(8,128)(2,1)S(1)}, u32[]{:S(2)}, u32[]{:S(2)}) collective-permute-start(bf16[2,16,2048]{2,1,0:T(8,128)(2,1)S(1)} %merge.1.x_ref.refs_0_), channel_id=1, source_target_pairs={{0,8},{2,10},{4,12},{6,14},{8,0},{10,2},{12,4},{14,6},{1,9},{3,11}... | collective-permute-start | bytes 393224 | tf_op jit(solution)/shard_map/ppermute | solution.py:562
  43.2 7.4 %collective-permute-start.9 = (bf16[2,16,2048]{2,1,0:T(8,128)(2,1)S(1)}, bf16[2,16,2048]{2,1,0:T(8,128)(2,1)S(1)}, u32[]{:S(2)}, u32[]{:S(2)}) collective-permute-start(bf16[2,16,2048]{2,1,0:T(8,128)(2,1)S(1)} %get-tuple-element.17), channel_id=1, source_target_pairs={{0,12},{2,14},{4,0},{6,2},{8,4},{10,6},{12,8},{14,10},{1,13},{3,15... | collective-permute-start | bytes 393224 | tf_op jit(solution)/shard_map/ppermute | solution.py:562
  45.2 6.9 %collective-permute-start.7 = (bf16[2,16,2048]{2,1,0:T(8,128)(2,1)S(1)}, bf16[2,16,2048]{2,1,0:T(8,128)(2,1)S(1)}, u32[]{:S(2)}, u32[]{:S(2)}) collective-permute-start(bf16[2,16,2048]{2,1,0:T(8,128)(2,1)S(1)} %get-tuple-element.17), channel_id=1, source_target_pairs={{0,4},{2,6},{4,8},{6,10},{8,12},{10,14},{12,0},{14,2},{1,5},{3,7},... | collective-permute-start | bytes 393224 | tf_op jit(solution)/shard_map/ppermute | solution.py:562
  45.3 8.2 %collective-permute-start.10 = (bf16[2,16,2048]{2,1,0:T(8,128)(2,1)S(1)}, bf16[2,16,2048]{2,1,0:T(8,128)(2,1)S(1)}, u32[]{:S(2)}, u32[]{:S(2)}) collective-permute-start(bf16[2,16,2048]{2,1,0:T(8,128)(2,1)S(1)} %merge.1.x_ref.refs_0_), channel_id=1, source_target_pairs={{0,2},{2,0},{4,6},{6,4},{8,10},{10,8},{12,14},{14,12},{1,3},{3,1},... | collective-permute-start | bytes 393224 | tf_op jit(solution)/shard_map/ppermute | solution.py:563
  49.9 5.0 %collective-permute-start.12 = (bf16[2,16,2048]{2,1,0:T(8,128)(2,1)S(1)}, bf16[2,16,2048]{2,1,0:T(8,128)(2,1)S(1)}, u32[]{:S(2)}, u32[]{:S(2)}) collective-permute-start(bf16[2,16,2048]{2,1,0:T(8,128)(2,1)S(1)} %collective-permute-done.8.refs_2_), channel_id=1, source_target_pairs={{0,2},{2,0},{4,6},{6,4},{8,10},{10,8},{12,14},{14,12},{1,3},{3,1},... | collective-permute-start | bytes 393224 | tf_op jit(solution)/shard_map/ppermute | solution.py:563
  50.6 5.6 %collective-permute-start.13 = (bf16[2,16,2048]{2,1,0:T(8,128)(2,1)S(1)}, bf16[2,16,2048]{2,1,0:T(8,128)(2,1)S(1)}, u32[]{:S(2)}, u32[]{:S(2)}) collective-permute-start(bf16[2,16,2048]{2,1,0:T(8,128)(2,1)S(1)} %collective-permute-done.9.refs_3_), channel_id=1, source_target_pairs={{0,2},{2,0},{4,6},{6,4},{8,10},{10,8},{12,14},{14,12},{1,3},{3,1},... | collective-permute-start | bytes 393224 | tf_op jit(solution)/shard_map/ppermute | solution.py:563
  52.0 5.6 %collective-permute-start.11 = (bf16[2,16,2048]{2,1,0:T(8,128)(2,1)S(1)}, bf16[2,16,2048]{2,1,0:T(8,128)(2,1)S(1)}, u32[]{:S(2)}, u32[]{:S(2)}) collective-permute-start(bf16[2,16,2048]{2,1,0:T(8,128)(2,1)S(1)} %collective-permute-done.7.refs_1_), channel_id=1, source_target_pairs={{0,2},{2,0},{4,6},{6,4},{8,10},{10,8},{12,14},{14,12},{1,3},{3,1},... | collective-permute-start | bytes 393224 | tf_op jit(solution)/shard_map/ppermute | solution.py:563
  59.0 2.0 %collective-permute-start.14 = (f32[2,128,512]{2,1,0:T(8,128)S(1)}, f32[2,128,512]{2,1,0:T(8,128)S(1)}, u32[]{:S(2)}, u32[]{:S(2)}) collective-permute-start(f32[2,128,512]{2,1,0:T(8,128)S(1)} %get-tuple-element.20), channel_id=1, source_target_pairs={{0,1},{1,0},{2,3},{3,2},{4,5},{5,4},{6,7},{7,6},{8,9},{9,8},{10,11... | collective-permute-start | bytes 1572872 | tf_op jit(solution)/shard_map/ppermute | solution.py:569

commit v14 on v13

--- a/solution.py
+++ b/solution.py
@@ -409,24 +409,26 @@
         readers.append(x[6:7])
     empty = [jnp.zeros((LANES // 2 - npool, LANES), F32)]
     turned[...] = jnp.transpose(jnp.concatenate(tops + empty + totals + empty, axis=0), (1, 0))
+    items = []
     for d in range(npool):
         for p in range(pair):
             part = lax.rem(place_of(me, npool, d) * pair + p, LANES // block)
             r = read_scalar(readers[d], chain == part)
-            there = r >= 0
             at = pl.ds(pl.multiple_of(jnp.maximum(r, 0) * block, block), block)
             lane = pl.ds(pl.multiple_of(part * block, block), block)
             m = jnp.broadcast_to(turned[lane, d : d + 1], (block, head_dim))
             l = jnp.broadcast_to(turned[lane, LANES // 2 + d : LANES // 2 + d + 1], (block, head_dim))
-            seen = (l > 0.0) & there
-            o = parts_ref[d, p * block : (p + 1) * block, :].astype(F32)
-            old = top[at, :]
-            new = jnp.where(seen, jnp.maximum(old, m), old)
-            a = jnp.exp(old - new)
-            b = jnp.where(seen, jnp.exp(m - new), 0.0)
-            top[at, :] = new
-            total[at, :] = total[at, :] * a + l * b
-            mixed[at, :] = mixed[at, :] * a + o * b
+            items.append((d, p, at, m, l, (l > 0.0) & (r >= 0)))
+    for d, p, at, m, l, seen in items:
+        top[at, :] = jnp.where(seen, jnp.maximum(top[at, :], m), top[at, :])
+    scale = jnp.exp(jnp.broadcast_to(stat_ref[:, group : group + 1], shape) - top[...])
+    total[...] = total[...] * scale
+    mixed[...] = mixed[...] * scale
+    shares = [jnp.where(seen, jnp.exp(m - top[at, :]), 0.0) for _, _, at, m, _, seen in items]
+    for (d, p, at, m, l, seen), share in zip(items, shares):
+        o = parts_ref[d, p * block : (p + 1) * block, :].astype(F32)
+        total[at, :] = total[at, :] + l * share
+        mixed[at, :] = mixed[at, :] + o * share
     for s in range(steps):
         for h in range(heads * per):
             k, g = divmod(h, per)
@@ -494,7 +496,7 @@
         at = pl.ds(pl.multiple_of(which * half + i * tile, LANES), tile)
         terms = jnp.dot(lhs[...], weight_ref[:, at], preferred_element_type=F32)
         for s in range(steps):
-            out_ref[s, :, i * tile : (i + 1) * tile] = terms[s * every : (s + 1) * every]
+            out_ref[s, :, i * tile : (i + 1) * tile] = terms[s * every : (s + 1) * every].astype(out_ref.dtype)
 
 
 def other_projection(place, blocks, weight):
@@ -505,7 +507,7 @@
     return pl.pallas_call(
         functools.partial(rows_kernel, npool),
         out_shape=[
-            jax.ShapeDtypeStruct((steps, npool * rows, half), F32),
+            jax.ShapeDtypeStruct((steps, npool * rows, half), BF16),
             jax.ShapeDtypeStruct((every, width), BF16),
         ],
         in_specs=[SMEM] + [VMEM] * (npool + 1),
@@ -562,7 +564,9 @@
     ahead = lambda x, by: lax.ppermute(x, "pool", [(i, (i + 2 * by) % npool) for i in range(npool)])
     across = lambda x: lax.ppermute(x, "pool", [(i, i ^ 1) for i in range(npool)])
     straight = [x] + [ahead(x if by == half // 2 else later, by) for by in range(1, half)]
-    return straight + [across(y) for y in straight]
+    partners = {by: across(straight[by]) for by in range(half) if by != 1}
+    partners[1] = ahead(partners[0], 1)
+    return straight + [partners[by] for by in range(half)]
 
 
 def swap_halves(x):
@@ -602,7 +606,7 @@
     other_terms, lhs = other_projection(place, blocks, weight)
     other_terms = swap_halves(other_terms)
     terms = own_projection(place, lhs, weight, queries.shape[0])
-    return (terms + other_terms).astype(BF16)
+    return (terms + other_terms.astype(F32)).astype(BF16)
 
 
 def solution(mesh):

time: 62.1 us -> 66.9 us (1.077)
  waiting for transfers between devices: 22 us -> 27.5 us
  starting transfers between devices: 21.9 us -> 20.9 us
    ppermute x6 -> x8, waiting for transfers between devices: 11.2 us -> 18.3 us  [gathered(): lax.ppermute(x, 'pool', [(i, (i + 2 * by) % npool) for i in range(npool)])]
    ppermute x8 -> x6, starting transfers between devices: 9.81 us -> 5.64 us  [gathered(): lax.ppermute(x, 'pool', [(i, i ^ 1) for i in range(npool)])]
    ppermute x6 -> x8, starting transfers between devices: 8.6 us -> 11.8 us  [gathered(): lax.ppermute(x, 'pool', [(i, (i + 2 * by) % npool) for i in range(npool)])]
    ppermute x8 -> x6, waiting for transfers between devices: 6.94 us -> 5.83 us  [gathered(): lax.ppermute(x, 'pool', [(i, i ^ 1) for i in range(npool)])]
  transfers between devices with their start and end apart: 16 -> 16, of which waited for: 12 -> 9; matrix products, arithmetic and copies ran while one was open for 0% -> 0% of each run, Pallas kernels for 17% -> 16%
where the time goes in v14:
time: 66.9 us; the launch traced here: 66.5 us
  waiting for transfers between devices  27.5 us (41%)
  starting transfers between devices  20.9 us (31%)
  Pallas kernels  17.2 us (26%)
  other arithmetic  0.86 us (1%)
    ppermute x8, waiting for transfers between devices, gathered(): lax.ppermute(x, 'pool', [(i, (i + 2 * by) % npool) for i in range(npool)])  18.3 us
    ppermute x8, starting transfers between devices, gathered(): lax.ppermute(x, 'pool', [(i, (i + 2 * by) % npool) for i in range(npool)])  11.8 us
    ppermute x6, waiting for transfers between devices, gathered(): lax.ppermute(x, 'pool', [(i, i ^ 1) for i in range(npool)])  5.83 us
    ppermute x6, starting transfers between devices, gathered(): lax.ppermute(x, 'pool', [(i, i ^ 1) for i in range(npool)])  5.64 us
    pallas_call x1, Pallas kernels, local_attention(): pl.pallas_call(functools.partial(local_kernel, page_len, heads), out_shap...  4.38 us
    all_to_all x1, starting transfers between devices, shards(): lax.all_to_all(parts, 'pool', split_axis=0, concat_axis=0, tiled=True)  3.38 us
    all_to_all x1, waiting for transfers between devices, shards(): lax.all_to_all(parts, 'pool', split_axis=0, concat_axis=0, tiled=True)  3.08 us
    pallas_call x1, Pallas kernels, rotated_pages(): pl.pallas_call(functools.partial(rope_kernel, npool, cache_pages, per), g...  2.96 us
  transfers between devices with their start and end apart: 16, of which 9 were waited for; matrix products, arithmetic and copies ran while one was open for 0% of the time, Pallas kernels for 16%

profile of v14, /device:TPU:0, one launch (start us, length us, event | category | flops | bytes accessed | tf_op | source)
XLA Modules:
  0.0 66.5 jit_solution(9945167601732797855)
XLA Ops:
  0.0 1.2 %asked_queries.1.refs_0_.q_ref = bf16[17,32,128]{2,1,0:T(8,128)(2,1)S(1)} custom-call(s32[3,16]{1,0:T(4,128)} %bitcast.3, s32[16]{0:T(128)} %context_ref.3, bf16[2,16,2048]{2,1,0:T(8,128)(2,1)} %q_ref.1), custom_call_target="tpu_custom_call" | custom-call | flops 100000 | bytes 300000 | tf_op jit(solution)/shard_map/asked_queries/pallas_call | solution.py:138
  1.2 3.0 %collective-permute-start.3 = (bf16[17,32,128]{2,1,0:T(8,128)(2,1)S(1)}, bf16[17,32,128]{2,1,0:T(8,128)(2,1)S(1)}, u32[]{:S(2)}, u32[]{:S(2)}) collective-permute-start(bf16[17,32,128]{2,1,0:T(8,128)(2,1)S(1)} %asked_queries.1.refs_0_.q_ref), channel_id=1, source_target_pairs={{0,2},{2,0},{4,6},{6,4},{8,10},{10,8},{12,14},{14,12},{1,3},{3,1},... | collective-permute-start | bytes 417800 | tf_op jit(solution)/shard_map/ppermute | solution.py:565
  4.3 3.6 %collective-permute-start.2 = (bf16[17,32,128]{2,1,0:T(8,128)(2,1)S(1)}, bf16[17,32,128]{2,1,0:T(8,128)(2,1)S(1)}, u32[]{:S(2)}, u32[]{:S(2)}) collective-permute-start(bf16[17,32,128]{2,1,0:T(8,128)(2,1)S(1)} %asked_queries.1.refs_0_.q_ref), channel_id=1, source_target_pairs={{0,12},{2,14},{4,0},{6,2},{8,4},{10,6},{12,8},{14,10},{1,13},{3,15... | collective-permute-start | bytes 417800 | tf_op jit(solution)/shard_map/ppermute | solution.py:564
  7.9 1.0 %collective-permute-start = (bf16[17,32,128]{2,1,0:T(8,128)(2,1)S(1)}, bf16[17,32,128]{2,1,0:T(8,128)(2,1)S(1)}, u32[]{:S(2)}, u32[]{:S(2)}) collective-permute-start(bf16[17,32,128]{2,1,0:T(8,128)(2,1)S(1)} %asked_queries.1.refs_0_.q_ref), channel_id=1, source_target_pairs={{0,4},{2,6},{4,8},{6,10},{8,12},{10,14},{12,0},{14,2},{1,5},{3,7},... | collective-permute-start | bytes 417800 | tf_op jit(solution)/shard_map/ppermute | solution.py:564
  8.9 2.5 %collective-permute-start.4 = (bf16[17,32,128]{2,1,0:T(8,128)(2,1)S(1)}, bf16[17,32,128]{2,1,0:T(8,128)(2,1)S(1)}, u32[]{:S(2)}, u32[]{:S(2)}) collective-permute-start(bf16[17,32,128]{2,1,0:T(8,128)(2,1)S(1)} %collective-permute-done.3.refs_4_), channel_id=1, source_target_pairs={{0,4},{2,6},{4,8},{6,10},{8,12},{10,14},{12,0},{14,2},{1,5},{3,7},... | collective-permute-start | bytes 417800 | tf_op jit(solution)/shard_map/ppermute | solution.py:564
  12.5 9.9 %collective-permute-done.1.refs_2_ = bf16[17,32,128]{2,1,0:T(8,128)(2,1)S(1)} collective-permute-done((bf16[17,32,128]{2,1,0:T(8,128)(2,1)S(1)}, bf16[17,32,128]{2,1,0:T(8,128)(2,1)S(1)}, u32[]{:S(2)}, u32[]{:S(2)}) %collective-permute-start.1) | collective-permute-done | bytes 139296 | tf_op jit(solution)/shard_map/ppermute | solution.py:564
  22.9 3.0 %rope_pages.1 = (bf16[16,2,2,128,128]{4,3,2,1,0:T(8,128)(2,1)S(1)}, s32[48]{0:T(128)S(1)}) custom-call(s32[16]{0:T(128)} %slot_ref.1, s32[1,4]{1,0:T(1,128)} %len_ref.1, bf16[16,2,2,128,128]{4,3,2,1,0:T(8,128)(2,1)} %pages_ref.1, f32[128,128]{1,0:T(8,128)} %constant.20.clone.ct_ref, f32[128,128]{1,0:T(8,128)} %constant.21.clone.st_ref, ...), custom_call_target="tpu_custom_call" | custom-call | flops 6000000 | bytes 2000000 | tf_op jit(solution)/shard_map/rope_pages/pallas_call | solution.py:86
  25.9 1.5 %collective-permute-done.5.refs_6_ = bf16[17,32,128]{2,1,0:T(8,128)(2,1)S(1)} collective-permute-done((bf16[17,32,128]{2,1,0:T(8,128)(2,1)S(1)}, bf16[17,32,128]{2,1,0:T(8,128)(2,1)S(1)}, u32[]{:S(2)}, u32[]{:S(2)}) %collective-permute-start.5) | collective-permute-done | bytes 139296 | tf_op jit(solution)/shard_map/ppermute | solution.py:565
  27.4 2.1 %arrived_attention.1 = bf16[8,80,128]{2,1,0:T(8,128)(2,1)} custom-call(s32[2]{0:T(128)S(1)} %pad_add_fusion.me_ref.place_ref, s32[48]{0:T(128)S(1)} %get-tuple-element.13.own_ref, bf16[17,32,128]{2,1,0:T(8,128)(2,1)S(1)} %asked_queries.1.refs_0_.q_ref, bf16[17,32,128]{2,1,0:T(8,128)(2,1)S(1)} %collective-permute-done.refs_1_, ...), custom_call_target="tpu_custom_call" | custom-call | flops 200000000 | bytes 4000000 | tf_op jit(solution)/shard_map/arrived_attention/pallas_call | solution.py:379
  29.5 3.4 %all-to-all-start = ((bf16[8,80,128]{2,1,0:T(8,128)(2,1)}), bf16[8,80,128]{2,1,0:T(8,128)(2,1)S(1)}, u32[]{:S(2)}, u32[]{:S(2)}) async-start(bf16[8,80,128]{2,1,0:T(8,128)(2,1)} %arrived_attention.1), calls=%async_computation | async-start | bytes 327680 | tf_op jit(solution)/shard_map/all_to_all | solution.py:602
  32.9 4.4 %local_attention.1 = (f32[512,128]{1,0:T(8,128)S(1)}, f32[512,128]{1,0:T(8,128)S(1)}) custom-call(s32[3,16]{1,0:T(4,128)} %bitcast.4, s32[16]{0:T(128)} %context_ref.3, s32[48]{0:T(128)} %fill_ref.1, bf16[17,32,128]{2,1,0:T(8,128)(2,1)S(1)} %asked_queries.1.refs_0_.q_ref, bf16[2,16,512]{2,1,0:T(8,128)(2,1)S(1)} %reshape.3.new_ref, ...), custom_call_target="tpu_custom_call" | custom-call | flops 800000000 | bytes 12000000 | tf_op jit(solution)/shard_map/local_attention/pallas_call | solution.py:294
  37.3 3.1 %all-to-all-done.parts_ref = bf16[8,80,128]{2,1,0:T(8,128)(2,1)S(1)} async-done(((bf16[8,80,128]{2,1,0:T(8,128)(2,1)}), bf16[8,80,128]{2,1,0:T(8,128)(2,1)S(1)}, u32[]{:S(2)}, u32[]{:S(2)}) %all-to-all-start) | async-done | bytes 163872 | tf_op jit(solution)/shard_map/all_to_all | solution.py:602
  40.4 1.7 %merge.1.x_ref.refs_0_ = bf16[2,16,2048]{2,1,0:T(8,128)(2,1)S(1)} custom-call(s32[2]{0:T(128)S(1)} %pad_add_fusion.me_ref.place_ref, bf16[8,80,128]{2,1,0:T(8,128)(2,1)S(1)} %all-to-all-done.parts_ref, f32[512,128]{1,0:T(8,128)S(1)} %get-tuple-element.15.o_ref, f32[512,128]{1,0:T(8,128)S(1)} %get-tuple-element.16.stat_ref), custom_call_target="tpu_custom_call" | custom-call | flops 2000000 | bytes 1500000 | tf_op jit(solution)/shard_map/merge/pallas_call | solution.py:441
  42.3 1.2 %collective-permute-start.8 = (bf16[2,16,2048]{2,1,0:T(8,128)(2,1)S(1)}, bf16[2,16,2048]{2,1,0:T(8,128)(2,1)S(1)}, u32[]{:S(2)}, u32[]{:S(2)}) collective-permute-start(bf16[2,16,2048]{2,1,0:T(8,128)(2,1)S(1)} %merge.1.x_ref.refs_0_), channel_id=1, source_target_pairs={{0,8},{2,10},{4,12},{6,14},{8,0},{10,2},{12,4},{14,6},{1,9},{3,11}... | collective-permute-start | bytes 393224 | tf_op jit(solution)/shard_map/ppermute | solution.py:564
  43.5 2.2 %fetch_weight.1 = (bf16[2048,1024]{1,0:T(8,128)(2,1)S(1)}, bf16[2,16,2048]{2,1,0:T(8,128)(2,1)S(1)}) custom-call(bf16[2048,1024]{1,0:T(8,128)(2,1)} %weight_ref.1, bf16[2,16,2048]{2,1,0:T(8,128)(2,1)S(1)} %merge.1.x_ref.refs_0_), custom_call_target="tpu_custom_call" | custom-call | bytes 8388608 | tf_op jit(solution)/shard_map/fetch_weight/pallas_call | solution.py:468
  45.7 2.4 %collective-permute-start.9 = (bf16[2,16,2048]{2,1,0:T(8,128)(2,1)S(1)}, bf16[2,16,2048]{2,1,0:T(8,128)(2,1)S(1)}, u32[]{:S(2)}, u32[]{:S(2)}) collective-permute-start(bf16[2,16,2048]{2,1,0:T(8,128)(2,1)S(1)} %get-tuple-element.17), channel_id=1, source_target_pairs={{0,12},{2,14},{4,0},{6,2},{8,4},{10,6},{12,8},{14,10},{1,13},{3,15... | collective-permute-start | bytes 393224 | tf_op jit(solution)/shard_map/ppermute | solution.py:564
  48.2 1.1 %collective-permute-start.11 = (bf16[2,16,2048]{2,1,0:T(8,128)(2,1)S(1)}, bf16[2,16,2048]{2,1,0:T(8,128)(2,1)S(1)}, u32[]{:S(2)}, u32[]{:S(2)}) collective-permute-start(bf16[2,16,2048]{2,1,0:T(8,128)(2,1)S(1)} %collective-permute-done.10.refs_4_), channel_id=1, source_target_pairs={{0,4},{2,6},{4,8},{6,10},{8,12},{10,14},{12,0},{14,2},{1,5},{3,7},... | collective-permute-start | bytes 393224 | tf_op jit(solution)/shard_map/ppermute | solution.py:564
  49.2 7.2 %collective-permute-done.8.refs_2_ = bf16[2,16,2048]{2,1,0:T(8,128)(2,1)S(1)} collective-permute-done((bf16[2,16,2048]{2,1,0:T(8,128)(2,1)S(1)}, bf16[2,16,2048]{2,1,0:T(8,128)(2,1)S(1)}, u32[]{:S(2)}, u32[]{:S(2)}) %collective-permute-start.8) | collective-permute-done | bytes 131104 | tf_op jit(solution)/shard_map/ppermute | solution.py:564
  57.1 1.4 %collective-permute-start.13 = (bf16[2,16,2048]{2,1,0:T(8,128)(2,1)S(1)}, bf16[2,16,2048]{2,1,0:T(8,128)(2,1)S(1)}, u32[]{:S(2)}, u32[]{:S(2)}) collective-permute-start(bf16[2,16,2048]{2,1,0:T(8,128)(2,1)S(1)} %collective-permute-done.9.refs_3_), channel_id=1, source_target_pairs={{0,2},{2,0},{4,6},{6,4},{8,10},{10,8},{12,14},{14,12},{1,3},{3,1},... | collective-permute-start | bytes 393224 | tf_op jit(solution)/shard_map/ppermute | solution.py:565
  58.5 2.9 %collective-permute-done.12.refs_6_ = bf16[2,16,2048]{2,1,0:T(8,128)(2,1)S(1)} collective-permute-done((bf16[2,16,2048]{2,1,0:T(8,128)(2,1)S(1)}, bf16[2,16,2048]{2,1,0:T(8,128)(2,1)S(1)}, u32[]{:S(2)}, u32[]{:S(2)}) %collective-permute-start.12) | collective-permute-done | bytes 131104 | tf_op jit(solution)/shard_map/ppermute | solution.py:565
  61.4 1.4 %collective-permute-done.13.refs_7_ = bf16[2,16,2048]{2,1,0:T(8,128)(2,1)S(1)} collective-permute-done((bf16[2,16,2048]{2,1,0:T(8,128)(2,1)S(1)}, bf16[2,16,2048]{2,1,0:T(8,128)(2,1)S(1)}, u32[]{:S(2)}, u32[]{:S(2)}) %collective-permute-start.13) | collective-permute-done | bytes 131104 | tf_op jit(solution)/shard_map/ppermute | solution.py:565
  62.8 1.3 %project_other.1 = (bf16[2,128,512]{2,1,0:T(8,128)(2,1)S(1)}, bf16[256,2048]{1,0:T(8,128)(2,1)S(1)}) custom-call(s32[2]{0:T(128)S(1)} %pad_add_fusion.me_ref.place_ref, bf16[2,16,2048]{2,1,0:T(8,128)(2,1)S(1)} %merge.1.x_ref.refs_0_, bf16[2,16,2048]{2,1,0:T(8,128)(2,1)S(1)} %collective-permute-done.7.refs_1_, ...), custom_call_target="tpu_custom_call" | custom-call | flops 536870912 | bytes 4000000 | tf_op jit(solution)/shard_map/project_other/pallas_call | solution.py:507
  64.2 1.3 %project_own.1 = f32[2,128,512]{2,1,0:T(8,128)S(1)} custom-call(s32[2]{0:T(128)S(1)} %pad_add_fusion.me_ref.place_ref, bf16[256,2048]{1,0:T(8,128)(2,1)S(1)} %get-tuple-element.19.lhs, bf16[2048,1024]{1,0:T(8,128)(2,1)S(1)} %get-tuple-element.18.refs_8_.weight_ref), custom_call_target="tpu_custom_call" | custom-call | flops 536870912 | bytes 4000000 | tf_op jit(solution)/shard_map/project_own/pallas_call | solution.py:528
  65.8 0.8 %add_convert_fusion = bf16[2,128,512]{2,1,0:T(8,128)(2,1)} fusion(f32[2,128,512]{2,1,0:T(8,128)S(1)} %project_own.1, bf16[2,128,512]{2,1,0:T(8,128)(2,1)S(1)} %collective-permute-done.14), kind=kLoop, calls=%fused_computation | loop fusion | flops 393216 | bytes 1048576 | tf_op jit(solution)/shard_map/convert_element_type | solution.py:609
  (21 shorter events, 2.9 us)
Async XLA Ops:
  0.0 32.9 %copy-start = (bf16[2,16,2,2,128]{4,3,2,1,0:T(2,128)(2,1)S(1)}, bf16[2,16,2,2,128]{4,3,2,1,0:T(2,128)(2,1)}, u32[]{:S(2)}) copy-start(bf16[2,16,2,2,128]{4,3,2,1,0:T(2,128)(2,1)} %param.24) | copy-start | bytes 98308
  1.2 7.7 %collective-permute-start.3 = (bf16[17,32,128]{2,1,0:T(8,128)(2,1)S(1)}, bf16[17,32,128]{2,1,0:T(8,128)(2,1)S(1)}, u32[]{:S(2)}, u32[]{:S(2)}) collective-permute-start(bf16[17,32,128]{2,1,0:T(8,128)(2,1)S(1)} %asked_queries.1.refs_0_.q_ref), channel_id=1, source_target_pairs={{0,2},{2,0},{4,6},{6,4},{8,10},{10,8},{12,14},{14,12},{1,3},{3,1},... | collective-permute-start | bytes 417800 | tf_op jit(solution)/shard_map/ppermute | solution.py:565
  4.3 7.7 %collective-permute-start.2 = (bf16[17,32,128]{2,1,0:T(8,128)(2,1)S(1)}, bf16[17,32,128]{2,1,0:T(8,128)(2,1)S(1)}, u32[]{:S(2)}, u32[]{:S(2)}) collective-permute-start(bf16[17,32,128]{2,1,0:T(8,128)(2,1)S(1)} %asked_queries.1.refs_0_.q_ref), channel_id=1, source_target_pairs={{0,12},{2,14},{4,0},{6,2},{8,4},{10,6},{12,8},{14,10},{1,13},{3,15... | collective-permute-start | bytes 417800 | tf_op jit(solution)/shard_map/ppermute | solution.py:564
  7.9 14.5 %collective-permute-start.1 = (bf16[17,32,128]{2,1,0:T(8,128)(2,1)S(1)}, bf16[17,32,128]{2,1,0:T(8,128)(2,1)S(1)}, u32[]{:S(2)}, u32[]{:S(2)}) collective-permute-start(bf16[17,32,128]{2,1,0:T(8,128)(2,1)S(1)} %asked_queries.1.refs_0_.q_ref), channel_id=1, source_target_pairs={{0,8},{2,10},{4,12},{6,14},{8,0},{10,2},{12,4},{14,6},{1,9},{3,11}... | collective-permute-start | bytes 417800 | tf_op jit(solution)/shard_map/ppermute | solution.py:564
  7.9 18.0 %collective-permute-start = (bf16[17,32,128]{2,1,0:T(8,128)(2,1)S(1)}, bf16[17,32,128]{2,1,0:T(8,128)(2,1)S(1)}, u32[]{:S(2)}, u32[]{:S(2)}) collective-permute-start(bf16[17,32,128]{2,1,0:T(8,128)(2,1)S(1)} %asked_queries.1.refs_0_.q_ref), channel_id=1, source_target_pairs={{0,4},{2,6},{4,8},{6,10},{8,12},{10,14},{12,0},{14,2},{1,5},{3,7},... | collective-permute-start | bytes 417800 | tf_op jit(solution)/shard_map/ppermute | solution.py:564
  8.9 17.0 %collective-permute-start.4 = (bf16[17,32,128]{2,1,0:T(8,128)(2,1)S(1)}, bf16[17,32,128]{2,1,0:T(8,128)(2,1)S(1)}, u32[]{:S(2)}, u32[]{:S(2)}) collective-permute-start(bf16[17,32,128]{2,1,0:T(8,128)(2,1)S(1)} %collective-permute-done.3.refs_4_), channel_id=1, source_target_pairs={{0,4},{2,6},{4,8},{6,10},{8,12},{10,14},{12,0},{14,2},{1,5},{3,7},... | collective-permute-start | bytes 417800 | tf_op jit(solution)/shard_map/ppermute | solution.py:564
  12.0 13.9 %collective-permute-start.6 = (bf16[17,32,128]{2,1,0:T(8,128)(2,1)S(1)}, bf16[17,32,128]{2,1,0:T(8,128)(2,1)S(1)}, u32[]{:S(2)}, u32[]{:S(2)}) collective-permute-start(bf16[17,32,128]{2,1,0:T(8,128)(2,1)S(1)} %collective-permute-done.2.refs_3_), channel_id=1, source_target_pairs={{0,2},{2,0},{4,6},{6,4},{8,10},{10,8},{12,14},{14,12},{1,3},{3,1},... | collective-permute-start | bytes 417800 | tf_op jit(solution)/shard_map/ppermute | solution.py:565
  22.3 5.1 %collective-permute-start.5 = (bf16[17,32,128]{2,1,0:T(8,128)(2,1)S(1)}, bf16[17,32,128]{2,1,0:T(8,128)(2,1)S(1)}, u32[]{:S(2)}, u32[]{:S(2)}) collective-permute-start(bf16[17,32,128]{2,1,0:T(8,128)(2,1)S(1)} %collective-permute-done.1.refs_2_), channel_id=1, source_target_pairs={{0,2},{2,0},{4,6},{6,4},{8,10},{10,8},{12,14},{14,12},{1,3},{3,1},... | collective-permute-start | bytes 417800 | tf_op jit(solution)/shard_map/ppermute | solution.py:565
  29.5 10.9 %all-to-all-start = ((bf16[8,80,128]{2,1,0:T(8,128)(2,1)}), bf16[8,80,128]{2,1,0:T(8,128)(2,1)S(1)}, u32[]{:S(2)}, u32[]{:S(2)}) async-start(bf16[8,80,128]{2,1,0:T(8,128)(2,1)} %arrived_attention.1), calls=%async_computation | async-start | bytes 327680 | tf_op jit(solution)/shard_map/all_to_all | solution.py:602
  42.1 6.1 %collective-permute-start.10 = (bf16[2,16,2048]{2,1,0:T(8,128)(2,1)S(1)}, bf16[2,16,2048]{2,1,0:T(8,128)(2,1)S(1)}, u32[]{:S(2)}, u32[]{:S(2)}) collective-permute-start(bf16[2,16,2048]{2,1,0:T(8,128)(2,1)S(1)} %merge.1.x_ref.refs_0_), channel_id=1, source_target_pairs={{0,2},{2,0},{4,6},{6,4},{8,10},{10,8},{12,14},{14,12},{1,3},{3,1},... | collective-permute-start | bytes 393224 | tf_op jit(solution)/shard_map/ppermute | solution.py:565
  42.3 14.2 %collective-permute-start.8 = (bf16[2,16,2048]{2,1,0:T(8,128)(2,1)S(1)}, bf16[2,16,2048]{2,1,0:T(8,128)(2,1)S(1)}, u32[]{:S(2)}, u32[]{:S(2)}) collective-permute-start(bf16[2,16,2048]{2,1,0:T(8,128)(2,1)S(1)} %merge.1.x_ref.refs_0_), channel_id=1, source_target_pairs={{0,8},{2,10},{4,12},{6,14},{8,0},{10,2},{12,4},{14,6},{1,9},{3,11}... | collective-permute-start | bytes 393224 | tf_op jit(solution)/shard_map/ppermute | solution.py:564
  45.7 11.3 %collective-permute-start.9 = (bf16[2,16,2048]{2,1,0:T(8,128)(2,1)S(1)}, bf16[2,16,2048]{2,1,0:T(8,128)(2,1)S(1)}, u32[]{:S(2)}, u32[]{:S(2)}) collective-permute-start(bf16[2,16,2048]{2,1,0:T(8,128)(2,1)S(1)} %get-tuple-element.17), channel_id=1, source_target_pairs={{0,12},{2,14},{4,0},{6,2},{8,4},{10,6},{12,8},{14,10},{1,13},{3,15... | collective-permute-start | bytes 393224 | tf_op jit(solution)/shard_map/ppermute | solution.py:564
  48.1 10.3 %collective-permute-start.7 = (bf16[2,16,2048]{2,1,0:T(8,128)(2,1)S(1)}, bf16[2,16,2048]{2,1,0:T(8,128)(2,1)S(1)}, u32[]{:S(2)}, u32[]{:S(2)}) collective-permute-start(bf16[2,16,2048]{2,1,0:T(8,128)(2,1)S(1)} %get-tuple-element.17), channel_id=1, source_target_pairs={{0,4},{2,6},{4,8},{6,10},{8,12},{10,14},{12,0},{14,2},{1,5},{3,7},... | collective-permute-start | bytes 393224 | tf_op jit(solution)/shard_map/ppermute | solution.py:564
  48.2 10.3 %collective-permute-start.11 = (bf16[2,16,2048]{2,1,0:T(8,128)(2,1)S(1)}, bf16[2,16,2048]{2,1,0:T(8,128)(2,1)S(1)}, u32[]{:S(2)}, u32[]{:S(2)}) collective-permute-start(bf16[2,16,2048]{2,1,0:T(8,128)(2,1)S(1)} %collective-permute-done.10.refs_4_), channel_id=1, source_target_pairs={{0,4},{2,6},{4,8},{6,10},{8,12},{10,14},{12,0},{14,2},{1,5},{3,7},... | collective-permute-start | bytes 393224 | tf_op jit(solution)/shard_map/ppermute | solution.py:564
  56.4 5.0 %collective-permute-start.12 = (bf16[2,16,2048]{2,1,0:T(8,128)(2,1)S(1)}, bf16[2,16,2048]{2,1,0:T(8,128)(2,1)S(1)}, u32[]{:S(2)}, u32[]{:S(2)}) collective-permute-start(bf16[2,16,2048]{2,1,0:T(8,128)(2,1)S(1)} %collective-permute-done.8.refs_2_), channel_id=1, source_target_pairs={{0,2},{2,0},{4,6},{6,4},{8,10},{10,8},{12,14},{14,12},{1,3},{3,1},... | collective-permute-start | bytes 393224 | tf_op jit(solution)/shard_map/ppermute | solution.py:565
  57.1 5.7 %collective-permute-start.13 = (bf16[2,16,2048]{2,1,0:T(8,128)(2,1)S(1)}, bf16[2,16,2048]{2,1,0:T(8,128)(2,1)S(1)}, u32[]{:S(2)}, u32[]{:S(2)}) collective-permute-start(bf16[2,16,2048]{2,1,0:T(8,128)(2,1)S(1)} %collective-permute-done.9.refs_3_), channel_id=1, source_target_pairs={{0,2},{2,0},{4,6},{6,4},{8,10},{10,8},{12,14},{14,12},{1,3},{3,1},... | collective-permute-start | bytes 393224 | tf_op jit(solution)/shard_map/ppermute | solution.py:565
  64.2 1.6 %collective-permute-start.14 = (bf16[2,128,512]{2,1,0:T(8,128)(2,1)S(1)}, bf16[2,128,512]{2,1,0:T(8,128)(2,1)S(1)}, u32[]{:S(2)}, u32[]{:S(2)}) collective-permute-start(bf16[2,128,512]{2,1,0:T(8,128)(2,1)S(1)} %get-tuple-element.20), channel_id=1, source_target_pairs={{0,1},{1,0},{2,3},{3,2},{4,5},{5,4},{6,7},{7,6},{8,9},{9,8},{10,11... | collective-permute-start | bytes 786440 | tf_op jit(solution)/shard_map/ppermute | solution.py:573

commit v15 on v13

--- a/solution.py
+++ b/solution.py
@@ -494,7 +494,7 @@
         at = pl.ds(pl.multiple_of(which * half + i * tile, LANES), tile)
         terms = jnp.dot(lhs[...], weight_ref[:, at], preferred_element_type=F32)
         for s in range(steps):
-            out_ref[s, :, i * tile : (i + 1) * tile] = terms[s * every : (s + 1) * every]
+            out_ref[s, :, i * tile : (i + 1) * tile] = terms[s * every : (s + 1) * every].astype(out_ref.dtype)
 
 
 def other_projection(place, blocks, weight):
@@ -505,7 +505,7 @@
     return pl.pallas_call(
         functools.partial(rows_kernel, npool),
         out_shape=[
-            jax.ShapeDtypeStruct((steps, npool * rows, half), F32),
+            jax.ShapeDtypeStruct((steps, npool * rows, half), BF16),
             jax.ShapeDtypeStruct((every, width), BF16),
         ],
         in_specs=[SMEM] + [VMEM] * (npool + 1),
@@ -561,8 +561,13 @@
     later = x if later is None else later
     ahead = lambda x, by: lax.ppermute(x, "pool", [(i, (i + 2 * by) % npool) for i in range(npool)])
     across = lambda x: lax.ppermute(x, "pool", [(i, i ^ 1) for i in range(npool)])
-    straight = [x] + [ahead(x if by == half // 2 else later, by) for by in range(1, half)]
-    return straight + [across(y) for y in straight]
+    partner = across(x)
+    last = x
+    if later is not x:
+        last, partner = lax.optimization_barrier((later, partner))
+    sent = {half // 2: x, 1: last}
+    straight = [x] + [ahead(sent.get(by, later), by) for by in range(1, half)]
+    return straight + [partner] + [across(y) for y in straight[1:]]
 
 
 def swap_halves(x):
@@ -602,7 +607,7 @@
     other_terms, lhs = other_projection(place, blocks, weight)
     other_terms = swap_halves(other_terms)
     terms = own_projection(place, lhs, weight, queries.shape[0])
-    return (terms + other_terms).astype(BF16)
+    return (terms + other_terms.astype(F32)).astype(BF16)
 
 
 def solution(mesh):

time: 62.1 us -> 62.9 us (1.013)
  starting transfers between devices: 21.9 us -> 21 us
  waiting for transfers between devices: 22 us -> 22.9 us
    ppermute x8, starting transfers between devices: 9.81 us -> 7.84 us  [gathered(): lax.ppermute(x, 'pool', [(i, i ^ 1) for i in range(npool)])]
    ppermute x6, waiting for transfers between devices: 11.2 us -> 12.6 us  [gathered(): lax.ppermute(x, 'pool', [(i, (i + 2 * by) % npool) for i in range(npool)])]
    ppermute x6, starting transfers between devices: 8.6 us -> 9.75 us  [gathered(): lax.ppermute(x, 'pool', [(i, (i + 2 * by) % npool) for i in range(npool)])]
  transfers between devices with their start and end apart: 16 -> 16, of which waited for: 12 -> 11; matrix products, arithmetic and copies ran while one was open for 0% -> 0% of each run, Pallas kernels for 17% -> 18%
where the time goes in v15:
time: 62.9 us; the launch traced here: 62.3 us
  waiting for transfers between devices  22.9 us (36%)
  starting transfers between devices  21 us (33%)
  Pallas kernels  17.3 us (28%)
  other arithmetic  0.86 us (1%)
    ppermute x6, waiting for transfers between devices, gathered(): lax.ppermute(x, 'pool', [(i, (i + 2 * by) % npool) for i in range(npool)])  12.6 us
    ppermute x6, starting transfers between devices, gathered(): lax.ppermute(x, 'pool', [(i, (i + 2 * by) % npool) for i in range(npool)])  9.75 us
    ppermute x8, starting transfers between devices, gathered(): lax.ppermute(x, 'pool', [(i, i ^ 1) for i in range(npool)])  7.84 us
    ppermute x8, waiting for transfers between devices, gathered(): lax.ppermute(x, 'pool', [(i, i ^ 1) for i in range(npool)])  7.33 us
    pallas_call x1, Pallas kernels, local_attention(): pl.pallas_call(functools.partial(local_kernel, page_len, heads), out_shap...  4.7 us
    all_to_all x1, starting transfers between devices, shards(): lax.all_to_all(parts, 'pool', split_axis=0, concat_axis=0, tiled=True)  3.38 us
    pallas_call x1, Pallas kernels, rotated_pages(): pl.pallas_call(functools.partial(rope_kernel, npool, cache_pages, per), g...  2.96 us
    all_to_all x1, waiting for transfers between devices, shards(): lax.all_to_all(parts, 'pool', split_axis=0, concat_axis=0, tiled=True)  2.76 us
  transfers between devices with their start and end apart: 16, of which 11 were waited for; matrix products, arithmetic and copies ran while one was open for 0% of the time, Pallas kernels for 18%

profile of v15, /device:TPU:0, one launch (start us, length us, event | category | flops | bytes accessed | tf_op | source)
XLA Modules:
  0.0 62.3 jit_solution(4600506249935569472)
XLA Ops:
  0.0 1.2 %asked_queries.1.refs_0_.q_ref = bf16[17,32,128]{2,1,0:T(8,128)(2,1)S(1)} custom-call(s32[3,16]{1,0:T(4,128)} %bitcast.3, s32[16]{0:T(128)} %context_ref.3, bf16[2,16,2048]{2,1,0:T(8,128)(2,1)} %q_ref.1), custom_call_target="tpu_custom_call" | custom-call | flops 100000 | bytes 300000 | tf_op jit(solution)/shard_map/asked_queries/pallas_call | solution.py:138
  1.2 5.1 %collective-permute-start.2 = (bf16[17,32,128]{2,1,0:T(8,128)(2,1)S(1)}, bf16[17,32,128]{2,1,0:T(8,128)(2,1)S(1)}, u32[]{:S(2)}, u32[]{:S(2)}) collective-permute-start(bf16[17,32,128]{2,1,0:T(8,128)(2,1)S(1)} %asked_queries.1.refs_0_.q_ref), channel_id=1, source_target_pairs={{0,12},{2,14},{4,0},{6,2},{8,4},{10,6},{12,8},{14,10},{1,13},{3,15... | collective-permute-start | bytes 417800 | tf_op jit(solution)/shard_map/ppermute | solution.py:562
  7.3 1.5 %collective-permute-start.3 = (bf16[17,32,128]{2,1,0:T(8,128)(2,1)S(1)}, bf16[17,32,128]{2,1,0:T(8,128)(2,1)S(1)}, u32[]{:S(2)}, u32[]{:S(2)}) collective-permute-start(bf16[17,32,128]{2,1,0:T(8,128)(2,1)S(1)} %asked_queries.1.refs_0_.q_ref), channel_id=1, source_target_pairs={{0,2},{2,0},{4,6},{6,4},{8,10},{10,8},{12,14},{14,12},{1,3},{3,1},... | collective-permute-start | bytes 417800 | tf_op jit(solution)/shard_map/ppermute | solution.py:563
  8.9 1.6 %collective-permute-done.2.refs_3_ = bf16[17,32,128]{2,1,0:T(8,128)(2,1)S(1)} collective-permute-done((bf16[17,32,128]{2,1,0:T(8,128)(2,1)S(1)}, bf16[17,32,128]{2,1,0:T(8,128)(2,1)S(1)}, u32[]{:S(2)}, u32[]{:S(2)}) %collective-permute-start.2) | collective-permute-done | bytes 139296 | tf_op jit(solution)/shard_map/ppermute | solution.py:562
  10.4 1.5 %collective-permute-start.6 = (bf16[17,32,128]{2,1,0:T(8,128)(2,1)S(1)}, bf16[17,32,128]{2,1,0:T(8,128)(2,1)S(1)}, u32[]{:S(2)}, u32[]{:S(2)}) collective-permute-start(bf16[17,32,128]{2,1,0:T(8,128)(2,1)S(1)} %collective-permute-done.2.refs_3_), channel_id=1, source_target_pairs={{0,2},{2,0},{4,6},{6,4},{8,10},{10,8},{12,14},{14,12},{1,3},{3,1},... | collective-permute-start | bytes 417800 | tf_op jit(solution)/shard_map/ppermute | solution.py:563
  11.9 6.2 %collective-permute-done.1.refs_2_ = bf16[17,32,128]{2,1,0:T(8,128)(2,1)S(1)} collective-permute-done((bf16[17,32,128]{2,1,0:T(8,128)(2,1)S(1)}, bf16[17,32,128]{2,1,0:T(8,128)(2,1)S(1)}, u32[]{:S(2)}, u32[]{:S(2)}) %collective-permute-start.1) | collective-permute-done | bytes 139296 | tf_op jit(solution)/shard_map/ppermute | solution.py:562
  18.1 1.5 %collective-permute-start.5 = (bf16[17,32,128]{2,1,0:T(8,128)(2,1)S(1)}, bf16[17,32,128]{2,1,0:T(8,128)(2,1)S(1)}, u32[]{:S(2)}, u32[]{:S(2)}) collective-permute-start(bf16[17,32,128]{2,1,0:T(8,128)(2,1)S(1)} %collective-permute-done.1.refs_2_), channel_id=1, source_target_pairs={{0,2},{2,0},{4,6},{6,4},{8,10},{10,8},{12,14},{14,12},{1,3},{3,1},... | collective-permute-start | bytes 417800 | tf_op jit(solution)/shard_map/ppermute | solution.py:563
  20.2 3.0 %rope_pages.1 = (bf16[16,2,2,128,128]{4,3,2,1,0:T(8,128)(2,1)S(1)}, s32[48]{0:T(128)S(1)}) custom-call(s32[16]{0:T(128)} %slot_ref.1, s32[1,4]{1,0:T(1,128)} %len_ref.1, bf16[16,2,2,128,128]{4,3,2,1,0:T(8,128)(2,1)} %pages_ref.1, f32[128,128]{1,0:T(8,128)} %constant.20.clone.ct_ref, f32[128,128]{1,0:T(8,128)} %constant.21.clone.st_ref, ...), custom_call_target="tpu_custom_call" | custom-call | flops 6000000 | bytes 2000000 | tf_op jit(solution)/shard_map/rope_pages/pallas_call | solution.py:86
  23.2 1.3 %collective-permute-done.5.refs_6_ = bf16[17,32,128]{2,1,0:T(8,128)(2,1)S(1)} collective-permute-done((bf16[17,32,128]{2,1,0:T(8,128)(2,1)S(1)}, bf16[17,32,128]{2,1,0:T(8,128)(2,1)S(1)}, u32[]{:S(2)}, u32[]{:S(2)}) %collective-permute-start.5) | collective-permute-done | bytes 139296 | tf_op jit(solution)/shard_map/ppermute | solution.py:563
  24.6 1.5 %collective-permute-done.4.refs_5_ = bf16[17,32,128]{2,1,0:T(8,128)(2,1)S(1)} collective-permute-done((bf16[17,32,128]{2,1,0:T(8,128)(2,1)S(1)}, bf16[17,32,128]{2,1,0:T(8,128)(2,1)S(1)}, u32[]{:S(2)}, u32[]{:S(2)}) %collective-permute-start.4) | collective-permute-done | bytes 139296 | tf_op jit(solution)/shard_map/ppermute | solution.py:563
  26.1 2.1 %arrived_attention.1 = bf16[8,80,128]{2,1,0:T(8,128)(2,1)} custom-call(s32[2]{0:T(128)S(1)} %pad_add_fusion.me_ref.place_ref, s32[48]{0:T(128)S(1)} %get-tuple-element.15.own_ref, bf16[17,32,128]{2,1,0:T(8,128)(2,1)S(1)} %asked_queries.1.refs_0_.q_ref, bf16[17,32,128]{2,1,0:T(8,128)(2,1)S(1)} %collective-permute-done.refs_1_, ...), custom_call_target="tpu_custom_call" | custom-call | flops 200000000 | bytes 4000000 | tf_op jit(solution)/shard_map/arrived_attention/pallas_call | solution.py:379
  28.2 3.4 %all-to-all-start = ((bf16[8,80,128]{2,1,0:T(8,128)(2,1)}), bf16[8,80,128]{2,1,0:T(8,128)(2,1)S(1)}, u32[]{:S(2)}, u32[]{:S(2)}) async-start(bf16[8,80,128]{2,1,0:T(8,128)(2,1)} %arrived_attention.1), calls=%async_computation | async-start | bytes 327680 | tf_op jit(solution)/shard_map/all_to_all | solution.py:603
  31.6 4.7 %local_attention.1 = (f32[512,128]{1,0:T(8,128)S(1)}, f32[512,128]{1,0:T(8,128)S(1)}) custom-call(s32[3,16]{1,0:T(4,128)} %bitcast.4, s32[16]{0:T(128)} %context_ref.3, s32[48]{0:T(128)} %fill_ref.1, bf16[17,32,128]{2,1,0:T(8,128)(2,1)S(1)} %asked_queries.1.refs_0_.q_ref, bf16[2,16,512]{2,1,0:T(8,128)(2,1)S(1)} %reshape.3.new_ref, ...), custom_call_target="tpu_custom_call" | custom-call | flops 800000000 | bytes 12000000 | tf_op jit(solution)/shard_map/local_attention/pallas_call | solution.py:294
  36.3 2.8 %all-to-all-done.parts_ref = bf16[8,80,128]{2,1,0:T(8,128)(2,1)S(1)} async-done(((bf16[8,80,128]{2,1,0:T(8,128)(2,1)}), bf16[8,80,128]{2,1,0:T(8,128)(2,1)S(1)}, u32[]{:S(2)}, u32[]{:S(2)}) %all-to-all-start) | async-done | bytes 163872 | tf_op jit(solution)/shard_map/all_to_all | solution.py:603
  39.1 1.5 %merge.1.x_ref.refs_0_ = bf16[2,16,2048]{2,1,0:T(8,128)(2,1)S(1)} custom-call(s32[2]{0:T(128)S(1)} %pad_add_fusion.me_ref.place_ref, bf16[8,80,128]{2,1,0:T(8,128)(2,1)S(1)} %all-to-all-done.parts_ref, f32[512,128]{1,0:T(8,128)S(1)} %get-tuple-element.17.o_ref, f32[512,128]{1,0:T(8,128)S(1)} %get-tuple-element.18.stat_ref), custom_call_target="tpu_custom_call" | custom-call | flops 2000000 | bytes 1500000 | tf_op jit(solution)/shard_map/merge/pallas_call | solution.py:439
  40.8 1.2 %collective-permute-start.9 = (bf16[2,16,2048]{2,1,0:T(8,128)(2,1)S(1)}, bf16[2,16,2048]{2,1,0:T(8,128)(2,1)S(1)}, u32[]{:S(2)}, u32[]{:S(2)}) collective-permute-start(bf16[2,16,2048]{2,1,0:T(8,128)(2,1)S(1)} %merge.1.x_ref.refs_0_), channel_id=1, source_target_pairs={{0,8},{2,10},{4,12},{6,14},{8,0},{10,2},{12,4},{14,6},{1,9},{3,11}... | collective-permute-start | bytes 393224 | tf_op jit(solution)/shard_map/ppermute | solution.py:562
  41.9 2.2 %fetch_weight.1 = (bf16[2048,1024]{1,0:T(8,128)(2,1)S(1)}, bf16[2,16,2048]{2,1,0:T(8,128)(2,1)S(1)}) custom-call(bf16[2048,1024]{1,0:T(8,128)(2,1)} %weight_ref.1, bf16[2,16,2048]{2,1,0:T(8,128)(2,1)S(1)} %merge.1.x_ref.refs_0_), custom_call_target="tpu_custom_call" | custom-call | bytes 8388608 | tf_op jit(solution)/shard_map/fetch_weight/pallas_call | solution.py:466
  44.2 2.5 %collective-permute-start.10 = (bf16[2,16,2048]{2,1,0:T(8,128)(2,1)S(1)}, bf16[2,16,2048]{2,1,0:T(8,128)(2,1)S(1)}, u32[]{:S(2)}, u32[]{:S(2)}) collective-permute-start(bf16[2,16,2048]{2,1,0:T(8,128)(2,1)S(1)} %get-tuple-element.20), channel_id=1, source_target_pairs={{0,12},{2,14},{4,0},{6,2},{8,4},{10,6},{12,8},{14,10},{1,13},{3,15... | collective-permute-start | bytes 393224 | tf_op jit(solution)/shard_map/ppermute | solution.py:562
  46.7 4.1 %collective-permute-done.9.refs_2_ = bf16[2,16,2048]{2,1,0:T(8,128)(2,1)S(1)} collective-permute-done((bf16[2,16,2048]{2,1,0:T(8,128)(2,1)S(1)}, bf16[2,16,2048]{2,1,0:T(8,128)(2,1)S(1)}, u32[]{:S(2)}, u32[]{:S(2)}) %collective-permute-start.9) | collective-permute-done | bytes 131104 | tf_op jit(solution)/shard_map/ppermute | solution.py:562
  54.1 1.7 %collective-permute-done.12.refs_6_ = bf16[2,16,2048]{2,1,0:T(8,128)(2,1)S(1)} collective-permute-done((bf16[2,16,2048]{2,1,0:T(8,128)(2,1)S(1)}, bf16[2,16,2048]{2,1,0:T(8,128)(2,1)S(1)}, u32[]{:S(2)}, u32[]{:S(2)}) %collective-permute-start.12) | collective-permute-done | bytes 131104 | tf_op jit(solution)/shard_map/ppermute | solution.py:563
  55.8 1.4 %collective-permute-done.13.refs_7_ = bf16[2,16,2048]{2,1,0:T(8,128)(2,1)S(1)} collective-permute-done((bf16[2,16,2048]{2,1,0:T(8,128)(2,1)S(1)}, bf16[2,16,2048]{2,1,0:T(8,128)(2,1)S(1)}, u32[]{:S(2)}, u32[]{:S(2)}) %collective-permute-start.13) | collective-permute-done | bytes 131104 | tf_op jit(solution)/shard_map/ppermute | solution.py:563
  57.2 1.4 %collective-permute-done.11.refs_5_ = bf16[2,16,2048]{2,1,0:T(8,128)(2,1)S(1)} collective-permute-done((bf16[2,16,2048]{2,1,0:T(8,128)(2,1)S(1)}, bf16[2,16,2048]{2,1,0:T(8,128)(2,1)S(1)}, u32[]{:S(2)}, u32[]{:S(2)}) %collective-permute-start.11) | collective-permute-done | bytes 131104 | tf_op jit(solution)/shard_map/ppermute | solution.py:563
  58.6 1.3 %project_other.1 = (bf16[2,128,512]{2,1,0:T(8,128)(2,1)S(1)}, bf16[256,2048]{1,0:T(8,128)(2,1)S(1)}) custom-call(s32[2]{0:T(128)S(1)} %pad_add_fusion.me_ref.place_ref, bf16[2,16,2048]{2,1,0:T(8,128)(2,1)S(1)} %merge.1.x_ref.refs_0_, bf16[2,16,2048]{2,1,0:T(8,128)(2,1)S(1)} %collective-permute-done.8.refs_1_, ...), custom_call_target="tpu_custom_call" | custom-call | flops 536870912 | bytes 4000000 | tf_op jit(solution)/shard_map/project_other/pallas_call | solution.py:505
  60.0 1.3 %project_own.1 = f32[2,128,512]{2,1,0:T(8,128)S(1)} custom-call(s32[2]{0:T(128)S(1)} %pad_add_fusion.me_ref.place_ref, bf16[256,2048]{1,0:T(8,128)(2,1)S(1)} %get-tuple-element.23.lhs, bf16[2048,1024]{1,0:T(8,128)(2,1)S(1)} %get-tuple-element.22.refs_8_.weight_ref), custom_call_target="tpu_custom_call" | custom-call | flops 536870912 | bytes 4000000 | tf_op jit(solution)/shard_map/project_own/pallas_call | solution.py:526
  (21 shorter events, 6.2 us)
Async XLA Ops:
  0.0 31.6 %copy-start = (bf16[2,16,2,2,128]{4,3,2,1,0:T(2,128)(2,1)S(1)}, bf16[2,16,2,2,128]{4,3,2,1,0:T(2,128)(2,1)}, u32[]{:S(2)}) copy-start(bf16[2,16,2,2,128]{4,3,2,1,0:T(2,128)(2,1)} %param.24) | copy-start | bytes 98308
  1.2 9.2 %collective-permute-start.2 = (bf16[17,32,128]{2,1,0:T(8,128)(2,1)S(1)}, bf16[17,32,128]{2,1,0:T(8,128)(2,1)S(1)}, u32[]{:S(2)}, u32[]{:S(2)}) collective-permute-start(bf16[17,32,128]{2,1,0:T(8,128)(2,1)S(1)} %asked_queries.1.refs_0_.q_ref), channel_id=1, source_target_pairs={{0,12},{2,14},{4,0},{6,2},{8,4},{10,6},{12,8},{14,10},{1,13},{3,15... | collective-permute-start | bytes 417800 | tf_op jit(solution)/shard_map/ppermute | solution.py:562
  6.3 11.8 %collective-permute-start.1 = (bf16[17,32,128]{2,1,0:T(8,128)(2,1)S(1)}, bf16[17,32,128]{2,1,0:T(8,128)(2,1)S(1)}, u32[]{:S(2)}, u32[]{:S(2)}) collective-permute-start(bf16[17,32,128]{2,1,0:T(8,128)(2,1)S(1)} %asked_queries.1.refs_0_.q_ref), channel_id=1, source_target_pairs={{0,8},{2,10},{4,12},{6,14},{8,0},{10,2},{12,4},{14,6},{1,9},{3,11}... | collective-permute-start | bytes 417800 | tf_op jit(solution)/shard_map/ppermute | solution.py:562
  6.3 13.3 %collective-permute-start = (bf16[17,32,128]{2,1,0:T(8,128)(2,1)S(1)}, bf16[17,32,128]{2,1,0:T(8,128)(2,1)S(1)}, u32[]{:S(2)}, u32[]{:S(2)}) collective-permute-start(bf16[17,32,128]{2,1,0:T(8,128)(2,1)S(1)} %asked_queries.1.refs_0_.q_ref), channel_id=1, source_target_pairs={{0,4},{2,6},{4,8},{6,10},{8,12},{10,14},{12,0},{14,2},{1,5},{3,7},... | collective-permute-start | bytes 417800 | tf_op jit(solution)/shard_map/ppermute | solution.py:562
  7.3 15.9 %collective-permute-start.3 = (bf16[17,32,128]{2,1,0:T(8,128)(2,1)S(1)}, bf16[17,32,128]{2,1,0:T(8,128)(2,1)S(1)}, u32[]{:S(2)}, u32[]{:S(2)}) collective-permute-start(bf16[17,32,128]{2,1,0:T(8,128)(2,1)S(1)} %asked_queries.1.refs_0_.q_ref), channel_id=1, source_target_pairs={{0,2},{2,0},{4,6},{6,4},{8,10},{10,8},{12,14},{14,12},{1,3},{3,1},... | collective-permute-start | bytes 417800 | tf_op jit(solution)/shard_map/ppermute | solution.py:563
  10.4 12.8 %collective-permute-start.6 = (bf16[17,32,128]{2,1,0:T(8,128)(2,1)S(1)}, bf16[17,32,128]{2,1,0:T(8,128)(2,1)S(1)}, u32[]{:S(2)}, u32[]{:S(2)}) collective-permute-start(bf16[17,32,128]{2,1,0:T(8,128)(2,1)S(1)} %collective-permute-done.2.refs_3_), channel_id=1, source_target_pairs={{0,2},{2,0},{4,6},{6,4},{8,10},{10,8},{12,14},{14,12},{1,3},{3,1},... | collective-permute-start | bytes 417800 | tf_op jit(solution)/shard_map/ppermute | solution.py:563
  18.1 6.4 %collective-permute-start.5 = (bf16[17,32,128]{2,1,0:T(8,128)(2,1)S(1)}, bf16[17,32,128]{2,1,0:T(8,128)(2,1)S(1)}, u32[]{:S(2)}, u32[]{:S(2)}) collective-permute-start(bf16[17,32,128]{2,1,0:T(8,128)(2,1)S(1)} %collective-permute-done.1.refs_2_), channel_id=1, source_target_pairs={{0,2},{2,0},{4,6},{6,4},{8,10},{10,8},{12,14},{14,12},{1,3},{3,1},... | collective-permute-start | bytes 417800 | tf_op jit(solution)/shard_map/ppermute | solution.py:563
  19.7 6.4 %collective-permute-start.4 = (bf16[17,32,128]{2,1,0:T(8,128)(2,1)S(1)}, bf16[17,32,128]{2,1,0:T(8,128)(2,1)S(1)}, u32[]{:S(2)}, u32[]{:S(2)}) collective-permute-start(bf16[17,32,128]{2,1,0:T(8,128)(2,1)S(1)} %collective-permute-done.refs_1_), channel_id=1, source_target_pairs={{0,2},{2,0},{4,6},{6,4},{8,10},{10,8},{12,14},{14,12},{1,3},{3,1},... | collective-permute-start | bytes 417800 | tf_op jit(solution)/shard_map/ppermute | solution.py:563
  28.2 10.9 %all-to-all-start = ((bf16[8,80,128]{2,1,0:T(8,128)(2,1)}), bf16[8,80,128]{2,1,0:T(8,128)(2,1)S(1)}, u32[]{:S(2)}, u32[]{:S(2)}) async-start(bf16[8,80,128]{2,1,0:T(8,128)(2,1)} %arrived_attention.1), calls=%async_computation | async-start | bytes 327680 | tf_op jit(solution)/shard_map/all_to_all | solution.py:603
  40.6 6.1 %collective-permute-start.7 = (bf16[2,16,2048]{2,1,0:T(8,128)(2,1)S(1)}, bf16[2,16,2048]{2,1,0:T(8,128)(2,1)S(1)}, u32[]{:S(2)}, u32[]{:S(2)}) collective-permute-start(bf16[2,16,2048]{2,1,0:T(8,128)(2,1)S(1)} %merge.1.x_ref.refs_0_), channel_id=1, source_target_pairs={{0,2},{2,0},{4,6},{6,4},{8,10},{10,8},{12,14},{14,12},{1,3},{3,1},... | collective-permute-start | bytes 393224 | tf_op jit(solution)/shard_map/ppermute | solution.py:563
  40.8 10.0 %collective-permute-start.9 = (bf16[2,16,2048]{2,1,0:T(8,128)(2,1)S(1)}, bf16[2,16,2048]{2,1,0:T(8,128)(2,1)S(1)}, u32[]{:S(2)}, u32[]{:S(2)}) collective-permute-start(bf16[2,16,2048]{2,1,0:T(8,128)(2,1)S(1)} %merge.1.x_ref.refs_0_), channel_id=1, source_target_pairs={{0,8},{2,10},{4,12},{6,14},{8,0},{10,2},{12,4},{14,6},{1,9},{3,11}... | collective-permute-start | bytes 393224 | tf_op jit(solution)/shard_map/ppermute | solution.py:562
  44.2 7.6 %collective-permute-start.10 = (bf16[2,16,2048]{2,1,0:T(8,128)(2,1)S(1)}, bf16[2,16,2048]{2,1,0:T(8,128)(2,1)S(1)}, u32[]{:S(2)}, u32[]{:S(2)}) collective-permute-start(bf16[2,16,2048]{2,1,0:T(8,128)(2,1)S(1)} %get-tuple-element.20), channel_id=1, source_target_pairs={{0,12},{2,14},{4,0},{6,2},{8,4},{10,6},{12,8},{14,10},{1,13},{3,15... | collective-permute-start | bytes 393224 | tf_op jit(solution)/shard_map/ppermute | solution.py:562
  46.7 6.9 %collective-permute-start.8 = (bf16[2,16,2048]{2,1,0:T(8,128)(2,1)S(1)}, bf16[2,16,2048]{2,1,0:T(8,128)(2,1)S(1)}, u32[]{:S(2)}, u32[]{:S(2)}) collective-permute-start(bf16[2,16,2048]{2,1,0:T(8,128)(2,1)S(1)} %get-tuple-element.20), channel_id=1, source_target_pairs={{0,4},{2,6},{4,8},{6,10},{8,12},{10,14},{12,0},{14,2},{1,5},{3,7},... | collective-permute-start | bytes 393224 | tf_op jit(solution)/shard_map/ppermute | solution.py:562
  50.8 5.0 %collective-permute-start.12 = (bf16[2,16,2048]{2,1,0:T(8,128)(2,1)S(1)}, bf16[2,16,2048]{2,1,0:T(8,128)(2,1)S(1)}, u32[]{:S(2)}, u32[]{:S(2)}) collective-permute-start(bf16[2,16,2048]{2,1,0:T(8,128)(2,1)S(1)} %collective-permute-done.9.refs_2_), channel_id=1, source_target_pairs={{0,2},{2,0},{4,6},{6,4},{8,10},{10,8},{12,14},{14,12},{1,3},{3,1},... | collective-permute-start | bytes 393224 | tf_op jit(solution)/shard_map/ppermute | solution.py:563
  51.8 5.4 %collective-permute-start.13 = (bf16[2,16,2048]{2,1,0:T(8,128)(2,1)S(1)}, bf16[2,16,2048]{2,1,0:T(8,128)(2,1)S(1)}, u32[]{:S(2)}, u32[]{:S(2)}) collective-permute-start(bf16[2,16,2048]{2,1,0:T(8,128)(2,1)S(1)} %collective-permute-done.10.refs_3_), channel_id=1, source_target_pairs={{0,2},{2,0},{4,6},{6,4},{8,10},{10,8},{12,14},{14,12},{1,3},{3,1},... | collective-permute-start | bytes 393224 | tf_op jit(solution)/shard_map/ppermute | solution.py:563
  53.5 5.0 %collective-permute-start.11 = (bf16[2,16,2048]{2,1,0:T(8,128)(2,1)S(1)}, bf16[2,16,2048]{2,1,0:T(8,128)(2,1)S(1)}, u32[]{:S(2)}, u32[]{:S(2)}) collective-permute-start(bf16[2,16,2048]{2,1,0:T(8,128)(2,1)S(1)} %collective-permute-done.8.refs_1_), channel_id=1, source_target_pairs={{0,2},{2,0},{4,6},{6,4},{8,10},{10,8},{12,14},{14,12},{1,3},{3,1},... | collective-permute-start | bytes 393224 | tf_op jit(solution)/shard_map/ppermute | solution.py:563
  59.9 1.6 %collective-permute-start.14 = (bf16[2,128,512]{2,1,0:T(8,128)(2,1)S(1)}, bf16[2,128,512]{2,1,0:T(8,128)(2,1)S(1)}, u32[]{:S(2)}, u32[]{:S(2)}) collective-permute-start(bf16[2,128,512]{2,1,0:T(8,128)(2,1)S(1)} %get-tuple-element.24), channel_id=1, source_target_pairs={{0,1},{1,0},{2,3},{3,2},{4,5},{5,4},{6,7},{7,6},{8,9},{9,8},{10,11... | collective-permute-start | bytes 786440 | tf_op jit(solution)/shard_map/ppermute | solution.py:574

commit v16 on v13

--- a/solution.py
+++ b/solution.py
@@ -334,16 +334,14 @@
     lane = lax.broadcasted_iota(I32, (1, LANES), 1)
     codes = [x[rows, :STAT_ROWS, :].astype(F32) for x in blocks]
     codes = [x[0:1] * CODE + x[1:2] for x in codes]
-    number, seen, request = [], [], []
+    places = [owners[x // pair] * pair + x % pair for x in range(items)]
+    slots = [own_ref[2 * items + at] for at in places]
+    read = [jnp.maximum(read_scalar(codes[x // pair], lane == slots[x]), 0) for x in range(items)]
+    number = [own_ref[at] for at in places]
+    seen = [jnp.minimum(code % CODE, own_ref[items + at]) for code, at in zip(read, places)]
+    request = [jnp.where(slot >= 0, code // CODE, -1) for slot, code in zip(slots, read)]
     for x in range(items):
-        at = owners[x // pair] * pair + x % pair
-        slot = own_ref[2 * items + at]
-        code = jnp.maximum(read_scalar(codes[x // pair], lane == slot), 0)
-        reader, left = code // CODE, code % CODE
-        queries[x * block : (x + 1) * block, :] = blocks[x // pair][reader]
-        number.append(own_ref[at])
-        seen.append(jnp.minimum(left, own_ref[items + at]))
-        request.append(jnp.where(slot >= 0, reader, -1))
+        queries[x * block : (x + 1) * block, :] = blocks[x // pair][read[x] // CODE]
     token = lax.broadcasted_iota(I32, (page_len, LANES), 0)
     groups = [range(i * together, (i + 1) * together) for i in range(items // together)]
     all_scores, all_weights = [], []
@@ -475,16 +473,16 @@
     )(in_hbm(weight), x)
 
 
-def rows_kernel(npool, place_ref, *refs):
+def rows_kernel(npool, me_ref, core_ref, *refs):
     blocks = refs[:npool]
     weight_ref, out_ref, lhs = refs[npool:]
     steps, rows, _ = blocks[0].shape
     every = npool * rows
     for x, (apart, flip) in enumerate(block_order(npool)):
-        owner = owner_of(place_ref[0], npool, apart, flip)
+        owner = owner_of(me_ref[0], npool, apart, flip)
         for s in range(steps):
             lhs[pl.ds(pl.multiple_of(s * every + owner * rows, rows), rows), :] = blocks[x][s]
-    multiply(lhs, weight_ref, out_ref, 1 - place_ref[1])
+    multiply(lhs, weight_ref, out_ref, 1 - core_ref[0])
 
 
 def multiply(lhs, weight_ref, out_ref, which):
@@ -494,10 +492,10 @@
         at = pl.ds(pl.multiple_of(which * half + i * tile, LANES), tile)
         terms = jnp.dot(lhs[...], weight_ref[:, at], preferred_element_type=F32)
         for s in range(steps):
-            out_ref[s, :, i * tile : (i + 1) * tile] = terms[s * every : (s + 1) * every]
-
-
-def other_projection(place, blocks, weight):
+            out_ref[s, :, i * tile : (i + 1) * tile] = terms[s * every : (s + 1) * every].astype(out_ref.dtype)
+
+
+def other_projection(me, core, blocks, weight):
     npool = len(blocks)
     steps, rows, width = blocks[0].shape
     half = weight.shape[1] // 2
@@ -505,22 +503,22 @@
     return pl.pallas_call(
         functools.partial(rows_kernel, npool),
         out_shape=[
-            jax.ShapeDtypeStruct((steps, npool * rows, half), F32),
+            jax.ShapeDtypeStruct((steps, npool * rows, half), BF16),
             jax.ShapeDtypeStruct((every, width), BF16),
         ],
-        in_specs=[SMEM] + [VMEM] * (npool + 1),
+        in_specs=[SMEM] * 2 + [VMEM] * (npool + 1),
         out_specs=[VMEM] * 2,
         compiler_params=PARAMS,
         cost_estimate=pl.CostEstimate(flops=2 * every * width * half, bytes_accessed=4_000_000, transcendentals=0),
         name="project_other",
-    )(place, *blocks, weight)
-
-
-def own_kernel(place_ref, lhs, weight_ref, out_ref):
-    multiply(lhs, weight_ref, out_ref, place_ref[1])
-
-
-def own_projection(place, lhs, weight, steps):
+    )(me, core, *blocks, weight)
+
+
+def own_kernel(core_ref, lhs, weight_ref, out_ref):
+    multiply(lhs, weight_ref, out_ref, core_ref[0])
+
+
+def own_projection(core, lhs, weight, steps):
     every, width = lhs.shape
     half = weight.shape[1] // 2
     return pl.pallas_call(
@@ -531,7 +529,7 @@
         compiler_params=PARAMS,
         cost_estimate=pl.CostEstimate(flops=2 * every * width * half, bytes_accessed=4_000_000, transcendentals=0),
         name="project_own",
-    )(place, lhs, weight)
+    )(core, lhs, weight)
 
 
 def block_order(npool):
@@ -587,22 +585,22 @@
     cache_pages = cache_kv.shape[0]
     pair = (pages + npool - 1) // npool
     tabs = tables(page_len, head_dim, pages)
-    place = jnp.stack([me, lax.axis_index("tp").astype(I32)])
+    me1, core1 = me[None], lax.axis_index("tp").astype(I32)[None]
     table = page_table.T
 
     asked = asked_queries(table, context_lengths, queries, page_len, heads, head_dim)
     asked_all = gathered(asked, npool)
     arrived, own = rotated_pages(prompt_kv, page_slot, prompt_lengths, tabs, npool, pair, cache_pages)
     local = local_attention(table, context_lengths, cache_fill, asked, new_kv, cache_kv, tabs)
-    parts = arrived_attention(place, own, asked_all, arrived)
+    parts = arrived_attention(me1, own, asked_all, arrived)
     parts = lax.all_to_all(parts, "pool", split_axis=0, concat_axis=0, tiled=True)
-    attention = merged(place, parts, local, queries.shape, heads, pair)
+    attention = merged(me1, parts, local, queries.shape, heads, pair)
     weight, again = fetched(out_weight, attention)
     blocks = gathered(attention, npool, again)
-    other_terms, lhs = other_projection(place, blocks, weight)
+    other_terms, lhs = other_projection(me1, core1, blocks, weight)
     other_terms = swap_halves(other_terms)
-    terms = own_projection(place, lhs, weight, queries.shape[0])
-    return (terms + other_terms).astype(BF16)
+    terms = own_projection(core1, lhs, weight, queries.shape[0])
+    return (terms + other_terms.astype(F32)).astype(BF16)
 
 
 def solution(mesh):

time: 62.1 us -> 64.5 us (1.039)
  local copies, waits for them, and re-layouts: 0.02 us -> 5.46 us
  waiting for transfers between devices: 22 us -> 20.5 us
  Pallas kernels: 16.9 us -> 15.5 us
    unnamed x2 -> x8, local copies, waits for them, and re-layouts: 0.01 us -> 5.44 us
  transfers between devices with their start and end apart: 16 -> 16, of which waited for: 12 -> 10; matrix products, arithmetic and copies ran while one was open for 0% -> 0% of each run, Pallas kernels for 17% -> 16%
where the time goes in v16:
time: 64.5 us; the launch traced here: 64.2 us
  starting transfers between devices  21.8 us (34%)
  waiting for transfers between devices  20.5 us (32%)
  Pallas kernels  15.5 us (24%)
  local copies, waits for them, and re-layouts  5.46 us (8%)
  other arithmetic  0.77 us (1%)
    ppermute x6, waiting for transfers between devices, gathered(): lax.ppermute(x, 'pool', [(i, (i + 2 * by) % npool) for i in range(npool)])  11.1 us
    ppermute x8, starting transfers between devices, gathered(): lax.ppermute(x, 'pool', [(i, i ^ 1) for i in range(npool)])  9.82 us
    ppermute x6, starting transfers between devices, gathered(): lax.ppermute(x, 'pool', [(i, (i + 2 * by) % npool) for i in range(npool)])  8.55 us
    ppermute x8, waiting for transfers between devices, gathered(): lax.ppermute(x, 'pool', [(i, i ^ 1) for i in range(npool)])  6.4 us
    unnamed x8, local copies, waits for them, and re-layouts  5.44 us
    pallas_call x1, Pallas kernels, local_attention(): pl.pallas_call(functools.partial(local_kernel, page_len, heads), out_shap...  4.46 us
    all_to_all x1, starting transfers between devices, shards(): lax.all_to_all(parts, 'pool', split_axis=0, concat_axis=0, tiled=True)  3.38 us
    all_to_all x1, waiting for transfers between devices, shards(): lax.all_to_all(parts, 'pool', split_axis=0, concat_axis=0, tiled=True)  2.99 us
  transfers between devices with their start and end apart: 16, of which 10 were waited for; matrix products, arithmetic and copies ran while one was open for 0% of the time, Pallas kernels for 16%

profile of v16, /device:TPU:0, one launch (start us, length us, event | category | flops | bytes accessed | tf_op | source)
XLA Modules:
  0.0 64.2 jit_solution(7503085158309779871)
XLA Ops:
  1.2 5.1 %collective-permute-start.2 = (bf16[17,32,128]{2,1,0:T(8,128)(2,1)S(1)}, bf16[17,32,128]{2,1,0:T(8,128)(2,1)S(1)}, u32[]{:S(2)}, u32[]{:S(2)}) collective-permute-start(bf16[17,32,128]{2,1,0:T(8,128)(2,1)S(1)} %asked_queries.1.refs_0_.q_ref), channel_id=1, source_target_pairs={{0,12},{2,14},{4,0},{6,2},{8,4},{10,6},{12,8},{14,10},{1,13},{3,15... | collective-permute-start | bytes 417800 | tf_op jit(solution)/shard_map/ppermute | solution.py:560
  7.3 1.5 %collective-permute-start.3 = (bf16[17,32,128]{2,1,0:T(8,128)(2,1)S(1)}, bf16[17,32,128]{2,1,0:T(8,128)(2,1)S(1)}, u32[]{:S(2)}, u32[]{:S(2)}) collective-permute-start(bf16[17,32,128]{2,1,0:T(8,128)(2,1)S(1)} %asked_queries.1.refs_0_.q_ref), channel_id=1, source_target_pairs={{0,2},{2,0},{4,6},{6,4},{8,10},{10,8},{12,14},{14,12},{1,3},{3,1},... | collective-permute-start | bytes 417800 | tf_op jit(solution)/shard_map/ppermute | solution.py:561
  8.9 1.6 %collective-permute-done.2.refs_3_ = bf16[17,32,128]{2,1,0:T(8,128)(2,1)S(1)} collective-permute-done((bf16[17,32,128]{2,1,0:T(8,128)(2,1)S(1)}, bf16[17,32,128]{2,1,0:T(8,128)(2,1)S(1)}, u32[]{:S(2)}, u32[]{:S(2)}) %collective-permute-start.2) | collective-permute-done | bytes 139296 | tf_op jit(solution)/shard_map/ppermute | solution.py:560
  10.4 1.5 %collective-permute-start.6 = (bf16[17,32,128]{2,1,0:T(8,128)(2,1)S(1)}, bf16[17,32,128]{2,1,0:T(8,128)(2,1)S(1)}, u32[]{:S(2)}, u32[]{:S(2)}) collective-permute-start(bf16[17,32,128]{2,1,0:T(8,128)(2,1)S(1)} %collective-permute-done.2.refs_3_), channel_id=1, source_target_pairs={{0,2},{2,0},{4,6},{6,4},{8,10},{10,8},{12,14},{14,12},{1,3},{3,1},... | collective-permute-start | bytes 417800 | tf_op jit(solution)/shard_map/ppermute | solution.py:561
  11.9 6.2 %collective-permute-done.1.refs_2_ = bf16[17,32,128]{2,1,0:T(8,128)(2,1)S(1)} collective-permute-done((bf16[17,32,128]{2,1,0:T(8,128)(2,1)S(1)}, bf16[17,32,128]{2,1,0:T(8,128)(2,1)S(1)}, u32[]{:S(2)}, u32[]{:S(2)}) %collective-permute-start.1) | collective-permute-done | bytes 139296 | tf_op jit(solution)/shard_map/ppermute | solution.py:560
  18.1 1.5 %collective-permute-start.5 = (bf16[17,32,128]{2,1,0:T(8,128)(2,1)S(1)}, bf16[17,32,128]{2,1,0:T(8,128)(2,1)S(1)}, u32[]{:S(2)}, u32[]{:S(2)}) collective-permute-start(bf16[17,32,128]{2,1,0:T(8,128)(2,1)S(1)} %collective-permute-done.1.refs_2_), channel_id=1, source_target_pairs={{0,2},{2,0},{4,6},{6,4},{8,10},{10,8},{12,14},{14,12},{1,3},{3,1},... | collective-permute-start | bytes 417800 | tf_op jit(solution)/shard_map/ppermute | solution.py:561
  20.2 3.0 %rope_pages.1 = (bf16[16,2,2,128,128]{4,3,2,1,0:T(8,128)(2,1)S(1)}, s32[48]{0:T(128)S(1)}) custom-call(s32[16]{0:T(128)} %slot_ref.1, s32[1,4]{1,0:T(1,128)} %len_ref.1, bf16[16,2,2,128,128]{4,3,2,1,0:T(8,128)(2,1)} %pages_ref.1, f32[128,128]{1,0:T(8,128)} %constant.20.clone.ct_ref, f32[128,128]{1,0:T(8,128)} %constant.21.clone.st_ref, ...), custom_call_target="tpu_custom_call" | custom-call | flops 6000000 | bytes 2000000 | tf_op jit(solution)/shard_map/rope_pages/pallas_call | solution.py:86
  23.2 1.4 %collective-permute-done.5.refs_6_ = bf16[17,32,128]{2,1,0:T(8,128)(2,1)S(1)} collective-permute-done((bf16[17,32,128]{2,1,0:T(8,128)(2,1)S(1)}, bf16[17,32,128]{2,1,0:T(8,128)(2,1)S(1)}, u32[]{:S(2)}, u32[]{:S(2)}) %collective-permute-start.5) | collective-permute-done | bytes 139296 | tf_op jit(solution)/shard_map/ppermute | solution.py:561
  24.6 1.5 %collective-permute-done.4.refs_5_ = bf16[17,32,128]{2,1,0:T(8,128)(2,1)S(1)} collective-permute-done((bf16[17,32,128]{2,1,0:T(8,128)(2,1)S(1)}, bf16[17,32,128]{2,1,0:T(8,128)(2,1)S(1)}, u32[]{:S(2)}, u32[]{:S(2)}) %collective-permute-start.4) | collective-permute-done | bytes 139296 | tf_op jit(solution)/shard_map/ppermute | solution.py:561
  26.1 2.1 %arrived_attention.1 = bf16[8,80,128]{2,1,0:T(8,128)(2,1)} custom-call(s32[1]{0:T(128)} %bitcast.1.me_ref, s32[48]{0:T(128)S(1)} %get-tuple-element.13.own_ref, bf16[17,32,128]{2,1,0:T(8,128)(2,1)S(1)} %asked_queries.1.refs_0_.q_ref, bf16[17,32,128]{2,1,0:T(8,128)(2,1)S(1)} %collective-permute-done.refs_1_, ...), custom_call_target="tpu_custom_call" | custom-call | flops 200000000 | bytes 4000000 | tf_op jit(solution)/shard_map/arrived_attention/pallas_call | solution.py:377
  28.2 3.4 %all-to-all-start = ((bf16[8,80,128]{2,1,0:T(8,128)(2,1)}), bf16[8,80,128]{2,1,0:T(8,128)(2,1)S(1)}, u32[]{:S(2)}, u32[]{:S(2)}) async-start(bf16[8,80,128]{2,1,0:T(8,128)(2,1)} %arrived_attention.1), calls=%async_computation | async-start | bytes 327680 | tf_op jit(solution)/shard_map/all_to_all | solution.py:596
  31.6 4.5 %local_attention.1 = (f32[512,128]{1,0:T(8,128)S(1)}, f32[512,128]{1,0:T(8,128)S(1)}) custom-call(s32[3,16]{1,0:T(4,128)} %bitcast.4, s32[16]{0:T(128)} %context_ref.3, s32[48]{0:T(128)} %fill_ref.1, bf16[17,32,128]{2,1,0:T(8,128)(2,1)S(1)} %asked_queries.1.refs_0_.q_ref, bf16[2,16,512]{2,1,0:T(8,128)(2,1)S(1)} %reshape.3.new_ref, ...), custom_call_target="tpu_custom_call" | custom-call | flops 800000000 | bytes 12000000 | tf_op jit(solution)/shard_map/local_attention/pallas_call | solution.py:294
  36.1 3.0 %all-to-all-done.parts_ref = bf16[8,80,128]{2,1,0:T(8,128)(2,1)S(1)} async-done(((bf16[8,80,128]{2,1,0:T(8,128)(2,1)}), bf16[8,80,128]{2,1,0:T(8,128)(2,1)S(1)}, u32[]{:S(2)}, u32[]{:S(2)}) %all-to-all-start) | async-done | bytes 163872 | tf_op jit(solution)/shard_map/all_to_all | solution.py:596
  40.5 2.2 %fetch_weight.1 = (bf16[2048,1024]{1,0:T(8,128)(2,1)S(1)}, bf16[2,16,2048]{2,1,0:T(8,128)(2,1)S(1)}) custom-call(bf16[2048,1024]{1,0:T(8,128)(2,1)} %weight_ref.1, bf16[2,16,2048]{2,1,0:T(8,128)(2,1)S(1)} %merge.1.x_ref.refs_0_), custom_call_target="tpu_custom_call" | custom-call | bytes 8388608 | tf_op jit(solution)/shard_map/fetch_weight/pallas_call | solution.py:464
  42.7 1.9 %copy-done = bf16[2048,1024]{1,0:T(8,128)(2,1)} copy-done((bf16[2048,1024]{1,0:T(8,128)(2,1)}, bf16[2048,1024]{1,0:T(8,128)(2,1)S(1)}, u32[]{:S(2)}) %copy-start) | copy-done | bytes 4194328
  44.6 1.9 %collective-permute-start.9 = (bf16[2,16,2048]{2,1,0:T(8,128)(2,1)S(1)}, bf16[2,16,2048]{2,1,0:T(8,128)(2,1)S(1)}, u32[]{:S(2)}, u32[]{:S(2)}) collective-permute-start(bf16[2,16,2048]{2,1,0:T(8,128)(2,1)S(1)} %get-tuple-element.17), channel_id=1, source_target_pairs={{0,12},{2,14},{4,0},{6,2},{8,4},{10,6},{12,8},{14,10},{1,13},{3,15... | collective-permute-start | bytes 393224 | tf_op jit(solution)/shard_map/ppermute | solution.py:560
  46.7 1.3 %collective-permute-start.10 = (bf16[2,16,2048]{2,1,0:T(8,128)(2,1)S(1)}, bf16[2,16,2048]{2,1,0:T(8,128)(2,1)S(1)}, u32[]{:S(2)}, u32[]{:S(2)}) collective-permute-start(bf16[2,16,2048]{2,1,0:T(8,128)(2,1)S(1)} %merge.1.x_ref.refs_0_), channel_id=1, source_target_pairs={{0,2},{2,0},{4,6},{6,4},{8,10},{10,8},{12,14},{14,12},{1,3},{3,1},... | collective-permute-start | bytes 393224 | tf_op jit(solution)/shard_map/ppermute | solution.py:561
  48.7 2.0 %collective-permute-done.9.refs_3_ = bf16[2,16,2048]{2,1,0:T(8,128)(2,1)S(1)} collective-permute-done((bf16[2,16,2048]{2,1,0:T(8,128)(2,1)S(1)}, bf16[2,16,2048]{2,1,0:T(8,128)(2,1)S(1)}, u32[]{:S(2)}, u32[]{:S(2)}) %collective-permute-start.9) | collective-permute-done | bytes 131104 | tf_op jit(solution)/shard_map/ppermute | solution.py:560
  51.9 1.4 %collective-permute-done.7.refs_1_ = bf16[2,16,2048]{2,1,0:T(8,128)(2,1)S(1)} collective-permute-done((bf16[2,16,2048]{2,1,0:T(8,128)(2,1)S(1)}, bf16[2,16,2048]{2,1,0:T(8,128)(2,1)S(1)}, u32[]{:S(2)}, u32[]{:S(2)}) %collective-permute-start.7) | collective-permute-done | bytes 131104 | tf_op jit(solution)/shard_map/ppermute | solution.py:560
  53.3 1.5 %collective-permute-start.11 = (bf16[2,16,2048]{2,1,0:T(8,128)(2,1)S(1)}, bf16[2,16,2048]{2,1,0:T(8,128)(2,1)S(1)}, u32[]{:S(2)}, u32[]{:S(2)}) collective-permute-start(bf16[2,16,2048]{2,1,0:T(8,128)(2,1)S(1)} %collective-permute-done.7.refs_1_), channel_id=1, source_target_pairs={{0,2},{2,0},{4,6},{6,4},{8,10},{10,8},{12,14},{14,12},{1,3},{3,1},... | collective-permute-start | bytes 393224 | tf_op jit(solution)/shard_map/ppermute | solution.py:561
  55.4 1.4 %collective-permute-done.13.refs_7_ = bf16[2,16,2048]{2,1,0:T(8,128)(2,1)S(1)} collective-permute-done((bf16[2,16,2048]{2,1,0:T(8,128)(2,1)S(1)}, bf16[2,16,2048]{2,1,0:T(8,128)(2,1)S(1)}, u32[]{:S(2)}, u32[]{:S(2)}) %collective-permute-start.13) | collective-permute-done | bytes 131104 | tf_op jit(solution)/shard_map/ppermute | solution.py:561
  56.8 1.5 %collective-permute-done.11.refs_5_ = bf16[2,16,2048]{2,1,0:T(8,128)(2,1)S(1)} collective-permute-done((bf16[2,16,2048]{2,1,0:T(8,128)(2,1)S(1)}, bf16[2,16,2048]{2,1,0:T(8,128)(2,1)S(1)}, u32[]{:S(2)}, u32[]{:S(2)}) %collective-permute-start.11) | collective-permute-done | bytes 131104 | tf_op jit(solution)/shard_map/ppermute | solution.py:561
  58.3 2.2 %copy-done.1 = bf16[2048,1024]{1,0:T(8,128)(2,1)S(1)} copy-done((bf16[2048,1024]{1,0:T(8,128)(2,1)S(1)}, bf16[2048,1024]{1,0:T(8,128)(2,1)}, u32[]{:S(2)}) %copy-start.1) | copy-done | bytes 4194328
  61.3 1.3 %copy-done.2 = bf16[2048,1024]{1,0:T(8,128)(2,1)S(1)} copy-done((bf16[2048,1024]{1,0:T(8,128)(2,1)S(1)}, bf16[2048,1024]{1,0:T(8,128)(2,1)}, u32[]{:S(2)}) %copy-start.2) | copy-done | bytes 4194328
  (26 shorter events, 9.2 us)
Async XLA Ops:
  0.0 31.6 %copy-start.3 = (bf16[2,16,2,2,128]{4,3,2,1,0:T(2,128)(2,1)S(1)}, bf16[2,16,2,2,128]{4,3,2,1,0:T(2,128)(2,1)}, u32[]{:S(2)}) copy-start(bf16[2,16,2,2,128]{4,3,2,1,0:T(2,128)(2,1)} %param.24) | copy-start | bytes 98308
  1.2 9.2 %collective-permute-start.2 = (bf16[17,32,128]{2,1,0:T(8,128)(2,1)S(1)}, bf16[17,32,128]{2,1,0:T(8,128)(2,1)S(1)}, u32[]{:S(2)}, u32[]{:S(2)}) collective-permute-start(bf16[17,32,128]{2,1,0:T(8,128)(2,1)S(1)} %asked_queries.1.refs_0_.q_ref), channel_id=1, source_target_pairs={{0,12},{2,14},{4,0},{6,2},{8,4},{10,6},{12,8},{14,10},{1,13},{3,15... | collective-permute-start | bytes 417800 | tf_op jit(solution)/shard_map/ppermute | solution.py:560
  6.3 11.8 %collective-permute-start.1 = (bf16[17,32,128]{2,1,0:T(8,128)(2,1)S(1)}, bf16[17,32,128]{2,1,0:T(8,128)(2,1)S(1)}, u32[]{:S(2)}, u32[]{:S(2)}) collective-permute-start(bf16[17,32,128]{2,1,0:T(8,128)(2,1)S(1)} %asked_queries.1.refs_0_.q_ref), channel_id=1, source_target_pairs={{0,8},{2,10},{4,12},{6,14},{8,0},{10,2},{12,4},{14,6},{1,9},{3,11}... | collective-permute-start | bytes 417800 | tf_op jit(solution)/shard_map/ppermute | solution.py:560
  6.3 13.3 %collective-permute-start = (bf16[17,32,128]{2,1,0:T(8,128)(2,1)S(1)}, bf16[17,32,128]{2,1,0:T(8,128)(2,1)S(1)}, u32[]{:S(2)}, u32[]{:S(2)}) collective-permute-start(bf16[17,32,128]{2,1,0:T(8,128)(2,1)S(1)} %asked_queries.1.refs_0_.q_ref), channel_id=1, source_target_pairs={{0,4},{2,6},{4,8},{6,10},{8,12},{10,14},{12,0},{14,2},{1,5},{3,7},... | collective-permute-start | bytes 417800 | tf_op jit(solution)/shard_map/ppermute | solution.py:560
  7.3 15.8 %collective-permute-start.3 = (bf16[17,32,128]{2,1,0:T(8,128)(2,1)S(1)}, bf16[17,32,128]{2,1,0:T(8,128)(2,1)S(1)}, u32[]{:S(2)}, u32[]{:S(2)}) collective-permute-start(bf16[17,32,128]{2,1,0:T(8,128)(2,1)S(1)} %asked_queries.1.refs_0_.q_ref), channel_id=1, source_target_pairs={{0,2},{2,0},{4,6},{6,4},{8,10},{10,8},{12,14},{14,12},{1,3},{3,1},... | collective-permute-start | bytes 417800 | tf_op jit(solution)/shard_map/ppermute | solution.py:561
  10.4 12.7 %collective-permute-start.6 = (bf16[17,32,128]{2,1,0:T(8,128)(2,1)S(1)}, bf16[17,32,128]{2,1,0:T(8,128)(2,1)S(1)}, u32[]{:S(2)}, u32[]{:S(2)}) collective-permute-start(bf16[17,32,128]{2,1,0:T(8,128)(2,1)S(1)} %collective-permute-done.2.refs_3_), channel_id=1, source_target_pairs={{0,2},{2,0},{4,6},{6,4},{8,10},{10,8},{12,14},{14,12},{1,3},{3,1},... | collective-permute-start | bytes 417800 | tf_op jit(solution)/shard_map/ppermute | solution.py:561
  18.1 6.4 %collective-permute-start.5 = (bf16[17,32,128]{2,1,0:T(8,128)(2,1)S(1)}, bf16[17,32,128]{2,1,0:T(8,128)(2,1)S(1)}, u32[]{:S(2)}, u32[]{:S(2)}) collective-permute-start(bf16[17,32,128]{2,1,0:T(8,128)(2,1)S(1)} %collective-permute-done.1.refs_2_), channel_id=1, source_target_pairs={{0,2},{2,0},{4,6},{6,4},{8,10},{10,8},{12,14},{14,12},{1,3},{3,1},... | collective-permute-start | bytes 417800 | tf_op jit(solution)/shard_map/ppermute | solution.py:561
  19.7 6.4 %collective-permute-start.4 = (bf16[17,32,128]{2,1,0:T(8,128)(2,1)S(1)}, bf16[17,32,128]{2,1,0:T(8,128)(2,1)S(1)}, u32[]{:S(2)}, u32[]{:S(2)}) collective-permute-start(bf16[17,32,128]{2,1,0:T(8,128)(2,1)S(1)} %collective-permute-done.refs_1_), channel_id=1, source_target_pairs={{0,2},{2,0},{4,6},{6,4},{8,10},{10,8},{12,14},{14,12},{1,3},{3,1},... | collective-permute-start | bytes 417800 | tf_op jit(solution)/shard_map/ppermute | solution.py:561
  28.2 10.9 %all-to-all-start = ((bf16[8,80,128]{2,1,0:T(8,128)(2,1)}), bf16[8,80,128]{2,1,0:T(8,128)(2,1)S(1)}, u32[]{:S(2)}, u32[]{:S(2)}) async-start(bf16[8,80,128]{2,1,0:T(8,128)(2,1)} %arrived_attention.1), calls=%async_computation | async-start | bytes 327680 | tf_op jit(solution)/shard_map/all_to_all | solution.py:596
  40.0 8.0 %collective-permute-start.8 = (bf16[2,16,2048]{2,1,0:T(8,128)(2,1)S(1)}, bf16[2,16,2048]{2,1,0:T(8,128)(2,1)S(1)}, u32[]{:S(2)}, u32[]{:S(2)}) collective-permute-start(bf16[2,16,2048]{2,1,0:T(8,128)(2,1)S(1)} %merge.1.x_ref.refs_0_), channel_id=1, source_target_pairs={{0,8},{2,10},{4,12},{6,14},{8,0},{10,2},{12,4},{14,6},{1,9},{3,11}... | collective-permute-start | bytes 393224 | tf_op jit(solution)/shard_map/ppermute | solution.py:560
  42.7 1.9 %copy-start = (bf16[2048,1024]{1,0:T(8,128)(2,1)}, bf16[2048,1024]{1,0:T(8,128)(2,1)S(1)}, u32[]{:S(2)}) copy-start(bf16[2048,1024]{1,0:T(8,128)(2,1)S(1)} %get-tuple-element.18.refs_8_.weight_ref) | copy-start | bytes 12582916
  44.6 6.0 %collective-permute-start.9 = (bf16[2,16,2048]{2,1,0:T(8,128)(2,1)S(1)}, bf16[2,16,2048]{2,1,0:T(8,128)(2,1)S(1)}, u32[]{:S(2)}, u32[]{:S(2)}) collective-permute-start(bf16[2,16,2048]{2,1,0:T(8,128)(2,1)S(1)} %get-tuple-element.17), channel_id=1, source_target_pairs={{0,12},{2,14},{4,0},{6,2},{8,4},{10,6},{12,8},{14,10},{1,13},{3,15... | collective-permute-start | bytes 393224 | tf_op jit(solution)/shard_map/ppermute | solution.py:560
  46.5 6.8 %collective-permute-start.7 = (bf16[2,16,2048]{2,1,0:T(8,128)(2,1)S(1)}, bf16[2,16,2048]{2,1,0:T(8,128)(2,1)S(1)}, u32[]{:S(2)}, u32[]{:S(2)}) collective-permute-start(bf16[2,16,2048]{2,1,0:T(8,128)(2,1)S(1)} %get-tuple-element.17), channel_id=1, source_target_pairs={{0,4},{2,6},{4,8},{6,10},{8,12},{10,14},{12,0},{14,2},{1,5},{3,7},... | collective-permute-start | bytes 393224 | tf_op jit(solution)/shard_map/ppermute | solution.py:560
  46.7 8.1 %collective-permute-start.10 = (bf16[2,16,2048]{2,1,0:T(8,128)(2,1)S(1)}, bf16[2,16,2048]{2,1,0:T(8,128)(2,1)S(1)}, u32[]{:S(2)}, u32[]{:S(2)}) collective-permute-start(bf16[2,16,2048]{2,1,0:T(8,128)(2,1)S(1)} %merge.1.x_ref.refs_0_), channel_id=1, source_target_pairs={{0,2},{2,0},{4,6},{6,4},{8,10},{10,8},{12,14},{14,12},{1,3},{3,1},... | collective-permute-start | bytes 393224 | tf_op jit(solution)/shard_map/ppermute | solution.py:561
  48.0 7.4 %collective-permute-start.12 = (bf16[2,16,2048]{2,1,0:T(8,128)(2,1)S(1)}, bf16[2,16,2048]{2,1,0:T(8,128)(2,1)S(1)}, u32[]{:S(2)}, u32[]{:S(2)}) collective-permute-start(bf16[2,16,2048]{2,1,0:T(8,128)(2,1)S(1)} %collective-permute-done.8.refs_2_), channel_id=1, source_target_pairs={{0,2},{2,0},{4,6},{6,4},{8,10},{10,8},{12,14},{14,12},{1,3},{3,1},... | collective-permute-start | bytes 393224 | tf_op jit(solution)/shard_map/ppermute | solution.py:561
  50.7 6.1 %collective-permute-start.13 = (bf16[2,16,2048]{2,1,0:T(8,128)(2,1)S(1)}, bf16[2,16,2048]{2,1,0:T(8,128)(2,1)S(1)}, u32[]{:S(2)}, u32[]{:S(2)}) collective-permute-start(bf16[2,16,2048]{2,1,0:T(8,128)(2,1)S(1)} %collective-permute-done.9.refs_3_), channel_id=1, source_target_pairs={{0,2},{2,0},{4,6},{6,4},{8,10},{10,8},{12,14},{14,12},{1,3},{3,1},... | collective-permute-start | bytes 393224 | tf_op jit(solution)/shard_map/ppermute | solution.py:561
  53.3 5.0 %collective-permute-start.11 = (bf16[2,16,2048]{2,1,0:T(8,128)(2,1)S(1)}, bf16[2,16,2048]{2,1,0:T(8,128)(2,1)S(1)}, u32[]{:S(2)}, u32[]{:S(2)}) collective-permute-start(bf16[2,16,2048]{2,1,0:T(8,128)(2,1)S(1)} %collective-permute-done.7.refs_1_), channel_id=1, source_target_pairs={{0,2},{2,0},{4,6},{6,4},{8,10},{10,8},{12,14},{14,12},{1,3},{3,1},... | collective-permute-start | bytes 393224 | tf_op jit(solution)/shard_map/ppermute | solution.py:561
  58.3 2.2 %copy-start.1 = (bf16[2048,1024]{1,0:T(8,128)(2,1)S(1)}, bf16[2048,1024]{1,0:T(8,128)(2,1)}, u32[]{:S(2)}) copy-start(bf16[2048,1024]{1,0:T(8,128)(2,1)} %copy-done) | copy-start | bytes 12582916
  60.5 2.2 %copy-start.2 = (bf16[2048,1024]{1,0:T(8,128)(2,1)S(1)}, bf16[2048,1024]{1,0:T(8,128)(2,1)}, u32[]{:S(2)}) copy-start(bf16[2048,1024]{1,0:T(8,128)(2,1)} %copy-done) | copy-start | bytes 12582916
  61.3 2.1 %collective-permute-start.14 = (bf16[2,128,512]{2,1,0:T(8,128)(2,1)S(1)}, bf16[2,128,512]{2,1,0:T(8,128)(2,1)S(1)}, u32[]{:S(2)}, u32[]{:S(2)}) collective-permute-start(bf16[2,128,512]{2,1,0:T(8,128)(2,1)S(1)} %get-tuple-element.20), channel_id=1, source_target_pairs={{0,1},{1,0},{2,3},{3,2},{4,5},{5,4},{6,7},{7,6},{8,9},{9,8},{10,11... | collective-permute-start | bytes 786440 | tf_op jit(solution)/shard_map/ppermute | solution.py:567

commit v17 on v16

--- a/solution.py
+++ b/solution.py
@@ -386,7 +386,8 @@
     )(me, own, *blocks, arrived)
 
 
-def merge_kernel(pair, heads, me_ref, parts_ref, o_ref, stat_ref, out_ref, mixed, top, total, turned):
+def merge_kernel(pair, heads, me_ref, core_ref, parts_ref, o_ref, stat_ref, out_ref, mixed, top, total, turned):
+    del core_ref
     npool = parts_ref.shape[0]
     steps, rows, width = out_ref.shape
     head_dim = o_ref.shape[1]
@@ -432,18 +433,18 @@
             out_ref[s, :, h * head_dim : (h + 1) * head_dim] = (mixed[at, :] / total[at, :]).astype(BF16)
 
 
-def merged(me, parts, local, shape, heads, pair):
+def merged(me, core, parts, local, shape, heads, pair):
     flat = local[0].shape
     return pl.pallas_call(
         functools.partial(merge_kernel, pair, heads),
         out_shape=jax.ShapeDtypeStruct(shape, BF16),
-        in_specs=[SMEM] + [VMEM] * 3,
+        in_specs=[SMEM] * 2 + [VMEM] * 3,
         out_specs=VMEM,
         scratch_shapes=[pltpu.VMEM(flat, F32)] * 3 + [pltpu.VMEM((LANES, LANES), F32)],
         compiler_params=PARAMS,
         cost_estimate=pl.CostEstimate(flops=2_000_000, bytes_accessed=1_500_000, transcendentals=100_000),
         name="merge",
-    )(me, parts, *local)
+    )(me, core, parts, *local)
 
 
 def fetch_kernel(weight_ref, x_ref, weight_out, x_out, sems):
@@ -594,7 +595,7 @@
     local = local_attention(table, context_lengths, cache_fill, asked, new_kv, cache_kv, tabs)
     parts = arrived_attention(me1, own, asked_all, arrived)
     parts = lax.all_to_all(parts, "pool", split_axis=0, concat_axis=0, tiled=True)
-    attention = merged(me1, parts, local, queries.shape, heads, pair)
+    attention = merged(me1, core1, parts, local, queries.shape, heads, pair)
     weight, again = fetched(out_weight, attention)
     blocks = gathered(attention, npool, again)
     other_terms, lhs = other_projection(me1, core1, blocks, weight)

time: 64.5 us -> 60.6 us (0.940)
  local copies, waits for them, and re-layouts: 5.46 us -> 0.02 us
  waiting for transfers between devices: 20.5 us -> 22.1 us
    unnamed x8 -> x2, local copies, waits for them, and re-layouts: 5.44 us -> 0.01 us
    ppermute x1, waiting for transfers between devices: 0.01 us -> 0.78 us  [swap_halves(): return lax.ppermute(x, 'tp', [(0, 1), (1, 0)])]
    ppermute x8, waiting for transfers between devices: 6.4 us -> 7.04 us  [gathered(): lax.ppermute(x, 'pool', [(i, i ^ 1) for i in range(npool)])]
  transfers between devices with their start and end apart: 16 -> 16, of which waited for: 10 -> 12; matrix products, arithmetic and copies ran while one was open for 0% -> 0% of each run, Pallas kernels for 16% -> 17%
where the time goes in v17:
time: 60.6 us; the launch traced here: 60.3 us
  waiting for transfers between devices  22.1 us (36%)
  starting transfers between devices  21.7 us (36%)
  Pallas kernels  15.6 us (26%)
  other arithmetic  0.77 us (1%)
    ppermute x6, waiting for transfers between devices, gathered(): lax.ppermute(x, 'pool', [(i, (i + 2 * by) % npool) for i in range(npool)])  11.4 us
    ppermute x8, starting transfers between devices, gathered(): lax.ppermute(x, 'pool', [(i, i ^ 1) for i in range(npool)])  9.66 us
    ppermute x6, starting transfers between devices, gathered(): lax.ppermute(x, 'pool', [(i, (i + 2 * by) % npool) for i in range(npool)])  8.6 us
    ppermute x8, waiting for transfers between devices, gathered(): lax.ppermute(x, 'pool', [(i, i ^ 1) for i in range(npool)])  7.04 us
    pallas_call x1, Pallas kernels, local_attention(): pl.pallas_call(functools.partial(local_kernel, page_len, heads), out_shap...  4.54 us
    all_to_all x1, starting transfers between devices, shards(): lax.all_to_all(parts, 'pool', split_axis=0, concat_axis=0, tiled=True)  3.38 us
    pallas_call x1, Pallas kernels, rotated_pages(): pl.pallas_call(functools.partial(rope_kernel, npool, cache_pages, per), g...  2.96 us
    all_to_all x1, waiting for transfers between devices, shards(): lax.all_to_all(parts, 'pool', split_axis=0, concat_axis=0, tiled=True)  2.91 us
  transfers between devices with their start and end apart: 16, of which 12 were waited for; matrix products, arithmetic and copies ran while one was open for 0% of the time, Pallas kernels for 17%

profile of v17, /device:TPU:0, one launch (start us, length us, event | category | flops | bytes accessed | tf_op | source)
XLA Modules:
  0.0 60.3 jit_solution(11855448463583228595)
XLA Ops:
  0.0 1.2 %asked_queries.1.refs_0_.q_ref = bf16[17,32,128]{2,1,0:T(8,128)(2,1)S(1)} custom-call(s32[3,16]{1,0:T(4,128)} %bitcast.3, s32[16]{0:T(128)} %context_ref.3, bf16[2,16,2048]{2,1,0:T(8,128)(2,1)} %q_ref.1), custom_call_target="tpu_custom_call" | custom-call | flops 100000 | bytes 300000 | tf_op jit(solution)/shard_map/asked_queries/pallas_call | solution.py:138
  1.2 5.1 %collective-permute-start.2 = (bf16[17,32,128]{2,1,0:T(8,128)(2,1)S(1)}, bf16[17,32,128]{2,1,0:T(8,128)(2,1)S(1)}, u32[]{:S(2)}, u32[]{:S(2)}) collective-permute-start(bf16[17,32,128]{2,1,0:T(8,128)(2,1)S(1)} %asked_queries.1.refs_0_.q_ref), channel_id=1, source_target_pairs={{0,12},{2,14},{4,0},{6,2},{8,4},{10,6},{12,8},{14,10},{1,13},{3,15... | collective-permute-start | bytes 417800 | tf_op jit(solution)/shard_map/ppermute | solution.py:561
  6.3 1.0 %collective-permute-start = (bf16[17,32,128]{2,1,0:T(8,128)(2,1)S(1)}, bf16[17,32,128]{2,1,0:T(8,128)(2,1)S(1)}, u32[]{:S(2)}, u32[]{:S(2)}) collective-permute-start(bf16[17,32,128]{2,1,0:T(8,128)(2,1)S(1)} %asked_queries.1.refs_0_.q_ref), channel_id=1, source_target_pairs={{0,4},{2,6},{4,8},{6,10},{8,12},{10,14},{12,0},{14,2},{1,5},{3,7},... | collective-permute-start | bytes 417800 | tf_op jit(solution)/shard_map/ppermute | solution.py:561
  7.3 1.5 %collective-permute-start.3 = (bf16[17,32,128]{2,1,0:T(8,128)(2,1)S(1)}, bf16[17,32,128]{2,1,0:T(8,128)(2,1)S(1)}, u32[]{:S(2)}, u32[]{:S(2)}) collective-permute-start(bf16[17,32,128]{2,1,0:T(8,128)(2,1)S(1)} %asked_queries.1.refs_0_.q_ref), channel_id=1, source_target_pairs={{0,2},{2,0},{4,6},{6,4},{8,10},{10,8},{12,14},{14,12},{1,3},{3,1},... | collective-permute-start | bytes 417800 | tf_op jit(solution)/shard_map/ppermute | solution.py:562
  8.9 1.6 %collective-permute-done.2.refs_3_ = bf16[17,32,128]{2,1,0:T(8,128)(2,1)S(1)} collective-permute-done((bf16[17,32,128]{2,1,0:T(8,128)(2,1)S(1)}, bf16[17,32,128]{2,1,0:T(8,128)(2,1)S(1)}, u32[]{:S(2)}, u32[]{:S(2)}) %collective-permute-start.2) | collective-permute-done | bytes 139296 | tf_op jit(solution)/shard_map/ppermute | solution.py:561
  10.4 1.5 %collective-permute-start.6 = (bf16[17,32,128]{2,1,0:T(8,128)(2,1)S(1)}, bf16[17,32,128]{2,1,0:T(8,128)(2,1)S(1)}, u32[]{:S(2)}, u32[]{:S(2)}) collective-permute-start(bf16[17,32,128]{2,1,0:T(8,128)(2,1)S(1)} %collective-permute-done.2.refs_3_), channel_id=1, source_target_pairs={{0,2},{2,0},{4,6},{6,4},{8,10},{10,8},{12,14},{14,12},{1,3},{3,1},... | collective-permute-start | bytes 417800 | tf_op jit(solution)/shard_map/ppermute | solution.py:562
  11.9 6.2 %collective-permute-done.1.refs_2_ = bf16[17,32,128]{2,1,0:T(8,128)(2,1)S(1)} collective-permute-done((bf16[17,32,128]{2,1,0:T(8,128)(2,1)S(1)}, bf16[17,32,128]{2,1,0:T(8,128)(2,1)S(1)}, u32[]{:S(2)}, u32[]{:S(2)}) %collective-permute-start.1) | collective-permute-done | bytes 139296 | tf_op jit(solution)/shard_map/ppermute | solution.py:561
  18.1 1.5 %collective-permute-start.5 = (bf16[17,32,128]{2,1,0:T(8,128)(2,1)S(1)}, bf16[17,32,128]{2,1,0:T(8,128)(2,1)S(1)}, u32[]{:S(2)}, u32[]{:S(2)}) collective-permute-start(bf16[17,32,128]{2,1,0:T(8,128)(2,1)S(1)} %collective-permute-done.1.refs_2_), channel_id=1, source_target_pairs={{0,2},{2,0},{4,6},{6,4},{8,10},{10,8},{12,14},{14,12},{1,3},{3,1},... | collective-permute-start | bytes 417800 | tf_op jit(solution)/shard_map/ppermute | solution.py:562
  20.2 3.0 %rope_pages.1 = (bf16[16,2,2,128,128]{4,3,2,1,0:T(8,128)(2,1)S(1)}, s32[48]{0:T(128)S(1)}) custom-call(s32[16]{0:T(128)} %slot_ref.1, s32[1,4]{1,0:T(1,128)} %len_ref.1, bf16[16,2,2,128,128]{4,3,2,1,0:T(8,128)(2,1)} %pages_ref.1, f32[128,128]{1,0:T(8,128)} %constant.20.clone.ct_ref, f32[128,128]{1,0:T(8,128)} %constant.21.clone.st_ref, ...), custom_call_target="tpu_custom_call" | custom-call | flops 6000000 | bytes 2000000 | tf_op jit(solution)/shard_map/rope_pages/pallas_call | solution.py:86
  23.2 1.4 %collective-permute-done.5.refs_6_ = bf16[17,32,128]{2,1,0:T(8,128)(2,1)S(1)} collective-permute-done((bf16[17,32,128]{2,1,0:T(8,128)(2,1)S(1)}, bf16[17,32,128]{2,1,0:T(8,128)(2,1)S(1)}, u32[]{:S(2)}, u32[]{:S(2)}) %collective-permute-start.5) | collective-permute-done | bytes 139296 | tf_op jit(solution)/shard_map/ppermute | solution.py:562
  24.6 1.5 %collective-permute-done.4.refs_5_ = bf16[17,32,128]{2,1,0:T(8,128)(2,1)S(1)} collective-permute-done((bf16[17,32,128]{2,1,0:T(8,128)(2,1)S(1)}, bf16[17,32,128]{2,1,0:T(8,128)(2,1)S(1)}, u32[]{:S(2)}, u32[]{:S(2)}) %collective-permute-start.4) | collective-permute-done | bytes 139296 | tf_op jit(solution)/shard_map/ppermute | solution.py:562
  26.1 2.1 %arrived_attention.1 = bf16[8,80,128]{2,1,0:T(8,128)(2,1)} custom-call(s32[1]{0:T(128)} %bitcast.1.me_ref, s32[48]{0:T(128)S(1)} %get-tuple-element.13.own_ref, bf16[17,32,128]{2,1,0:T(8,128)(2,1)S(1)} %asked_queries.1.refs_0_.q_ref, bf16[17,32,128]{2,1,0:T(8,128)(2,1)S(1)} %collective-permute-done.refs_1_, ...), custom_call_target="tpu_custom_call" | custom-call | flops 200000000 | bytes 4000000 | tf_op jit(solution)/shard_map/arrived_attention/pallas_call | solution.py:377
  28.2 3.4 %all-to-all-start = ((bf16[8,80,128]{2,1,0:T(8,128)(2,1)}), bf16[8,80,128]{2,1,0:T(8,128)(2,1)S(1)}, u32[]{:S(2)}, u32[]{:S(2)}) async-start(bf16[8,80,128]{2,1,0:T(8,128)(2,1)} %arrived_attention.1), calls=%async_computation | async-start | bytes 327680 | tf_op jit(solution)/shard_map/all_to_all | solution.py:597
  31.6 4.5 %local_attention.1 = (f32[512,128]{1,0:T(8,128)S(1)}, f32[512,128]{1,0:T(8,128)S(1)}) custom-call(s32[3,16]{1,0:T(4,128)} %bitcast.4, s32[16]{0:T(128)} %context_ref.3, s32[48]{0:T(128)} %fill_ref.1, bf16[17,32,128]{2,1,0:T(8,128)(2,1)S(1)} %asked_queries.1.refs_0_.q_ref, bf16[2,16,512]{2,1,0:T(8,128)(2,1)S(1)} %reshape.3.new_ref, ...), custom_call_target="tpu_custom_call" | custom-call | flops 800000000 | bytes 12000000 | tf_op jit(solution)/shard_map/local_attention/pallas_call | solution.py:294
  36.1 2.9 %all-to-all-done.parts_ref = bf16[8,80,128]{2,1,0:T(8,128)(2,1)S(1)} async-done(((bf16[8,80,128]{2,1,0:T(8,128)(2,1)}), bf16[8,80,128]{2,1,0:T(8,128)(2,1)S(1)}, u32[]{:S(2)}, u32[]{:S(2)}) %all-to-all-start) | async-done | bytes 163872 | tf_op jit(solution)/shard_map/all_to_all | solution.py:597
  40.5 2.2 %fetch_weight.1 = (bf16[2048,1024]{1,0:T(8,128)(2,1)S(1)}, bf16[2,16,2048]{2,1,0:T(8,128)(2,1)S(1)}) custom-call(bf16[2048,1024]{1,0:T(8,128)(2,1)} %weight_ref.1, bf16[2,16,2048]{2,1,0:T(8,128)(2,1)S(1)} %merge.1.x_ref.refs_0_), custom_call_target="tpu_custom_call" | custom-call | bytes 8388608 | tf_op jit(solution)/shard_map/fetch_weight/pallas_call | solution.py:465
  42.7 1.9 %collective-permute-start.9 = (bf16[2,16,2048]{2,1,0:T(8,128)(2,1)S(1)}, bf16[2,16,2048]{2,1,0:T(8,128)(2,1)S(1)}, u32[]{:S(2)}, u32[]{:S(2)}) collective-permute-start(bf16[2,16,2048]{2,1,0:T(8,128)(2,1)S(1)} %get-tuple-element.17), channel_id=1, source_target_pairs={{0,12},{2,14},{4,0},{6,2},{8,4},{10,6},{12,8},{14,10},{1,13},{3,15... | collective-permute-start | bytes 393224 | tf_op jit(solution)/shard_map/ppermute | solution.py:561
  44.8 1.3 %collective-permute-start.10 = (bf16[2,16,2048]{2,1,0:T(8,128)(2,1)S(1)}, bf16[2,16,2048]{2,1,0:T(8,128)(2,1)S(1)}, u32[]{:S(2)}, u32[]{:S(2)}) collective-permute-start(bf16[2,16,2048]{2,1,0:T(8,128)(2,1)S(1)} %merge.1.x_ref.refs_0_), channel_id=1, source_target_pairs={{0,2},{2,0},{4,6},{6,4},{8,10},{10,8},{12,14},{14,12},{1,3},{3,1},... | collective-permute-start | bytes 393224 | tf_op jit(solution)/shard_map/ppermute | solution.py:562
  46.1 3.2 %collective-permute-done.8.refs_2_ = bf16[2,16,2048]{2,1,0:T(8,128)(2,1)S(1)} collective-permute-done((bf16[2,16,2048]{2,1,0:T(8,128)(2,1)S(1)}, bf16[2,16,2048]{2,1,0:T(8,128)(2,1)S(1)}, u32[]{:S(2)}, u32[]{:S(2)}) %collective-permute-start.8) | collective-permute-done | bytes 131104 | tf_op jit(solution)/shard_map/ppermute | solution.py:561
  50.1 1.3 %collective-permute-start.13 = (bf16[2,16,2048]{2,1,0:T(8,128)(2,1)S(1)}, bf16[2,16,2048]{2,1,0:T(8,128)(2,1)S(1)}, u32[]{:S(2)}, u32[]{:S(2)}) collective-permute-start(bf16[2,16,2048]{2,1,0:T(8,128)(2,1)S(1)} %collective-permute-done.9.refs_3_), channel_id=1, source_target_pairs={{0,2},{2,0},{4,6},{6,4},{8,10},{10,8},{12,14},{14,12},{1,3},{3,1},... | collective-permute-start | bytes 393224 | tf_op jit(solution)/shard_map/ppermute | solution.py:562
  51.5 1.5 %collective-permute-start.11 = (bf16[2,16,2048]{2,1,0:T(8,128)(2,1)S(1)}, bf16[2,16,2048]{2,1,0:T(8,128)(2,1)S(1)}, u32[]{:S(2)}, u32[]{:S(2)}) collective-permute-start(bf16[2,16,2048]{2,1,0:T(8,128)(2,1)S(1)} %collective-permute-done.7.refs_1_), channel_id=1, source_target_pairs={{0,2},{2,0},{4,6},{6,4},{8,10},{10,8},{12,14},{14,12},{1,3},{3,1},... | collective-permute-start | bytes 393224 | tf_op jit(solution)/shard_map/ppermute | solution.py:562
  53.0 1.3 %collective-permute-done.12.refs_6_ = bf16[2,16,2048]{2,1,0:T(8,128)(2,1)S(1)} collective-permute-done((bf16[2,16,2048]{2,1,0:T(8,128)(2,1)S(1)}, bf16[2,16,2048]{2,1,0:T(8,128)(2,1)S(1)}, u32[]{:S(2)}, u32[]{:S(2)}) %collective-permute-start.12) | collective-permute-done | bytes 131104 | tf_op jit(solution)/shard_map/ppermute | solution.py:562
  54.3 1.4 %collective-permute-done.13.refs_7_ = bf16[2,16,2048]{2,1,0:T(8,128)(2,1)S(1)} collective-permute-done((bf16[2,16,2048]{2,1,0:T(8,128)(2,1)S(1)}, bf16[2,16,2048]{2,1,0:T(8,128)(2,1)S(1)}, u32[]{:S(2)}, u32[]{:S(2)}) %collective-permute-start.13) | collective-permute-done | bytes 131104 | tf_op jit(solution)/shard_map/ppermute | solution.py:562
  55.7 1.4 %collective-permute-done.11.refs_5_ = bf16[2,16,2048]{2,1,0:T(8,128)(2,1)S(1)} collective-permute-done((bf16[2,16,2048]{2,1,0:T(8,128)(2,1)S(1)}, bf16[2,16,2048]{2,1,0:T(8,128)(2,1)S(1)}, u32[]{:S(2)}, u32[]{:S(2)}) %collective-permute-start.11) | collective-permute-done | bytes 131104 | tf_op jit(solution)/shard_map/ppermute | solution.py:562
  (20 shorter events, 6.1 us)
Async XLA Ops:
  0.0 31.6 %copy-start = (bf16[2,16,2,2,128]{4,3,2,1,0:T(2,128)(2,1)S(1)}, bf16[2,16,2,2,128]{4,3,2,1,0:T(2,128)(2,1)}, u32[]{:S(2)}) copy-start(bf16[2,16,2,2,128]{4,3,2,1,0:T(2,128)(2,1)} %param.24) | copy-start | bytes 98308
  1.2 9.2 %collective-permute-start.2 = (bf16[17,32,128]{2,1,0:T(8,128)(2,1)S(1)}, bf16[17,32,128]{2,1,0:T(8,128)(2,1)S(1)}, u32[]{:S(2)}, u32[]{:S(2)}) collective-permute-start(bf16[17,32,128]{2,1,0:T(8,128)(2,1)S(1)} %asked_queries.1.refs_0_.q_ref), channel_id=1, source_target_pairs={{0,12},{2,14},{4,0},{6,2},{8,4},{10,6},{12,8},{14,10},{1,13},{3,15... | collective-permute-start | bytes 417800 | tf_op jit(solution)/shard_map/ppermute | solution.py:561
  6.3 11.8 %collective-permute-start.1 = (bf16[17,32,128]{2,1,0:T(8,128)(2,1)S(1)}, bf16[17,32,128]{2,1,0:T(8,128)(2,1)S(1)}, u32[]{:S(2)}, u32[]{:S(2)}) collective-permute-start(bf16[17,32,128]{2,1,0:T(8,128)(2,1)S(1)} %asked_queries.1.refs_0_.q_ref), channel_id=1, source_target_pairs={{0,8},{2,10},{4,12},{6,14},{8,0},{10,2},{12,4},{14,6},{1,9},{3,11}... | collective-permute-start | bytes 417800 | tf_op jit(solution)/shard_map/ppermute | solution.py:561
  6.3 13.3 %collective-permute-start = (bf16[17,32,128]{2,1,0:T(8,128)(2,1)S(1)}, bf16[17,32,128]{2,1,0:T(8,128)(2,1)S(1)}, u32[]{:S(2)}, u32[]{:S(2)}) collective-permute-start(bf16[17,32,128]{2,1,0:T(8,128)(2,1)S(1)} %asked_queries.1.refs_0_.q_ref), channel_id=1, source_target_pairs={{0,4},{2,6},{4,8},{6,10},{8,12},{10,14},{12,0},{14,2},{1,5},{3,7},... | collective-permute-start | bytes 417800 | tf_op jit(solution)/shard_map/ppermute | solution.py:561
  7.3 15.8 %collective-permute-start.3 = (bf16[17,32,128]{2,1,0:T(8,128)(2,1)S(1)}, bf16[17,32,128]{2,1,0:T(8,128)(2,1)S(1)}, u32[]{:S(2)}, u32[]{:S(2)}) collective-permute-start(bf16[17,32,128]{2,1,0:T(8,128)(2,1)S(1)} %asked_queries.1.refs_0_.q_ref), channel_id=1, source_target_pairs={{0,2},{2,0},{4,6},{6,4},{8,10},{10,8},{12,14},{14,12},{1,3},{3,1},... | collective-permute-start | bytes 417800 | tf_op jit(solution)/shard_map/ppermute | solution.py:562
  10.4 12.7 %collective-permute-start.6 = (bf16[17,32,128]{2,1,0:T(8,128)(2,1)S(1)}, bf16[17,32,128]{2,1,0:T(8,128)(2,1)S(1)}, u32[]{:S(2)}, u32[]{:S(2)}) collective-permute-start(bf16[17,32,128]{2,1,0:T(8,128)(2,1)S(1)} %collective-permute-done.2.refs_3_), channel_id=1, source_target_pairs={{0,2},{2,0},{4,6},{6,4},{8,10},{10,8},{12,14},{14,12},{1,3},{3,1},... | collective-permute-start | bytes 417800 | tf_op jit(solution)/shard_map/ppermute | solution.py:562
  18.1 6.4 %collective-permute-start.5 = (bf16[17,32,128]{2,1,0:T(8,128)(2,1)S(1)}, bf16[17,32,128]{2,1,0:T(8,128)(2,1)S(1)}, u32[]{:S(2)}, u32[]{:S(2)}) collective-permute-start(bf16[17,32,128]{2,1,0:T(8,128)(2,1)S(1)} %collective-permute-done.1.refs_2_), channel_id=1, source_target_pairs={{0,2},{2,0},{4,6},{6,4},{8,10},{10,8},{12,14},{14,12},{1,3},{3,1},... | collective-permute-start | bytes 417800 | tf_op jit(solution)/shard_map/ppermute | solution.py:562
  19.7 6.4 %collective-permute-start.4 = (bf16[17,32,128]{2,1,0:T(8,128)(2,1)S(1)}, bf16[17,32,128]{2,1,0:T(8,128)(2,1)S(1)}, u32[]{:S(2)}, u32[]{:S(2)}) collective-permute-start(bf16[17,32,128]{2,1,0:T(8,128)(2,1)S(1)} %collective-permute-done.refs_1_), channel_id=1, source_target_pairs={{0,2},{2,0},{4,6},{6,4},{8,10},{10,8},{12,14},{14,12},{1,3},{3,1},... | collective-permute-start | bytes 417800 | tf_op jit(solution)/shard_map/ppermute | solution.py:562
  28.2 10.9 %all-to-all-start = ((bf16[8,80,128]{2,1,0:T(8,128)(2,1)}), bf16[8,80,128]{2,1,0:T(8,128)(2,1)S(1)}, u32[]{:S(2)}, u32[]{:S(2)}) async-start(bf16[8,80,128]{2,1,0:T(8,128)(2,1)} %arrived_attention.1), calls=%async_computation | async-start | bytes 327680 | tf_op jit(solution)/shard_map/all_to_all | solution.py:597
  40.0 9.3 %collective-permute-start.8 = (bf16[2,16,2048]{2,1,0:T(8,128)(2,1)S(1)}, bf16[2,16,2048]{2,1,0:T(8,128)(2,1)S(1)}, u32[]{:S(2)}, u32[]{:S(2)}) collective-permute-start(bf16[2,16,2048]{2,1,0:T(8,128)(2,1)S(1)} %merge.1.x_ref.refs_0_), channel_id=1, source_target_pairs={{0,8},{2,10},{4,12},{6,14},{8,0},{10,2},{12,4},{14,6},{1,9},{3,11}... | collective-permute-start | bytes 393224 | tf_op jit(solution)/shard_map/ppermute | solution.py:561
  42.7 7.4 %collective-permute-start.9 = (bf16[2,16,2048]{2,1,0:T(8,128)(2,1)S(1)}, bf16[2,16,2048]{2,1,0:T(8,128)(2,1)S(1)}, u32[]{:S(2)}, u32[]{:S(2)}) collective-permute-start(bf16[2,16,2048]{2,1,0:T(8,128)(2,1)S(1)} %get-tuple-element.17), channel_id=1, source_target_pairs={{0,12},{2,14},{4,0},{6,2},{8,4},{10,6},{12,8},{14,10},{1,13},{3,15... | collective-permute-start | bytes 393224 | tf_op jit(solution)/shard_map/ppermute | solution.py:561
  44.6 6.9 %collective-permute-start.7 = (bf16[2,16,2048]{2,1,0:T(8,128)(2,1)S(1)}, bf16[2,16,2048]{2,1,0:T(8,128)(2,1)S(1)}, u32[]{:S(2)}, u32[]{:S(2)}) collective-permute-start(bf16[2,16,2048]{2,1,0:T(8,128)(2,1)S(1)} %get-tuple-element.17), channel_id=1, source_target_pairs={{0,4},{2,6},{4,8},{6,10},{8,12},{10,14},{12,0},{14,2},{1,5},{3,7},... | collective-permute-start | bytes 393224 | tf_op jit(solution)/shard_map/ppermute | solution.py:561
  44.8 8.2 %collective-permute-start.10 = (bf16[2,16,2048]{2,1,0:T(8,128)(2,1)S(1)}, bf16[2,16,2048]{2,1,0:T(8,128)(2,1)S(1)}, u32[]{:S(2)}, u32[]{:S(2)}) collective-permute-start(bf16[2,16,2048]{2,1,0:T(8,128)(2,1)S(1)} %merge.1.x_ref.refs_0_), channel_id=1, source_target_pairs={{0,2},{2,0},{4,6},{6,4},{8,10},{10,8},{12,14},{14,12},{1,3},{3,1},... | collective-permute-start | bytes 393224 | tf_op jit(solution)/shard_map/ppermute | solution.py:562
  49.3 5.0 %collective-permute-start.12 = (bf16[2,16,2048]{2,1,0:T(8,128)(2,1)S(1)}, bf16[2,16,2048]{2,1,0:T(8,128)(2,1)S(1)}, u32[]{:S(2)}, u32[]{:S(2)}) collective-permute-start(bf16[2,16,2048]{2,1,0:T(8,128)(2,1)S(1)} %collective-permute-done.8.refs_2_), channel_id=1, source_target_pairs={{0,2},{2,0},{4,6},{6,4},{8,10},{10,8},{12,14},{14,12},{1,3},{3,1},... | collective-permute-start | bytes 393224 | tf_op jit(solution)/shard_map/ppermute | solution.py:562
  50.1 5.6 %collective-permute-start.13 = (bf16[2,16,2048]{2,1,0:T(8,128)(2,1)S(1)}, bf16[2,16,2048]{2,1,0:T(8,128)(2,1)S(1)}, u32[]{:S(2)}, u32[]{:S(2)}) collective-permute-start(bf16[2,16,2048]{2,1,0:T(8,128)(2,1)S(1)} %collective-permute-done.9.refs_3_), channel_id=1, source_target_pairs={{0,2},{2,0},{4,6},{6,4},{8,10},{10,8},{12,14},{14,12},{1,3},{3,1},... | collective-permute-start | bytes 393224 | tf_op jit(solution)/shard_map/ppermute | solution.py:562
  51.5 5.6 %collective-permute-start.11 = (bf16[2,16,2048]{2,1,0:T(8,128)(2,1)S(1)}, bf16[2,16,2048]{2,1,0:T(8,128)(2,1)S(1)}, u32[]{:S(2)}, u32[]{:S(2)}) collective-permute-start(bf16[2,16,2048]{2,1,0:T(8,128)(2,1)S(1)} %collective-permute-done.7.refs_1_), channel_id=1, source_target_pairs={{0,2},{2,0},{4,6},{6,4},{8,10},{10,8},{12,14},{14,12},{1,3},{3,1},... | collective-permute-start | bytes 393224 | tf_op jit(solution)/shard_map/ppermute | solution.py:562
  57.9 1.6 %collective-permute-start.14 = (bf16[2,128,512]{2,1,0:T(8,128)(2,1)S(1)}, bf16[2,128,512]{2,1,0:T(8,128)(2,1)S(1)}, u32[]{:S(2)}, u32[]{:S(2)}) collective-permute-start(bf16[2,128,512]{2,1,0:T(8,128)(2,1)S(1)} %get-tuple-element.20), channel_id=1, source_target_pairs={{0,1},{1,0},{2,3},{3,2},{4,5},{5,4},{6,7},{7,6},{8,9},{9,8},{10,11... | collective-permute-start | bytes 786440 | tf_op jit(solution)/shard_map/ppermute | solution.py:568

commit v18 on v17

--- a/solution.py
+++ b/solution.py
@@ -560,7 +560,7 @@
     later = x if later is None else later
     ahead = lambda x, by: lax.ppermute(x, "pool", [(i, (i + 2 * by) % npool) for i in range(npool)])
     across = lambda x: lax.ppermute(x, "pool", [(i, i ^ 1) for i in range(npool)])
-    straight = [x] + [ahead(x if by == half // 2 else later, by) for by in range(1, half)]
+    straight = [x] + [ahead(later if by == 1 else x, by) for by in range(1, half)]
     return straight + [across(y) for y in straight]
 
 

time: 60.6 us -> 61.8 us (1.020)
  waiting for transfers between devices: 22.1 us -> 25 us
  starting transfers between devices: 21.7 us -> 20.2 us
    ppermute x6, waiting for transfers between devices: 11.4 us -> 14 us  [gathered(): lax.ppermute(x, 'pool', [(i, (i + 2 * by) % npool) for i in range(npool)])]
    ppermute x8, starting transfers between devices: 9.66 us -> 8.14 us  [gathered(): lax.ppermute(x, 'pool', [(i, i ^ 1) for i in range(npool)])]
  transfers between devices with their start and end apart: 16 -> 16, of which waited for: 12 -> 10; matrix products, arithmetic and copies ran while one was open for 0% -> 0% of each run, Pallas kernels for 17% -> 17%
where the time goes in v18:
time: 61.8 us; the launch traced here: 61.5 us
  waiting for transfers between devices  25 us (40%)
  starting transfers between devices  20.2 us (33%)
  Pallas kernels  15.4 us (25%)
  other arithmetic  0.77 us (1%)
    ppermute x6, waiting for transfers between devices, gathered(): lax.ppermute(x, 'pool', [(i, (i + 2 * by) % npool) for i in range(npool)])  14 us
    ppermute x6, starting transfers between devices, gathered(): lax.ppermute(x, 'pool', [(i, (i + 2 * by) % npool) for i in range(npool)])  8.59 us
    ppermute x8, starting transfers between devices, gathered(): lax.ppermute(x, 'pool', [(i, i ^ 1) for i in range(npool)])  8.14 us
    ppermute x8, waiting for transfers between devices, gathered(): lax.ppermute(x, 'pool', [(i, i ^ 1) for i in range(npool)])  7.24 us
    pallas_call x1, Pallas kernels, local_attention(): pl.pallas_call(functools.partial(local_kernel, page_len, heads), out_shap...  4.42 us
    all_to_all x1, starting transfers between devices, shards(): lax.all_to_all(parts, 'pool', split_axis=0, concat_axis=0, tiled=True)  3.38 us
    all_to_all x1, waiting for transfers between devices, shards(): lax.all_to_all(parts, 'pool', split_axis=0, concat_axis=0, tiled=True)  3.03 us
    pallas_call x1, Pallas kernels, rotated_pages(): pl.pallas_call(functools.partial(rope_kernel, npool, cache_pages, per), g...  2.96 us
  transfers between devices with their start and end apart: 16, of which 10 were waited for; matrix products, arithmetic and copies ran while one was open for 0% of the time, Pallas kernels for 17%

profile of v18, /device:TPU:0, one launch (start us, length us, event | category | flops | bytes accessed | tf_op | source)
XLA Modules:
  0.0 61.5 jit_solution(10622469307372455260)
XLA Ops:
  0.0 1.2 %asked_queries.1.refs_0_.q_ref = bf16[17,32,128]{2,1,0:T(8,128)(2,1)S(1)} custom-call(s32[3,16]{1,0:T(4,128)} %bitcast.3, s32[16]{0:T(128)} %context_ref.3, bf16[2,16,2048]{2,1,0:T(8,128)(2,1)} %q_ref.1), custom_call_target="tpu_custom_call" | custom-call | flops 100000 | bytes 300000 | tf_op jit(solution)/shard_map/asked_queries/pallas_call | solution.py:138
  1.2 5.1 %collective-permute-start.2 = (bf16[17,32,128]{2,1,0:T(8,128)(2,1)S(1)}, bf16[17,32,128]{2,1,0:T(8,128)(2,1)S(1)}, u32[]{:S(2)}, u32[]{:S(2)}) collective-permute-start(bf16[17,32,128]{2,1,0:T(8,128)(2,1)S(1)} %asked_queries.1.refs_0_.q_ref), channel_id=1, source_target_pairs={{0,12},{2,14},{4,0},{6,2},{8,4},{10,6},{12,8},{14,10},{1,13},{3,15... | collective-permute-start | bytes 417800 | tf_op jit(solution)/shard_map/ppermute | solution.py:561
  6.3 1.0 %collective-permute-start = (bf16[17,32,128]{2,1,0:T(8,128)(2,1)S(1)}, bf16[17,32,128]{2,1,0:T(8,128)(2,1)S(1)}, u32[]{:S(2)}, u32[]{:S(2)}) collective-permute-start(bf16[17,32,128]{2,1,0:T(8,128)(2,1)S(1)} %asked_queries.1.refs_0_.q_ref), channel_id=1, source_target_pairs={{0,4},{2,6},{4,8},{6,10},{8,12},{10,14},{12,0},{14,2},{1,5},{3,7},... | collective-permute-start | bytes 417800 | tf_op jit(solution)/shard_map/ppermute | solution.py:561
  7.3 1.5 %collective-permute-start.3 = (bf16[17,32,128]{2,1,0:T(8,128)(2,1)S(1)}, bf16[17,32,128]{2,1,0:T(8,128)(2,1)S(1)}, u32[]{:S(2)}, u32[]{:S(2)}) collective-permute-start(bf16[17,32,128]{2,1,0:T(8,128)(2,1)S(1)} %asked_queries.1.refs_0_.q_ref), channel_id=1, source_target_pairs={{0,2},{2,0},{4,6},{6,4},{8,10},{10,8},{12,14},{14,12},{1,3},{3,1},... | collective-permute-start | bytes 417800 | tf_op jit(solution)/shard_map/ppermute | solution.py:562
  8.9 1.6 %collective-permute-done.2.refs_3_ = bf16[17,32,128]{2,1,0:T(8,128)(2,1)S(1)} collective-permute-done((bf16[17,32,128]{2,1,0:T(8,128)(2,1)S(1)}, bf16[17,32,128]{2,1,0:T(8,128)(2,1)S(1)}, u32[]{:S(2)}, u32[]{:S(2)}) %collective-permute-start.2) | collective-permute-done | bytes 139296 | tf_op jit(solution)/shard_map/ppermute | solution.py:561
  10.4 1.5 %collective-permute-start.6 = (bf16[17,32,128]{2,1,0:T(8,128)(2,1)S(1)}, bf16[17,32,128]{2,1,0:T(8,128)(2,1)S(1)}, u32[]{:S(2)}, u32[]{:S(2)}) collective-permute-start(bf16[17,32,128]{2,1,0:T(8,128)(2,1)S(1)} %collective-permute-done.2.refs_3_), channel_id=1, source_target_pairs={{0,2},{2,0},{4,6},{6,4},{8,10},{10,8},{12,14},{14,12},{1,3},{3,1},... | collective-permute-start | bytes 417800 | tf_op jit(solution)/shard_map/ppermute | solution.py:562
  11.9 6.2 %collective-permute-done.1.refs_2_ = bf16[17,32,128]{2,1,0:T(8,128)(2,1)S(1)} collective-permute-done((bf16[17,32,128]{2,1,0:T(8,128)(2,1)S(1)}, bf16[17,32,128]{2,1,0:T(8,128)(2,1)S(1)}, u32[]{:S(2)}, u32[]{:S(2)}) %collective-permute-start.1) | collective-permute-done | bytes 139296 | tf_op jit(solution)/shard_map/ppermute | solution.py:561
  18.1 1.5 %collective-permute-start.5 = (bf16[17,32,128]{2,1,0:T(8,128)(2,1)S(1)}, bf16[17,32,128]{2,1,0:T(8,128)(2,1)S(1)}, u32[]{:S(2)}, u32[]{:S(2)}) collective-permute-start(bf16[17,32,128]{2,1,0:T(8,128)(2,1)S(1)} %collective-permute-done.1.refs_2_), channel_id=1, source_target_pairs={{0,2},{2,0},{4,6},{6,4},{8,10},{10,8},{12,14},{14,12},{1,3},{3,1},... | collective-permute-start | bytes 417800 | tf_op jit(solution)/shard_map/ppermute | solution.py:562
  20.2 3.0 %rope_pages.1 = (bf16[16,2,2,128,128]{4,3,2,1,0:T(8,128)(2,1)S(1)}, s32[48]{0:T(128)S(1)}) custom-call(s32[16]{0:T(128)} %slot_ref.1, s32[1,4]{1,0:T(1,128)} %len_ref.1, bf16[16,2,2,128,128]{4,3,2,1,0:T(8,128)(2,1)} %pages_ref.1, f32[128,128]{1,0:T(8,128)} %constant.20.clone.ct_ref, f32[128,128]{1,0:T(8,128)} %constant.21.clone.st_ref, ...), custom_call_target="tpu_custom_call" | custom-call | flops 6000000 | bytes 2000000 | tf_op jit(solution)/shard_map/rope_pages/pallas_call | solution.py:86
  23.2 1.4 %collective-permute-done.5.refs_6_ = bf16[17,32,128]{2,1,0:T(8,128)(2,1)S(1)} collective-permute-done((bf16[17,32,128]{2,1,0:T(8,128)(2,1)S(1)}, bf16[17,32,128]{2,1,0:T(8,128)(2,1)S(1)}, u32[]{:S(2)}, u32[]{:S(2)}) %collective-permute-start.5) | collective-permute-done | bytes 139296 | tf_op jit(solution)/shard_map/ppermute | solution.py:562
  24.6 1.5 %collective-permute-done.4.refs_5_ = bf16[17,32,128]{2,1,0:T(8,128)(2,1)S(1)} collective-permute-done((bf16[17,32,128]{2,1,0:T(8,128)(2,1)S(1)}, bf16[17,32,128]{2,1,0:T(8,128)(2,1)S(1)}, u32[]{:S(2)}, u32[]{:S(2)}) %collective-permute-start.4) | collective-permute-done | bytes 139296 | tf_op jit(solution)/shard_map/ppermute | solution.py:562
  26.1 2.1 %arrived_attention.1 = bf16[8,80,128]{2,1,0:T(8,128)(2,1)} custom-call(s32[1]{0:T(128)} %bitcast.1.me_ref, s32[48]{0:T(128)S(1)} %get-tuple-element.13.own_ref, bf16[17,32,128]{2,1,0:T(8,128)(2,1)S(1)} %asked_queries.1.refs_0_.q_ref, bf16[17,32,128]{2,1,0:T(8,128)(2,1)S(1)} %collective-permute-done.refs_1_, ...), custom_call_target="tpu_custom_call" | custom-call | flops 200000000 | bytes 4000000 | tf_op jit(solution)/shard_map/arrived_attention/pallas_call | solution.py:377
  28.2 3.4 %all-to-all-start = ((bf16[8,80,128]{2,1,0:T(8,128)(2,1)}), bf16[8,80,128]{2,1,0:T(8,128)(2,1)S(1)}, u32[]{:S(2)}, u32[]{:S(2)}) async-start(bf16[8,80,128]{2,1,0:T(8,128)(2,1)} %arrived_attention.1), calls=%async_computation | async-start | bytes 327680 | tf_op jit(solution)/shard_map/all_to_all | solution.py:597
  31.6 4.4 %local_attention.1 = (f32[512,128]{1,0:T(8,128)S(1)}, f32[512,128]{1,0:T(8,128)S(1)}) custom-call(s32[3,16]{1,0:T(4,128)} %bitcast.4, s32[16]{0:T(128)} %context_ref.3, s32[48]{0:T(128)} %fill_ref.1, bf16[17,32,128]{2,1,0:T(8,128)(2,1)S(1)} %asked_queries.1.refs_0_.q_ref, bf16[2,16,512]{2,1,0:T(8,128)(2,1)S(1)} %reshape.3.new_ref, ...), custom_call_target="tpu_custom_call" | custom-call | flops 800000000 | bytes 12000000 | tf_op jit(solution)/shard_map/local_attention/pallas_call | solution.py:294
  36.0 3.0 %all-to-all-done.parts_ref = bf16[8,80,128]{2,1,0:T(8,128)(2,1)S(1)} async-done(((bf16[8,80,128]{2,1,0:T(8,128)(2,1)}), bf16[8,80,128]{2,1,0:T(8,128)(2,1)S(1)}, u32[]{:S(2)}, u32[]{:S(2)}) %all-to-all-start) | async-done | bytes 163872 | tf_op jit(solution)/shard_map/all_to_all | solution.py:597
  39.0 1.0 %merge.1.x_ref.refs_0_ = bf16[2,16,2048]{2,1,0:T(8,128)(2,1)S(1)} custom-call(s32[1]{0:T(128)} %bitcast.1.me_ref, s32[1]{0:T(128)} %bitcast.core_ref, bf16[8,80,128]{2,1,0:T(8,128)(2,1)S(1)} %all-to-all-done.parts_ref, f32[512,128]{1,0:T(8,128)S(1)} %get-tuple-element.15.o_ref, f32[512,128]{1,0:T(8,128)S(1)} %get-tuple-element.16.stat_ref), custom_call_target="tpu_custom_call" | custom-call | flops 2000000 | bytes 1500000 | tf_op jit(solution)/shard_map/merge/pallas_call | solution.py:438
  41.4 2.2 %fetch_weight.1 = (bf16[2048,1024]{1,0:T(8,128)(2,1)S(1)}, bf16[2,16,2048]{2,1,0:T(8,128)(2,1)S(1)}) custom-call(bf16[2048,1024]{1,0:T(8,128)(2,1)} %weight_ref.1, bf16[2,16,2048]{2,1,0:T(8,128)(2,1)S(1)} %merge.1.x_ref.refs_0_), custom_call_target="tpu_custom_call" | custom-call | bytes 8388608 | tf_op jit(solution)/shard_map/fetch_weight/pallas_call | solution.py:465
  43.7 1.1 %collective-permute-start.7 = (bf16[2,16,2048]{2,1,0:T(8,128)(2,1)S(1)}, bf16[2,16,2048]{2,1,0:T(8,128)(2,1)S(1)}, u32[]{:S(2)}, u32[]{:S(2)}) collective-permute-start(bf16[2,16,2048]{2,1,0:T(8,128)(2,1)S(1)} %get-tuple-element.17), channel_id=1, source_target_pairs={{0,4},{2,6},{4,8},{6,10},{8,12},{10,14},{12,0},{14,2},{1,5},{3,7},... | collective-permute-start | bytes 393224 | tf_op jit(solution)/shard_map/ppermute | solution.py:561
  44.8 1.0 %collective-permute-start.10 = (bf16[2,16,2048]{2,1,0:T(8,128)(2,1)S(1)}, bf16[2,16,2048]{2,1,0:T(8,128)(2,1)S(1)}, u32[]{:S(2)}, u32[]{:S(2)}) collective-permute-start(bf16[2,16,2048]{2,1,0:T(8,128)(2,1)S(1)} %merge.1.x_ref.refs_0_), channel_id=1, source_target_pairs={{0,2},{2,0},{4,6},{6,4},{8,10},{10,8},{12,14},{14,12},{1,3},{3,1},... | collective-permute-start | bytes 393224 | tf_op jit(solution)/shard_map/ppermute | solution.py:562
  45.8 1.2 %collective-permute-done.9.refs_3_ = bf16[2,16,2048]{2,1,0:T(8,128)(2,1)S(1)} collective-permute-done((bf16[2,16,2048]{2,1,0:T(8,128)(2,1)S(1)}, bf16[2,16,2048]{2,1,0:T(8,128)(2,1)S(1)}, u32[]{:S(2)}, u32[]{:S(2)}) %collective-permute-start.9) | collective-permute-done | bytes 131104 | tf_op jit(solution)/shard_map/ppermute | solution.py:561
  47.0 5.0 %collective-permute-done.8.refs_2_ = bf16[2,16,2048]{2,1,0:T(8,128)(2,1)S(1)} collective-permute-done((bf16[2,16,2048]{2,1,0:T(8,128)(2,1)S(1)}, bf16[2,16,2048]{2,1,0:T(8,128)(2,1)S(1)}, u32[]{:S(2)}, u32[]{:S(2)}) %collective-permute-start.8) | collective-permute-done | bytes 131104 | tf_op jit(solution)/shard_map/ppermute | solution.py:561
  52.9 1.1 %collective-permute-start.11 = (bf16[2,16,2048]{2,1,0:T(8,128)(2,1)S(1)}, bf16[2,16,2048]{2,1,0:T(8,128)(2,1)S(1)}, u32[]{:S(2)}, u32[]{:S(2)}) collective-permute-start(bf16[2,16,2048]{2,1,0:T(8,128)(2,1)S(1)} %collective-permute-done.7.refs_1_), channel_id=1, source_target_pairs={{0,2},{2,0},{4,6},{6,4},{8,10},{10,8},{12,14},{14,12},{1,3},{3,1},... | collective-permute-start | bytes 393224 | tf_op jit(solution)/shard_map/ppermute | solution.py:562
  54.0 2.9 %collective-permute-done.12.refs_6_ = bf16[2,16,2048]{2,1,0:T(8,128)(2,1)S(1)} collective-permute-done((bf16[2,16,2048]{2,1,0:T(8,128)(2,1)S(1)}, bf16[2,16,2048]{2,1,0:T(8,128)(2,1)S(1)}, u32[]{:S(2)}, u32[]{:S(2)}) %collective-permute-start.12) | collective-permute-done | bytes 131104 | tf_op jit(solution)/shard_map/ppermute | solution.py:562
  57.0 1.4 %collective-permute-done.11.refs_5_ = bf16[2,16,2048]{2,1,0:T(8,128)(2,1)S(1)} collective-permute-done((bf16[2,16,2048]{2,1,0:T(8,128)(2,1)S(1)}, bf16[2,16,2048]{2,1,0:T(8,128)(2,1)S(1)}, u32[]{:S(2)}, u32[]{:S(2)}) %collective-permute-start.11) | collective-permute-done | bytes 131104 | tf_op jit(solution)/shard_map/ppermute | solution.py:562
  (20 shorter events, 6.0 us)
Async XLA Ops:
  0.0 31.6 %copy-start = (bf16[2,16,2,2,128]{4,3,2,1,0:T(2,128)(2,1)S(1)}, bf16[2,16,2,2,128]{4,3,2,1,0:T(2,128)(2,1)}, u32[]{:S(2)}) copy-start(bf16[2,16,2,2,128]{4,3,2,1,0:T(2,128)(2,1)} %param.24) | copy-start | bytes 98308
  1.2 9.2 %collective-permute-start.2 = (bf16[17,32,128]{2,1,0:T(8,128)(2,1)S(1)}, bf16[17,32,128]{2,1,0:T(8,128)(2,1)S(1)}, u32[]{:S(2)}, u32[]{:S(2)}) collective-permute-start(bf16[17,32,128]{2,1,0:T(8,128)(2,1)S(1)} %asked_queries.1.refs_0_.q_ref), channel_id=1, source_target_pairs={{0,12},{2,14},{4,0},{6,2},{8,4},{10,6},{12,8},{14,10},{1,13},{3,15... | collective-permute-start | bytes 417800 | tf_op jit(solution)/shard_map/ppermute | solution.py:561
  6.3 11.8 %collective-permute-start.1 = (bf16[17,32,128]{2,1,0:T(8,128)(2,1)S(1)}, bf16[17,32,128]{2,1,0:T(8,128)(2,1)S(1)}, u32[]{:S(2)}, u32[]{:S(2)}) collective-permute-start(bf16[17,32,128]{2,1,0:T(8,128)(2,1)S(1)} %asked_queries.1.refs_0_.q_ref), channel_id=1, source_target_pairs={{0,8},{2,10},{4,12},{6,14},{8,0},{10,2},{12,4},{14,6},{1,9},{3,11}... | collective-permute-start | bytes 417800 | tf_op jit(solution)/shard_map/ppermute | solution.py:561
  6.3 13.3 %collective-permute-start = (bf16[17,32,128]{2,1,0:T(8,128)(2,1)S(1)}, bf16[17,32,128]{2,1,0:T(8,128)(2,1)S(1)}, u32[]{:S(2)}, u32[]{:S(2)}) collective-permute-start(bf16[17,32,128]{2,1,0:T(8,128)(2,1)S(1)} %asked_queries.1.refs_0_.q_ref), channel_id=1, source_target_pairs={{0,4},{2,6},{4,8},{6,10},{8,12},{10,14},{12,0},{14,2},{1,5},{3,7},... | collective-permute-start | bytes 417800 | tf_op jit(solution)/shard_map/ppermute | solution.py:561
  7.3 15.8 %collective-permute-start.3 = (bf16[17,32,128]{2,1,0:T(8,128)(2,1)S(1)}, bf16[17,32,128]{2,1,0:T(8,128)(2,1)S(1)}, u32[]{:S(2)}, u32[]{:S(2)}) collective-permute-start(bf16[17,32,128]{2,1,0:T(8,128)(2,1)S(1)} %asked_queries.1.refs_0_.q_ref), channel_id=1, source_target_pairs={{0,2},{2,0},{4,6},{6,4},{8,10},{10,8},{12,14},{14,12},{1,3},{3,1},... | collective-permute-start | bytes 417800 | tf_op jit(solution)/shard_map/ppermute | solution.py:562
  10.4 12.7 %collective-permute-start.6 = (bf16[17,32,128]{2,1,0:T(8,128)(2,1)S(1)}, bf16[17,32,128]{2,1,0:T(8,128)(2,1)S(1)}, u32[]{:S(2)}, u32[]{:S(2)}) collective-permute-start(bf16[17,32,128]{2,1,0:T(8,128)(2,1)S(1)} %collective-permute-done.2.refs_3_), channel_id=1, source_target_pairs={{0,2},{2,0},{4,6},{6,4},{8,10},{10,8},{12,14},{14,12},{1,3},{3,1},... | collective-permute-start | bytes 417800 | tf_op jit(solution)/shard_map/ppermute | solution.py:562
  18.1 6.4 %collective-permute-start.5 = (bf16[17,32,128]{2,1,0:T(8,128)(2,1)S(1)}, bf16[17,32,128]{2,1,0:T(8,128)(2,1)S(1)}, u32[]{:S(2)}, u32[]{:S(2)}) collective-permute-start(bf16[17,32,128]{2,1,0:T(8,128)(2,1)S(1)} %collective-permute-done.1.refs_2_), channel_id=1, source_target_pairs={{0,2},{2,0},{4,6},{6,4},{8,10},{10,8},{12,14},{14,12},{1,3},{3,1},... | collective-permute-start | bytes 417800 | tf_op jit(solution)/shard_map/ppermute | solution.py:562
  19.7 6.4 %collective-permute-start.4 = (bf16[17,32,128]{2,1,0:T(8,128)(2,1)S(1)}, bf16[17,32,128]{2,1,0:T(8,128)(2,1)S(1)}, u32[]{:S(2)}, u32[]{:S(2)}) collective-permute-start(bf16[17,32,128]{2,1,0:T(8,128)(2,1)S(1)} %collective-permute-done.refs_1_), channel_id=1, source_target_pairs={{0,2},{2,0},{4,6},{6,4},{8,10},{10,8},{12,14},{14,12},{1,3},{3,1},... | collective-permute-start | bytes 417800 | tf_op jit(solution)/shard_map/ppermute | solution.py:562
  28.2 10.9 %all-to-all-start = ((bf16[8,80,128]{2,1,0:T(8,128)(2,1)}), bf16[8,80,128]{2,1,0:T(8,128)(2,1)S(1)}, u32[]{:S(2)}, u32[]{:S(2)}) async-start(bf16[8,80,128]{2,1,0:T(8,128)(2,1)} %arrived_attention.1), calls=%async_computation | async-start | bytes 327680 | tf_op jit(solution)/shard_map/all_to_all | solution.py:597
  40.0 7.0 %collective-permute-start.9 = (bf16[2,16,2048]{2,1,0:T(8,128)(2,1)S(1)}, bf16[2,16,2048]{2,1,0:T(8,128)(2,1)S(1)}, u32[]{:S(2)}, u32[]{:S(2)}) collective-permute-start(bf16[2,16,2048]{2,1,0:T(8,128)(2,1)S(1)} %merge.1.x_ref.refs_0_), channel_id=1, source_target_pairs={{0,12},{2,14},{4,0},{6,2},{8,4},{10,6},{12,8},{14,10},{1,13},{3,15... | collective-permute-start | bytes 393224 | tf_op jit(solution)/shard_map/ppermute | solution.py:561
  40.9 11.1 %collective-permute-start.8 = (bf16[2,16,2048]{2,1,0:T(8,128)(2,1)S(1)}, bf16[2,16,2048]{2,1,0:T(8,128)(2,1)S(1)}, u32[]{:S(2)}, u32[]{:S(2)}) collective-permute-start(bf16[2,16,2048]{2,1,0:T(8,128)(2,1)S(1)} %merge.1.x_ref.refs_0_), channel_id=1, source_target_pairs={{0,8},{2,10},{4,12},{6,14},{8,0},{10,2},{12,4},{14,6},{1,9},{3,11}... | collective-permute-start | bytes 393224 | tf_op jit(solution)/shard_map/ppermute | solution.py:561
  43.7 9.2 %collective-permute-start.7 = (bf16[2,16,2048]{2,1,0:T(8,128)(2,1)S(1)}, bf16[2,16,2048]{2,1,0:T(8,128)(2,1)S(1)}, u32[]{:S(2)}, u32[]{:S(2)}) collective-permute-start(bf16[2,16,2048]{2,1,0:T(8,128)(2,1)S(1)} %get-tuple-element.17), channel_id=1, source_target_pairs={{0,4},{2,6},{4,8},{6,10},{8,12},{10,14},{12,0},{14,2},{1,5},{3,7},... | collective-permute-start | bytes 393224 | tf_op jit(solution)/shard_map/ppermute | solution.py:561
  44.8 9.3 %collective-permute-start.10 = (bf16[2,16,2048]{2,1,0:T(8,128)(2,1)S(1)}, bf16[2,16,2048]{2,1,0:T(8,128)(2,1)S(1)}, u32[]{:S(2)}, u32[]{:S(2)}) collective-permute-start(bf16[2,16,2048]{2,1,0:T(8,128)(2,1)S(1)} %merge.1.x_ref.refs_0_), channel_id=1, source_target_pairs={{0,2},{2,0},{4,6},{6,4},{8,10},{10,8},{12,14},{14,12},{1,3},{3,1},... | collective-permute-start | bytes 393224 | tf_op jit(solution)/shard_map/ppermute | solution.py:562
  47.0 7.0 %collective-permute-start.13 = (bf16[2,16,2048]{2,1,0:T(8,128)(2,1)S(1)}, bf16[2,16,2048]{2,1,0:T(8,128)(2,1)S(1)}, u32[]{:S(2)}, u32[]{:S(2)}) collective-permute-start(bf16[2,16,2048]{2,1,0:T(8,128)(2,1)S(1)} %collective-permute-done.9.refs_3_), channel_id=1, source_target_pairs={{0,2},{2,0},{4,6},{6,4},{8,10},{10,8},{12,14},{14,12},{1,3},{3,1},... | collective-permute-start | bytes 393224 | tf_op jit(solution)/shard_map/ppermute | solution.py:562
  52.0 5.0 %collective-permute-start.12 = (bf16[2,16,2048]{2,1,0:T(8,128)(2,1)S(1)}, bf16[2,16,2048]{2,1,0:T(8,128)(2,1)S(1)}, u32[]{:S(2)}, u32[]{:S(2)}) collective-permute-start(bf16[2,16,2048]{2,1,0:T(8,128)(2,1)S(1)} %collective-permute-done.8.refs_2_), channel_id=1, source_target_pairs={{0,2},{2,0},{4,6},{6,4},{8,10},{10,8},{12,14},{14,12},{1,3},{3,1},... | collective-permute-start | bytes 393224 | tf_op jit(solution)/shard_map/ppermute | solution.py:562
  52.9 5.4 %collective-permute-start.11 = (bf16[2,16,2048]{2,1,0:T(8,128)(2,1)S(1)}, bf16[2,16,2048]{2,1,0:T(8,128)(2,1)S(1)}, u32[]{:S(2)}, u32[]{:S(2)}) collective-permute-start(bf16[2,16,2048]{2,1,0:T(8,128)(2,1)S(1)} %collective-permute-done.7.refs_1_), channel_id=1, source_target_pairs={{0,2},{2,0},{4,6},{6,4},{8,10},{10,8},{12,14},{14,12},{1,3},{3,1},... | collective-permute-start | bytes 393224 | tf_op jit(solution)/shard_map/ppermute | solution.py:562
  59.2 1.6 %collective-permute-start.14 = (bf16[2,128,512]{2,1,0:T(8,128)(2,1)S(1)}, bf16[2,128,512]{2,1,0:T(8,128)(2,1)S(1)}, u32[]{:S(2)}, u32[]{:S(2)}) collective-permute-start(bf16[2,128,512]{2,1,0:T(8,128)(2,1)S(1)} %get-tuple-element.20), channel_id=1, source_target_pairs={{0,1},{1,0},{2,3},{3,2},{4,5},{5,4},{6,7},{7,6},{8,9},{9,8},{10,11... | collective-permute-start | bytes 786440 | tf_op jit(solution)/shard_map/ppermute | solution.py:568

commit v19 on v18

--- a/solution.py
+++ b/solution.py
@@ -447,13 +447,13 @@
     )(me, core, parts, *local)
 
 
-def fetch_kernel(weight_ref, x_ref, weight_out, x_out, sems):
+def fetch_kernel(first, weight_ref, x_ref, weight_out, x_out, sems):
     chunks = sems.shape[0] - 1
-    rows = weight_ref.shape[0] // chunks
+    rows = weight_out.shape[0] // chunks
     copies = []
     for i in range(chunks):
         at = pl.ds(i * rows, rows)
-        copies.append(pltpu.make_async_copy(weight_ref.at[at], weight_out.at[at], sems.at[i]))
+        copies.append(pltpu.make_async_copy(weight_ref.at[pl.ds(first + i * rows, rows)], weight_out.at[at], sems.at[i]))
     copies.append(pltpu.make_async_copy(x_ref, x_out, sems.at[chunks]))
     for copy in copies:
         copy.start()
@@ -461,37 +461,39 @@
         copy.wait()
 
 
-def fetched(weight, x):
-    return pl.pallas_call(
-        fetch_kernel,
-        out_shape=[pltpu.VMEM(weight.shape, weight.dtype), pltpu.VMEM(x.shape, x.dtype)],
+def fetched(weight, x, part):
+    return pl.pallas_call(
+        functools.partial(fetch_kernel, part * weight.shape[0] // 2),
+        out_shape=[pltpu.VMEM((weight.shape[0] // 2, weight.shape[1]), weight.dtype), pltpu.VMEM(x.shape, x.dtype)],
         in_specs=[ANY, ANY],
         out_specs=[ANY, ANY],
         scratch_shapes=[pltpu.SemaphoreType.DMA((9,))],
         compiler_params=PARAMS,
-        cost_estimate=pl.CostEstimate(flops=0, bytes_accessed=2 * weight.size * 2, transcendentals=0),
+        cost_estimate=pl.CostEstimate(flops=0, bytes_accessed=weight.size * 2, transcendentals=0),
         name="fetch_weight",
     )(in_hbm(weight), x)
 
 
 def rows_kernel(npool, me_ref, core_ref, *refs):
     blocks = refs[:npool]
-    weight_ref, out_ref, lhs = refs[npool:]
+    *weights, out_ref, lhs = refs[npool:]
     steps, rows, _ = blocks[0].shape
     every = npool * rows
     for x, (apart, flip) in enumerate(block_order(npool)):
         owner = owner_of(me_ref[0], npool, apart, flip)
         for s in range(steps):
             lhs[pl.ds(pl.multiple_of(s * every + owner * rows, rows), rows), :] = blocks[x][s]
-    multiply(lhs, weight_ref, out_ref, 1 - core_ref[0])
-
-
-def multiply(lhs, weight_ref, out_ref, which):
+    multiply(lhs, weights, out_ref, 1 - core_ref[0])
+
+
+def multiply(lhs, weights, out_ref, which):
     steps, every, half = out_ref.shape
     tile = min(half, 256)
     for i in range(half // tile):
         at = pl.ds(pl.multiple_of(which * half + i * tile, LANES), tile)
-        terms = jnp.dot(lhs[...], weight_ref[:, at], preferred_element_type=F32)
+        depth = weights[0].shape[0]
+        terms = jnp.dot(lhs[:, :depth], weights[0][:, at], preferred_element_type=F32)
+        terms = terms + jnp.dot(lhs[:, depth:], weights[1][:, at], preferred_element_type=F32)
         for s in range(steps):
             out_ref[s, :, i * tile : (i + 1) * tile] = terms[s * every : (s + 1) * every].astype(out_ref.dtype)
 
@@ -499,7 +501,7 @@
 def other_projection(me, core, blocks, weight):
     npool = len(blocks)
     steps, rows, width = blocks[0].shape
-    half = weight.shape[1] // 2
+    half = weight[0].shape[1] // 2
     every = steps * npool * rows
     return pl.pallas_call(
         functools.partial(rows_kernel, npool),
@@ -507,30 +509,30 @@
             jax.ShapeDtypeStruct((steps, npool * rows, half), BF16),
             jax.ShapeDtypeStruct((every, width), BF16),
         ],
-        in_specs=[SMEM] * 2 + [VMEM] * (npool + 1),
+        in_specs=[SMEM] * 2 + [VMEM] * (npool + 2),
         out_specs=[VMEM] * 2,
         compiler_params=PARAMS,
         cost_estimate=pl.CostEstimate(flops=2 * every * width * half, bytes_accessed=4_000_000, transcendentals=0),
         name="project_other",
-    )(me, core, *blocks, weight)
-
-
-def own_kernel(core_ref, lhs, weight_ref, out_ref):
-    multiply(lhs, weight_ref, out_ref, core_ref[0])
+    )(me, core, *blocks, *weight)
+
+
+def own_kernel(core_ref, lhs, low, high, out_ref):
+    multiply(lhs, (low, high), out_ref, core_ref[0])
 
 
 def own_projection(core, lhs, weight, steps):
     every, width = lhs.shape
-    half = weight.shape[1] // 2
+    half = weight[0].shape[1] // 2
     return pl.pallas_call(
         own_kernel,
         out_shape=jax.ShapeDtypeStruct((steps, every // steps, half), F32),
-        in_specs=[SMEM] + [VMEM] * 2,
+        in_specs=[SMEM] + [VMEM] * 3,
         out_specs=VMEM,
         compiler_params=PARAMS,
         cost_estimate=pl.CostEstimate(flops=2 * every * width * half, bytes_accessed=4_000_000, transcendentals=0),
         name="project_own",
-    )(core, lhs, weight)
+    )(core, lhs, *weight)
 
 
 def block_order(npool):
@@ -555,12 +557,13 @@
     return pltpu.with_memory_space_constraint(x, pltpu.HBM)
 
 
-def gathered(x, npool, later=None):
+def gathered(x, npool, later=None, last=None):
     half = npool // 2
     later = x if later is None else later
+    last = later if last is None else last
     ahead = lambda x, by: lax.ppermute(x, "pool", [(i, (i + 2 * by) % npool) for i in range(npool)])
     across = lambda x: lax.ppermute(x, "pool", [(i, i ^ 1) for i in range(npool)])
-    straight = [x] + [ahead(later if by == 1 else x, by) for by in range(1, half)]
+    straight = [x] + [ahead(x if by == half // 2 else last if by == 1 else later, by) for by in range(1, half)]
     return straight + [across(y) for y in straight]
 
 
@@ -596,8 +599,10 @@
     parts = arrived_attention(me1, own, asked_all, arrived)
     parts = lax.all_to_all(parts, "pool", split_axis=0, concat_axis=0, tiled=True)
     attention = merged(me1, core1, parts, local, queries.shape, heads, pair)
-    weight, again = fetched(out_weight, attention)
-    blocks = gathered(attention, npool, again)
+    low, again = fetched(out_weight, attention, 0)
+    high, last = fetched(out_weight, again, 1)
+    weight = (low, high)
+    blocks = gathered(attention, npool, again, last)
     other_terms, lhs = other_projection(me1, core1, blocks, weight)
     other_terms = swap_halves(other_terms)
     terms = own_projection(core1, lhs, weight, queries.shape[0])

time: 61.8 us -> 60.9 us (0.985)
  waiting for transfers between devices: 25 us -> 21.2 us
  starting transfers between devices: 20.2 us -> 21.8 us
  Pallas kernels: 15.4 us -> 16.6 us
    ppermute x6, waiting for transfers between devices: 14 us -> 11.2 us  [gathered(): lax.ppermute(x, 'pool', [(i, (i + 2 * by) % npool) for i in range(npool)])]
    ppermute x8, starting transfers between devices: 8.14 us -> 9.73 us  [gathered(): lax.ppermute(x, 'pool', [(i, i ^ 1) for i in range(npool)])]
    pallas_call x1 -> x2, Pallas kernels: 2.22 us -> 3.16 us  [fetched(): pl.pallas_call(functools.partial(fetch_kernel, part * weight.shape[0] //...]
    ppermute x8, waiting for transfers between devices: 7.24 us -> 6.39 us  [gathered(): lax.ppermute(x, 'pool', [(i, i ^ 1) for i in range(npool)])]
  transfers between devices with their start and end apart: 16 -> 16, of which waited for: 10 -> 12; matrix products, arithmetic and copies ran while one was open for 0% -> 0% of each run, Pallas kernels for 17% -> 19%
where the time goes in v19:
time: 60.9 us; the launch traced here: 60.5 us
  starting transfers between devices  21.8 us (36%)
  waiting for transfers between devices  21.2 us (35%)
  Pallas kernels  16.6 us (27%)
  other arithmetic  0.78 us (1%)
    ppermute x6, waiting for transfers between devices, gathered(): lax.ppermute(x, 'pool', [(i, (i + 2 * by) % npool) for i in range(npool)])  11.2 us
    ppermute x8, starting transfers between devices, gathered(): lax.ppermute(x, 'pool', [(i, i ^ 1) for i in range(npool)])  9.73 us
    ppermute x6, starting transfers between devices, gathered(): lax.ppermute(x, 'pool', [(i, (i + 2 * by) % npool) for i in range(npool)])  8.66 us
    ppermute x8, waiting for transfers between devices, gathered(): lax.ppermute(x, 'pool', [(i, i ^ 1) for i in range(npool)])  6.39 us
    pallas_call x1, Pallas kernels, local_attention(): pl.pallas_call(functools.partial(local_kernel, page_len, heads), out_shap...  4.61 us
    all_to_all x1, starting transfers between devices, shards(): lax.all_to_all(parts, 'pool', split_axis=0, concat_axis=0, tiled=True)  3.38 us
    pallas_call x2, Pallas kernels, fetched(): pl.pallas_call(functools.partial(fetch_kernel, part * weight.shape[0] //...  3.16 us
    pallas_call x1, Pallas kernels, rotated_pages(): pl.pallas_call(functools.partial(rope_kernel, npool, cache_pages, per), g...  2.96 us
  transfers between devices with their start and end apart: 16, of which 12 were waited for; matrix products, arithmetic and copies ran while one was open for 0% of the time, Pallas kernels for 19%

profile of v19, /device:TPU:0, one launch (start us, length us, event | category | flops | bytes accessed | tf_op | source)
XLA Modules:
  0.0 60.5 jit_solution(6316869376594607906)
XLA Ops:
  0.0 1.2 %asked_queries.1.refs_0_.q_ref = bf16[17,32,128]{2,1,0:T(8,128)(2,1)S(1)} custom-call(s32[3,16]{1,0:T(4,128)} %bitcast.3, s32[16]{0:T(128)} %context_ref.3, bf16[2,16,2048]{2,1,0:T(8,128)(2,1)} %q_ref.1), custom_call_target="tpu_custom_call" | custom-call | flops 100000 | bytes 300000 | tf_op jit(solution)/shard_map/asked_queries/pallas_call | solution.py:138
  1.2 5.1 %collective-permute-start.2 = (bf16[17,32,128]{2,1,0:T(8,128)(2,1)S(1)}, bf16[17,32,128]{2,1,0:T(8,128)(2,1)S(1)}, u32[]{:S(2)}, u32[]{:S(2)}) collective-permute-start(bf16[17,32,128]{2,1,0:T(8,128)(2,1)S(1)} %asked_queries.1.refs_0_.q_ref), channel_id=1, source_target_pairs={{0,12},{2,14},{4,0},{6,2},{8,4},{10,6},{12,8},{14,10},{1,13},{3,15... | collective-permute-start | bytes 417800 | tf_op jit(solution)/shard_map/ppermute | solution.py:564
  7.3 1.5 %collective-permute-start.3 = (bf16[17,32,128]{2,1,0:T(8,128)(2,1)S(1)}, bf16[17,32,128]{2,1,0:T(8,128)(2,1)S(1)}, u32[]{:S(2)}, u32[]{:S(2)}) collective-permute-start(bf16[17,32,128]{2,1,0:T(8,128)(2,1)S(1)} %asked_queries.1.refs_0_.q_ref), channel_id=1, source_target_pairs={{0,2},{2,0},{4,6},{6,4},{8,10},{10,8},{12,14},{14,12},{1,3},{3,1},... | collective-permute-start | bytes 417800 | tf_op jit(solution)/shard_map/ppermute | solution.py:565
  8.9 1.6 %collective-permute-done.2.refs_3_ = bf16[17,32,128]{2,1,0:T(8,128)(2,1)S(1)} collective-permute-done((bf16[17,32,128]{2,1,0:T(8,128)(2,1)S(1)}, bf16[17,32,128]{2,1,0:T(8,128)(2,1)S(1)}, u32[]{:S(2)}, u32[]{:S(2)}) %collective-permute-start.2) | collective-permute-done | bytes 139296 | tf_op jit(solution)/shard_map/ppermute | solution.py:564
  10.4 1.5 %collective-permute-start.6 = (bf16[17,32,128]{2,1,0:T(8,128)(2,1)S(1)}, bf16[17,32,128]{2,1,0:T(8,128)(2,1)S(1)}, u32[]{:S(2)}, u32[]{:S(2)}) collective-permute-start(bf16[17,32,128]{2,1,0:T(8,128)(2,1)S(1)} %collective-permute-done.2.refs_3_), channel_id=1, source_target_pairs={{0,2},{2,0},{4,6},{6,4},{8,10},{10,8},{12,14},{14,12},{1,3},{3,1},... | collective-permute-start | bytes 417800 | tf_op jit(solution)/shard_map/ppermute | solution.py:565
  11.9 6.2 %collective-permute-done.1.refs_2_ = bf16[17,32,128]{2,1,0:T(8,128)(2,1)S(1)} collective-permute-done((bf16[17,32,128]{2,1,0:T(8,128)(2,1)S(1)}, bf16[17,32,128]{2,1,0:T(8,128)(2,1)S(1)}, u32[]{:S(2)}, u32[]{:S(2)}) %collective-permute-start.1) | collective-permute-done | bytes 139296 | tf_op jit(solution)/shard_map/ppermute | solution.py:564
  18.1 1.5 %collective-permute-start.5 = (bf16[17,32,128]{2,1,0:T(8,128)(2,1)S(1)}, bf16[17,32,128]{2,1,0:T(8,128)(2,1)S(1)}, u32[]{:S(2)}, u32[]{:S(2)}) collective-permute-start(bf16[17,32,128]{2,1,0:T(8,128)(2,1)S(1)} %collective-permute-done.1.refs_2_), channel_id=1, source_target_pairs={{0,2},{2,0},{4,6},{6,4},{8,10},{10,8},{12,14},{14,12},{1,3},{3,1},... | collective-permute-start | bytes 417800 | tf_op jit(solution)/shard_map/ppermute | solution.py:565
  20.2 3.0 %rope_pages.1 = (bf16[16,2,2,128,128]{4,3,2,1,0:T(8,128)(2,1)S(1)}, s32[48]{0:T(128)S(1)}) custom-call(s32[16]{0:T(128)} %slot_ref.1, s32[1,4]{1,0:T(1,128)} %len_ref.1, bf16[16,2,2,128,128]{4,3,2,1,0:T(8,128)(2,1)} %pages_ref.1, f32[128,128]{1,0:T(8,128)} %constant.20.clone.ct_ref, f32[128,128]{1,0:T(8,128)} %constant.21.clone.st_ref, ...), custom_call_target="tpu_custom_call" | custom-call | flops 6000000 | bytes 2000000 | tf_op jit(solution)/shard_map/rope_pages/pallas_call | solution.py:86
  23.2 1.4 %collective-permute-done.5.refs_6_ = bf16[17,32,128]{2,1,0:T(8,128)(2,1)S(1)} collective-permute-done((bf16[17,32,128]{2,1,0:T(8,128)(2,1)S(1)}, bf16[17,32,128]{2,1,0:T(8,128)(2,1)S(1)}, u32[]{:S(2)}, u32[]{:S(2)}) %collective-permute-start.5) | collective-permute-done | bytes 139296 | tf_op jit(solution)/shard_map/ppermute | solution.py:565
  24.6 1.5 %collective-permute-done.4.refs_5_ = bf16[17,32,128]{2,1,0:T(8,128)(2,1)S(1)} collective-permute-done((bf16[17,32,128]{2,1,0:T(8,128)(2,1)S(1)}, bf16[17,32,128]{2,1,0:T(8,128)(2,1)S(1)}, u32[]{:S(2)}, u32[]{:S(2)}) %collective-permute-start.4) | collective-permute-done | bytes 139296 | tf_op jit(solution)/shard_map/ppermute | solution.py:565
  26.1 2.1 %arrived_attention.1 = bf16[8,80,128]{2,1,0:T(8,128)(2,1)} custom-call(s32[1]{0:T(128)} %bitcast.1.me_ref, s32[48]{0:T(128)S(1)} %get-tuple-element.15.own_ref, bf16[17,32,128]{2,1,0:T(8,128)(2,1)S(1)} %asked_queries.1.refs_0_.q_ref, bf16[17,32,128]{2,1,0:T(8,128)(2,1)S(1)} %collective-permute-done.refs_1_, ...), custom_call_target="tpu_custom_call" | custom-call | flops 200000000 | bytes 4000000 | tf_op jit(solution)/shard_map/arrived_attention/pallas_call | solution.py:377
  28.1 3.4 %all-to-all-start = ((bf16[8,80,128]{2,1,0:T(8,128)(2,1)}), bf16[8,80,128]{2,1,0:T(8,128)(2,1)S(1)}, u32[]{:S(2)}, u32[]{:S(2)}) async-start(bf16[8,80,128]{2,1,0:T(8,128)(2,1)} %arrived_attention.1), calls=%async_computation | async-start | bytes 327680 | tf_op jit(solution)/shard_map/all_to_all | solution.py:600
  31.6 4.6 %local_attention.1 = (f32[512,128]{1,0:T(8,128)S(1)}, f32[512,128]{1,0:T(8,128)S(1)}) custom-call(s32[3,16]{1,0:T(4,128)} %bitcast.4, s32[16]{0:T(128)} %context_ref.3, s32[48]{0:T(128)} %fill_ref.1, bf16[17,32,128]{2,1,0:T(8,128)(2,1)S(1)} %asked_queries.1.refs_0_.q_ref, bf16[2,16,512]{2,1,0:T(8,128)(2,1)S(1)} %reshape.3.new_ref, ...), custom_call_target="tpu_custom_call" | custom-call | flops 800000000 | bytes 12000000 | tf_op jit(solution)/shard_map/local_attention/pallas_call | solution.py:294
  36.2 2.8 %all-to-all-done.parts_ref = bf16[8,80,128]{2,1,0:T(8,128)(2,1)S(1)} async-done(((bf16[8,80,128]{2,1,0:T(8,128)(2,1)}), bf16[8,80,128]{2,1,0:T(8,128)(2,1)S(1)}, u32[]{:S(2)}, u32[]{:S(2)}) %all-to-all-start) | async-done | bytes 163872 | tf_op jit(solution)/shard_map/all_to_all | solution.py:600
  40.4 1.6 %fetch_weight.2 = (bf16[1024,1024]{1,0:T(8,128)(2,1)S(1)}, bf16[2,16,2048]{2,1,0:T(8,128)(2,1)S(1)}) custom-call(bf16[2048,1024]{1,0:T(8,128)(2,1)} %weight_ref.3, bf16[2,16,2048]{2,1,0:T(8,128)(2,1)S(1)} %merge.1.x_ref.refs_0_), custom_call_target="tpu_custom_call" | custom-call | bytes 4194304 | tf_op jit(solution)/shard_map/fetch_weight/pallas_call | solution.py:465
  42.0 1.9 %collective-permute-start.9 = (bf16[2,16,2048]{2,1,0:T(8,128)(2,1)S(1)}, bf16[2,16,2048]{2,1,0:T(8,128)(2,1)S(1)}, u32[]{:S(2)}, u32[]{:S(2)}) collective-permute-start(bf16[2,16,2048]{2,1,0:T(8,128)(2,1)S(1)} %get-tuple-element.19.x_ref), channel_id=1, source_target_pairs={{0,12},{2,14},{4,0},{6,2},{8,4},{10,6},{12,8},{14,10},{1,13},{3,15... | collective-permute-start | bytes 393224 | tf_op jit(solution)/shard_map/ppermute | solution.py:564
  44.0 1.6 %fetch_weight.3 = (bf16[1024,1024]{1,0:T(8,128)(2,1)S(1)}, bf16[2,16,2048]{2,1,0:T(8,128)(2,1)S(1)}) custom-call(bf16[2048,1024]{1,0:T(8,128)(2,1)} %weight_ref.3, bf16[2,16,2048]{2,1,0:T(8,128)(2,1)S(1)} %get-tuple-element.19.x_ref), custom_call_target="tpu_custom_call" | custom-call | bytes 4194304 | tf_op jit(solution)/shard_map/fetch_weight/pallas_call | solution.py:465
  45.7 1.4 %collective-permute-start.10 = (bf16[2,16,2048]{2,1,0:T(8,128)(2,1)S(1)}, bf16[2,16,2048]{2,1,0:T(8,128)(2,1)S(1)}, u32[]{:S(2)}, u32[]{:S(2)}) collective-permute-start(bf16[2,16,2048]{2,1,0:T(8,128)(2,1)S(1)} %merge.1.x_ref.refs_0_), channel_id=1, source_target_pairs={{0,2},{2,0},{4,6},{6,4},{8,10},{10,8},{12,14},{14,12},{1,3},{3,1},... | collective-permute-start | bytes 393224 | tf_op jit(solution)/shard_map/ppermute | solution.py:565
  47.2 1.5 %collective-permute-done.8.refs_2_ = bf16[2,16,2048]{2,1,0:T(8,128)(2,1)S(1)} collective-permute-done((bf16[2,16,2048]{2,1,0:T(8,128)(2,1)S(1)}, bf16[2,16,2048]{2,1,0:T(8,128)(2,1)S(1)}, u32[]{:S(2)}, u32[]{:S(2)}) %collective-permute-start.8) | collective-permute-done | bytes 131104 | tf_op jit(solution)/shard_map/ppermute | solution.py:564
  49.5 1.2 %collective-permute-start.13 = (bf16[2,16,2048]{2,1,0:T(8,128)(2,1)S(1)}, bf16[2,16,2048]{2,1,0:T(8,128)(2,1)S(1)}, u32[]{:S(2)}, u32[]{:S(2)}) collective-permute-start(bf16[2,16,2048]{2,1,0:T(8,128)(2,1)S(1)} %collective-permute-done.9.refs_3_), channel_id=1, source_target_pairs={{0,2},{2,0},{4,6},{6,4},{8,10},{10,8},{12,14},{14,12},{1,3},{3,1},... | collective-permute-start | bytes 393224 | tf_op jit(solution)/shard_map/ppermute | solution.py:565
  50.7 1.6 %collective-permute-done.7.refs_1_ = bf16[2,16,2048]{2,1,0:T(8,128)(2,1)S(1)} collective-permute-done((bf16[2,16,2048]{2,1,0:T(8,128)(2,1)S(1)}, bf16[2,16,2048]{2,1,0:T(8,128)(2,1)S(1)}, u32[]{:S(2)}, u32[]{:S(2)}) %collective-permute-start.7) | collective-permute-done | bytes 131104 | tf_op jit(solution)/shard_map/ppermute | solution.py:564
  52.4 1.5 %collective-permute-start.11 = (bf16[2,16,2048]{2,1,0:T(8,128)(2,1)S(1)}, bf16[2,16,2048]{2,1,0:T(8,128)(2,1)S(1)}, u32[]{:S(2)}, u32[]{:S(2)}) collective-permute-start(bf16[2,16,2048]{2,1,0:T(8,128)(2,1)S(1)} %collective-permute-done.7.refs_1_), channel_id=1, source_target_pairs={{0,2},{2,0},{4,6},{6,4},{8,10},{10,8},{12,14},{14,12},{1,3},{3,1},... | collective-permute-start | bytes 393224 | tf_op jit(solution)/shard_map/ppermute | solution.py:565
  54.1 1.4 %collective-permute-done.13.refs_7_ = bf16[2,16,2048]{2,1,0:T(8,128)(2,1)S(1)} collective-permute-done((bf16[2,16,2048]{2,1,0:T(8,128)(2,1)S(1)}, bf16[2,16,2048]{2,1,0:T(8,128)(2,1)S(1)}, u32[]{:S(2)}, u32[]{:S(2)}) %collective-permute-start.13) | collective-permute-done | bytes 131104 | tf_op jit(solution)/shard_map/ppermute | solution.py:565
  55.5 1.8 %collective-permute-done.11.refs_5_ = bf16[2,16,2048]{2,1,0:T(8,128)(2,1)S(1)} collective-permute-done((bf16[2,16,2048]{2,1,0:T(8,128)(2,1)S(1)}, bf16[2,16,2048]{2,1,0:T(8,128)(2,1)S(1)}, u32[]{:S(2)}, u32[]{:S(2)}) %collective-permute-start.11) | collective-permute-done | bytes 131104 | tf_op jit(solution)/shard_map/ppermute | solution.py:565
  (21 shorter events, 7.4 us)
Async XLA Ops:
  1.2 9.2 %collective-permute-start.2 = (bf16[17,32,128]{2,1,0:T(8,128)(2,1)S(1)}, bf16[17,32,128]{2,1,0:T(8,128)(2,1)S(1)}, u32[]{:S(2)}, u32[]{:S(2)}) collective-permute-start(bf16[17,32,128]{2,1,0:T(8,128)(2,1)S(1)} %asked_queries.1.refs_0_.q_ref), channel_id=1, source_target_pairs={{0,12},{2,14},{4,0},{6,2},{8,4},{10,6},{12,8},{14,10},{1,13},{3,15... | collective-permute-start | bytes 417800 | tf_op jit(solution)/shard_map/ppermute | solution.py:564
  6.3 11.8 %collective-permute-start.1 = (bf16[17,32,128]{2,1,0:T(8,128)(2,1)S(1)}, bf16[17,32,128]{2,1,0:T(8,128)(2,1)S(1)}, u32[]{:S(2)}, u32[]{:S(2)}) collective-permute-start(bf16[17,32,128]{2,1,0:T(8,128)(2,1)S(1)} %asked_queries.1.refs_0_.q_ref), channel_id=1, source_target_pairs={{0,8},{2,10},{4,12},{6,14},{8,0},{10,2},{12,4},{14,6},{1,9},{3,11}... | collective-permute-start | bytes 417800 | tf_op jit(solution)/shard_map/ppermute | solution.py:564
  6.3 13.3 %collective-permute-start = (bf16[17,32,128]{2,1,0:T(8,128)(2,1)S(1)}, bf16[17,32,128]{2,1,0:T(8,128)(2,1)S(1)}, u32[]{:S(2)}, u32[]{:S(2)}) collective-permute-start(bf16[17,32,128]{2,1,0:T(8,128)(2,1)S(1)} %asked_queries.1.refs_0_.q_ref), channel_id=1, source_target_pairs={{0,4},{2,6},{4,8},{6,10},{8,12},{10,14},{12,0},{14,2},{1,5},{3,7},... | collective-permute-start | bytes 417800 | tf_op jit(solution)/shard_map/ppermute | solution.py:564
  7.3 15.8 %collective-permute-start.3 = (bf16[17,32,128]{2,1,0:T(8,128)(2,1)S(1)}, bf16[17,32,128]{2,1,0:T(8,128)(2,1)S(1)}, u32[]{:S(2)}, u32[]{:S(2)}) collective-permute-start(bf16[17,32,128]{2,1,0:T(8,128)(2,1)S(1)} %asked_queries.1.refs_0_.q_ref), channel_id=1, source_target_pairs={{0,2},{2,0},{4,6},{6,4},{8,10},{10,8},{12,14},{14,12},{1,3},{3,1},... | collective-permute-start | bytes 417800 | tf_op jit(solution)/shard_map/ppermute | solution.py:565
  10.4 12.7 %collective-permute-start.6 = (bf16[17,32,128]{2,1,0:T(8,128)(2,1)S(1)}, bf16[17,32,128]{2,1,0:T(8,128)(2,1)S(1)}, u32[]{:S(2)}, u32[]{:S(2)}) collective-permute-start(bf16[17,32,128]{2,1,0:T(8,128)(2,1)S(1)} %collective-permute-done.2.refs_3_), channel_id=1, source_target_pairs={{0,2},{2,0},{4,6},{6,4},{8,10},{10,8},{12,14},{14,12},{1,3},{3,1},... | collective-permute-start | bytes 417800 | tf_op jit(solution)/shard_map/ppermute | solution.py:565
  18.1 6.4 %collective-permute-start.5 = (bf16[17,32,128]{2,1,0:T(8,128)(2,1)S(1)}, bf16[17,32,128]{2,1,0:T(8,128)(2,1)S(1)}, u32[]{:S(2)}, u32[]{:S(2)}) collective-permute-start(bf16[17,32,128]{2,1,0:T(8,128)(2,1)S(1)} %collective-permute-done.1.refs_2_), channel_id=1, source_target_pairs={{0,2},{2,0},{4,6},{6,4},{8,10},{10,8},{12,14},{14,12},{1,3},{3,1},... | collective-permute-start | bytes 417800 | tf_op jit(solution)/shard_map/ppermute | solution.py:565
  19.7 6.4 %collective-permute-start.4 = (bf16[17,32,128]{2,1,0:T(8,128)(2,1)S(1)}, bf16[17,32,128]{2,1,0:T(8,128)(2,1)S(1)}, u32[]{:S(2)}, u32[]{:S(2)}) collective-permute-start(bf16[17,32,128]{2,1,0:T(8,128)(2,1)S(1)} %collective-permute-done.refs_1_), channel_id=1, source_target_pairs={{0,2},{2,0},{4,6},{6,4},{8,10},{10,8},{12,14},{14,12},{1,3},{3,1},... | collective-permute-start | bytes 417800 | tf_op jit(solution)/shard_map/ppermute | solution.py:565
  23.1 8.4 %copy-start = (bf16[2,16,2,2,128]{4,3,2,1,0:T(2,128)(2,1)S(1)}, bf16[2,16,2,2,128]{4,3,2,1,0:T(2,128)(2,1)}, u32[]{:S(2)}) copy-start(bf16[2,16,2,2,128]{4,3,2,1,0:T(2,128)(2,1)} %param.24) | copy-start | bytes 98308
  28.1 10.9 %all-to-all-start = ((bf16[8,80,128]{2,1,0:T(8,128)(2,1)}), bf16[8,80,128]{2,1,0:T(8,128)(2,1)S(1)}, u32[]{:S(2)}, u32[]{:S(2)}) async-start(bf16[8,80,128]{2,1,0:T(8,128)(2,1)} %arrived_attention.1), calls=%async_computation | async-start | bytes 327680 | tf_op jit(solution)/shard_map/all_to_all | solution.py:600
  40.0 8.7 %collective-permute-start.8 = (bf16[2,16,2048]{2,1,0:T(8,128)(2,1)S(1)}, bf16[2,16,2048]{2,1,0:T(8,128)(2,1)S(1)}, u32[]{:S(2)}, u32[]{:S(2)}) collective-permute-start(bf16[2,16,2048]{2,1,0:T(8,128)(2,1)S(1)} %merge.1.x_ref.refs_0_), channel_id=1, source_target_pairs={{0,8},{2,10},{4,12},{6,14},{8,0},{10,2},{12,4},{14,6},{1,9},{3,11}... | collective-permute-start | bytes 393224 | tf_op jit(solution)/shard_map/ppermute | solution.py:564
  42.0 7.5 %collective-permute-start.9 = (bf16[2,16,2048]{2,1,0:T(8,128)(2,1)S(1)}, bf16[2,16,2048]{2,1,0:T(8,128)(2,1)S(1)}, u32[]{:S(2)}, u32[]{:S(2)}) collective-permute-start(bf16[2,16,2048]{2,1,0:T(8,128)(2,1)S(1)} %get-tuple-element.19.x_ref), channel_id=1, source_target_pairs={{0,12},{2,14},{4,0},{6,2},{8,4},{10,6},{12,8},{14,10},{1,13},{3,15... | collective-permute-start | bytes 393224 | tf_op jit(solution)/shard_map/ppermute | solution.py:564
  45.6 6.8 %collective-permute-start.7 = (bf16[2,16,2048]{2,1,0:T(8,128)(2,1)S(1)}, bf16[2,16,2048]{2,1,0:T(8,128)(2,1)S(1)}, u32[]{:S(2)}, u32[]{:S(2)}) collective-permute-start(bf16[2,16,2048]{2,1,0:T(8,128)(2,1)S(1)} %get-tuple-element.20), channel_id=1, source_target_pairs={{0,4},{2,6},{4,8},{6,10},{8,12},{10,14},{12,0},{14,2},{1,5},{3,7},... | collective-permute-start | bytes 393224 | tf_op jit(solution)/shard_map/ppermute | solution.py:564
  45.7 8.1 %collective-permute-start.10 = (bf16[2,16,2048]{2,1,0:T(8,128)(2,1)S(1)}, bf16[2,16,2048]{2,1,0:T(8,128)(2,1)S(1)}, u32[]{:S(2)}, u32[]{:S(2)}) collective-permute-start(bf16[2,16,2048]{2,1,0:T(8,128)(2,1)S(1)} %merge.1.x_ref.refs_0_), channel_id=1, source_target_pairs={{0,2},{2,0},{4,6},{6,4},{8,10},{10,8},{12,14},{14,12},{1,3},{3,1},... | collective-permute-start | bytes 393224 | tf_op jit(solution)/shard_map/ppermute | solution.py:565
  48.7 5.4 %collective-permute-start.12 = (bf16[2,16,2048]{2,1,0:T(8,128)(2,1)S(1)}, bf16[2,16,2048]{2,1,0:T(8,128)(2,1)S(1)}, u32[]{:S(2)}, u32[]{:S(2)}) collective-permute-start(bf16[2,16,2048]{2,1,0:T(8,128)(2,1)S(1)} %collective-permute-done.8.refs_2_), channel_id=1, source_target_pairs={{0,2},{2,0},{4,6},{6,4},{8,10},{10,8},{12,14},{14,12},{1,3},{3,1},... | collective-permute-start | bytes 393224 | tf_op jit(solution)/shard_map/ppermute | solution.py:565
  49.5 6.0 %collective-permute-start.13 = (bf16[2,16,2048]{2,1,0:T(8,128)(2,1)S(1)}, bf16[2,16,2048]{2,1,0:T(8,128)(2,1)S(1)}, u32[]{:S(2)}, u32[]{:S(2)}) collective-permute-start(bf16[2,16,2048]{2,1,0:T(8,128)(2,1)S(1)} %collective-permute-done.9.refs_3_), channel_id=1, source_target_pairs={{0,2},{2,0},{4,6},{6,4},{8,10},{10,8},{12,14},{14,12},{1,3},{3,1},... | collective-permute-start | bytes 393224 | tf_op jit(solution)/shard_map/ppermute | solution.py:565
  52.4 5.0 %collective-permute-start.11 = (bf16[2,16,2048]{2,1,0:T(8,128)(2,1)S(1)}, bf16[2,16,2048]{2,1,0:T(8,128)(2,1)S(1)}, u32[]{:S(2)}, u32[]{:S(2)}) collective-permute-start(bf16[2,16,2048]{2,1,0:T(8,128)(2,1)S(1)} %collective-permute-done.7.refs_1_), channel_id=1, source_target_pairs={{0,2},{2,0},{4,6},{6,4},{8,10},{10,8},{12,14},{14,12},{1,3},{3,1},... | collective-permute-start | bytes 393224 | tf_op jit(solution)/shard_map/ppermute | solution.py:565
  58.1 1.6 %collective-permute-start.14 = (bf16[2,128,512]{2,1,0:T(8,128)(2,1)S(1)}, bf16[2,128,512]{2,1,0:T(8,128)(2,1)S(1)}, u32[]{:S(2)}, u32[]{:S(2)}) collective-permute-start(bf16[2,128,512]{2,1,0:T(8,128)(2,1)S(1)} %get-tuple-element.24), channel_id=1, source_target_pairs={{0,1},{1,0},{2,3},{3,2},{4,5},{5,4},{6,7},{7,6},{8,9},{9,8},{10,11... | collective-permute-start | bytes 786440 | tf_op jit(solution)/shard_map/ppermute | solution.py:571
